TPU v7x, 32 devices: a whole 2x2x4 slice. The times are simulated.
32 devices in a mesh: grp: 2 (over x), fsdp: 4 (over y, core), dp: 4 (over z).
Axes of the slice: x: 2, y: 2, z: 4, core: 2. Of those that a mesh axis runs over, the one named last changes fastest.
Arguments:
- tokens: bfloat16 [2, 34816, 1024], P(None, ('grp', 'fsdp', 'dp')), may hold values from -6 to 6
- cotangent: bfloat16 [2, 34816, 1024], P(None, ('grp', 'fsdp', 'dp')), may hold values from -6 to 6
- lengths: int32 [2, 32, 8], P(None, ('grp', 'fsdp', 'dp')), may hold values from 0 to 1088, as said below
- selected: int32 [2, 32, 136], P(None, ('grp', 'fsdp', 'dp')), may hold values from 0 to 1087, as said below
- weights: float32 [12288, 1024], P(('fsdp', 'dp')), may hold values from -0.25 to 0.25
- vectors: float32 [3, 1024], replicated, may hold values from -0.09375 to 1.1
- first_moment: float32 [2, 12288, 1024], P('grp', ('fsdp', 'dp')), may hold values from -7.836799 to 7.836799
- second_moment: float32 [2, 12288, 1024], P('grp', ('fsdp', 'dp')), may hold values from 4.352 to 43.52
- vec_first: float32 [2, 3, 1024], P('grp'), may hold values from -186.59046 to 186.59046
- vec_second: float32 [2, 3, 1024], P('grp'), may hold values from 12.6208 to 55705.6
- outer_moment: float32 [12288, 1024], P(('fsdp', 'dp'), 'grp'), may hold values from -0.3125 to 0.3125
- smoothed_matrix_mean: float32 [12288, 1024], P(('fsdp', 'dp'), 'grp'), may hold values from -0.1875 to 0.1875
- vec_outer: float32 [3, 1024], replicated, may hold values from -1.25 to 1.25
- vec_average: float32 [3, 1024], replicated, may hold values from -0.3125 to 0.3125
Outputs:
- activations: bfloat16 [2, 34816, 1024], P(None, ('grp', 'fsdp', 'dp'))
- input_grad: bfloat16 [2, 34816, 1024], P(None, ('grp', 'fsdp', 'dp'))
- weights_new: float32 [12288, 1024], P(('fsdp', 'dp'))
- weights_low: bfloat16 [12288, 1024], P(('fsdp', 'dp'))
- first_new: float32 [2, 12288, 1024], P('grp', ('fsdp', 'dp'))
- second_new: float32 [2, 12288, 1024], P('grp', ('fsdp', 'dp'))
- outer_new: float32 [12288, 1024], P(('fsdp', 'dp'), 'grp')
- diff_mean: float32 [12288, 1024], P(('fsdp', 'dp'), 'grp')
- average_new: float32 [12288, 1024], P(('fsdp', 'dp'), 'grp')
- vectors_new: float32 [3, 1024], replicated
- vec_first_new: float32 [2, 3, 1024], P('grp')
- gains_second_new: float32 [2, 2, 1024], P('grp')
- router_second_new: float32 [2, 1024], P('grp')
- vec_outer_new: float32 [3, 1024], replicated
- vec_average_new: float32 [3, 1024], replicated
Inputs may be any that keep to these rules, and one draw needn't show every extreme that they name: Each device's 8 lengths are multiples of 8 that sum to 1088; zero marks an unused slot; in every draw some device holds a single sequence of 1088 tokens. Each device's selected positions ascend; a sequence of length L on it has exactly L / 8 of them, all inside it; the device's first and last positions are always among them.
All inputs are finite; a program needn't handle non-finite values.
Results may differ from a plain program's by a relative error of at most 0.018.
Values may be sent and summed in bfloat16 or wider, within the bound.
No kernel may reach another device: no remote copies, remote signals or barrier semaphores. Data moves between devices by JAX's collectives and lax.ppermute only.
A program may use at most 384 MiB of HBM per device.

v0:
```python
import jax
import jax.numpy as jnp
from jax import lax
from jax.sharding import PartitionSpec as P

HEAD = 64
INNER = 2
STEP = 5


EPS_NORM = 1e-06
EPS_ADAM = 1e-08
BETA_ONE = 0.9
BETA_TWO = 0.95
INNER_RATE = 0.03
DECAY_RATE = 0.1
OUTER_RATE = 0.7
OUTER_MOMENTUM = 0.9
AVERAGE_KEEP = 0.9


def segments_of(seq_lengths, positions):
    ends = jnp.cumsum(seq_lengths)
    sequence_indices = jnp.arange(positions, dtype=jnp.int32)
    return jnp.sum((ends[None, :] <= sequence_indices[:, None]).astype(jnp.int32), axis=1)


def contract_last(left, right):
    return lax.dot_general(
        left, right, (((1,), (1,)), ((), ())), preferred_element_type=jnp.float32
    )


def contract_first(left, right):
    return lax.dot_general(
        left, right, (((0,), (0,)), ((), ())), preferred_element_type=jnp.float32
    )


def split_rows(gathered, model_width):
    hidden_units = (gathered.shape[0] - 4 * model_width) // 2
    w_qkv = gathered[: 3 * model_width]
    w_out = gathered[3 * model_width : 4 * model_width]
    w_up = gathered[4 * model_width : 4 * model_width + hidden_units]
    w_down = gathered[4 * model_width + hidden_units :]
    return (w_qkv, w_out, w_up, w_down)


def attention_scores(query_rows, key_rows, allowed):
    selection_logits = jnp.einsum(
        "qhe,khe->hqk", query_rows, key_rows, preferred_element_type=jnp.float32
    ) * HEAD ** (-0.5)
    return jnp.where(allowed[None], selection_logits, -1e30)


def gelu_tanh(values):
    return jax.nn.gelu(values, approximate=True)


def norm_back(d_normed, normed, inverse):
    return inverse * (d_normed - normed * jnp.mean(d_normed * normed, axis=-1, keepdims=True))


def forward_pass(gathered, vec_now, tokens_now, seq_lengths, picked):
    model_width = tokens_now.shape[1]
    count_of_heads = model_width // HEAD
    picked_count = picked.shape[0]
    w_qkv, w_out, w_up, w_down = split_rows(gathered, model_width)
    segment_ids = segments_of(seq_lengths, tokens_now.shape[0])
    seg_picked = segment_ids[picked]
    sel_rows = tokens_now[picked].astype(jnp.float32)
    gate_value = jax.nn.sigmoid(jnp.dot(sel_rows, vec_now[2], precision=lax.Precision.HIGHEST))
    inv_one = lax.rsqrt(jnp.mean(sel_rows * sel_rows, axis=-1, keepdims=True) + EPS_NORM)
    normed_one = sel_rows * inv_one
    h1_low = (normed_one * vec_now[0]).astype(jnp.bfloat16)
    projected = contract_last(h1_low, w_qkv).astype(jnp.bfloat16)
    heads_view = projected.reshape(picked_count, 3, count_of_heads, HEAD)
    allowed = (seg_picked[:, None] == seg_picked[None, :]) & (picked[None, :] <= picked[:, None])
    selection_logits = attention_scores(heads_view[:, 0], heads_view[:, 1], allowed)
    row_max = jnp.max(selection_logits, axis=-1, keepdims=True)
    log_total = row_max + jnp.log(
        jnp.sum(jnp.exp(selection_logits - row_max), axis=-1, keepdims=True)
    )
    probs_low = jnp.exp(selection_logits - log_total).astype(jnp.bfloat16)
    mixed = jnp.einsum(
        "hqk,khe->qhe", probs_low, heads_view[:, 2], preferred_element_type=jnp.float32
    )
    mixed = mixed.reshape(picked_count, model_width).astype(jnp.bfloat16)
    attn_out = contract_last(mixed, w_out)
    first_sum = sel_rows + attn_out
    inv_two = lax.rsqrt(jnp.mean(first_sum * first_sum, axis=-1, keepdims=True) + EPS_NORM)
    normed_two = first_sum * inv_two
    h2_low = (normed_two * vec_now[1]).astype(jnp.bfloat16)
    pre_act = contract_last(h2_low, w_up)
    act_low = gelu_tanh(pre_act).astype(jnp.bfloat16)
    down_out = jnp.dot(act_low, w_down, preferred_element_type=jnp.float32)
    branch = attn_out + down_out
    out_rows = sel_rows + gate_value[:, None] * branch
    return {
        "gate_value": gate_value,
        "sel_rows": sel_rows,
        "inv_one": inv_one,
        "normed_one": normed_one,
        "h1_low": h1_low,
        "projected": projected,
        "allowed": allowed,
        "log_total": log_total,
        "mixed": mixed,
        "inv_two": inv_two,
        "normed_two": normed_two,
        "h2_low": h2_low,
        "pre_act": pre_act,
        "act_low": act_low,
        "branch": branch,
        "out_rows": out_rows,
    }


def backward_pass(gathered, vec_now, saved, cot_now, picked):
    model_width = cot_now.shape[1]
    count_of_heads = model_width // HEAD
    picked_count = picked.shape[0]
    w_qkv, w_out, w_up, w_down = split_rows(gathered, model_width)
    cot_rows = cot_now[picked].astype(jnp.float32)
    gate_value = saved["gate_value"]
    d_branch = gate_value[:, None] * cot_rows
    d_logit = jnp.sum(cot_rows * saved["branch"], axis=-1) * gate_value * (1.0 - gate_value)
    d_down = d_branch.astype(jnp.bfloat16)
    d_act = contract_last(d_down, w_down)
    gelu_pull = jax.vjp(gelu_tanh, saved["pre_act"])[1]
    d_pre = gelu_pull(d_act)[0].astype(jnp.bfloat16)
    d_h2 = jnp.dot(d_pre, w_up, preferred_element_type=jnp.float32)
    grad_gain_two = jnp.sum(d_h2 * saved["normed_two"], axis=0)
    d_first = norm_back(d_h2 * vec_now[1], saved["normed_two"], saved["inv_two"])
    d_attn_low = (d_branch + d_first).astype(jnp.bfloat16)
    d_mixed = jnp.dot(d_attn_low, w_out, preferred_element_type=jnp.float32).astype(jnp.bfloat16)
    d_mixed = d_mixed.reshape(picked_count, count_of_heads, HEAD)
    heads_view = saved["projected"].reshape(picked_count, 3, count_of_heads, HEAD)
    query_rows = heads_view[:, 0]
    key_rows = heads_view[:, 1]
    value_rows = heads_view[:, 2]
    selection_logits = attention_scores(query_rows, key_rows, saved["allowed"])
    attn_probs = jnp.exp(selection_logits - saved["log_total"])
    probs_low = attn_probs.astype(jnp.bfloat16)
    d_probs = jnp.einsum("qhe,khe->hqk", d_mixed, value_rows, preferred_element_type=jnp.float32)
    d_scores = attn_probs * (d_probs - jnp.sum(d_probs * attn_probs, axis=-1, keepdims=True))
    d_scores = d_scores.astype(jnp.bfloat16)
    grad_query = jnp.einsum(
        "hqk,khe->qhe", d_scores, key_rows, preferred_element_type=jnp.float32
    ) * HEAD ** (-0.5)
    grad_key = jnp.einsum(
        "hqk,qhe->khe", d_scores, query_rows, preferred_element_type=jnp.float32
    ) * HEAD ** (-0.5)
    grad_value = jnp.einsum("hqk,qhe->khe", probs_low, d_mixed, preferred_element_type=jnp.float32)
    d_proj = jnp.stack([grad_query, grad_key, grad_value], axis=1).reshape(
        picked_count, 3 * model_width
    )
    d_proj = d_proj.astype(jnp.bfloat16)
    d_h1 = jnp.dot(d_proj, w_qkv, preferred_element_type=jnp.float32)
    derivative_first_gain_factor = jnp.sum(d_h1 * saved["normed_one"], axis=0)
    d_zero = norm_back(d_h1 * vec_now[0], saved["normed_one"], saved["inv_one"])
    d_rows = cot_rows + d_first + d_zero + d_logit[:, None] * vec_now[2][None, :]
    grad_router = jnp.dot(d_logit, saved["sel_rows"], precision=lax.Precision.HIGHEST)
    grad_vec = jnp.stack([derivative_first_gain_factor, grad_gain_two, grad_router])
    columns = jnp.concatenate([d_proj, d_attn_low, d_pre, saved["act_low"]], axis=1)
    operands = (saved["h1_low"], saved["mixed"], saved["h2_low"], d_down)
    return (d_rows, grad_vec, columns, operands)


def local_gradient(columns, operands, model_width):
    hidden_units = (columns.shape[1] - 4 * model_width) // 2
    bounds = [0, 3 * model_width, 4 * model_width, 4 * model_width + hidden_units, columns.shape[1]]
    pieces = [
        contract_first(columns[:, bounds[index] : bounds[index + 1]], operands[index])
        for index in range(4)
    ]
    return jnp.concatenate(pieces, axis=0)


def adamw(param, grad, first, second, step_count, rate, decay):
    first = BETA_ONE * first + (1.0 - BETA_ONE) * grad
    second = BETA_TWO * second + (1.0 - BETA_TWO) * grad * grad
    fixed_one = 1.0 - BETA_ONE**step_count
    fixed_two = 1.0 - BETA_TWO**step_count
    direction = first / fixed_one / (jnp.sqrt(second / fixed_two) + EPS_ADAM)
    return (param - rate * (direction + decay * param), first, second)


def vector_rates():
    return jnp.array([[0.1], [0.1], [0.02]], dtype=jnp.float32)


def on_device(
    tokens,
    cotangent,
    lengths,
    selected,
    weights,
    vectors,
    first_moment,
    second_moment,
    vec_first,
    vec_second,
    outer_moment,
    smoothed_matrix_mean,
    vec_outer,
    vec_average,
):
    master = weights
    vec_now = vectors
    first_now = first_moment[0]
    second_now = second_moment[0]
    vfirst_now = vec_first[0]
    vsecond_now = vec_second[0]
    model_width = tokens.shape[2]
    forward_steps = []
    backward_steps = []
    for inner_step in range(INNER):
        tokens_now = tokens[inner_step]
        cot_now = cotangent[inner_step]
        seq_lengths = lengths[inner_step, 0]
        picked = selected[inner_step, 0]
        shard_low = master.astype(jnp.bfloat16)
        gathered = lax.all_gather(shard_low, ("fsdp", "dp"), axis=0, tiled=True)
        saved = forward_pass(gathered, vec_now, tokens_now, seq_lengths, picked)
        forward_steps.append(tokens_now.at[picked].set(saved["out_rows"].astype(jnp.bfloat16)))
        gathered = lax.all_gather(shard_low, ("fsdp", "dp"), axis=0, tiled=True)
        d_rows, grad_vec, columns, operands = backward_pass(
            gathered, vec_now, saved, cot_now, picked
        )
        backward_steps.append(cot_now.at[picked].set(d_rows.astype(jnp.bfloat16)))
        grad_full = local_gradient(columns, operands, model_width)
        grad_shard = lax.psum_scatter(grad_full, ("fsdp", "dp"), scatter_dimension=0, tiled=True)
        grad_vec = lax.psum(grad_vec, ("fsdp", "dp"))
        step_count = STEP + inner_step
        master, first_now, second_now = adamw(
            master, grad_shard, first_now, second_now, step_count, INNER_RATE, DECAY_RATE
        )
        vec_now, vfirst_now, vsecond_now = adamw(
            vec_now, grad_vec, vfirst_now, vsecond_now, step_count, vector_rates(), 0.0
        )
    groups = lax.axis_size("grp")
    delta = weights - master
    vector_change = vectors - vec_now
    col_width = weights.shape[1] // groups
    col_start = lax.axis_index("grp") * col_width
    diff_share = (
        lax.psum_scatter(delta.astype(jnp.bfloat16), "grp", scatter_dimension=1, tiled=True).astype(
            jnp.float32
        )
        / groups
    )
    vec_diff = lax.psum(vector_change, "grp") / groups
    moment_share = OUTER_MOMENTUM * outer_moment + diff_share
    base_share = lax.dynamic_slice_in_dim(weights, col_start, col_width, 1)
    new_share = base_share - OUTER_RATE * (diff_share + OUTER_MOMENTUM * moment_share)
    weights_new = lax.all_gather(new_share.astype(jnp.bfloat16), "grp", axis=1, tiled=True).astype(
        new_share.dtype
    )
    average_new = AVERAGE_KEEP * smoothed_matrix_mean + (1.0 - AVERAGE_KEEP) * new_share
    vec_moment = OUTER_MOMENTUM * vec_outer + vec_diff
    vectors_new = vectors - OUTER_RATE * (vec_diff + OUTER_MOMENTUM * vec_moment)
    vec_average_new = AVERAGE_KEEP * vec_average + (1.0 - AVERAGE_KEEP) * vectors_new
    return (
        jnp.stack(forward_steps),
        jnp.stack(backward_steps),
        weights_new,
        weights_new.astype(jnp.bfloat16),
        first_now[None],
        second_now[None],
        moment_share,
        diff_share,
        average_new,
        vectors_new,
        vfirst_now[None],
        vsecond_now[None, :2],
        vsecond_now[None, 2],
        vec_moment,
        vec_average_new,
    )


def solution(mesh):
    placed = (
        P(None, ("grp", "fsdp", "dp"), None),
        P(None, ("grp", "fsdp", "dp"), None),
        P(None, ("grp", "fsdp", "dp"), None),
        P(None, ("grp", "fsdp", "dp"), None),
        P(("fsdp", "dp"), None),
        P(),
        P("grp", ("fsdp", "dp"), None),
        P("grp", ("fsdp", "dp"), None),
        P("grp", None, None),
        P("grp", None, None),
        P(("fsdp", "dp"), "grp"),
        P(("fsdp", "dp"), "grp"),
        P(),
        P(),
    )
    return jax.shard_map(
        on_device,
        mesh=mesh,
        in_specs=placed,
        out_specs=(
            P(None, ("grp", "fsdp", "dp"), None),
            P(None, ("grp", "fsdp", "dp"), None),
            P(("fsdp", "dp"), None),
            P(("fsdp", "dp"), None),
            P("grp", ("fsdp", "dp"), None),
            P("grp", ("fsdp", "dp"), None),
            P(("fsdp", "dp"), "grp"),
            P(("fsdp", "dp"), "grp"),
            P(("fsdp", "dp"), "grp"),
            P(),
            P("grp", None, None),
            P("grp", None, None),
            P("grp", None),
            P(),
            P(),
        ),
        check_vma=False,
    )
```

profile of v0, /device:TPU:0, one launch (start us, length us, event | category | flops | bytes accessed | tf_op | source)
XLA Modules:
  0.0 1600.0 jit_solution(9886027862984300894)
XLA Ops:
  7.2 3.3 convert_element_type.139
  11.5 1.4 gather_fusion.1
  12.9 4.1 slice_bitcast_fusion.3
  17.0 1.4 copy-done.3
  19.3 4.4 slice_bitcast_fusion
  25.9 123.3 %all-gather.4.cloned.1.call-done = bf16[12288,1024]{1,0:T(8,128)(2,1)} async-done(((bf16[768,1024]{1,0:T(8,128)(2,1)}), bf16[12288,1024]{1,0:T(8,128)(2,1)}) %all-gather.4.cloned.1.call-update) | async-done | bytes 25165840 | tf_op jit(solution)/shard_map/all_gather | solution.py:224
  149.2 5.9 fusion.24
  155.1 2.9 copy.99
  158.1 1.8 fusion.58
  160.4 1.7 convolution_convert_fusion.3
  162.2 2.8 multiply_reduce_fusion.7
  165.0 6.5 fusion.14
  171.5 6.7 fusion.100
  178.2 7.0 fusion.38
  185.2 5.3 multiply_reduce_fusion.5
  192.3 2.8 fusion.76
  195.1 2.0 copy.100
  197.0 1.8 fusion.64
  201.7 2.8 fusion.186
  204.5 8.2 fusion.149
  212.7 8.2 fusion.179
  222.4 6.4 fusion.152
  228.8 35.9 %pad_maximum_fusion = f32[12288,1024]{1,0:T(8,128)} fusion(f32[4096,1024]{1,0:T(8,128)} %fusion.149, f32[4096,1024]{1,0:T(8,128)} %fusion.179, f32[1024,1024]{1,0:T(8,128)} %fusion.186, f32[3072,1024]{1,0:T(8,128)} %fusion.152), kind=kLoop, calls=%fused_computation.10 | loop fusion | flops 37748736 | bytes 100663296 | tf_op jit(solution)/shard_map/concatenate | solution.py:177
  264.8 467.9 %reduce-scatter.4.cloned.1.call-done = f32[768,1024]{1,0:T(8,128)} async-done(((f32[12288,1024]{1,0:T(8,128)}), f32[768,1024]{1,0:T(8,128)}) %reduce-scatter.4.cloned.1.call-update) | async-done | bytes 3145744 | tf_op jit(solution)/shard_map/reduce_scatter | solution.py:233
  732.6 6.1 fusion.168
  739.1 1.4 gather_fusion.4
  740.5 3.7 gather_fusion.2
  744.2 3.8 gather_fusion.5
  749.5 5.8 fusion.115
  755.4 61.3 %psum.21 = f32[3,1024]{1,0:T(4,128)S(1)} all-reduce(f32[3,1024]{1,0:T(4,128)S(1)} %pad_maximum_fusion.6), channel_id=1, replica_groups=mesh['grp'=2,'fsdp'=4,'dp'=4] {'fsdp','dp'}, use_global_device_ids=true, to_apply=%region_12.13 | all-reduce | flops 3072 | bytes 24576 | tf_op jit(solution)/shard_map/psum | solution.py:234
  817.4 1.9 fusion.160
  819.3 57.2 %all-gather.6.cloned.1.call-done = bf16[12288,1024]{1,0:T(8,128)(2,1)} async-done(((bf16[768,1024]{1,0:T(8,128)(2,1)}), bf16[12288,1024]{1,0:T(8,128)(2,1)}) %all-gather.6.cloned.1.call-update) | async-done | bytes 25165840 | tf_op jit(solution)/shard_map/all_gather | solution.py:224
  876.4 6.0 fusion.27
  882.5 2.8 copy.101
  885.3 1.8 fusion.59
  887.6 2.0 convolution_convert_fusion.1
  889.7 2.7 multiply_reduce_fusion.4
  892.5 6.5 fusion.6
  899.0 6.7 fusion.107
  906.3 7.0 fusion.45
  913.4 5.9 multiply_reduce_fusion.2
  920.8 2.8 fusion.79
  923.6 2.0 copy.102
  925.5 2.6 fusion.65
  928.1 2.1 multiply_reduce_fusion
  932.7 2.8 fusion.187
  935.5 8.3 fusion.146
  943.8 8.3 fusion.180
  953.6 6.4 fusion.155
  960.0 35.9 %pad_maximum_fusion.1 = f32[12288,1024]{1,0:T(8,128)} fusion(f32[4096,1024]{1,0:T(8,128)} %fusion.146, f32[4096,1024]{1,0:T(8,128)} %fusion.180, f32[1024,1024]{1,0:T(8,128)} %fusion.187, f32[3072,1024]{1,0:T(8,128)} %fusion.155), kind=kLoop, calls=%fused_computation.11 | loop fusion | flops 37748736 | bytes 100663296 | tf_op jit(solution)/shard_map/concatenate | solution.py:177
  996.0 467.9 %reduce-scatter.6.cloned.1.call-done = f32[768,1024]{1,0:T(8,128)} async-done(((f32[12288,1024]{1,0:T(8,128)}), f32[768,1024]{1,0:T(8,128)}) %reduce-scatter.6.cloned.1.call-update) | async-done | bytes 3145744 | tf_op jit(solution)/shard_map/reduce_scatter | solution.py:233
  1463.9 11.3 fusion.93
  1475.3 5.1 scatter_custom_fusion
  1480.5 5.9 scatter_custom_fusion.2
  1486.3 5.2 scatter_custom_fusion.1
  1491.8 5.7 fusion.112
  1497.6 60.5 %psum.22 = f32[3,1024]{1,0:T(4,128)S(1)} all-reduce(f32[3,1024]{1,0:T(4,128)S(1)} %pad_maximum_fusion.7), channel_id=1, replica_groups=mesh['grp'=2,'fsdp'=4,'dp'=4] {'fsdp','dp'}, use_global_device_ids=true, to_apply=%region_32.33 | all-reduce | flops 3072 | bytes 24576 | tf_op jit(solution)/shard_map/psum | solution.py:234
  1558.1 5.1 multiply_add_fusion.1
  1565.3 6.3 scatter_custom_fusion.3
  1571.5 8.3 psum.23
  1581.1 5.8 pad_maximum_fusion.2
  1586.9 1.3 all-gather.8.cloned.1.call-done
  1588.2 3.6 convert_element_type.180
  1591.8 1.1 copy.124
  (221 shorter events, 23.4 us)
Async XLA Ops:
  7.2 3.4 copy-start.75
  7.2 3.6 copy-start.68
  7.2 142.0 %all-gather.4.cloned.1.call-start = ((), (), s32[]{:S(2)}) async-start(), calls=%async_computation.3 | async-start | bytes 26738688 | tf_op jit(solution)/shard_map/all_gather | solution.py:224
  10.6 722.1 %reduce-scatter.4.cloned.1.call-start = ((), (), s32[]{:S(2)}) async-start(), calls=%async_computation.4 | async-start | bytes 53477376 | tf_op jit(solution)/shard_map/reduce_scatter | solution.py:233
  10.8 728.2 %copy-start.71 = (s32[136,1]{0,1:T(1,128)}, s32[136,1]{0,1:T(1,128)S(1)}, u32[]{:S(2)}) copy-start(s32[136,1]{0,1:T(1,128)S(1)} %get-tuple-element.57) | copy-start | bytes 1636
  23.7 131.4 %copy-start.2 = (bf16[1088,1024]{1,0:T(8,128)(2,1)}, bf16[1088,1024]{1,0:T(8,128)(2,1)S(1)}, u32[]{:S(2)}) copy-start(bf16[1088,1024]{1,0:T(8,128)(2,1)S(1)} %get-tuple-element.45) | copy-start | bytes 6684676
  24.6 179.8 %copy-start.17 = (bf16[136,1024]{1,0:T(8,128)(2,1)}, bf16[136,1024]{1,0:T(8,128)(2,1)S(1)}, u32[]{:S(2)}) copy-start(bf16[136,1024]{1,0:T(8,128)(2,1)S(1)} %gather_fusion.3) | copy-start | bytes 835588
  24.8 724.7 %copy-start.58 = (f32[136]{0:T(256)}, f32[136]{0:T(256)S(1)}, u32[]{:S(2)}) copy-start(f32[136]{0:T(256)S(1)} %add_rsqrt_fusion.3) | copy-start | bytes 1636
  25.4 187.3 %copy-start.41 = (f32[1,1024]{1,0:T(1,128)}, f32[1,1024]{1,0:T(1,128)S(1)}, u32[]{:S(2)}) copy-start(f32[1,1024]{1,0:T(1,128)S(1)} %get-tuple-element.49) | copy-start | bytes 12292
  162.2 2.8 copy-start.26
  164.9 47.8 %copy-start.9 = (f32[136,1024]{1,0:T(8,128)}, f32[136,1024]{1,0:T(8,128)S(1)}, u32[]{:S(2)}) copy-start(f32[136,1024]{1,0:T(8,128)S(1)} %get-tuple-element.40) | copy-start | bytes 1671172
  165.0 47.8 %copy-start.51 = (f32[136]{0:T(256)}, f32[136]{0:T(256)S(1)}, u32[]{:S(2)}) copy-start(f32[136]{0:T(256)S(1)} %add_rsqrt_fusion.2) | copy-start | bytes 1636
  171.4 6.7 copy-start.20
  178.2 26.3 %copy-start.54 = (f32[136]{0:T(256)}, f32[136]{0:T(256)S(1)}, u32[]{:S(2)}) copy-start(f32[136]{0:T(256)S(1)} %get-tuple-element.38) | copy-start | bytes 1636
  178.2 571.1 %copy-start.62 = (f32[136]{0:T(256)}, f32[136]{0:T(256)S(1)}, u32[]{:S(2)}) copy-start(f32[136]{0:T(256)S(1)} %get-tuple-element.37) | copy-start | bytes 1636
  185.2 5.3 copy-start.32
  190.6 4.5 copy-start.65
  201.7 2.8 copy-start.21
  204.5 8.3 copy-start.33
  264.7 467.9 %copy-start = (f32[768,1024]{1,0:T(8,128)S(1)}, f32[768,1024]{1,0:T(8,128)}, u32[]{:S(2)}) copy-start(f32[768,1024]{1,0:T(8,128)} %param.20) | copy-start | bytes 9437188
  264.7 611.7 %all-gather.6.cloned.1.call-start = ((), (), s32[]{:S(2)}) async-start(), calls=%async_computation.5 | async-start | bytes 26738688 | tf_op jit(solution)/shard_map/all_gather | solution.py:224
  738.7 725.1 %reduce-scatter.6.cloned.1.call-start = ((), (), s32[]{:S(2)}) async-start(), calls=%async_computation.6 | async-start | bytes 53477376 | tf_op jit(solution)/shard_map/reduce_scatter | solution.py:233
  749.1 127.3 %copy-start.60 = (f32[136]{0:T(256)}, f32[136]{0:T(256)S(1)}, u32[]{:S(2)}) copy-start(f32[136]{0:T(256)S(1)} %add_rsqrt_fusion.1) | copy-start | bytes 1636
  749.5 67.2 %copy-start.43 = (f32[1,3,1024]{2,0,1:T(1,128)S(1)}, f32[1,3,1024]{2,0,1:T(1,128)}, u32[]{:S(2)}) copy-start(f32[1,3,1024]{2,0,1:T(1,128)} %param.24) | copy-start | bytes 36868
  749.5 67.2 %copy-start.44 = (f32[1,3,1024]{2,0,1:T(1,128)S(1)}, f32[1,3,1024]{2,0,1:T(1,128)}, u32[]{:S(2)}) copy-start(f32[1,3,1024]{2,0,1:T(1,128)} %param.25) | copy-start | bytes 36868
  749.5 67.2 %copy-start.73 = (f32[3]{0:T(128)S(1)}, f32[3]{0:T(128)}, u32[]{:S(2)}) copy-start(f32[3]{0:T(128)} %constant.110) | copy-start | bytes 40
  817.4 674.4 %copy-start.45 = (f32[1,1024]{1,0:T(1,128)}, f32[1,1024]{1,0:T(1,128)S(1)}, u32[]{:S(2)}) copy-start(f32[1,1024]{1,0:T(1,128)S(1)} %get-tuple-element.53) | copy-start | bytes 12292
  887.1 2.6 copy-start.4
  889.7 2.8 copy-start.28
  892.4 26.8 %copy-start.10 = (f32[136,1024]{1,0:T(8,128)}, f32[136,1024]{1,0:T(8,128)S(1)}, u32[]{:S(2)}) copy-start(f32[136,1024]{1,0:T(8,128)S(1)} %get-tuple-element.36) | copy-start | bytes 1671172
  892.5 51.4 %copy-start.53 = (f32[136]{0:T(256)}, f32[136]{0:T(256)S(1)}, u32[]{:S(2)}) copy-start(f32[136]{0:T(256)S(1)} %add_rsqrt_fusion) | copy-start | bytes 1636
  892.5 6.5 copy-start.18
  899.0 7.4 copy-start.22
  899.0 6.7 copy-start.69
  906.3 13.0 copy-start.56
  913.4 5.9 copy-start.34
  925.5 2.6 copy-start.5
  925.5 2.6 copy-start.31
  932.7 2.8 copy-start.19
  932.7 2.8 copy-start.23
  932.7 2.8 copy-start.57
  935.5 8.3 copy-start.11
  935.5 8.3 copy-start.35
  995.9 479.4 %copy-start.55 = (f32[136]{0:T(256)S(1)}, f32[136]{0:T(256)}, u32[]{:S(2)}) copy-start(f32[136]{0:T(256)} %copy-done.54) | copy-start | bytes 1636
  995.9 562.2 %reduce-scatter.8.cloned.1.call-start = ((), (), s32[]{:S(2)}) async-start(), calls=%async_computation.7 | async-start | bytes 2359296 | tf_op jit(solution)/shard_map/reduce_scatter | solution.py:248
  1475.1 5.3 copy-start.76
  1475.1 5.3 copy-start.42
  1475.1 5.3 copy-start.47
  1475.1 5.3 copy-start.52
  1475.2 5.3 copy-start.59
  1475.2 5.3 copy-start.63
  1475.2 5.3 copy-start.66
  1475.2 113.0 %all-gather.8.cloned.1.call-start = ((), (), s32[]{:S(2)}) async-start(), calls=%async_computation.8 | async-start | bytes 2359296 | tf_op jit(solution)/shard_map/all_gather | solution.py:257
  1486.3 5.2 copy-start.8
  1486.3 5.2 copy-start.64
  1491.8 5.7 copy-start.70
  1558.1 5.2 copy-start.74
  1558.1 7.2 copy-start.77
  1558.1 7.2 copy-start.46
  1558.1 7.2 copy-start.48
  1565.2 15.2 copy-start.49
  1565.2 15.2 copy-start.50
  1565.3 15.8 copy-start.1
  1588.2 3.6 copy-start.14
  (20 other events, 23.6 us)
Sparse Core Ops, SparseCore 0:
  10.7 138.4 all-gather.3
  264.8 467.7 reduce-scatter.3
  738.9 137.5 all-gather.5
  996.0 467.8 reduce-scatter.5
  1475.3 25.1 reduce-scatter.7
  1563.3 24.7 all-gather.7
where the time goes:
time: 1610 us; the launch traced here: 1600 us
  waiting for transfers between devices  1120 us (70%)
  matrix products  157 us (10%)
  other arithmetic  137 us (9%)
  blocking collectives  130 us (8%)
  local copies, waits for them, and re-layouts  43.1 us (3%)
    reduce_scatter x2, waiting for transfers between devices, on_device(): lax.psum_scatter(grad_full, ('fsdp', 'dp'), scatter_dimension=0, tiled=True)  936 us
    all_gather x2, waiting for transfers between devices, on_device(): gathered = lax.all_gather(shard_low, ('fsdp', 'dp'), axis=0, tiled=True)  181 us
    psum x2, blocking collectives, on_device(): grad_vec = lax.psum(grad_vec, ('fsdp', 'dp'))  122 us
    concatenate x2, other arithmetic, local_gradient(): return jnp.concatenate(pieces, axis=0)  71.7 us
    dot_general x8, matrix products, contract_first(): lax.dot_general(left, right, (((0,), (0,)), ((), ())), preferred_element_...  51.4 us
    dot_general x8, matrix products, contract_last(): lax.dot_general(left, right, (((1,), (1,)), ((), ())), preferred_element_...  44.5 us
  transfers between devices with their start and end apart: 6, of which 5 were waited for; matrix products, arithmetic and copies ran while one was open for 4% of the time, Pallas kernels for 0%

commit v1 on v0

--- a/solution.py
+++ b/solution.py
@@ -1,5 +1,6 @@
 import jax
 import jax.numpy as jnp
+import numpy as np
 from jax import lax
 from jax.sharding import PartitionSpec as P
 
@@ -167,14 +168,122 @@
     return (d_rows, grad_vec, columns, operands)
 
 
-def local_gradient(columns, operands, model_width):
+def pad_rows(rows):
+    return jnp.pad(rows, ((0, -rows.shape[0] % 16), (0, 0)))
+
+
+def swap(values, axis, delta):
+    size = lax.axis_size(axis)
+    return lax.ppermute(values, axis, [(i, i ^ delta) for i in range(size)])
+
+
+def sum_over(values, axes):
+    for axis in axes:
+        delta = 1
+        while delta < lax.axis_size(axis):
+            values = values + swap(values, axis, delta)
+            delta *= 2
+    return values
+
+
+def line_order(line):
+    due = np.zeros((line, line), np.int32)
+    for here in range(line):
+        for there in range(line):
+            if there > here:
+                due[here, there] = line - 1 - there + here
+            elif there < here:
+                due[here, there] = there - here + line - 1
+            else:
+                due[here, there] = line
+    return np.argsort(due, axis=1, kind="stable").astype(np.int32)
+
+
+def line_slots(line, order):
+    ups = np.zeros((line - 1, line), np.int32)
+    downs = np.zeros((line - 1, line), np.int32)
+    for step in range(line - 1):
+        for here in range(line):
+            if here <= step:
+                ups[step, here] = list(order[here]).index(line - 1 - step + here)
+            if line - 1 - here <= step:
+                downs[step, here] = list(order[here]).index(step - (line - 1) + here)
+    return ups, downs
+
+
+def choose(terms, slots, here):
+    used = sorted(set(int(slot) for slot in slots))
+    picked = terms[used[0]]
+    for slot in used[1:]:
+        picked = jnp.where(jnp.asarray(slots)[here] == slot, terms[slot], picked)
+    return picked
+
+
+def gradient_share(columns, operands, shard_rows, model_width):
+    planes, line = lax.axis_size("fsdp"), lax.axis_size("dp")
+    plane, here = lax.axis_index("fsdp"), lax.axis_index("dp")
+    columns = pad_rows(columns)
+    tokens = columns.shape[0]
     hidden_units = (columns.shape[1] - 4 * model_width) // 2
-    bounds = [0, 3 * model_width, 4 * model_width, 4 * model_width + hidden_units, columns.shape[1]]
-    pieces = [
-        contract_first(columns[:, bounds[index] : bounds[index + 1]], operands[index])
-        for index in range(4)
-    ]
-    return jnp.concatenate(pieces, axis=0)
+    edges = (3 * model_width, 4 * model_width, 4 * model_width + hidden_units)
+    stacked = jnp.stack([pad_rows(operand) for operand in operands])[:, None]
+    deltas = [0]
+    bit = planes // 2
+    while bit >= 1:
+        stacked = jnp.concatenate([stacked, swap(stacked, "fsdp", bit)], axis=1)
+        deltas = deltas + [delta ^ bit for delta in deltas]
+        bit //= 2
+    stacked = stacked.reshape(4, planes * tokens, model_width)
+    order = line_order(line)
+    ups, downs = line_slots(line, order)
+    pieces = 3
+    piece = shard_rows // pieces
+    terms = []
+    for slot in range(line):
+        there = jnp.asarray(order[:, slot])[here]
+        parts = []
+        for delta in deltas:
+            start = ((plane ^ delta) * line + there) * shard_rows
+            part = lax.dynamic_slice_in_dim(columns, start, shard_rows, axis=1)
+            parts.append(part if delta == 0 else swap(part, "fsdp", delta))
+        factors = jnp.concatenate(parts, axis=0)
+        first_row = (plane * line + there) * shard_rows
+        made = []
+        for index in range(pieces):
+            row = first_row + index * piece
+            which = sum((row >= edge).astype(jnp.int32) for edge in edges)
+            made.append(
+                contract_first(
+                    factors[:, index * piece : (index + 1) * piece],
+                    lax.dynamic_index_in_dim(stacked, which, 0, keepdims=False),
+                )
+            )
+        terms.append(made)
+    zero = jnp.zeros((piece, model_width), jnp.bfloat16)
+    from_below = [zero] * pieces
+    from_above = [zero] * pieces
+    for step in range(line - 1):
+        for index in range(pieces):
+            made = [terms[slot][index] for slot in range(line)]
+            up = (choose(made, ups[step], here) + from_below[index].astype(jnp.float32)).astype(
+                jnp.bfloat16
+            )
+            down = (choose(made, downs[step], here) + from_above[index].astype(jnp.float32)).astype(
+                jnp.bfloat16
+            )
+            from_below[index] = lax.ppermute(up, "dp", [(p, p + 1) for p in range(step + 1)])
+            from_above[index] = lax.ppermute(
+                down, "dp", [(line - 1 - p, line - 2 - p) for p in range(step + 1)]
+            )
+    return jnp.concatenate(
+        [
+            terms[line - 1][index]
+            + from_below[index].astype(jnp.float32)
+            + from_above[index].astype(jnp.float32)
+            for index in range(pieces)
+        ],
+        axis=0,
+    )
 
 
 def adamw(param, grad, first, second, step_count, rate, decay):
@@ -224,14 +333,12 @@
         gathered = lax.all_gather(shard_low, ("fsdp", "dp"), axis=0, tiled=True)
         saved = forward_pass(gathered, vec_now, tokens_now, seq_lengths, picked)
         forward_steps.append(tokens_now.at[picked].set(saved["out_rows"].astype(jnp.bfloat16)))
-        gathered = lax.all_gather(shard_low, ("fsdp", "dp"), axis=0, tiled=True)
         d_rows, grad_vec, columns, operands = backward_pass(
             gathered, vec_now, saved, cot_now, picked
         )
         backward_steps.append(cot_now.at[picked].set(d_rows.astype(jnp.bfloat16)))
-        grad_full = local_gradient(columns, operands, model_width)
-        grad_shard = lax.psum_scatter(grad_full, ("fsdp", "dp"), scatter_dimension=0, tiled=True)
-        grad_vec = lax.psum(grad_vec, ("fsdp", "dp"))
+        grad_shard = gradient_share(columns, operands, weights.shape[0], model_width)
+        grad_vec = sum_over(grad_vec, ("fsdp", "dp"))
         step_count = STEP + inner_step
         master, first_now, second_now = adamw(
             master, grad_shard, first_now, second_now, step_count, INNER_RATE, DECAY_RATE
@@ -244,19 +351,28 @@
     vector_change = vectors - vec_now
     col_width = weights.shape[1] // groups
     col_start = lax.axis_index("grp") * col_width
-    diff_share = (
-        lax.psum_scatter(delta.astype(jnp.bfloat16), "grp", scatter_dimension=1, tiled=True).astype(
-            jnp.float32
+    here = lax.axis_index("grp")
+    diff_share = lax.dynamic_slice_in_dim(delta, col_start, col_width, 1)
+    for step in range(1, groups):
+        there = lax.rem(here + step, groups)
+        part = lax.dynamic_slice_in_dim(delta, there * col_width, col_width, 1)
+        part = lax.ppermute(
+            part.astype(jnp.bfloat16), "grp", [(i, (i + step) % groups) for i in range(groups)]
         )
-        / groups
-    )
-    vec_diff = lax.psum(vector_change, "grp") / groups
+        diff_share = diff_share + part.astype(jnp.float32)
+    diff_share = diff_share / groups
+    vec_diff = sum_over(vector_change, ("grp",)) / groups
     moment_share = OUTER_MOMENTUM * outer_moment + diff_share
     base_share = lax.dynamic_slice_in_dim(weights, col_start, col_width, 1)
     new_share = base_share - OUTER_RATE * (diff_share + OUTER_MOMENTUM * moment_share)
-    weights_new = lax.all_gather(new_share.astype(jnp.bfloat16), "grp", axis=1, tiled=True).astype(
-        new_share.dtype
-    )
+    low_share = new_share.astype(jnp.bfloat16)
+    weights_low = jnp.zeros(weights.shape, jnp.bfloat16)
+    weights_low = lax.dynamic_update_slice_in_dim(weights_low, low_share, col_start, 1)
+    for step in range(1, groups):
+        there = lax.rem(here + groups - step, groups)
+        part = lax.ppermute(low_share, "grp", [(i, (i + step) % groups) for i in range(groups)])
+        weights_low = lax.dynamic_update_slice_in_dim(weights_low, part, there * col_width, 1)
+    weights_new = weights_low.astype(jnp.float32)
     average_new = AVERAGE_KEEP * smoothed_matrix_mean + (1.0 - AVERAGE_KEEP) * new_share
     vec_moment = OUTER_MOMENTUM * vec_outer + vec_diff
     vectors_new = vectors - OUTER_RATE * (vec_diff + OUTER_MOMENTUM * vec_moment)
@@ -265,7 +381,7 @@
         jnp.stack(forward_steps),
         jnp.stack(backward_steps),
         weights_new,
-        weights_new.astype(jnp.bfloat16),
+        weights_low,
         first_now[None],
         second_now[None],
         moment_share,

time: 1610 us -> 848 us (0.53)
  waiting for transfers between devices: 1120 us -> 425 us
  blocking collectives: 130 us -> 0 us
  starting transfers between devices: 0.25 us -> 119 us
  other arithmetic: 137 us -> 91 us
  matrix products: 157 us -> 117 us
    reduce_scatter x3 -> x0, waiting for transfers between devices: 936 us -> none  [the longest x2 936 us: on_device(): lax.psum_scatter(grad_full, ('fsdp', 'dp'), scatter_dimension=0, tiled=True)]
    ppermute x0 -> x75, waiting for transfers between devices: none -> 206 us  [the longest x18 110 us: gradient_share(): lax.ppermute(up, 'dp', [(p, p + 1) for p in range(step + 1)])]
    psum x3 -> x0, blocking collectives: 130 us -> none  [the longest x2 122 us: on_device(): grad_vec = lax.psum(grad_vec, ('fsdp', 'dp'))]
    ppermute x0 -> x75, starting transfers between devices: none -> 119 us  [the longest x18 69.4 us: gradient_share(): lax.ppermute(up, 'dp', [(p, p + 1) for p in range(step + 1)])]
    concatenate x2 -> x14, other arithmetic: 71.7 us -> 19.5 us  [the longest x4 12.1 us: gradient_share(): stacked = jnp.concatenate([stacked, swap(stacked, 'fsdp', bit)], axis=1)]
    all_gather x2, waiting for transfers between devices: 181 us -> 219 us  [on_device(): gathered = lax.all_gather(shard_low, ('fsdp', 'dp'), axis=0, tiled=True)]
    dot_general x8 -> x24, matrix products: 51.4 us -> 14.3 us  [contract_first(): lax.dot_general(left, right, (((0,), (0,)), ((), ())), preferred_element_...]
  transfers between devices with their start and end apart: 6 -> 77, of which waited for: 5 -> 37; matrix products, arithmetic and copies ran while one was open for 4% -> 16% of each run, Pallas kernels for 0% -> 0%
where the time goes in v1:
time: 848 us; the launch traced here: 839 us
  waiting for transfers between devices  425 us (50%)
  starting transfers between devices  119 us (14%)
  matrix products  117 us (14%)
  other arithmetic  91 us (11%)
  local copies, waits for them, and re-layouts  59.1 us (7%)
  between operations  27.5 us (3%)
    all_gather x2, waiting for transfers between devices, on_device(): gathered = lax.all_gather(shard_low, ('fsdp', 'dp'), axis=0, tiled=True)  219 us
    ppermute x18, waiting for transfers between devices, gradient_share(): lax.ppermute(up, 'dp', [(p, p + 1) for p in range(step + 1)])  110 us
    ppermute x37, waiting for transfers between devices, swap(): return lax.ppermute(values, axis, [(i, i ^ delta) for i in range(size)])  70.3 us
    ppermute x18, starting transfers between devices, gradient_share(): lax.ppermute(up, 'dp', [(p, p + 1) for p in range(step + 1)])  69.4 us
    dot_general x8, matrix products, contract_last(): lax.dot_general(left, right, (((1,), (1,)), ((), ())), preferred_element_...  43.4 us
    ppermute x37, starting transfers between devices, swap(): return lax.ppermute(values, axis, [(i, i ^ delta) for i in range(size)])  30.8 us
  transfers between devices with their start and end apart: 77, of which 37 were waited for; matrix products, arithmetic and copies ran while one was open for 16% of the time, Pallas kernels for 0%

profile of v1, /device:TPU:0, one launch (start us, length us, event | category | flops | bytes accessed | tf_op | source)
XLA Modules:
  0.0 838.5 jit_solution(4516793638560929782)
XLA Ops:
  22.1 4.1 slice_bitcast_fusion.3
  28.5 4.2 slice_bitcast_fusion
  35.8 113.5 %all-gather.3.cloned.1.call-done = bf16[12288,1024]{1,0:T(8,128)(2,1)} async-done(((bf16[768,1024]{1,0:T(8,128)(2,1)}), bf16[12288,1024]{1,0:T(8,128)(2,1)}) %all-gather.3.cloned.1.call-update) | async-done | bytes 25165840 | tf_op jit(solution)/shard_map/all_gather | solution.py:333
  149.2 5.9 fusion.32
  167.3 5.9 multiply_convert_fusion.3
  173.2 5.9 fusion.193
  180.0 7.1 fusion.60
  187.1 5.3 multiply_reduce_fusion.6
  204.6 24.2 %collective-permute-done.7 = bf16[4,1,144,1024]{3,2,0,1:T(8,128)(2,1)} collective-permute-done((bf16[4,1,144,1024]{3,2,0,1:T(8,128)(2,1)}, bf16[4,1,144,1024]{3,2,0,1:T(8,128)(2,1)}, u32[]{:S(2)}, u32[]{:S(2)}) %collective-permute-start.7) | collective-permute-done | bytes 1179680 | tf_op jit(solution)/shard_map/ppermute | solution.py:177
  238.0 4.4 collective-permute-done.14
  244.1 4.2 collective-permute-done.12
  248.4 3.5 collective-permute-done.11
  263.7 3.5 collective-permute-done.4
  267.2 4.7 collective-permute-done.15
  271.9 3.8 collective-permute-done.17
  296.2 4.4 collective-permute-start.31
  301.3 5.7 collective-permute-done.24
  307.4 4.4 collective-permute-start.25
  312.6 5.7 collective-permute-done.18
  318.7 4.4 collective-permute-start.19
  323.1 6.4 collective-permute-done.31
  330.7 5.0 collective-permute-start.32
  335.8 5.0 collective-permute-done.25
  342.6 5.0 collective-permute-start.26
  347.6 4.3 collective-permute-done.19
  353.8 5.0 collective-permute-start.20
  358.9 4.3 collective-permute-done.32
  365.1 9.3 %collective-permute-done.26 = bf16[256,1024]{1,0:T(8,128)(2,1)S(1)} collective-permute-done((bf16[256,1024]{1,0:T(8,128)(2,1)S(1)}, bf16[256,1024]{1,0:T(8,128)(2,1)S(1)}, u32[]{:S(2)}, u32[]{:S(2)}) %collective-permute-start.26) | collective-permute-done | bytes 524320 | tf_op jit(solution)/shard_map/ppermute | solution.py:274
  375.1 9.9 %collective-permute-done.20 = bf16[256,1024]{1,0:T(8,128)(2,1)S(1)} collective-permute-done((bf16[256,1024]{1,0:T(8,128)(2,1)S(1)}, bf16[256,1024]{1,0:T(8,128)(2,1)S(1)}, u32[]{:S(2)}, u32[]{:S(2)}) %collective-permute-start.20) | collective-permute-done | bytes 524320 | tf_op jit(solution)/shard_map/ppermute | solution.py:274
  386.6 3.9 fusion.88
  391.0 5.7 fusion.208
  401.3 3.7 gather_fusion.2
  411.8 3.9 gather_fusion.5
  421.6 105.9 %all-gather.5.cloned.1.call-done = bf16[12288,1024]{1,0:T(8,128)(2,1)} async-done(((bf16[768,1024]{1,0:T(8,128)(2,1)}), bf16[12288,1024]{1,0:T(8,128)(2,1)}) %all-gather.5.cloned.1.call-update) | async-done | bytes 25165840 | tf_op jit(solution)/shard_map/all_gather | solution.py:333
  527.4 6.0 fusion.35
  546.6 5.9 multiply_convert_fusion.1
  552.5 5.9 fusion.200
  559.9 7.1 fusion.67
  567.0 5.9 multiply_reduce_fusion.2
  588.0 5.8 fusion.205
  596.5 5.3 scatter_custom_fusion
  601.8 5.9 scatter_custom_fusion.2
  610.8 5.2 collective-permute-done.39
  624.2 5.1 scatter_custom_fusion.1
  632.3 4.8 pad_maximum_fusion.2
  647.0 5.8 scatter_custom_fusion.3
  685.0 7.7 collective-permute-done.62
  692.8 4.4 collective-permute-start.50
  698.9 5.1 collective-permute-done.56
  705.1 8.2 collective-permute-start.57
  716.3 10.2 %collective-permute-done.63 = bf16[256,1024]{1,0:T(8,128)(2,1)S(1)} collective-permute-done((bf16[256,1024]{1,0:T(8,128)(2,1)S(1)}, bf16[256,1024]{1,0:T(8,128)(2,1)S(1)}, u32[]{:S(2)}, u32[]{:S(2)}) %collective-permute-start.63) | collective-permute-done | bytes 524320 | tf_op jit(solution)/shard_map/ppermute | solution.py:274
  726.5 4.4 collective-permute-start.51
  732.1 5.6 collective-permute-done.57
  737.7 4.4 collective-permute-start.64
  744.0 5.0 collective-permute-done.51
  748.9 4.4 collective-permute-start.58
  755.2 5.0 collective-permute-done.64
  760.2 4.4 collective-permute-start.52
  766.5 4.9 collective-permute-done.58
  772.0 10.4 %collective-permute-done.52 = bf16[256,1024]{1,0:T(8,128)(2,1)S(1)} collective-permute-done((bf16[256,1024]{1,0:T(8,128)(2,1)S(1)}, bf16[256,1024]{1,0:T(8,128)(2,1)S(1)}, u32[]{:S(2)}, u32[]{:S(2)}) %collective-permute-start.52) | collective-permute-done | bytes 524320 | tf_op jit(solution)/shard_map/ppermute | solution.py:274
  783.1 5.0 subtract_subtract_fusion
  794.8 13.0 %collective-permute-done.68 = bf16[768,512]{1,0:T(8,128)(2,1)S(1)} collective-permute-done((bf16[768,512]{1,0:T(8,128)(2,1)S(1)}, bf16[768,512]{1,0:T(8,128)(2,1)S(1)}, u32[]{:S(2)}, u32[]{:S(2)}) %collective-permute-start.68) | collective-permute-done | bytes 786464 | tf_op jit(solution)/shard_map/ppermute | solution.py:359
  813.1 3.6 fusion.53
  816.6 12.6 %collective-permute-done.69 = bf16[768,512]{1,0:T(8,128)(2,1)S(1)} collective-permute-done((bf16[768,512]{1,0:T(8,128)(2,1)S(1)}, bf16[768,512]{1,0:T(8,128)(2,1)S(1)}, u32[]{:S(2)}, u32[]{:S(2)}) %collective-permute-start.69) | collective-permute-done | bytes 786464 | tf_op jit(solution)/shard_map/ppermute | solution.py:373
  (483 shorter events, 221.7 us)
Async XLA Ops:
  7.2 142.0 %all-gather.3.cloned.1.call-start = ((), (), s32[]{:S(2)}) async-start(), calls=%async_computation | async-start | bytes 26738688 | tf_op jit(solution)/shard_map/all_gather | solution.py:333
  10.6 516.8 %all-gather.5.cloned.1.call-start = ((), (), s32[]{:S(2)}) async-start(), calls=%async_computation.1 | async-start | bytes 26738688 | tf_op jit(solution)/shard_map/all_gather | solution.py:333
  200.3 28.4 %collective-permute-start.7 = (bf16[4,1,144,1024]{3,2,0,1:T(8,128)(2,1)}, bf16[4,1,144,1024]{3,2,0,1:T(8,128)(2,1)}, u32[]{:S(2)}, u32[]{:S(2)}) collective-permute-start(bf16[4,1,144,1024]{3,2,0,1:T(8,128)(2,1)} %maximum_bitcast_fusion), channel_id=1, source_target_pairs={{0,8},{4,12},{8,0},{12,4},{1,9},{5,13},{9,1},{13,5},{2,10},{6,14},... | collective-permute-start | bytes 3538952 | tf_op jit(solution)/shard_map/ppermute | solution.py:177
  232.0 43.8 %collective-permute-start.8 = (bf16[4,2,144,1024]{3,2,0,1:T(8,128)(2,1)}, bf16[4,2,144,1024]{3,2,0,1:T(8,128)(2,1)}, u32[]{:S(2)}, u32[]{:S(2)}) collective-permute-start(bf16[4,2,144,1024]{3,2,0,1:T(8,128)(2,1)} %pad_maximum_fusion.8), channel_id=1, source_target_pairs={{0,4},{4,0},{8,12},{12,8},{1,5},{5,1},{9,13},{13,9},{2,6},{6,2},{1... | collective-permute-start | bytes 7077896 | tf_op jit(solution)/shard_map/ppermute | solution.py:177
  236.3 12.1 %collective-permute-start.12 = (bf16[144,768]{1,0:T(8,128)(2,1)S(1)}, bf16[144,768]{1,0:T(8,128)(2,1)S(1)}, u32[]{:S(2)}, u32[]{:S(2)}) collective-permute-start(bf16[144,768]{1,0:T(8,128)(2,1)S(1)} %get-tuple-element.67), channel_id=1, source_target_pairs={{0,8},{4,12},{8,0},{12,4},{1,9},{5,13},{9,1},{13,5},{2,10},{6,14},... | collective-permute-start | bytes 663560 | tf_op jit(solution)/shard_map/ppermute | solution.py:177
  237.4 14.4 %collective-permute-start.11 = (bf16[144,768]{1,0:T(8,128)(2,1)S(1)}, bf16[144,768]{1,0:T(8,128)(2,1)S(1)}, u32[]{:S(2)}, u32[]{:S(2)}) collective-permute-start(bf16[144,768]{1,0:T(8,128)(2,1)S(1)} %get-tuple-element.69), channel_id=1, source_target_pairs={{0,12},{4,8},{8,4},{12,0},{1,13},{5,9},{9,5},{13,1},{2,14},{6,10},... | collective-permute-start | bytes 663560 | tf_op jit(solution)/shard_map/ppermute | solution.py:177
  242.4 16.2 %collective-permute-start.10 = (bf16[144,768]{1,0:T(8,128)(2,1)S(1)}, bf16[144,768]{1,0:T(8,128)(2,1)S(1)}, u32[]{:S(2)}, u32[]{:S(2)}) collective-permute-start(bf16[144,768]{1,0:T(8,128)(2,1)S(1)} %get-tuple-element.70), channel_id=1, source_target_pairs={{0,4},{4,0},{8,12},{12,8},{1,5},{5,1},{9,13},{13,9},{2,6},{6,2},{1... | collective-permute-start | bytes 663560 | tf_op jit(solution)/shard_map/ppermute | solution.py:177
  243.4 16.0 %collective-permute-start.9 = (bf16[144,768]{1,0:T(8,128)(2,1)}, bf16[144,768]{1,0:T(8,128)(2,1)S(1)}, u32[]{:S(2)}, u32[]{:S(2)}) collective-permute-start(bf16[144,768]{1,0:T(8,128)(2,1)} %get-tuple-element.71), channel_id=1, source_target_pairs={{0,8},{4,12},{8,0},{12,4},{1,9},{5,13},{9,1},{13,5},{2,10},{6,14},... | collective-permute-start | bytes 663560 | tf_op jit(solution)/shard_map/ppermute | solution.py:177
  248.4 13.0 %collective-permute-start.6 = (bf16[144,768]{1,0:T(8,128)(2,1)}, bf16[144,768]{1,0:T(8,128)(2,1)S(1)}, u32[]{:S(2)}, u32[]{:S(2)}) collective-permute-start(bf16[144,768]{1,0:T(8,128)(2,1)} %get-tuple-element.73), channel_id=1, source_target_pairs={{0,12},{4,8},{8,4},{12,0},{1,13},{5,9},{9,5},{13,1},{2,14},{6,10},... | collective-permute-start | bytes 663560 | tf_op jit(solution)/shard_map/ppermute | solution.py:177
  251.9 10.5 %collective-permute-start.5 = (bf16[144,768]{1,0:T(8,128)(2,1)S(1)}, bf16[144,768]{1,0:T(8,128)(2,1)S(1)}, u32[]{:S(2)}, u32[]{:S(2)}) collective-permute-start(bf16[144,768]{1,0:T(8,128)(2,1)S(1)} %get-tuple-element.74), channel_id=1, source_target_pairs={{0,4},{4,0},{8,12},{12,8},{1,5},{5,1},{9,13},{13,9},{2,6},{6,2},{1... | collective-permute-start | bytes 663560 | tf_op jit(solution)/shard_map/ppermute | solution.py:177
  261.4 10.5 %collective-permute-start.15 = (bf16[144,768]{1,0:T(8,128)(2,1)}, bf16[144,768]{1,0:T(8,128)(2,1)S(1)}, u32[]{:S(2)}, u32[]{:S(2)}) collective-permute-start(bf16[144,768]{1,0:T(8,128)(2,1)} %get-tuple-element.63), channel_id=1, source_target_pairs={{0,8},{4,12},{8,0},{12,4},{1,9},{5,13},{9,1},{13,5},{2,10},{6,14},... | collective-permute-start | bytes 663560 | tf_op jit(solution)/shard_map/ppermute | solution.py:177
  262.4 13.4 %collective-permute-start.17 = (bf16[144,768]{1,0:T(8,128)(2,1)}, bf16[144,768]{1,0:T(8,128)(2,1)S(1)}, u32[]{:S(2)}, u32[]{:S(2)}) collective-permute-start(bf16[144,768]{1,0:T(8,128)(2,1)} %get-tuple-element.76), channel_id=1, source_target_pairs={{0,12},{4,8},{8,4},{12,0},{1,13},{5,9},{9,5},{13,1},{2,14},{6,10},... | collective-permute-start | bytes 663560 | tf_op jit(solution)/shard_map/ppermute | solution.py:177
  279.7 11.4 %collective-permute-start.33 = (bf16[256,1024]{1,0:T(8,128)(2,1)S(1)}, bf16[256,1024]{1,0:T(8,128)(2,1)S(1)}, u32[]{:S(2)}, u32[]{:S(2)}) collective-permute-start(bf16[256,1024]{1,0:T(8,128)(2,1)S(1)} %get-tuple-element.125), channel_id=1, source_target_pairs={{3,2},{7,6},{11,10},{15,14},{19,18},{23,22},{27,26},{31,30}} | collective-permute-start | bytes 1572872 | tf_op jit(solution)/shard_map/ppermute | solution.py:275
  280.4 15.4 %collective-permute-start.30 = (bf16[256,1024]{1,0:T(8,128)(2,1)S(1)}, bf16[256,1024]{1,0:T(8,128)(2,1)S(1)}, u32[]{:S(2)}, u32[]{:S(2)}) collective-permute-start(bf16[256,1024]{1,0:T(8,128)(2,1)S(1)} %get-tuple-element.125), channel_id=1, source_target_pairs={{0,1},{4,5},{8,9},{12,13},{16,17},{20,21},{24,25},{28,29}} | collective-permute-start | bytes 1572872 | tf_op jit(solution)/shard_map/ppermute | solution.py:274
  284.2 16.5 %collective-permute-start.27 = (bf16[256,1024]{1,0:T(8,128)(2,1)S(1)}, bf16[256,1024]{1,0:T(8,128)(2,1)S(1)}, u32[]{:S(2)}, u32[]{:S(2)}) collective-permute-start(bf16[256,1024]{1,0:T(8,128)(2,1)S(1)} %get-tuple-element.127), channel_id=1, source_target_pairs={{3,2},{7,6},{11,10},{15,14},{19,18},{23,22},{27,26},{31,30}} | collective-permute-start | bytes 1572872 | tf_op jit(solution)/shard_map/ppermute | solution.py:275
  284.9 22.2 %collective-permute-start.24 = (bf16[256,1024]{1,0:T(8,128)(2,1)S(1)}, bf16[256,1024]{1,0:T(8,128)(2,1)S(1)}, u32[]{:S(2)}, u32[]{:S(2)}) collective-permute-start(bf16[256,1024]{1,0:T(8,128)(2,1)S(1)} %get-tuple-element.127), channel_id=1, source_target_pairs={{0,1},{4,5},{8,9},{12,13},{16,17},{20,21},{24,25},{28,29}} | collective-permute-start | bytes 1572872 | tf_op jit(solution)/shard_map/ppermute | solution.py:274
  288.6 23.3 %collective-permute-start.21 = (bf16[256,1024]{1,0:T(8,128)(2,1)S(1)}, bf16[256,1024]{1,0:T(8,128)(2,1)S(1)}, u32[]{:S(2)}, u32[]{:S(2)}) collective-permute-start(bf16[256,1024]{1,0:T(8,128)(2,1)S(1)} %get-tuple-element.129), channel_id=1, source_target_pairs={{3,2},{7,6},{11,10},{15,14},{19,18},{23,22},{27,26},{31,30}} | collective-permute-start | bytes 1572872 | tf_op jit(solution)/shard_map/ppermute | solution.py:275
  291.1 27.1 %collective-permute-start.18 = (bf16[256,1024]{1,0:T(8,128)(2,1)S(1)}, bf16[256,1024]{1,0:T(8,128)(2,1)S(1)}, u32[]{:S(2)}, u32[]{:S(2)}) collective-permute-start(bf16[256,1024]{1,0:T(8,128)(2,1)S(1)} %get-tuple-element.129), channel_id=1, source_target_pairs={{0,1},{4,5},{8,9},{12,13},{16,17},{20,21},{24,25},{28,29}} | collective-permute-start | bytes 1572872 | tf_op jit(solution)/shard_map/ppermute | solution.py:274
  296.2 33.3 %collective-permute-start.31 = (bf16[256,1024]{1,0:T(8,128)(2,1)S(1)}, bf16[256,1024]{1,0:T(8,128)(2,1)S(1)}, u32[]{:S(2)}, u32[]{:S(2)}) collective-permute-start(bf16[256,1024]{1,0:T(8,128)(2,1)S(1)} %get-tuple-element.99), channel_id=1, source_target_pairs={{0,1},{1,2},{4,5},{5,6},{8,9},{9,10},{12,13},{13,14},{16,17},{17,1... | collective-permute-start | bytes 1572872 | tf_op jit(solution)/shard_map/ppermute | solution.py:274
  300.6 29.6 %collective-permute-start.34 = (bf16[256,1024]{1,0:T(8,128)(2,1)S(1)}, bf16[256,1024]{1,0:T(8,128)(2,1)S(1)}, u32[]{:S(2)}, u32[]{:S(2)}) collective-permute-start(bf16[256,1024]{1,0:T(8,128)(2,1)S(1)} %get-tuple-element.100), channel_id=1, source_target_pairs={{3,2},{2,1},{7,6},{6,5},{11,10},{10,9},{15,14},{14,13},{19,18},{18... | collective-permute-start | bytes 1572872 | tf_op jit(solution)/shard_map/ppermute | solution.py:275
  307.4 33.3 %collective-permute-start.25 = (bf16[256,1024]{1,0:T(8,128)(2,1)S(1)}, bf16[256,1024]{1,0:T(8,128)(2,1)S(1)}, u32[]{:S(2)}, u32[]{:S(2)}) collective-permute-start(bf16[256,1024]{1,0:T(8,128)(2,1)S(1)} %get-tuple-element.95), channel_id=1, source_target_pairs={{0,1},{1,2},{4,5},{5,6},{8,9},{9,10},{12,13},{13,14},{16,17},{17,1... | collective-permute-start | bytes 1572872 | tf_op jit(solution)/shard_map/ppermute | solution.py:274
  311.9 30.2 %collective-permute-start.28 = (bf16[256,1024]{1,0:T(8,128)(2,1)S(1)}, bf16[256,1024]{1,0:T(8,128)(2,1)S(1)}, u32[]{:S(2)}, u32[]{:S(2)}) collective-permute-start(bf16[256,1024]{1,0:T(8,128)(2,1)S(1)} %get-tuple-element.96), channel_id=1, source_target_pairs={{3,2},{2,1},{7,6},{6,5},{11,10},{10,9},{15,14},{14,13},{19,18},{18... | collective-permute-start | bytes 1572872 | tf_op jit(solution)/shard_map/ppermute | solution.py:275
  318.7 33.3 %collective-permute-start.19 = (bf16[256,1024]{1,0:T(8,128)(2,1)S(1)}, bf16[256,1024]{1,0:T(8,128)(2,1)S(1)}, u32[]{:S(2)}, u32[]{:S(2)}) collective-permute-start(bf16[256,1024]{1,0:T(8,128)(2,1)S(1)} %get-tuple-element.91), channel_id=1, source_target_pairs={{0,1},{1,2},{4,5},{5,6},{8,9},{9,10},{12,13},{13,14},{16,17},{17,1... | collective-permute-start | bytes 1572872 | tf_op jit(solution)/shard_map/ppermute | solution.py:274
  329.5 23.8 %collective-permute-start.22 = (bf16[256,1024]{1,0:T(8,128)(2,1)S(1)}, bf16[256,1024]{1,0:T(8,128)(2,1)S(1)}, u32[]{:S(2)}, u32[]{:S(2)}) collective-permute-start(bf16[256,1024]{1,0:T(8,128)(2,1)S(1)} %get-tuple-element.92), channel_id=1, source_target_pairs={{3,2},{2,1},{7,6},{6,5},{11,10},{10,9},{15,14},{14,13},{19,18},{18... | collective-permute-start | bytes 1572872 | tf_op jit(solution)/shard_map/ppermute | solution.py:275
  330.7 32.5 %collective-permute-start.32 = (bf16[256,1024]{1,0:T(8,128)(2,1)S(1)}, bf16[256,1024]{1,0:T(8,128)(2,1)S(1)}, u32[]{:S(2)}, u32[]{:S(2)}) collective-permute-start(bf16[256,1024]{1,0:T(8,128)(2,1)S(1)} %get-tuple-element.97), channel_id=1, source_target_pairs={{0,1},{1,2},{2,3},{4,5},{5,6},{6,7},{8,9},{9,10},{10,11},{12,13},{... | collective-permute-start | bytes 1572872 | tf_op jit(solution)/shard_map/ppermute | solution.py:274
  340.7 23.8 %collective-permute-start.35 = (bf16[256,1024]{1,0:T(8,128)(2,1)S(1)}, bf16[256,1024]{1,0:T(8,128)(2,1)S(1)}, u32[]{:S(2)}, u32[]{:S(2)}) collective-permute-start(bf16[256,1024]{1,0:T(8,128)(2,1)S(1)} %get-tuple-element.98), channel_id=1, source_target_pairs={{3,2},{2,1},{1,0},{7,6},{6,5},{5,4},{11,10},{10,9},{9,8},{15,14},{... | collective-permute-start | bytes 1572872 | tf_op jit(solution)/shard_map/ppermute | solution.py:275
  342.6 31.9 %collective-permute-start.26 = (bf16[256,1024]{1,0:T(8,128)(2,1)S(1)}, bf16[256,1024]{1,0:T(8,128)(2,1)S(1)}, u32[]{:S(2)}, u32[]{:S(2)}) collective-permute-start(bf16[256,1024]{1,0:T(8,128)(2,1)S(1)} %get-tuple-element.93), channel_id=1, source_target_pairs={{0,1},{1,2},{2,3},{4,5},{5,6},{6,7},{8,9},{9,10},{10,11},{12,13},{... | collective-permute-start | bytes 1572872 | tf_op jit(solution)/shard_map/ppermute | solution.py:274
  352.0 22.5 %collective-permute-start.29 = (bf16[256,1024]{1,0:T(8,128)(2,1)S(1)}, bf16[256,1024]{1,0:T(8,128)(2,1)S(1)}, u32[]{:S(2)}, u32[]{:S(2)}) collective-permute-start(bf16[256,1024]{1,0:T(8,128)(2,1)S(1)} %get-tuple-element.94), channel_id=1, source_target_pairs={{3,2},{2,1},{1,0},{7,6},{6,5},{5,4},{11,10},{10,9},{9,8},{15,14},{... | collective-permute-start | bytes 1572872 | tf_op jit(solution)/shard_map/ppermute | solution.py:275
  353.8 31.2 %collective-permute-start.20 = (bf16[256,1024]{1,0:T(8,128)(2,1)S(1)}, bf16[256,1024]{1,0:T(8,128)(2,1)S(1)}, u32[]{:S(2)}, u32[]{:S(2)}) collective-permute-start(bf16[256,1024]{1,0:T(8,128)(2,1)S(1)} %get-tuple-element.89), channel_id=1, source_target_pairs={{0,1},{1,2},{2,3},{4,5},{5,6},{6,7},{8,9},{9,10},{10,11},{12,13},{... | collective-permute-start | bytes 1572872 | tf_op jit(solution)/shard_map/ppermute | solution.py:274
  363.2 21.8 %collective-permute-start.23 = (bf16[256,1024]{1,0:T(8,128)(2,1)S(1)}, bf16[256,1024]{1,0:T(8,128)(2,1)S(1)}, u32[]{:S(2)}, u32[]{:S(2)}) collective-permute-start(bf16[256,1024]{1,0:T(8,128)(2,1)S(1)} %get-tuple-element.90), channel_id=1, source_target_pairs={{3,2},{2,1},{1,0},{7,6},{6,5},{5,4},{11,10},{10,9},{9,8},{15,14},{... | collective-permute-start | bytes 1572872 | tf_op jit(solution)/shard_map/ppermute | solution.py:275
  587.6 28.4 %collective-permute-start.39 = (bf16[4,1,144,1024]{3,2,0,1:T(8,128)(2,1)}, bf16[4,1,144,1024]{3,2,0,1:T(8,128)(2,1)}, u32[]{:S(2)}, u32[]{:S(2)}) collective-permute-start(bf16[4,1,144,1024]{3,2,0,1:T(8,128)(2,1)} %maximum_bitcast_fusion.1), channel_id=1, source_target_pairs={{0,8},{4,12},{8,0},{12,4},{1,9},{5,13},{9,1},{13,5},{2,10},{6,14},... | collective-permute-start | bytes 3538952 | tf_op jit(solution)/shard_map/ppermute | solution.py:177
  594.4 15.6 %collective-permute-start.70 = (f32[3,1024]{1,0:T(4,128)}, f32[3,1024]{1,0:T(4,128)S(1)}, u32[]{:S(2)}, u32[]{:S(2)}) collective-permute-start(f32[3,1024]{1,0:T(4,128)} %pad_maximum_fusion.21), channel_id=1, source_target_pairs={{0,4},{4,0},{8,12},{12,8},{1,5},{5,1},{9,13},{13,9},{2,6},{6,2},{1... | collective-permute-start | bytes 36872 | tf_op jit(solution)/shard_map/ppermute | solution.py:177
  610.1 10.7 %collective-permute-start.71 = (f32[3,1024]{1,0:T(4,128)S(1)}, f32[3,1024]{1,0:T(4,128)S(1)}, u32[]{:S(2)}, u32[]{:S(2)}) collective-permute-start(f32[3,1024]{1,0:T(4,128)S(1)} %fusion.307), channel_id=1, source_target_pairs={{0,8},{4,12},{8,0},{12,4},{1,9},{5,13},{9,1},{13,5},{2,10},{6,14},... | collective-permute-start | bytes 36872 | tf_op jit(solution)/shard_map/ppermute | solution.py:177
  619.2 50.9 %collective-permute-start.40 = (bf16[4,2,144,1024]{3,2,0,1:T(8,128)(2,1)}, bf16[4,2,144,1024]{3,2,0,1:T(8,128)(2,1)}, u32[]{:S(2)}, u32[]{:S(2)}) collective-permute-start(bf16[4,2,144,1024]{3,2,0,1:T(8,128)(2,1)} %pad_maximum_fusion.9), channel_id=1, source_target_pairs={{0,4},{4,0},{8,12},{12,8},{1,5},{5,1},{9,13},{13,9},{2,6},{6,2},{1... | collective-permute-start | bytes 7077896 | tf_op jit(solution)/shard_map/ppermute | solution.py:177
  620.9 10.5 %collective-permute-start.72 = (f32[3,1024]{1,0:T(4,128)S(1)}, f32[3,1024]{1,0:T(4,128)S(1)}, u32[]{:S(2)}, u32[]{:S(2)}) collective-permute-start(f32[3,1024]{1,0:T(4,128)S(1)} %fusion.351), channel_id=1, source_target_pairs={{0,1},{1,0},{2,3},{3,2},{4,5},{5,4},{6,7},{7,6},{8,9},{9,8},{10,11... | collective-permute-start | bytes 36872 | tf_op jit(solution)/shard_map/ppermute | solution.py:177
  630.9 11.5 %collective-permute-start.44 = (bf16[144,768]{1,0:T(8,128)(2,1)}, bf16[144,768]{1,0:T(8,128)(2,1)}, u32[]{:S(2)}, u32[]{:S(2)}) collective-permute-start(bf16[144,768]{1,0:T(8,128)(2,1)} %get-tuple-element.51), channel_id=1, source_target_pairs={{0,8},{4,12},{8,0},{12,4},{1,9},{5,13},{9,1},{13,5},{2,10},{6,14},... | collective-permute-start | bytes 663560 | tf_op jit(solution)/shard_map/ppermute | solution.py:177
  631.5 15.1 %collective-permute-start.43 = (bf16[144,768]{1,0:T(8,128)(2,1)}, bf16[144,768]{1,0:T(8,128)(2,1)}, u32[]{:S(2)}, u32[]{:S(2)}) collective-permute-start(bf16[144,768]{1,0:T(8,128)(2,1)} %get-tuple-element.53), channel_id=1, source_target_pairs={{0,12},{4,8},{8,4},{12,0},{1,13},{5,9},{9,5},{13,1},{2,14},{6,10},... | collective-permute-start | bytes 663560 | tf_op jit(solution)/shard_map/ppermute | solution.py:177
  637.1 16.5 %collective-permute-start.42 = (bf16[144,768]{1,0:T(8,128)(2,1)}, bf16[144,768]{1,0:T(8,128)(2,1)}, u32[]{:S(2)}, u32[]{:S(2)}) collective-permute-start(bf16[144,768]{1,0:T(8,128)(2,1)} %get-tuple-element.54), channel_id=1, source_target_pairs={{0,4},{4,0},{8,12},{12,8},{1,5},{5,1},{9,13},{13,9},{2,6},{6,2},{1... | collective-permute-start | bytes 663560 | tf_op jit(solution)/shard_map/ppermute | solution.py:177
  637.9 18.5 %collective-permute-start.41 = (bf16[144,768]{1,0:T(8,128)(2,1)}, bf16[144,768]{1,0:T(8,128)(2,1)}, u32[]{:S(2)}, u32[]{:S(2)}) collective-permute-start(bf16[144,768]{1,0:T(8,128)(2,1)} %get-tuple-element.55), channel_id=1, source_target_pairs={{0,8},{4,12},{8,0},{12,4},{1,9},{5,13},{9,1},{13,5},{2,10},{6,14},... | collective-permute-start | bytes 663560 | tf_op jit(solution)/shard_map/ppermute | solution.py:177
  642.4 14.2 %collective-permute-start.38 = (bf16[144,768]{1,0:T(8,128)(2,1)}, bf16[144,768]{1,0:T(8,128)(2,1)}, u32[]{:S(2)}, u32[]{:S(2)}) collective-permute-start(bf16[144,768]{1,0:T(8,128)(2,1)} %get-tuple-element.57), channel_id=1, source_target_pairs={{0,12},{4,8},{8,4},{12,0},{1,13},{5,9},{9,5},{13,1},{2,14},{6,10},... | collective-permute-start | bytes 663560 | tf_op jit(solution)/shard_map/ppermute | solution.py:177
  646.6 11.2 %collective-permute-start.37 = (bf16[144,768]{1,0:T(8,128)(2,1)}, bf16[144,768]{1,0:T(8,128)(2,1)}, u32[]{:S(2)}, u32[]{:S(2)}) collective-permute-start(bf16[144,768]{1,0:T(8,128)(2,1)} %get-tuple-element.58), channel_id=1, source_target_pairs={{0,4},{4,0},{8,12},{12,8},{1,5},{5,1},{9,13},{13,9},{2,6},{6,2},{1... | collective-permute-start | bytes 663560 | tf_op jit(solution)/shard_map/ppermute | solution.py:177
  656.6 10.3 %collective-permute-start.47 = (bf16[144,768]{1,0:T(8,128)(2,1)}, bf16[144,768]{1,0:T(8,128)(2,1)S(1)}, u32[]{:S(2)}, u32[]{:S(2)}) collective-permute-start(bf16[144,768]{1,0:T(8,128)(2,1)} %get-tuple-element.47), channel_id=1, source_target_pairs={{0,8},{4,12},{8,0},{12,4},{1,9},{5,13},{9,1},{13,5},{2,10},{6,14},... | collective-permute-start | bytes 663560 | tf_op jit(solution)/shard_map/ppermute | solution.py:177
  657.8 12.3 %collective-permute-start.49 = (bf16[144,768]{1,0:T(8,128)(2,1)}, bf16[144,768]{1,0:T(8,128)(2,1)S(1)}, u32[]{:S(2)}, u32[]{:S(2)}) collective-permute-start(bf16[144,768]{1,0:T(8,128)(2,1)} %get-tuple-element.60), channel_id=1, source_target_pairs={{0,12},{4,8},{8,4},{12,0},{1,13},{5,9},{9,5},{13,1},{2,14},{6,10},... | collective-permute-start | bytes 663560 | tf_op jit(solution)/shard_map/ppermute | solution.py:177
  662.1 130.3 %collective-permute-start.73 = (f32[3,1024]{1,0:T(4,128)S(1)}, f32[3,1024]{1,0:T(4,128)S(1)}, u32[]{:S(2)}, u32[]{:S(2)}) collective-permute-start(f32[3,1024]{1,0:T(4,128)S(1)} %add.1157), channel_id=1, source_target_pairs={{0,2},{1,3},{2,0},{3,1},{4,6},{5,7},{6,4},{7,5},{8,10},{9,11},{10,... | collective-permute-start | bytes 36872 | tf_op jit(solution)/shard_map/ppermute | solution.py:177
  678.1 14.6 %collective-permute-start.62 = (bf16[256,1024]{1,0:T(8,128)(2,1)S(1)}, bf16[256,1024]{1,0:T(8,128)(2,1)S(1)}, u32[]{:S(2)}, u32[]{:S(2)}) collective-permute-start(bf16[256,1024]{1,0:T(8,128)(2,1)S(1)} %get-tuple-element.143), channel_id=1, source_target_pairs={{0,1},{4,5},{8,9},{12,13},{16,17},{20,21},{24,25},{28,29}} | collective-permute-start | bytes 1572872 | tf_op jit(solution)/shard_map/ppermute | solution.py:274
  681.1 16.5 %collective-permute-start.59 = (bf16[256,1024]{1,0:T(8,128)(2,1)S(1)}, bf16[256,1024]{1,0:T(8,128)(2,1)S(1)}, u32[]{:S(2)}, u32[]{:S(2)}) collective-permute-start(bf16[256,1024]{1,0:T(8,128)(2,1)S(1)} %get-tuple-element.145), channel_id=1, source_target_pairs={{3,2},{7,6},{11,10},{15,14},{19,18},{23,22},{27,26},{31,30}} | collective-permute-start | bytes 1572872 | tf_op jit(solution)/shard_map/ppermute | solution.py:275
  681.8 22.2 %collective-permute-start.56 = (bf16[256,1024]{1,0:T(8,128)(2,1)S(1)}, bf16[256,1024]{1,0:T(8,128)(2,1)S(1)}, u32[]{:S(2)}, u32[]{:S(2)}) collective-permute-start(bf16[256,1024]{1,0:T(8,128)(2,1)S(1)} %get-tuple-element.145), channel_id=1, source_target_pairs={{0,1},{4,5},{8,9},{12,13},{16,17},{20,21},{24,25},{28,29}} | collective-permute-start | bytes 1572872 | tf_op jit(solution)/shard_map/ppermute | solution.py:274
  684.3 20.7 %collective-permute-start.53 = (bf16[256,1024]{1,0:T(8,128)(2,1)S(1)}, bf16[256,1024]{1,0:T(8,128)(2,1)S(1)}, u32[]{:S(2)}, u32[]{:S(2)}) collective-permute-start(bf16[256,1024]{1,0:T(8,128)(2,1)S(1)} %get-tuple-element.147), channel_id=1, source_target_pairs={{3,2},{7,6},{11,10},{15,14},{19,18},{23,22},{27,26},{31,30}} | collective-permute-start | bytes 1572872 | tf_op jit(solution)/shard_map/ppermute | solution.py:275
  692.8 22.5 %collective-permute-start.50 = (bf16[256,1024]{1,0:T(8,128)(2,1)S(1)}, bf16[256,1024]{1,0:T(8,128)(2,1)S(1)}, u32[]{:S(2)}, u32[]{:S(2)}) collective-permute-start(bf16[256,1024]{1,0:T(8,128)(2,1)S(1)} %get-tuple-element.147), channel_id=1, source_target_pairs={{0,1},{4,5},{8,9},{12,13},{16,17},{20,21},{24,25},{28,29}} | collective-permute-start | bytes 1572872 | tf_op jit(solution)/shard_map/ppermute | solution.py:274
  697.6 28.9 %collective-permute-start.63 = (bf16[256,1024]{1,0:T(8,128)(2,1)S(1)}, bf16[256,1024]{1,0:T(8,128)(2,1)S(1)}, u32[]{:S(2)}, u32[]{:S(2)}) collective-permute-start(bf16[256,1024]{1,0:T(8,128)(2,1)S(1)} %get-tuple-element.87), channel_id=1, source_target_pairs={{0,1},{1,2},{4,5},{5,6},{8,9},{9,10},{12,13},{13,14},{16,17},{17,1... | collective-permute-start | bytes 1572872 | tf_op jit(solution)/shard_map/ppermute | solution.py:274
  704.0 26.9 %collective-permute-start.66 = (bf16[256,1024]{1,0:T(8,128)(2,1)S(1)}, bf16[256,1024]{1,0:T(8,128)(2,1)S(1)}, u32[]{:S(2)}, u32[]{:S(2)}) collective-permute-start(bf16[256,1024]{1,0:T(8,128)(2,1)S(1)} %get-tuple-element.88), channel_id=1, source_target_pairs={{3,2},{2,1},{7,6},{6,5},{11,10},{10,9},{15,14},{14,13},{19,18},{18... | collective-permute-start | bytes 1572872 | tf_op jit(solution)/shard_map/ppermute | solution.py:275
  705.1 32.6 %collective-permute-start.57 = (bf16[256,1024]{1,0:T(8,128)(2,1)S(1)}, bf16[256,1024]{1,0:T(8,128)(2,1)S(1)}, u32[]{:S(2)}, u32[]{:S(2)}) collective-permute-start(bf16[256,1024]{1,0:T(8,128)(2,1)S(1)} %get-tuple-element.83), channel_id=1, source_target_pairs={{0,1},{1,2},{4,5},{5,6},{8,9},{9,10},{12,13},{13,14},{16,17},{17,1... | collective-permute-start | bytes 1572872 | tf_op jit(solution)/shard_map/ppermute | solution.py:274
  715.2 26.9 %collective-permute-start.60 = (bf16[256,1024]{1,0:T(8,128)(2,1)S(1)}, bf16[256,1024]{1,0:T(8,128)(2,1)S(1)}, u32[]{:S(2)}, u32[]{:S(2)}) collective-permute-start(bf16[256,1024]{1,0:T(8,128)(2,1)S(1)} %get-tuple-element.84), channel_id=1, source_target_pairs={{3,2},{2,1},{7,6},{6,5},{11,10},{10,9},{15,14},{14,13},{19,18},{18... | collective-permute-start | bytes 1572872 | tf_op jit(solution)/shard_map/ppermute | solution.py:275
  726.5 22.5 %collective-permute-start.51 = (bf16[256,1024]{1,0:T(8,128)(2,1)S(1)}, bf16[256,1024]{1,0:T(8,128)(2,1)S(1)}, u32[]{:S(2)}, u32[]{:S(2)}) collective-permute-start(bf16[256,1024]{1,0:T(8,128)(2,1)S(1)} %get-tuple-element.79), channel_id=1, source_target_pairs={{0,1},{1,2},{4,5},{5,6},{8,9},{9,10},{12,13},{13,14},{16,17},{17,1... | collective-permute-start | bytes 1572872 | tf_op jit(solution)/shard_map/ppermute | solution.py:274
  730.9 22.5 %collective-permute-start.54 = (bf16[256,1024]{1,0:T(8,128)(2,1)S(1)}, bf16[256,1024]{1,0:T(8,128)(2,1)S(1)}, u32[]{:S(2)}, u32[]{:S(2)}) collective-permute-start(bf16[256,1024]{1,0:T(8,128)(2,1)S(1)} %get-tuple-element.80), channel_id=1, source_target_pairs={{3,2},{2,1},{7,6},{6,5},{11,10},{10,9},{15,14},{14,13},{19,18},{18... | collective-permute-start | bytes 1572872 | tf_op jit(solution)/shard_map/ppermute | solution.py:275
  737.7 22.5 %collective-permute-start.64 = (bf16[256,1024]{1,0:T(8,128)(2,1)S(1)}, bf16[256,1024]{1,0:T(8,128)(2,1)S(1)}, u32[]{:S(2)}, u32[]{:S(2)}) collective-permute-start(bf16[256,1024]{1,0:T(8,128)(2,1)S(1)} %get-tuple-element.85), channel_id=1, source_target_pairs={{0,1},{1,2},{2,3},{4,5},{5,6},{6,7},{8,9},{9,10},{10,11},{12,13},{... | collective-permute-start | bytes 1572872 | tf_op jit(solution)/shard_map/ppermute | solution.py:274
  742.1 22.5 %collective-permute-start.67 = (bf16[256,1024]{1,0:T(8,128)(2,1)S(1)}, bf16[256,1024]{1,0:T(8,128)(2,1)S(1)}, u32[]{:S(2)}, u32[]{:S(2)}) collective-permute-start(bf16[256,1024]{1,0:T(8,128)(2,1)S(1)} %get-tuple-element.86), channel_id=1, source_target_pairs={{3,2},{2,1},{1,0},{7,6},{6,5},{5,4},{11,10},{10,9},{9,8},{15,14},{... | collective-permute-start | bytes 1572872 | tf_op jit(solution)/shard_map/ppermute | solution.py:275
  748.9 22.5 %collective-permute-start.58 = (bf16[256,1024]{1,0:T(8,128)(2,1)S(1)}, bf16[256,1024]{1,0:T(8,128)(2,1)S(1)}, u32[]{:S(2)}, u32[]{:S(2)}) collective-permute-start(bf16[256,1024]{1,0:T(8,128)(2,1)S(1)} %get-tuple-element.81), channel_id=1, source_target_pairs={{0,1},{1,2},{2,3},{4,5},{5,6},{6,7},{8,9},{9,10},{10,11},{12,13},{... | collective-permute-start | bytes 1572872 | tf_op jit(solution)/shard_map/ppermute | solution.py:274
  753.4 18.0 %collective-permute-start.61 = (bf16[256,1024]{1,0:T(8,128)(2,1)S(1)}, bf16[256,1024]{1,0:T(8,128)(2,1)S(1)}, u32[]{:S(2)}, u32[]{:S(2)}) collective-permute-start(bf16[256,1024]{1,0:T(8,128)(2,1)S(1)} %get-tuple-element.82), channel_id=1, source_target_pairs={{3,2},{2,1},{1,0},{7,6},{6,5},{5,4},{11,10},{10,9},{9,8},{15,14},{... | collective-permute-start | bytes 1572872 | tf_op jit(solution)/shard_map/ppermute | solution.py:275
  760.2 22.2 %collective-permute-start.52 = (bf16[256,1024]{1,0:T(8,128)(2,1)S(1)}, bf16[256,1024]{1,0:T(8,128)(2,1)S(1)}, u32[]{:S(2)}, u32[]{:S(2)}) collective-permute-start(bf16[256,1024]{1,0:T(8,128)(2,1)S(1)} %get-tuple-element.77), channel_id=1, source_target_pairs={{0,1},{1,2},{2,3},{4,5},{5,6},{6,7},{8,9},{9,10},{10,11},{12,13},{... | collective-permute-start | bytes 1572872 | tf_op jit(solution)/shard_map/ppermute | solution.py:274
  764.6 17.8 %collective-permute-start.55 = (bf16[256,1024]{1,0:T(8,128)(2,1)S(1)}, bf16[256,1024]{1,0:T(8,128)(2,1)S(1)}, u32[]{:S(2)}, u32[]{:S(2)}) collective-permute-start(bf16[256,1024]{1,0:T(8,128)(2,1)S(1)} %get-tuple-element.78), channel_id=1, source_target_pairs={{3,2},{2,1},{1,0},{7,6},{6,5},{5,4},{11,10},{10,9},{9,8},{15,14},{... | collective-permute-start | bytes 1572872 | tf_op jit(solution)/shard_map/ppermute | solution.py:275
  788.3 19.5 %collective-permute-start.68 = (bf16[768,512]{1,0:T(8,128)(2,1)S(1)}, bf16[768,512]{1,0:T(8,128)(2,1)S(1)}, u32[]{:S(2)}, u32[]{:S(2)}) collective-permute-start(bf16[768,512]{1,0:T(8,128)(2,1)S(1)} %dynamic-slice_convert_fusion), channel_id=1, source_target_pairs={{0,16},{16,0},{1,17},{17,1},{2,18},{18,2},{3,19},{19,3},{4,20},{20... | collective-permute-start | bytes 2359304 | tf_op jit(solution)/shard_map/ppermute | solution.py:359
  793.7 18.7 %collective-permute-start.74 = (f32[3,1024]{1,0:T(4,128)S(1)}, f32[3,1024]{1,0:T(4,128)S(1)}, u32[]{:S(2)}, u32[]{:S(2)}) collective-permute-start(f32[3,1024]{1,0:T(4,128)S(1)} %get-tuple-element.26), channel_id=1, source_target_pairs={{0,16},{16,0},{1,17},{17,1},{2,18},{18,2},{3,19},{19,3},{4,20},{20... | collective-permute-start | bytes 36872 | tf_op jit(solution)/shard_map/ppermute | solution.py:177
  810.9 18.3 %collective-permute-start.69 = (bf16[768,512]{1,0:T(8,128)(2,1)S(1)}, bf16[768,512]{1,0:T(8,128)(2,1)S(1)}, u32[]{:S(2)}, u32[]{:S(2)}) collective-permute-start(bf16[768,512]{1,0:T(8,128)(2,1)S(1)} %get-tuple-element.34), channel_id=1, source_target_pairs={{0,16},{16,0},{1,17},{17,1},{2,18},{18,2},{3,19},{19,3},{4,20},{20... | collective-permute-start | bytes 2359304 | tf_op jit(solution)/shard_map/ppermute | solution.py:373
  (114 other events, 2451.5 us)
Sparse Core Ops, SparseCore 0:
  10.7 138.4 all-gather.2
  390.7 136.7 all-gather.4

commit v2 on v1

v2 whole, which is shorter than its diff:
```python
import functools

import jax
import jax.numpy as jnp
import numpy as np
from jax import lax
from jax.experimental import pallas as pl
from jax.experimental.pallas import tpu as pltpu
from jax.sharding import PartitionSpec as P

HEAD = 64
INNER = 2
STEP = 5


EPS_NORM = 1e-06
EPS_ADAM = 1e-08
BETA_ONE = 0.9
BETA_TWO = 0.95
INNER_RATE = 0.03
DECAY_RATE = 0.1
OUTER_RATE = 0.7
OUTER_MOMENTUM = 0.9
AVERAGE_KEEP = 0.9
GELU_SCALE = float(np.sqrt(2.0 / np.pi))
GELU_CUBE = 0.044715
PIECES = 3
LINE_FLOPS = 10**10
NOWHERE = 1 << 20


def nt(left, right):
    return lax.dot_general(
        left, right, (((1,), (1,)), ((), ())), preferred_element_type=jnp.float32
    )


def nn(left, right):
    return lax.dot_general(
        left, right, (((1,), (0,)), ((), ())), preferred_element_type=jnp.float32
    )


def tn(left, right):
    return lax.dot_general(
        left, right, (((0,), (0,)), ((), ())), preferred_element_type=jnp.float32
    )


def weight_copies(weights, held, sems, sources, rows):
    return [
        pltpu.make_async_copy(
            weights.at[pl.ds(source * rows, rows)], held.at[pl.ds(target * rows, rows)], sems.at[target]
        )
        for target, source in enumerate(sources)
    ]


def two_heads(values):
    low = lax.broadcasted_iota(jnp.int32, values.shape, 1) < HEAD
    zero = jnp.zeros_like(values)
    return jnp.concatenate([jnp.where(low, values, zero), jnp.where(low, zero, values)], axis=0)


def one_block(values):
    rows = values.shape[0] // 2
    low = lax.broadcasted_iota(jnp.int32, (rows, values.shape[1]), 1) < HEAD
    return jnp.where(low, values[:rows], values[rows:])


def row_mean(values):
    return jnp.mean(values, axis=-1, keepdims=True)


def gelu_and_slope(pre):
    square = pre * pre
    tanh = jnp.tanh(GELU_SCALE * pre * (1.0 + GELU_CUBE * square))
    half = 0.5 * (1.0 + tanh)
    slope = half + 0.5 * pre * (1.0 - tanh * tanh) * (
        GELU_SCALE * (1.0 + 3.0 * GELU_CUBE * square)
    )
    return ((pre * half).astype(jnp.bfloat16), slope)


def gather_kernel(lengths, picked_ref, across_ref, tokens_hbm, cot_hbm, *refs, steps):
    both_refs, mask_refs = refs[:steps], refs[steps : 2 * steps]
    held, sems = refs[2 * steps :]
    copies = [
        [
            pltpu.make_async_copy(source.at[step], held.at[step, at], sems.at[step, at])
            for at, source in enumerate((tokens_hbm, cot_hbm))
        ]
        for step in range(steps)
    ]
    for some in copies:
        for copy in some:
            copy.start()
    for step in range(steps):
        down, across = picked_ref[step], across_ref[step]
        segment_down, segment_across = jnp.zeros_like(down), jnp.zeros_like(across)
        end = jnp.int32(0)
        for slot in range(lengths.shape[1]):
            end = end + lengths[step, slot]
            segment_down += (down >= end).astype(jnp.int32)
            segment_across += (across >= end).astype(jnp.int32)
        allowed = (segment_down == segment_across) & (across <= down)
        allowed = allowed.astype(jnp.int32)
        mask_refs[step][...] = jnp.concatenate([allowed, allowed], axis=0)
        places = lax.broadcasted_iota(jnp.int32, (down.shape[0], held.shape[2]), 1)
        chosen = jnp.where(places == down, 1.0, 0.0).astype(jnp.bfloat16)
        for at in range(2):
            copies[step][at].wait()
            both_refs[step][at] = nn(chosen, held[step, at]).astype(jnp.bfloat16)


def scatter_kernel(across_ref, base_ref, rows_ref, out_ref):
    base = base_ref[0]
    across = across_ref[0]
    places = lax.broadcasted_iota(jnp.int32, (base.shape[0], across.shape[1]), 0)
    chosen = jnp.where(places == across, 1.0, 0.0)
    replaced = jnp.sum(chosen, axis=-1, keepdims=True) > 0.0
    rows = nn(chosen.astype(jnp.bfloat16), rows_ref[0]).astype(jnp.bfloat16)
    out_ref[0] = jnp.where(replaced, rows, base)


def attention_kernel(
    weights, info, needs, moves, both_ref, vec_ref, mask_ref, proj_ref, lse_ref, pair_ref, first_ref, held, sems
):
    rows_ref = both_ref.at[0]
    width = both_ref.shape[2]
    copies = weight_copies(weights, held, sems, range(4), width)
    for copy in copies:
        copy.start()
    xs = rows_ref[...].astype(jnp.float32)
    h1 = (xs * lax.rsqrt(row_mean(xs * xs) + EPS_NORM) * vec_ref[0:1, :]).astype(jnp.bfloat16)
    for index in range(3):
        copies[index].wait()
        proj_ref[:, index * width : (index + 1) * width] = nt(
            h1, held[pl.ds(index * width, width), :]
        ).astype(jnp.bfloat16)
    allowed = mask_ref[...] > 0
    lane = lax.broadcasted_iota(jnp.int32, lse_ref.shape, 1)
    lse = jnp.zeros(lse_ref.shape, jnp.float32)
    for pair in range(width // 128):
        at = pair * 128
        queries = two_heads(proj_ref[:, at : at + 128])
        keys = proj_ref[:, width + at : width + at + 128]
        values = proj_ref[:, 2 * width + at : 2 * width + at + 128]
        scores = jnp.where(allowed, nt(queries, keys) * HEAD ** (-0.5), -1e30)
        top = jnp.max(scores, axis=-1, keepdims=True)
        total = top + jnp.log(jnp.sum(jnp.exp(scores - top), axis=-1, keepdims=True))
        lse = jnp.where(lane == pair, total, lse)
        probs_low = jnp.exp(scores - total).astype(jnp.bfloat16)
        pair_ref[0, :, at : at + 128] = one_block(nn(probs_low, values)).astype(jnp.bfloat16)
    lse_ref[...] = lse
    copies[3].wait()
    first_sum = xs + nt(pair_ref[0], held[pl.ds(3 * width, width), :])
    first_ref[...] = first_sum
    inverse = lax.rsqrt(row_mean(first_sum * first_sum) + EPS_NORM)
    pair_ref[1] = (first_sum * inverse * vec_ref[1:2, :]).astype(jnp.bfloat16)


def feed_forward_kernel(
    weights,
    both_ref,
    vec_ref,
    first_ref,
    d_attn_ref,
    out_ref,
    base_ref,
    grad_ref,
    *refs,
    keep,
):
    held, sems = refs[-2:]
    rows_ref, cot_ref = both_ref.at[0], both_ref.at[1]
    width = both_ref.shape[2]
    hidden = (weights.shape[0] - 4 * width) // 2
    parts = hidden // width
    order = []
    for part in range(parts):
        order += [4 + part, 4 + parts + part]
    copies = weight_copies(weights, held, sems, order, width)
    for copy in copies:
        copy.start()

    def matrix(index):
        return held[pl.ds(index * width, width), :]

    xs = rows_ref[...].astype(jnp.float32)
    cot = cot_ref[...].astype(jnp.float32)
    gate = jax.nn.sigmoid(jnp.sum(xs * vec_ref[2:3, :], axis=-1, keepdims=True))
    first_sum = first_ref[...]
    inverse = lax.rsqrt(row_mean(first_sum * first_sum) + EPS_NORM)
    normed = first_sum * inverse
    h2 = (normed * vec_ref[1:2, :]).astype(jnp.bfloat16)
    d_branch = gate * cot
    d_down = d_branch.astype(jnp.bfloat16)
    branch = first_sum - xs
    d_h2 = jnp.zeros_like(branch)
    for part in range(parts):
        at = part * width
        copies[2 * part].wait()
        act, slope = gelu_and_slope(nt(h2, matrix(2 * part)))
        copies[2 * part + 1].wait()
        branch = branch + nn(act, matrix(2 * part + 1))
        d_pre = (nt(d_down, matrix(2 * part + 1)) * slope).astype(jnp.bfloat16)
        if keep:
            refs[0][:, at : at + width] = d_pre
            refs[0][:, at + hidden : at + hidden + width] = act
        d_h2 = d_h2 + nn(d_pre, matrix(2 * part))
    out_ref[...] = (xs + gate * branch).astype(jnp.bfloat16)
    d_logit = jnp.sum(cot * branch, axis=-1, keepdims=True) * gate * (1.0 - gate)
    grad_ref[0:1, :] = jnp.sum(d_h2 * normed, axis=0, keepdims=True)
    grad_ref[1:2, :] = jnp.sum(d_logit * xs, axis=0, keepdims=True)
    d_normed = d_h2 * vec_ref[1:2, :]
    d_first = inverse * (d_normed - normed * row_mean(d_normed * normed))
    d_attn_ref[...] = (d_branch + d_first).astype(jnp.bfloat16)
    base_ref[...] = cot + d_first + d_logit * vec_ref[2:3, :]


def attention_back_kernel(
    weights,
    d_attn_ref,
    proj_ref,
    lse_ref,
    mask_ref,
    both_ref,
    vec_ref,
    base_hbm,
    pair_hbm,
    got_hbm,
    late_ref,
    d_rows_ref,
    grad_ref,
    pairs_hbm,
    held,
    base_ref,
    sems,
    base_sem,
    pair_sems,
):
    rows_ref = both_ref.at[0]
    width = both_ref.shape[2]
    copies = weight_copies(weights, held, sems, [3, 0, 1, 2], width)
    for copy in copies:
        copy.start()
    base_copy = pltpu.make_async_copy(base_hbm, base_ref, base_sem)
    base_copy.start()
    pair_copies = [
        pltpu.make_async_copy(pair_hbm, pairs_hbm.at[0], pair_sems.at[0]),
        pltpu.make_async_copy(got_hbm.at[0], pairs_hbm.at[1], pair_sems.at[1]),
    ]
    for copy in pair_copies:
        copy.start()
    copies[0].wait()
    d_mixed = nn(d_attn_ref[...], held[pl.ds(0, width), :]).astype(jnp.bfloat16)
    allowed = mask_ref[...] > 0
    for pair in range(width // 128):
        at = pair * 128
        queries = two_heads(proj_ref[:, at : at + 128])
        keys = proj_ref[:, width + at : width + at + 128]
        values = proj_ref[:, 2 * width + at : 2 * width + at + 128]
        d_pair = two_heads(d_mixed[:, at : at + 128])
        scores = jnp.where(allowed, nt(queries, keys) * HEAD ** (-0.5), -1e30)
        probs = jnp.exp(scores - lse_ref[:, pair : pair + 1])
        probs_low = probs.astype(jnp.bfloat16)
        d_probs = nt(d_pair, values)
        d_scores = probs * (d_probs - jnp.sum(d_probs * probs, axis=-1, keepdims=True))
        d_scores = d_scores.astype(jnp.bfloat16)
        late_ref[:, at : at + 128] = (one_block(nn(d_scores, keys)) * HEAD ** (-0.5)).astype(
            jnp.bfloat16
        )
        late_ref[:, width + at : width + at + 128] = (
            tn(d_scores, queries) * HEAD ** (-0.5)
        ).astype(jnp.bfloat16)
        late_ref[:, 2 * width + at : 2 * width + at + 128] = tn(probs_low, d_pair).astype(
            jnp.bfloat16
        )
    xs = rows_ref[...].astype(jnp.float32)
    inverse = lax.rsqrt(row_mean(xs * xs) + EPS_NORM)
    normed = xs * inverse
    d_h1 = jnp.zeros(xs.shape, jnp.float32)
    for index in range(3):
        copies[1 + index].wait()
        d_h1 = d_h1 + nn(
            late_ref[:, index * width : (index + 1) * width], held[pl.ds((1 + index) * width, width), :]
        )
    grad_ref[...] = jnp.sum(d_h1 * normed, axis=0, keepdims=True)
    d_normed = d_h1 * vec_ref[0:1, :]
    base_copy.wait()
    d_rows_ref[...] = (
        base_ref[...] + inverse * (d_normed - normed * row_mean(d_normed * normed))
    ).astype(jnp.bfloat16)
    for copy in pair_copies:
        copy.wait()


def plane_copies(refs, target, sems, tokens):
    return [
        pltpu.make_async_copy(ref, target.at[pl.ds(at * tokens, tokens)], sems.at[at])
        for at, ref in enumerate(refs)
    ]


def pair_refs_of(refs, index):
    return [ref.at[at, index] for ref in refs for at in range(ref.shape[0])]


def feed_forward_products_kernel(info, needs, weights, d_down_ref, *refs):
    pair_refs = refs[:-7]
    out_ref, held, uppers, lowers, held_sems, upper_sems, lower_sems = refs[-7:]
    count, piece, _ = out_ref.shape
    sources, tokens, _ = d_down_ref.shape

    def row_copy(index, at, target, sems):
        start = pl.multiple_of(info[index, at], 16)
        return pltpu.make_async_copy(
            weights.at[pl.ds(start, piece)], target.at[index], sems.at[index]
        )

    def each_row_copy(index, act):
        @pl.when(info[index, 0] >= 2)
        def _():
            act(row_copy(index, 1, uppers, upper_sems))

        @pl.when(info[index, 0] == 2)
        def _():
            act(row_copy(index, 2, lowers, lower_sems))

    def each_held(act):
        @pl.when(needs[2] > 0)
        def _():
            copies = plane_copies(
                pair_refs_of(pair_refs, 1), held.at[0], held_sems.at[0], tokens
            ) + plane_copies(
                [d_down_ref.at[at] for at in range(sources)], held.at[1], held_sems.at[1], tokens
            )
            for copy in copies:
                act(copy)

    each_held(lambda copy: copy.start())

    @pl.loop(0, count)
    def _(index):
        each_row_copy(index, lambda copy: copy.start())

    each_held(lambda copy: copy.wait())

    @pl.loop(0, count)
    def _(index):
        each_row_copy(index, lambda copy: copy.wait())

        @pl.when(info[index, 0] == 2)
        def _():
            slope = gelu_and_slope(nt(held[0], uppers[index]))[1]
            d_pre = (nt(held[1], lowers[index]) * slope).astype(jnp.bfloat16)
            out_ref[index] = tn(d_pre, held[0]).astype(jnp.bfloat16)

        @pl.when(info[index, 0] == 3)
        def _():
            act = gelu_and_slope(nt(held[0], uppers[index]))[0]
            out_ref[index] = tn(act, held[1]).astype(jnp.bfloat16)


def attention_products_kernel(info, needs, h1_ref, *refs, sources):
    proj_refs, attn_refs = refs[:sources], refs[sources : 2 * sources]
    pair_refs = refs[2 * sources : -8]
    _, out_ref, held, factors, made, held_sems, factor_sems, out_sems = refs[-8:]
    count, piece, _ = made.shape
    tokens = h1_ref.shape[1]

    def factor_copies(index, parts):
        start = pl.multiple_of(info[index, 1], 128)
        return plane_copies(
            [part.at[:, pl.ds(start, piece)] for part in parts],
            factors.at[index],
            factor_sems.at[index],
            tokens,
        )

    def each_copy(index, act):
        for kind, parts in enumerate((proj_refs, attn_refs)):

            @pl.when(info[index, 0] == kind)
            def _(parts=parts):
                for copy in factor_copies(index, parts):
                    act(copy)

    def each_held(act):
        for kind in range(2):
            found = pair_refs_of(pair_refs, 0) if kind else [h1_ref.at[at] for at in range(sources)]

            @pl.when(needs[kind] > 0)
            def _(kind=kind, found=found):
                for copy in plane_copies(found, held.at[kind], held_sems.at[kind], tokens):
                    act(copy)

    def out_copy(index):
        return pltpu.make_async_copy(made.at[index], out_ref.at[index], out_sems.at[index])

    each_held(lambda copy: copy.start())

    @pl.loop(0, count)
    def _(index):
        each_copy(index, lambda copy: copy.start())

    each_held(lambda copy: copy.wait())

    @pl.loop(0, count)
    def _(index):
        each_copy(index, lambda copy: copy.wait())

        @pl.when(info[index, 0] < 2)
        def _():
            made[index] = tn(factors[index], held[info[index, 0]]).astype(jnp.bfloat16)
            out_copy(index).start()

    @pl.loop(0, count)
    def _(index):
        @pl.when(info[index, 0] < 2)
        def _():
            out_copy(index).wait()


def line_kernel(moves, below_ref, above_ref, terms_ref, up_ref, down_ref, held, sems, *, step, piece):
    pieces = terms_ref.shape[0] // (moves.shape[0] + 1)
    copies = [
        pltpu.make_async_copy(
            terms_ref.at[moves[step, way] * pieces + piece], held.at[way], sems.at[way]
        )
        for way in range(2)
    ]
    for copy in copies:
        copy.start()
    for way, (came, leaves) in enumerate(((below_ref, up_ref), (above_ref, down_ref))):
        copies[way].wait()
        leaves[...] = (held[way].astype(jnp.float32) + came[...].astype(jnp.float32)).astype(
            jnp.bfloat16
        )


def vmem(count):
    return [pl.BlockSpec(memory_space=pltpu.VMEM)] * count


def run_gather(lengths, picked, tokens_in, cot_in):
    steps, count = picked.shape
    _, places, width = tokens_in.shape
    tokens = count + -count % 16
    padded = jnp.pad(picked, ((0, 0), (0, tokens - count)), constant_values=NOWHERE)
    shape = jax.ShapeDtypeStruct
    made = pl.pallas_call(
        functools.partial(gather_kernel, steps=steps),
        in_specs=[pl.BlockSpec(memory_space=pltpu.SMEM)] + vmem(2) + anywhere(2),
        out_specs=vmem(2 * steps),
        out_shape=[shape((2, tokens, width), jnp.bfloat16)] * steps
        + [shape((2 * tokens, tokens), jnp.int32)] * steps,
        scratch_shapes=[
            pltpu.VMEM((steps, 2, places, width), jnp.bfloat16),
            pltpu.SemaphoreType.DMA((steps, 2)),
        ],
        compiler_params=pltpu.CompilerParams(vmem_limit_bytes=44 << 20),
        name="gather_rows",
    )(lengths, padded[:, :, None], padded[:, None, :], tokens_in, cot_in)
    return (made[:steps], made[steps:], padded[:, None, :])


def run_scatter(across, base, rows):
    steps, places, width = base.shape
    tokens = rows.shape[1]
    return pl.pallas_call(
        scatter_kernel,
        grid=(steps,),
        in_specs=[
            pl.BlockSpec((1, 1, tokens), lambda step: (step, 0, 0)),
            pl.BlockSpec((1, places, width), lambda step: (step, 0, 0)),
            pl.BlockSpec((1, tokens, width), lambda step: (step, 0, 0)),
        ],
        out_specs=pl.BlockSpec((1, places, width), lambda step: (step, 0, 0)),
        out_shape=jax.ShapeDtypeStruct(base.shape, base.dtype),
        compiler_params=pltpu.CompilerParams(vmem_limit_bytes=44 << 20),
        name="scatter_rows",
    )(across, base, rows)


def run_attention(gathered, info, needs, moves, both, vec_now, mask):
    _, tokens, width = both.shape
    shape = jax.ShapeDtypeStruct
    return pl.pallas_call(
        attention_kernel,
        in_specs=anywhere(1) + smem(3) + vmem(3),
        out_specs=vmem(4),
        out_shape=[
            shape((tokens, 3 * width), jnp.bfloat16),
            shape((2 * tokens, 128), jnp.float32),
            shape((2, tokens, width), jnp.bfloat16),
            shape((tokens, width), jnp.float32),
        ],
        scratch_shapes=[
            pltpu.VMEM((4 * width, width), jnp.bfloat16),
            pltpu.SemaphoreType.DMA((4,)),
        ],
        compiler_params=pltpu.CompilerParams(vmem_limit_bytes=44 << 20),
        cost_estimate=pl.CostEstimate(
            flops=8 * tokens * width * width, bytes_accessed=8 * width * width, transcendentals=0
        ),
        name="attention",
    )(gathered, info, needs, moves, both, vec_now, mask)


def run_feed_forward(gathered, both, vec_now, first_sum, keep):
    _, tokens, width = both.shape
    wide = gathered.shape[0]
    shape = jax.ShapeDtypeStruct
    kept = [shape((tokens, wide - 4 * width), jnp.bfloat16)] if keep else []
    return pl.pallas_call(
        functools.partial(feed_forward_kernel, keep=keep),
        in_specs=anywhere(1) + vmem(3),
        out_specs=vmem(4 + len(kept)),
        out_shape=[
            shape((tokens, width), jnp.bfloat16),
            shape((tokens, width), jnp.bfloat16),
            shape((tokens, width), jnp.float32),
            shape((2, width), jnp.float32),
        ]
        + kept,
        scratch_shapes=[
            pltpu.VMEM((wide - 4 * width, width), jnp.bfloat16),
            pltpu.SemaphoreType.DMA(((wide - 4 * width) // width,)),
        ],
        compiler_params=pltpu.CompilerParams(vmem_limit_bytes=44 << 20),
        cost_estimate=pl.CostEstimate(
            flops=8 * tokens * (wide - 4 * width) * width,
            bytes_accessed=2 * wide * width,
            transcendentals=0,
        ),
        name="feed_forward",
    )(gathered, both, vec_now, first_sum)


def smem(count):
    return [pl.BlockSpec(memory_space=pltpu.SMEM)] * count


def anywhere(count):
    return [pl.BlockSpec(memory_space=pl.ANY)] * count


def run_attention_back(gathered, d_attn_low, proj, lse, mask, both, vec_now, base, pair, got):
    _, tokens, width = both.shape
    shape = jax.ShapeDtypeStruct
    return pl.pallas_call(
        attention_back_kernel,
        in_specs=anywhere(1) + vmem(6) + anywhere(3),
        out_specs=vmem(3) + anywhere(1),
        out_shape=[
            shape((tokens, 3 * width), jnp.bfloat16),
            shape((tokens, width), jnp.bfloat16),
            shape((1, width), jnp.float32),
            shape((2,) + pair.shape, jnp.bfloat16),
        ],
        scratch_shapes=[
            pltpu.VMEM((4 * width, width), jnp.bfloat16),
            pltpu.VMEM((tokens, width), jnp.float32),
            pltpu.SemaphoreType.DMA((4,)),
            pltpu.SemaphoreType.DMA,
            pltpu.SemaphoreType.DMA((2,)),
        ],
        compiler_params=pltpu.CompilerParams(vmem_limit_bytes=44 << 20),
        cost_estimate=pl.CostEstimate(
            flops=16 * tokens * width * width, bytes_accessed=8 * width * width, transcendentals=0
        ),
        name="attention_back",
    )(gathered, d_attn_low, proj, lse, mask, both, vec_now, base, pair, got)


def run_line(moves, below, above, terms, step, piece):
    shape = jax.ShapeDtypeStruct(below.shape, jnp.bfloat16)
    return pl.pallas_call(
        functools.partial(line_kernel, step=step, piece=piece),
        in_specs=smem(1) + vmem(2) + anywhere(1),
        out_specs=vmem(2),
        out_shape=[shape, shape],
        scratch_shapes=[
            pltpu.VMEM((2,) + below.shape, jnp.bfloat16),
            pltpu.SemaphoreType.DMA((2,)),
        ],
        compiler_params=pltpu.CompilerParams(vmem_limit_bytes=16 << 20),
        cost_estimate=pl.CostEstimate(
            flops=LINE_FLOPS, bytes_accessed=6 * below.size * 2, transcendentals=0
        ),
        name="line",
    )(moves, below, above, terms)


def run_products(info, needs, gathered, proj_parts, attn_parts, plane_h1, plane_d_down, pairs, piece):
    count = info.shape[0]
    sources, tokens, width = plane_h1.shape
    shape = jax.ShapeDtypeStruct((count, piece, width), jnp.bfloat16)
    made = pl.pallas_call(
        feed_forward_products_kernel,
        in_specs=smem(2) + anywhere(2 + len(pairs)),
        out_specs=vmem(1)[0],
        out_shape=shape,
        scratch_shapes=[
            pltpu.VMEM((2, sources * tokens, width), jnp.bfloat16),
            pltpu.VMEM((count, piece, width), jnp.bfloat16),
            pltpu.VMEM((count, piece, width), jnp.bfloat16),
            pltpu.SemaphoreType.DMA((2, sources)),
            pltpu.SemaphoreType.DMA((count,)),
            pltpu.SemaphoreType.DMA((count,)),
        ],
        compiler_params=pltpu.CompilerParams(vmem_limit_bytes=44 << 20),
        cost_estimate=pl.CostEstimate(
            flops=6 * count * sources * tokens * piece * width,
            bytes_accessed=6 * count * piece * width,
            transcendentals=0,
        ),
        name="feed_forward_products",
    )(info, needs, gathered, plane_d_down, *pairs)
    operands = (info, needs, plane_h1, *proj_parts, *attn_parts, *pairs, made)
    return pl.pallas_call(
        functools.partial(attention_products_kernel, sources=sources),
        in_specs=smem(2) + anywhere(len(operands) - 2),
        out_specs=anywhere(1)[0],
        out_shape=shape,
        scratch_shapes=[
            pltpu.VMEM((2, sources * tokens, width), jnp.bfloat16),
            pltpu.VMEM((count, sources * tokens, piece), jnp.bfloat16),
            pltpu.VMEM((count, piece, width), jnp.bfloat16),
            pltpu.SemaphoreType.DMA((2, sources)),
            pltpu.SemaphoreType.DMA((count, sources)),
            pltpu.SemaphoreType.DMA((count,)),
        ],
        input_output_aliases={len(operands) - 1: 0},
        compiler_params=pltpu.CompilerParams(vmem_limit_bytes=44 << 20),
        cost_estimate=pl.CostEstimate(
            flops=2 * count * sources * tokens * piece * width,
            bytes_accessed=2 * count * piece * width,
            transcendentals=0,
        ),
        name="attention_products",
    )(*operands)


def pad_rows(rows):
    return jnp.pad(rows, ((0, -rows.shape[0] % 16), (0, 0)))


def swap(values, axis, delta):
    size = lax.axis_size(axis)
    return lax.ppermute(values, axis, [(i, i ^ delta) for i in range(size)])


def sum_over(values, axes):
    for axis in axes:
        delta = 1
        while delta < lax.axis_size(axis):
            values = values + swap(values, axis, delta)
            delta *= 2
    return values


def line_order(line):
    due = np.zeros((line, line), np.int32)
    for here in range(line):
        for there in range(line):
            if there > here:
                due[here, there] = line - 1 - there + here
            elif there < here:
                due[here, there] = there - here + line - 1
            else:
                due[here, there] = line
    return np.argsort(due, axis=1, kind="stable").astype(np.int32)


def line_slots(line, order):
    ups = np.zeros((line - 1, line), np.int32)
    downs = np.zeros((line - 1, line), np.int32)
    for step in range(line - 1):
        for here in range(line):
            if here <= step:
                ups[step, here] = list(order[here]).index(line - 1 - step + here)
            if line - 1 - here <= step:
                downs[step, here] = list(order[here]).index(step - (line - 1) + here)
    return ups, downs


def added(*parts):
    return sum(part.astype(jnp.float32) for part in parts)


def due_after(value, *marks):
    flag = sum(mark[(-1,) * mark.ndim].astype(jnp.float32) for mark in marks)
    return value + (flag != flag).astype(value.dtype)


def plane_order(planes):
    deltas = [0]
    bit = planes // 2
    while bit >= 1:
        deltas = deltas + [delta ^ bit for delta in deltas]
        bit //= 2
    return deltas


def plane_gather(values):
    values = values[None]
    bit = lax.axis_size("fsdp") // 2
    while bit >= 1:
        values = jnp.concatenate([values, swap(values, "fsdp", bit)], axis=0)
        bit //= 2
    return values


def plane_operands(plane_rows, vec_now):
    sel_rows = plane_rows[:, 0].astype(jnp.float32)
    cot_rows = plane_rows[:, 1].astype(jnp.float32)
    gate = jax.nn.sigmoid(jnp.sum(sel_rows * vec_now[2], axis=-1, keepdims=True))
    inverse = lax.rsqrt(row_mean(sel_rows * sel_rows) + EPS_NORM)
    h1 = (sel_rows * inverse * vec_now[0]).astype(jnp.bfloat16)
    return (h1, (gate * cot_rows).astype(jnp.bfloat16))


def send_window(values, start, block):
    planes = lax.axis_size("fsdp")
    plane = lax.axis_index("fsdp")
    span = min(block, values.shape[1])
    stop = start + values.shape[1]

    def first(target):
        return jnp.clip(target * block - start, 0, values.shape[1] - span)

    def window(target):
        if span == values.shape[1]:
            return values
        return lax.dynamic_slice_in_dim(values, first(target), span, axis=1)

    def goes(target):
        return target * block < stop and (target + 1) * block > start

    parts = [window(plane)]
    for delta in plane_order(planes)[1:]:
        pairs = [(i, i ^ delta) for i in range(planes) if goes(i ^ delta)]
        parts.append(lax.ppermute(window(plane ^ delta), "fsdp", pairs))
    return parts


def window_start(width, start, block):
    return start + jnp.clip(
        lax.axis_index("fsdp") * block - start, 0, width - min(block, width)
    )


def gradient_plan(shard_rows, model_width, columns):
    planes, line = lax.axis_size("fsdp"), lax.axis_size("dp")
    plane, here = lax.axis_index("fsdp"), lax.axis_index("dp")
    hidden_units = (columns - 4 * model_width) // 2
    edges = (3 * model_width, 4 * model_width, 4 * model_width + hidden_units)

    def kind_of(row):
        return sum((row >= edge).astype(jnp.int32) for edge in edges)

    block = line * shard_rows
    proj_start = window_start(3 * model_width, 0, block)
    attn_start = window_start(model_width, 3 * model_width, block)
    piece = shard_rows // PIECES
    theres = jnp.asarray(line_order(line))[here]
    rows = (plane * line + theres)[:, None] * shard_rows + jnp.arange(PIECES) * piece
    rows = rows.reshape(-1)
    kinds = kind_of(rows)
    at = jnp.select(
        [kinds == 0, kinds == 1, kinds == 2],
        [rows - proj_start, rows - attn_start, rows],
        rows - hidden_units,
    )
    info = jnp.stack([kinds, at, jnp.minimum(rows + hidden_units, columns - piece)], axis=1)
    low, high = kind_of(plane * line * shard_rows), kind_of((plane + 1) * line * shard_rows - 1)
    ff = (high >= 2).astype(jnp.int32)
    has_proj = (low == 0).astype(jnp.int32)
    has_attn = ((low <= 1) & (high >= 1)).astype(jnp.int32)
    moves = jnp.asarray(np.stack(line_slots(line, line_order(line)), axis=-1))[:, here]
    return (info.astype(jnp.int32), jnp.stack([has_proj, has_attn, ff, ff]), moves)


def in_planes(shard_rows):
    return (shard_rows // PIECES) % 128 == 0


def gradient_whole(columns, operands):
    hidden_units = columns[2].shape[1] // 2
    factors = (*columns[:2], columns[2][:, :hidden_units], columns[2][:, hidden_units:])
    products = [tn(factor, operand) for factor, operand in zip(factors, operands)]
    low = jnp.concatenate(products, axis=0).astype(jnp.bfloat16)
    share = lax.psum_scatter(low, ("fsdp", "dp"), scatter_dimension=0, tiled=True)
    return share.astype(jnp.float32)


def plane_terms(
    gathered, late, d_attn_low, pairs, plane_h1, plane_d_down, info, needs, shard_rows
):
    planes, line = lax.axis_size("fsdp"), lax.axis_size("dp")
    block = line * shard_rows
    attn_parts = send_window(d_attn_low, late.shape[1], block)
    pairs = [pairs]
    bit = planes // 4
    while bit >= 1:
        pairs.append(swap(jnp.concatenate(pairs, axis=0), "fsdp", bit))
        bit //= 2
    proj_parts = send_window(late, 0, block)
    return run_products(
        info,
        needs,
        gathered,
        proj_parts,
        attn_parts,
        plane_h1,
        plane_d_down,
        pairs,
        shard_rows // PIECES,
    )


def gradient_share(terms, moves):
    line = lax.axis_size("dp")
    below, above = [None] * PIECES, [None] * PIECES
    for step in range(line - 1):
        for index in range(PIECES):
            if step == 0:
                up = down = terms[index]
            else:
                up, down = run_line(moves, below[index], above[index], terms, step, index)
            below[index] = lax.ppermute(up, "dp", [(p, p + 1) for p in range(step + 1)])
            above[index] = lax.ppermute(
                down, "dp", [(line - 1 - p, line - 2 - p) for p in range(step + 1)]
            )
    own = (line - 1) * PIECES
    sums = [added(terms[own + index], below[index], above[index]) for index in range(PIECES)]
    return jnp.concatenate(sums, axis=0)


def adamw(param, grad, first, second, step_count, rate, decay):
    first = BETA_ONE * first + (1.0 - BETA_ONE) * grad
    second = BETA_TWO * second + (1.0 - BETA_TWO) * grad * grad
    fixed_one = 1.0 - BETA_ONE**step_count
    fixed_two = 1.0 - BETA_TWO**step_count
    direction = first / fixed_one / (jnp.sqrt(second / fixed_two) + EPS_ADAM)
    return (param - rate * (direction + decay * param), first, second)


def vector_rates():
    return jnp.array([[0.1], [0.1], [0.02]], dtype=jnp.float32)


def on_device(
    tokens,
    cotangent,
    lengths,
    selected,
    weights,
    vectors,
    first_moment,
    second_moment,
    vec_first,
    vec_second,
    outer_moment,
    smoothed_matrix_mean,
    vec_outer,
    vec_average,
):
    master = weights
    vec_now = vectors
    first_now = first_moment[0]
    second_now = second_moment[0]
    vfirst_now = vec_first[0]
    vsecond_now = vec_second[0]
    model_width = tokens.shape[2]
    forward_steps = []
    backward_steps = []
    planes, line = lax.axis_size("fsdp"), lax.axis_size("dp")
    shard_rows = weights.shape[0]
    info, needs, moves = gradient_plan(shard_rows, model_width, weights.shape[0] * planes * line)
    boths, masks, across = run_gather(lengths[:, 0], selected[:, 0], tokens, cotangent)
    for inner_step in range(INNER):
        both, mask = boths[inner_step], masks[inner_step]
        plane_rows = plane_gather(both)
        shard_low = master.astype(jnp.bfloat16)
        gathered = lax.all_gather(shard_low, ("fsdp", "dp"), axis=0, tiled=True)
        plane_h1, plane_d_down = plane_operands(plane_rows, vec_now)
        proj, lse, pair, first_sum = run_attention(gathered, info, needs, moves, both, vec_now, mask)
        split = in_planes(shard_rows)
        d_attn_low, out_rows, base, grad_two, *kept = run_feed_forward(
            gathered, both, vec_now, first_sum, not split
        )
        got = swap(pair[None], "fsdp", planes // 2)
        late, d_rows, grad_one, pairs = run_attention_back(
            gathered, d_attn_low, proj, lse, mask, both, vec_now, base, pair, got
        )
        grad_vec = jnp.concatenate([grad_one, grad_two], axis=0)
        forward_steps.append(out_rows)
        backward_steps.append(d_rows)
        if split:
            terms = plane_terms(
                gathered, late, d_attn_low, pairs, plane_h1, plane_d_down, info, needs, shard_rows
            )
            grad_shard = gradient_share(terms, moves)
        else:
            grad_shard = gradient_whole(
                (late, d_attn_low, *kept), (plane_h1[0], pair[0], pair[1], plane_d_down[0])
            )
        grad_vec = sum_over(due_after(grad_vec, grad_shard), ("fsdp", "dp"))
        step_count = STEP + inner_step
        master, first_now, second_now = adamw(
            master, grad_shard, first_now, second_now, step_count, INNER_RATE, DECAY_RATE
        )
        vec_now, vfirst_now, vsecond_now = adamw(
            vec_now, grad_vec, vfirst_now, vsecond_now, step_count, vector_rates(), 0.0
        )
    groups = lax.axis_size("grp")
    delta = weights - master
    vector_change = vectors - vec_now
    col_width = weights.shape[1] // groups
    col_start = lax.axis_index("grp") * col_width
    here = lax.axis_index("grp")
    diff_share = lax.dynamic_slice_in_dim(delta, col_start, col_width, 1)
    for step in range(1, groups):
        there = lax.rem(here + step, groups)
        part = lax.dynamic_slice_in_dim(delta, there * col_width, col_width, 1)
        part = lax.ppermute(
            part.astype(jnp.bfloat16), "grp", [(i, (i + step) % groups) for i in range(groups)]
        )
        diff_share = diff_share + part.astype(jnp.float32)
    diff_share = diff_share / groups
    vec_diff = sum_over(vector_change, ("grp",)) / groups
    moment_share = OUTER_MOMENTUM * outer_moment + diff_share
    base_share = lax.dynamic_slice_in_dim(weights, col_start, col_width, 1)
    new_share = base_share - OUTER_RATE * (diff_share + OUTER_MOMENTUM * moment_share)
    low_share = new_share.astype(jnp.bfloat16)
    weights_low = jnp.zeros(weights.shape, jnp.bfloat16)
    weights_low = lax.dynamic_update_slice_in_dim(weights_low, low_share, col_start, 1)
    for step in range(1, groups):
        there = lax.rem(here + groups - step, groups)
        part = lax.ppermute(low_share, "grp", [(i, (i + step) % groups) for i in range(groups)])
        weights_low = lax.dynamic_update_slice_in_dim(weights_low, part, there * col_width, 1)
    weights_new = weights_low.astype(jnp.float32)
    average_new = AVERAGE_KEEP * smoothed_matrix_mean + (1.0 - AVERAGE_KEEP) * new_share
    vec_moment = OUTER_MOMENTUM * vec_outer + vec_diff
    vectors_new = vectors - OUTER_RATE * (vec_diff + OUTER_MOMENTUM * vec_moment)
    vec_average_new = AVERAGE_KEEP * vec_average + (1.0 - AVERAGE_KEEP) * vectors_new
    return (
        run_scatter(across, tokens, jnp.stack(forward_steps)),
        run_scatter(across, cotangent, jnp.stack(backward_steps)),
        weights_new,
        weights_low,
        first_now[None],
        second_now[None],
        moment_share,
        diff_share,
        average_new,
        vectors_new,
        vfirst_now[None],
        vsecond_now[None, :2],
        vsecond_now[None, 2],
        vec_moment,
        vec_average_new,
    )


def solution(mesh):
    placed = (
        P(None, ("grp", "fsdp", "dp"), None),
        P(None, ("grp", "fsdp", "dp"), None),
        P(None, ("grp", "fsdp", "dp"), None),
        P(None, ("grp", "fsdp", "dp"), None),
        P(("fsdp", "dp"), None),
        P(),
        P("grp", ("fsdp", "dp"), None),
        P("grp", ("fsdp", "dp"), None),
        P("grp", None, None),
        P("grp", None, None),
        P(("fsdp", "dp"), "grp"),
        P(("fsdp", "dp"), "grp"),
        P(),
        P(),
    )
    return jax.shard_map(
        on_device,
        mesh=mesh,
        in_specs=placed,
        out_specs=(
            P(None, ("grp", "fsdp", "dp"), None),
            P(None, ("grp", "fsdp", "dp"), None),
            P(("fsdp", "dp"), None),
            P(("fsdp", "dp"), None),
            P("grp", ("fsdp", "dp"), None),
            P("grp", ("fsdp", "dp"), None),
            P(("fsdp", "dp"), "grp"),
            P(("fsdp", "dp"), "grp"),
            P(("fsdp", "dp"), "grp"),
            P(),
            P("grp", None, None),
            P("grp", None, None),
            P("grp", None),
            P(),
            P(),
        ),
        check_vma=False,
    )
```

time: 848 us -> 727 us (0.86)
  matrix products: 117 us -> 0 us
  Pallas kernels: 0 us -> 101 us
  other arithmetic: 91 us -> 39 us
  waiting for transfers between devices: 425 us -> 392 us
  local copies, waits for them, and re-layouts: 59.1 us -> 31.3 us
  starting transfers between devices: 119 us -> 142 us
  between operations: 27.5 us -> 18.4 us
    dot_general x56 -> x0, matrix products: 117 us -> none  [the longest x8 43.4 us: contract_last(): lax.dot_general(left, right, (((1,), (1,)), ((), ())), preferred_element_...]
    pallas_call x0 -> x25, Pallas kernels: none -> 101 us  [the longest x2 24.5 us: run_feed_forward(): pl.pallas_call(functools.partial(feed_forward_kernel, keep=keep), in_spec...]
    scatter x4 -> x0, other arithmetic: 22.2 us -> none  [the longest x2 11.7 us: on_device(): backward_steps.append(cot_now.at[picked].set(d_rows.astype(jnp.bfloat16)))]
    ppermute x37 -> x17, waiting for transfers between devices: 70.3 us -> 52.8 us  [swap(): return lax.ppermute(values, axis, [(i, i ^ delta) for i in range(size)])]
    unnamed x202 -> x88, local copies, waits for them, and re-layouts: 6.85 us -> 23 us
    ppermute x18 -> x30, starting transfers between devices: 69.4 us -> 85.2 us  [the longest x18 68.7 us: gradient_share(): below[index] = lax.ppermute(up, 'dp', [(p, p + 1) for p in range(step + 1)])]
    concatenate x14 -> x4, other arithmetic: 19.5 us -> 4.37 us  [plane_gather(): values = jnp.concatenate([values, swap(values, 'fsdp', bit)], axis=0)]
    ppermute x1, waiting for transfers between devices: 13 us -> 0.01 us  [on_device(): lax.ppermute(part.astype(jnp.bfloat16), 'grp', [(i, (i + step) % groups)...]
  transfers between devices with their start and end apart: 77 -> 69, of which waited for: 37 -> 34; matrix products, arithmetic and copies ran while one was open for 16% -> 3% of each run, Pallas kernels for 0% -> 9%
where the time goes in v2:
time: 727 us; the launch traced here: 723 us
  waiting for transfers between devices  392 us (54%)
  starting transfers between devices  142 us (20%)
  Pallas kernels  101 us (14%)
  other arithmetic  39 us (5%)
  local copies, waits for them, and re-layouts  31.3 us (4%)
  between operations  18.4 us (3%)
    all_gather x2, waiting for transfers between devices, on_device(): gathered = lax.all_gather(shard_low, ('fsdp', 'dp'), axis=0, tiled=True)  219 us
    ppermute x18, waiting for transfers between devices, gradient_share(): below[index] = lax.ppermute(up, 'dp', [(p, p + 1) for p in range(step + 1)])  84.5 us
    ppermute x18, starting transfers between devices, gradient_share(): below[index] = lax.ppermute(up, 'dp', [(p, p + 1) for p in range(step + 1)])  68.7 us
    ppermute x17, waiting for transfers between devices, swap(): return lax.ppermute(values, axis, [(i, i ^ delta) for i in range(size)])  52.8 us
    ppermute x17, starting transfers between devices, swap(): return lax.ppermute(values, axis, [(i, i ^ delta) for i in range(size)])  37.7 us
    ppermute x12, waiting for transfers between devices, send_window(): parts.append(lax.ppermute(window(plane ^ delta), 'fsdp', pairs))  35.7 us
    pallas_call x2, Pallas kernels, run_feed_forward(): pl.pallas_call(functools.partial(feed_forward_kernel, keep=keep), in_spec...  24.5 us
    unnamed x88, local copies, waits for them, and re-layouts  23 us
  transfers between devices with their start and end apart: 69, of which 34 were waited for; matrix products, arithmetic and copies ran while one was open for 3% of the time, Pallas kernels for 9%

profile of v2, /device:TPU:0, one launch (start us, length us, event | category | flops | bytes accessed | tf_op | source)
XLA Modules:
  0.0 723.4 jit_solution(5574514498239285194)
XLA Ops:
  7.2 3.3 convert_element_type.246
  13.1 4.2 gather_rows.1
  17.3 3.0 collective-permute-start
  23.5 16.3 %collective-permute-done = bf16[1,2,144,1024]{3,2,0,1:T(8,128)(2,1)S(1)} collective-permute-done((bf16[1,2,144,1024]{3,2,0,1:T(8,128)(2,1)S(1)}, bf16[1,2,144,1024]{3,2,0,1:T(8,128)(2,1)S(1)}, u32[]{:S(2)}, u32[]{:S(2)}) %collective-permute-start) | collective-permute-done | bytes 589856 | tf_op jit(solution)/shard_map/ppermute | solution.py:653
  40.9 112.7 %all-gather.3.cloned.1.call-done.weights = bf16[12288,1024]{1,0:T(8,128)(2,1)} async-done(((bf16[768,1024]{1,0:T(8,128)(2,1)}), bf16[12288,1024]{1,0:T(8,128)(2,1)}) %all-gather.3.cloned.1.call-update) | async-done | bytes 25165840 | tf_op jit(solution)/shard_map/all_gather | solution.py:889
  153.6 7.3 %attention.2 = (bf16[144,3072]{1,0:T(8,128)(2,1)S(1)}, f32[288,128]{1,0:T(8,128)S(1)}, bf16[2,144,1024]{2,1,0:T(8,128)(2,1)S(1)}, f32[144,1024]{1,0:T(8,128)S(1)}) custom-call(bf16[12288,1024]{1,0:T(8,128)(2,1)} %all-gather.3.cloned.1.call-done.weights, s32[12,3]{1,0:T(8,128)S(1)} %copy.57.info, s32[4]{0:T(128)S(1)} %add_convert_fusion.needs, ...), custom_call_target="tpu_custom_call" | custom-call | flops 1207959552 | bytes 8388608 | tf_op jit(solution)/shard_map/attention/pallas_call | solution.py:490
  161.0 8.6 %collective-permute-start.2 = (bf16[1,2,144,1024]{3,2,1,0:T(8,128)(2,1)S(1)}, bf16[1,2,144,1024]{3,2,1,0:T(8,128)(2,1)S(1)}, u32[]{:S(2)}, u32[]{:S(2)}) collective-permute-start(bf16[1,2,144,1024]{3,2,1,0:T(8,128)(2,1)S(1)} %bitcast.142), channel_id=1, source_target_pairs={{0,8},{4,12},{8,0},{12,4},{1,9},{5,13},{9,1},{13,5},{2,10},{6,14},... | collective-permute-start | bytes 1769480 | tf_op jit(solution)/shard_map/ppermute | solution.py:653
  169.6 12.2 %feed_forward.2 = (bf16[144,1024]{1,0:T(8,128)(2,1)S(1)}, bf16[144,1024]{1,0:T(8,128)(2,1)S(1)}, f32[144,1024]{1,0:T(8,128)S(1)}, f32[2,1024]{1,0:T(2,128)S(1)}) custom-call(bf16[12288,1024]{1,0:T(8,128)(2,1)} %all-gather.3.cloned.1.call-done.weights, bf16[2,144,1024]{2,1,0:T(8,128)(2,1)S(1)} %get-tuple-element.68.both_ref, f32[3,1024]{1,0:T(4,128)S(1)} %copy-done.7, ...), custom_call_target="tpu_custom_call" | custom-call | flops 9663676416 | bytes 25165824 | tf_op jit(solution)/shard_map/feed_forward/pallas_call | solution.py:517
  183.4 7.1 attention_back.2
  193.9 3.0 collective-permute-start.7
  205.6 17.2 %collective-permute-done.3.refs_1_ = bf16[144,3072]{1,0:T(8,128)(2,1)S(1)} collective-permute-done((bf16[144,3072]{1,0:T(8,128)(2,1)S(1)}, bf16[144,3072]{1,0:T(8,128)(2,1)S(1)}, u32[]{:S(2)}, u32[]{:S(2)}) %collective-permute-start.3) | collective-permute-done | bytes 884768 | tf_op jit(solution)/shard_map/ppermute | solution.py:746
  223.5 10.6 %attention_products.2.terms_ref = bf16[12,256,1024]{2,1,0:T(8,128)(2,1)} custom-call(s32[12,3]{1,0:T(8,128)S(1)} %copy.57.info, s32[4]{0:T(128)S(1)} %add_convert_fusion.needs, bf16[4,144,1024]{2,1,0:T(8,128)(2,1)S(1)} %get-tuple-element.184.h1_ref, bf16[144,3072]{1,0:T(8,128)(2,1)S(1)} %get-tuple-element.78.refs_0_, ...), custom_call_target="tpu_custom_call", output_to_operand_aliasing={{}: (13, {})} | custom-call | flops 3623878656 | bytes 6291456 | tf_op jit(solution)/shard_map/attention_products/pallas_call | solution.py:623
  241.0 8.3 %collective-permute-done.16.below_ref = bf16[256,1024]{1,0:T(8,128)(2,1)S(1)} collective-permute-done((bf16[256,1024]{1,0:T(8,128)(2,1)S(1)}, bf16[256,1024]{1,0:T(8,128)(2,1)S(1)}, u32[]{:S(2)}, u32[]{:S(2)}) %collective-permute-start.16) | collective-permute-done | bytes 524320 | tf_op jit(solution)/shard_map/ppermute | solution.py:834
  249.9 2.8 copy-done.6
  253.7 4.4 collective-permute-start.18
  262.2 5.0 collective-permute-start.24
  267.2 4.5 collective-permute-done.10.below_ref
  273.4 5.0 collective-permute-start.12
  278.4 4.5 collective-permute-done.18.below_ref
  284.6 5.0 collective-permute-start.20
  289.7 4.5 collective-permute-done.24.below_ref
  296.5 5.0 collective-permute-start.26
  301.5 3.9 collective-permute-done.12.below_ref
  307.7 5.0 collective-permute-start.14
  312.8 3.9 collective-permute-done.20
  318.2 6.4 collective-permute-done.26
  324.6 5.6 collective-permute-done.14
  333.9 3.7 fusion.20
  339.7 13.7 %collective-permute-done.33 = bf16[1,2,144,1024]{3,2,0,1:T(8,128)(2,1)S(1)} collective-permute-done((bf16[1,2,144,1024]{3,2,0,1:T(8,128)(2,1)S(1)}, bf16[1,2,144,1024]{3,2,0,1:T(8,128)(2,1)S(1)}, u32[]{:S(2)}, u32[]{:S(2)}) %collective-permute-start.33) | collective-permute-done | bytes 589856 | tf_op jit(solution)/shard_map/ppermute | solution.py:653
  353.6 2.9 collective-permute-start.34
  359.7 2.7 collective-permute-start.29
  364.2 3.9 collective-permute-done.30
  368.1 3.2 collective-permute-start.31
  373.3 106.1 %all-gather.5.cloned.1.call-done.weights = bf16[12288,1024]{1,0:T(8,128)(2,1)} async-done(((bf16[768,1024]{1,0:T(8,128)(2,1)}), bf16[12288,1024]{1,0:T(8,128)(2,1)}) %all-gather.5.cloned.1.call-update) | async-done | bytes 25165840 | tf_op jit(solution)/shard_map/all_gather | solution.py:889
  479.4 7.3 %attention.3 = (bf16[144,3072]{1,0:T(8,128)(2,1)S(1)}, f32[288,128]{1,0:T(8,128)S(1)}, bf16[2,144,1024]{2,1,0:T(8,128)(2,1)S(1)}, f32[144,1024]{1,0:T(8,128)S(1)}) custom-call(bf16[12288,1024]{1,0:T(8,128)(2,1)} %all-gather.5.cloned.1.call-done.weights, s32[12,3]{1,0:T(8,128)S(1)} %copy.57.info, s32[4]{0:T(128)S(1)} %add_convert_fusion.needs, ...), custom_call_target="tpu_custom_call" | custom-call | flops 1207959552 | bytes 8388608 | tf_op jit(solution)/shard_map/attention/pallas_call | solution.py:490
  486.7 4.2 collective-permute-start.32
  491.0 12.4 %feed_forward.3 = (bf16[144,1024]{1,0:T(8,128)(2,1)S(1)}, bf16[144,1024]{1,0:T(8,128)(2,1)S(1)}, f32[144,1024]{1,0:T(8,128)S(1)}, f32[2,1024]{1,0:T(2,128)S(1)}) custom-call(bf16[12288,1024]{1,0:T(8,128)(2,1)} %all-gather.5.cloned.1.call-done.weights, bf16[2,144,1024]{2,1,0:T(8,128)(2,1)S(1)} %get-tuple-element.92.both_ref, ...), custom_call_target="tpu_custom_call" | custom-call | flops 9663676416 | bytes 25165824 | tf_op jit(solution)/shard_map/feed_forward/pallas_call | solution.py:517
  504.0 7.2 %attention_back.3 = (bf16[144,3072]{1,0:T(8,128)(2,1)S(1)}, bf16[144,1024]{1,0:T(8,128)(2,1)S(1)}, f32[1,1024]{1,0:T(1,128)S(1)}, bf16[2,2,144,1024]{3,2,1,0:T(8,128)(2,1)S(1)}) custom-call(bf16[12288,1024]{1,0:T(8,128)(2,1)} %all-gather.5.cloned.1.call-done.weights, bf16[144,1024]{1,0:T(8,128)(2,1)S(1)} %get-tuple-element.99.d_attn_ref.refs_4_, ...), custom_call_target="tpu_custom_call" | custom-call | flops 2415919104 | bytes 8388608 | tf_op jit(solution)/shard_map/attention_back/pallas_call | solution.py:553
  513.1 3.0 collective-permute-start.39
  524.9 17.2 %collective-permute-done.35.refs_1_ = bf16[144,3072]{1,0:T(8,128)(2,1)S(1)} collective-permute-done((bf16[144,3072]{1,0:T(8,128)(2,1)S(1)}, bf16[144,3072]{1,0:T(8,128)(2,1)S(1)}, u32[]{:S(2)}, u32[]{:S(2)}) %collective-permute-start.35) | collective-permute-done | bytes 884768 | tf_op jit(solution)/shard_map/ppermute | solution.py:746
  542.7 10.6 %attention_products.3.terms_ref = bf16[12,256,1024]{2,1,0:T(8,128)(2,1)} custom-call(s32[12,3]{1,0:T(8,128)S(1)} %copy.57.info, s32[4]{0:T(128)S(1)} %add_convert_fusion.needs, bf16[4,144,1024]{2,1,0:T(8,128)(2,1)S(1)} %get-tuple-element.182.h1_ref, bf16[144,3072]{1,0:T(8,128)(2,1)S(1)} %get-tuple-element.105.refs_0_, ...), custom_call_target="tpu_custom_call", output_to_operand_aliasing={{}: (13, {})} | custom-call | flops 3623878656 | bytes 6291456 | tf_op jit(solution)/shard_map/attention_products/pallas_call | solution.py:623
  560.3 8.3 %collective-permute-done.48.below_ref = bf16[256,1024]{1,0:T(8,128)(2,1)S(1)} collective-permute-done((bf16[256,1024]{1,0:T(8,128)(2,1)S(1)}, bf16[256,1024]{1,0:T(8,128)(2,1)S(1)}, u32[]{:S(2)}, u32[]{:S(2)}) %collective-permute-start.48) | collective-permute-done | bytes 524320 | tf_op jit(solution)/shard_map/ppermute | solution.py:834
  569.3 2.8 copy-done.4
  573.1 4.4 collective-permute-start.50
  581.8 5.0 collective-permute-start.56
  586.8 4.2 collective-permute-done.42.below_ref
  592.7 5.0 collective-permute-start.44
  597.8 4.5 collective-permute-done.50.below_ref
  604.0 5.0 collective-permute-start.52
  609.0 4.5 collective-permute-done.56.below_ref
  615.8 5.8 collective-permute-start.58
  621.6 3.1 collective-permute-done.44.below_ref
  627.8 5.9 collective-permute-start.46
  638.1 5.8 collective-permute-done.58
  643.9 5.7 collective-permute-done.46
  649.6 3.3 fusion.23
  652.9 7.3 %subtract_subtract_fusion = f32[768,1024]{1,0:T(8,128)S(1)} fusion(f32[768,1024]{1,0:T(8,128)S(1)} %copy-done.12, f32[256,1024]{1,0:T(8,128)S(1)} %get-tuple-element.170, f32[256,1024]{1,0:T(8,128)S(1)} %get-tuple-element.171, f32[256,1024]{1,0:T(8,128)S(1)} %get-tuple-element.169, f32[256,1024]{1,0:T(8,128)} %copy-done.22, f32[256,1024]{1,0:T(8,128)} %copy-done.24, ...), kind=kLoop, calls=%fused_computation.26 | loop fusion | flops 27525120 | bytes 18874368 | tf_op jit(solution)/shard_map/sub | solution.py:921
  667.8 3.8 collective-permute-start.63
  673.9 3.0 scatter_rows.2
  681.5 3.1 scatter_rows.3
  684.7 4.0 collective-permute-start.65
  688.8 4.3 multiply_add_fusion.1
  695.1 3.6 fusion.9
  701.2 12.0 %collective-permute-done.66 = f32[3,1024]{1,0:T(4,128)S(1)} collective-permute-done((f32[3,1024]{1,0:T(4,128)S(1)}, f32[3,1024]{1,0:T(4,128)S(1)}, u32[]{:S(2)}, u32[]{:S(2)}) %collective-permute-start.66) | collective-permute-done | bytes 12320 | tf_op jit(solution)/shard_map/ppermute | solution.py:653
  (254 shorter events, 113.0 us)
Async XLA Ops:
  7.2 146.4 %all-gather.3.cloned.1.call-start = ((), (), s32[]{:S(2)}) async-start(), calls=%async_computation | async-start | bytes 26738688 | tf_op jit(solution)/shard_map/all_gather | solution.py:889
  10.6 468.8 %all-gather.5.cloned.1.call-start = ((), (), s32[]{:S(2)}) async-start(), calls=%async_computation.1 | async-start | bytes 26738688 | tf_op jit(solution)/shard_map/all_gather | solution.py:889
  17.3 22.5 %collective-permute-start = (bf16[1,2,144,1024]{3,2,0,1:T(8,128)(2,1)S(1)}, bf16[1,2,144,1024]{3,2,0,1:T(8,128)(2,1)S(1)}, u32[]{:S(2)}, u32[]{:S(2)}) collective-permute-start(bf16[1,2,144,1024]{3,2,0,1:T(8,128)(2,1)S(1)} %bitcast.138), channel_id=1, source_target_pairs={{0,8},{4,12},{8,0},{12,4},{1,9},{5,13},{9,1},{13,5},{2,10},{6,14},... | collective-permute-start | bytes 1769480 | tf_op jit(solution)/shard_map/ppermute | solution.py:653
  40.9 149.7 %collective-permute-start.1 = (bf16[2,2,144,1024]{3,2,0,1:T(8,128)(2,1)}, bf16[2,2,144,1024]{3,2,0,1:T(8,128)(2,1)}, u32[]{:S(2)}, u32[]{:S(2)}) collective-permute-start(bf16[2,2,144,1024]{3,2,0,1:T(8,128)(2,1)} %pad_maximum_fusion.6), channel_id=1, source_target_pairs={{0,4},{4,0},{8,12},{12,8},{1,5},{5,1},{9,13},{13,9},{2,6},{6,2},{1... | collective-permute-start | bytes 3538952 | tf_op jit(solution)/shard_map/ppermute | solution.py:653
  161.0 22.5 %collective-permute-start.2 = (bf16[1,2,144,1024]{3,2,1,0:T(8,128)(2,1)S(1)}, bf16[1,2,144,1024]{3,2,1,0:T(8,128)(2,1)S(1)}, u32[]{:S(2)}, u32[]{:S(2)}) collective-permute-start(bf16[1,2,144,1024]{3,2,1,0:T(8,128)(2,1)S(1)} %bitcast.142), channel_id=1, source_target_pairs={{0,8},{4,12},{8,0},{12,4},{1,9},{5,13},{9,1},{13,5},{2,10},{6,14},... | collective-permute-start | bytes 1769480 | tf_op jit(solution)/shard_map/ppermute | solution.py:653
  190.5 9.7 %collective-permute-start.9 = (bf16[2,2,144,1024]{3,2,1,0:T(8,128)(2,1)S(1)}, bf16[2,2,144,1024]{3,2,1,0:T(8,128)(2,1)S(1)}, u32[]{:S(2)}, u32[]{:S(2)}) collective-permute-start(bf16[2,2,144,1024]{3,2,1,0:T(8,128)(2,1)S(1)} %get-tuple-element.79.refs_0_.refs_8_), channel_id=1, source_target_pairs={{0,4},{4,0},{8,12},{12,8},{1,5},{5,1},{9,13},{13,9},{2,6},{6,2},{1... | collective-permute-start | bytes 3538952 | tf_op jit(solution)/shard_map/ppermute | solution.py:653
  192.7 6.2 collective-permute-start.6
  193.9 11.7 %collective-permute-start.7 = (bf16[144,1024]{1,0:T(8,128)(2,1)S(1)}, bf16[144,1024]{1,0:T(8,128)(2,1)S(1)}, u32[]{:S(2)}, u32[]{:S(2)}) collective-permute-start(bf16[144,1024]{1,0:T(8,128)(2,1)S(1)} %get-tuple-element.73.d_attn_ref.refs_4_), channel_id=1, source_target_pairs={{0,4},{1,5},{2,6},{3,7},{16,20},{17,21},{18,22},{19,23}} | collective-permute-start | bytes 884744 | tf_op jit(solution)/shard_map/ppermute | solution.py:746
  196.9 8.7 %collective-permute-start.8 = (bf16[144,1024]{1,0:T(8,128)(2,1)S(1)}, bf16[144,1024]{1,0:T(8,128)(2,1)S(1)}, u32[]{:S(2)}, u32[]{:S(2)}) collective-permute-start(bf16[144,1024]{1,0:T(8,128)(2,1)S(1)} %get-tuple-element.73.d_attn_ref.refs_4_), channel_id=1, source_target_pairs={{8,4},{9,5},{10,6},{11,7},{24,20},{25,21},{26,22},{27,23}} | collective-permute-start | bytes 884744 | tf_op jit(solution)/shard_map/ppermute | solution.py:746
  197.6 25.2 %collective-permute-start.3 = (bf16[144,3072]{1,0:T(8,128)(2,1)S(1)}, bf16[144,3072]{1,0:T(8,128)(2,1)S(1)}, u32[]{:S(2)}, u32[]{:S(2)}) collective-permute-start(bf16[144,3072]{1,0:T(8,128)(2,1)S(1)} %get-tuple-element.78.refs_0_), channel_id=1, source_target_pairs={{8,0},{9,1},{10,2},{11,3},{24,16},{25,17},{26,18},{27,19}} | collective-permute-start | bytes 2654216 | tf_op jit(solution)/shard_map/ppermute | solution.py:746
  198.9 23.9 %collective-permute-start.4 = (bf16[144,3072]{1,0:T(8,128)(2,1)S(1)}, bf16[144,3072]{1,0:T(8,128)(2,1)S(1)}, u32[]{:S(2)}, u32[]{:S(2)}) collective-permute-start(bf16[144,3072]{1,0:T(8,128)(2,1)S(1)} %get-tuple-element.78.refs_0_), channel_id=1, source_target_pairs={{4,0},{5,1},{6,2},{7,3},{20,16},{21,17},{22,18},{23,19}} | collective-permute-start | bytes 2654216 | tf_op jit(solution)/shard_map/ppermute | solution.py:746
  200.2 23.2 %collective-permute-start.5 = (bf16[144,3072]{1,0:T(8,128)(2,1)S(1)}, bf16[144,3072]{1,0:T(8,128)(2,1)S(1)}, u32[]{:S(2)}, u32[]{:S(2)}) collective-permute-start(bf16[144,3072]{1,0:T(8,128)(2,1)S(1)} %get-tuple-element.78.refs_0_), channel_id=1, source_target_pairs={{12,0},{13,1},{14,2},{15,3},{28,16},{29,17},{30,18},{31,19}} | collective-permute-start | bytes 2654216 | tf_op jit(solution)/shard_map/ppermute | solution.py:746
  235.6 13.7 %collective-permute-start.16 = (bf16[256,1024]{1,0:T(8,128)(2,1)S(1)}, bf16[256,1024]{1,0:T(8,128)(2,1)S(1)}, u32[]{:S(2)}, u32[]{:S(2)}) collective-permute-start(bf16[256,1024]{1,0:T(8,128)(2,1)S(1)} %get-tuple-element.180), channel_id=1, source_target_pairs={{0,1},{4,5},{8,9},{12,13},{16,17},{20,21},{24,25},{28,29}} | collective-permute-start | bytes 1572872 | tf_op jit(solution)/shard_map/ppermute | solution.py:834
  236.9 13.0 %collective-permute-start.17 = (bf16[256,1024]{1,0:T(8,128)(2,1)S(1)}, bf16[256,1024]{1,0:T(8,128)(2,1)S(1)}, u32[]{:S(2)}, u32[]{:S(2)}) collective-permute-start(bf16[256,1024]{1,0:T(8,128)(2,1)S(1)} %get-tuple-element.180), channel_id=1, source_target_pairs={{3,2},{7,6},{11,10},{15,14},{19,18},{23,22},{27,26},{31,30}} | collective-permute-start | bytes 1572872 | tf_op jit(solution)/shard_map/ppermute | solution.py:835
  237.6 22.9 %collective-permute-start.22 = (bf16[256,1024]{1,0:T(8,128)(2,1)S(1)}, bf16[256,1024]{1,0:T(8,128)(2,1)S(1)}, u32[]{:S(2)}, u32[]{:S(2)}) collective-permute-start(bf16[256,1024]{1,0:T(8,128)(2,1)S(1)} %get-tuple-element.179), channel_id=1, source_target_pairs={{0,1},{4,5},{8,9},{12,13},{16,17},{20,21},{24,25},{28,29}} | collective-permute-start | bytes 1572872 | tf_op jit(solution)/shard_map/ppermute | solution.py:834
  238.9 22.2 %collective-permute-start.23 = (bf16[256,1024]{1,0:T(8,128)(2,1)S(1)}, bf16[256,1024]{1,0:T(8,128)(2,1)S(1)}, u32[]{:S(2)}, u32[]{:S(2)}) collective-permute-start(bf16[256,1024]{1,0:T(8,128)(2,1)S(1)} %get-tuple-element.179), channel_id=1, source_target_pairs={{3,2},{7,6},{11,10},{15,14},{19,18},{23,22},{27,26},{31,30}} | collective-permute-start | bytes 1572872 | tf_op jit(solution)/shard_map/ppermute | solution.py:835
  239.6 32.1 %collective-permute-start.10 = (bf16[256,1024]{1,0:T(8,128)(2,1)S(1)}, bf16[256,1024]{1,0:T(8,128)(2,1)S(1)}, u32[]{:S(2)}, u32[]{:S(2)}) collective-permute-start(bf16[256,1024]{1,0:T(8,128)(2,1)S(1)} %get-tuple-element.178), channel_id=1, source_target_pairs={{0,1},{4,5},{8,9},{12,13},{16,17},{20,21},{24,25},{28,29}} | collective-permute-start | bytes 1572872 | tf_op jit(solution)/shard_map/ppermute | solution.py:834
  249.2 23.2 %collective-permute-start.11 = (bf16[256,1024]{1,0:T(8,128)(2,1)S(1)}, bf16[256,1024]{1,0:T(8,128)(2,1)S(1)}, u32[]{:S(2)}, u32[]{:S(2)}) collective-permute-start(bf16[256,1024]{1,0:T(8,128)(2,1)S(1)} %get-tuple-element.178), channel_id=1, source_target_pairs={{3,2},{7,6},{11,10},{15,14},{19,18},{23,22},{27,26},{31,30}} | collective-permute-start | bytes 1572872 | tf_op jit(solution)/shard_map/ppermute | solution.py:835
  253.7 29.2 %collective-permute-start.18 = (bf16[256,1024]{1,0:T(8,128)(2,1)S(1)}, bf16[256,1024]{1,0:T(8,128)(2,1)S(1)}, u32[]{:S(2)}, u32[]{:S(2)}) collective-permute-start(bf16[256,1024]{1,0:T(8,128)(2,1)S(1)} %get-tuple-element.84), channel_id=1, source_target_pairs={{0,1},{1,2},{4,5},{5,6},{8,9},{9,10},{12,13},{13,14},{16,17},{17,1... | collective-permute-start | bytes 1572872 | tf_op jit(solution)/shard_map/ppermute | solution.py:834
  260.5 23.2 %collective-permute-start.19 = (bf16[256,1024]{1,0:T(8,128)(2,1)S(1)}, bf16[256,1024]{1,0:T(8,128)(2,1)S(1)}, u32[]{:S(2)}, u32[]{:S(2)}) collective-permute-start(bf16[256,1024]{1,0:T(8,128)(2,1)S(1)} %get-tuple-element.85), channel_id=1, source_target_pairs={{3,2},{2,1},{7,6},{6,5},{11,10},{10,9},{15,14},{14,13},{19,18},{18... | collective-permute-start | bytes 1572872 | tf_op jit(solution)/shard_map/ppermute | solution.py:835
  262.2 32.0 %collective-permute-start.24 = (bf16[256,1024]{1,0:T(8,128)(2,1)S(1)}, bf16[256,1024]{1,0:T(8,128)(2,1)S(1)}, u32[]{:S(2)}, u32[]{:S(2)}) collective-permute-start(bf16[256,1024]{1,0:T(8,128)(2,1)S(1)} %get-tuple-element.88), channel_id=1, source_target_pairs={{0,1},{1,2},{4,5},{5,6},{8,9},{9,10},{12,13},{13,14},{16,17},{17,1... | collective-permute-start | bytes 1572872 | tf_op jit(solution)/shard_map/ppermute | solution.py:834
  271.7 23.8 %collective-permute-start.25 = (bf16[256,1024]{1,0:T(8,128)(2,1)S(1)}, bf16[256,1024]{1,0:T(8,128)(2,1)S(1)}, u32[]{:S(2)}, u32[]{:S(2)}) collective-permute-start(bf16[256,1024]{1,0:T(8,128)(2,1)S(1)} %get-tuple-element.89), channel_id=1, source_target_pairs={{3,2},{2,1},{7,6},{6,5},{11,10},{10,9},{15,14},{14,13},{19,18},{18... | collective-permute-start | bytes 1572872 | tf_op jit(solution)/shard_map/ppermute | solution.py:835
  273.4 32.0 %collective-permute-start.12 = (bf16[256,1024]{1,0:T(8,128)(2,1)S(1)}, bf16[256,1024]{1,0:T(8,128)(2,1)S(1)}, u32[]{:S(2)}, u32[]{:S(2)}) collective-permute-start(bf16[256,1024]{1,0:T(8,128)(2,1)S(1)} %get-tuple-element.80), channel_id=1, source_target_pairs={{0,1},{1,2},{4,5},{5,6},{8,9},{9,10},{12,13},{13,14},{16,17},{17,1... | collective-permute-start | bytes 1572872 | tf_op jit(solution)/shard_map/ppermute | solution.py:834
  282.9 23.8 %collective-permute-start.13 = (bf16[256,1024]{1,0:T(8,128)(2,1)S(1)}, bf16[256,1024]{1,0:T(8,128)(2,1)S(1)}, u32[]{:S(2)}, u32[]{:S(2)}) collective-permute-start(bf16[256,1024]{1,0:T(8,128)(2,1)S(1)} %get-tuple-element.81), channel_id=1, source_target_pairs={{3,2},{2,1},{7,6},{6,5},{11,10},{10,9},{15,14},{14,13},{19,18},{18... | collective-permute-start | bytes 1572872 | tf_op jit(solution)/shard_map/ppermute | solution.py:835
  284.6 32.0 %collective-permute-start.20 = (bf16[256,1024]{1,0:T(8,128)(2,1)S(1)}, bf16[256,1024]{1,0:T(8,128)(2,1)S(1)}, u32[]{:S(2)}, u32[]{:S(2)}) collective-permute-start(bf16[256,1024]{1,0:T(8,128)(2,1)S(1)} %get-tuple-element.86), channel_id=1, source_target_pairs={{0,1},{1,2},{2,3},{4,5},{5,6},{6,7},{8,9},{9,10},{10,11},{12,13},{... | collective-permute-start | bytes 1572872 | tf_op jit(solution)/shard_map/ppermute | solution.py:834
  294.2 24.0 %collective-permute-start.21 = (bf16[256,1024]{1,0:T(8,128)(2,1)S(1)}, bf16[256,1024]{1,0:T(8,128)(2,1)S(1)}, u32[]{:S(2)}, u32[]{:S(2)}) collective-permute-start(bf16[256,1024]{1,0:T(8,128)(2,1)S(1)} %get-tuple-element.87), channel_id=1, source_target_pairs={{3,2},{2,1},{1,0},{7,6},{6,5},{5,4},{11,10},{10,9},{9,8},{15,14},{... | collective-permute-start | bytes 1572872 | tf_op jit(solution)/shard_map/ppermute | solution.py:835
  296.5 28.2 %collective-permute-start.26 = (bf16[256,1024]{1,0:T(8,128)(2,1)S(1)}, bf16[256,1024]{1,0:T(8,128)(2,1)S(1)}, u32[]{:S(2)}, u32[]{:S(2)}) collective-permute-start(bf16[256,1024]{1,0:T(8,128)(2,1)S(1)} %get-tuple-element.90), channel_id=1, source_target_pairs={{0,1},{1,2},{2,3},{4,5},{5,6},{6,7},{8,9},{9,10},{10,11},{12,13},{... | collective-permute-start | bytes 1572872 | tf_op jit(solution)/shard_map/ppermute | solution.py:834
  305.4 19.2 %collective-permute-start.27 = (bf16[256,1024]{1,0:T(8,128)(2,1)S(1)}, bf16[256,1024]{1,0:T(8,128)(2,1)S(1)}, u32[]{:S(2)}, u32[]{:S(2)}) collective-permute-start(bf16[256,1024]{1,0:T(8,128)(2,1)S(1)} %get-tuple-element.91), channel_id=1, source_target_pairs={{3,2},{2,1},{1,0},{7,6},{6,5},{5,4},{11,10},{10,9},{9,8},{15,14},{... | collective-permute-start | bytes 1572872 | tf_op jit(solution)/shard_map/ppermute | solution.py:835
  307.7 22.5 %collective-permute-start.14 = (bf16[256,1024]{1,0:T(8,128)(2,1)S(1)}, bf16[256,1024]{1,0:T(8,128)(2,1)S(1)}, u32[]{:S(2)}, u32[]{:S(2)}) collective-permute-start(bf16[256,1024]{1,0:T(8,128)(2,1)S(1)} %get-tuple-element.82), channel_id=1, source_target_pairs={{0,1},{1,2},{2,3},{4,5},{5,6},{6,7},{8,9},{9,10},{10,11},{12,13},{... | collective-permute-start | bytes 1572872 | tf_op jit(solution)/shard_map/ppermute | solution.py:834
  316.6 13.6 %collective-permute-start.15 = (bf16[256,1024]{1,0:T(8,128)(2,1)S(1)}, bf16[256,1024]{1,0:T(8,128)(2,1)S(1)}, u32[]{:S(2)}, u32[]{:S(2)}) collective-permute-start(bf16[256,1024]{1,0:T(8,128)(2,1)S(1)} %get-tuple-element.83), channel_id=1, source_target_pairs={{3,2},{2,1},{1,0},{7,6},{6,5},{5,4},{11,10},{10,9},{9,8},{15,14},{... | collective-permute-start | bytes 1572872 | tf_op jit(solution)/shard_map/ppermute | solution.py:835
  337.6 15.8 %collective-permute-start.33 = (bf16[1,2,144,1024]{3,2,0,1:T(8,128)(2,1)S(1)}, bf16[1,2,144,1024]{3,2,0,1:T(8,128)(2,1)S(1)}, u32[]{:S(2)}, u32[]{:S(2)}) collective-permute-start(bf16[1,2,144,1024]{3,2,0,1:T(8,128)(2,1)S(1)} %bitcast.135), channel_id=1, source_target_pairs={{0,8},{4,12},{8,0},{12,4},{1,9},{5,13},{9,1},{13,5},{2,10},{6,14},... | collective-permute-start | bytes 1769480 | tf_op jit(solution)/shard_map/ppermute | solution.py:653
  353.6 17.7 %collective-permute-start.34 = (bf16[2,2,144,1024]{3,2,0,1:T(8,128)(2,1)S(1)}, bf16[2,2,144,1024]{3,2,0,1:T(8,128)(2,1)S(1)}, u32[]{:S(2)}, u32[]{:S(2)}) collective-permute-start(bf16[2,2,144,1024]{3,2,0,1:T(8,128)(2,1)S(1)} %pad_maximum_fusion.7), channel_id=1, source_target_pairs={{0,4},{4,0},{8,12},{12,8},{1,5},{5,1},{9,13},{13,9},{2,6},{6,2},{1... | collective-permute-start | bytes 3538952 | tf_op jit(solution)/shard_map/ppermute | solution.py:653
  486.7 17.3 %collective-permute-start.32 = (bf16[1,2,144,1024]{3,2,1,0:T(8,128)(2,1)S(1)}, bf16[1,2,144,1024]{3,2,1,0:T(8,128)(2,1)S(1)}, u32[]{:S(2)}, u32[]{:S(2)}) collective-permute-start(bf16[1,2,144,1024]{3,2,1,0:T(8,128)(2,1)S(1)} %bitcast.141), channel_id=1, source_target_pairs={{0,8},{4,12},{8,0},{12,4},{1,9},{5,13},{9,1},{13,5},{2,10},{6,14},... | collective-permute-start | bytes 1769480 | tf_op jit(solution)/shard_map/ppermute | solution.py:653
  511.3 8.2 %collective-permute-start.41 = (bf16[2,2,144,1024]{3,2,1,0:T(8,128)(2,1)S(1)}, bf16[2,2,144,1024]{3,2,1,0:T(8,128)(2,1)S(1)}, u32[]{:S(2)}, u32[]{:S(2)}) collective-permute-start(bf16[2,2,144,1024]{3,2,1,0:T(8,128)(2,1)S(1)} %get-tuple-element.106.refs_0_.refs_8_), channel_id=1, source_target_pairs={{0,4},{4,0},{8,12},{12,8},{1,5},{5,1},{9,13},{13,9},{2,6},{6,2},{1... | collective-permute-start | bytes 3538952 | tf_op jit(solution)/shard_map/ppermute | solution.py:653
  511.9 6.2 collective-permute-start.38
  513.1 11.7 %collective-permute-start.39 = (bf16[144,1024]{1,0:T(8,128)(2,1)S(1)}, bf16[144,1024]{1,0:T(8,128)(2,1)S(1)}, u32[]{:S(2)}, u32[]{:S(2)}) collective-permute-start(bf16[144,1024]{1,0:T(8,128)(2,1)S(1)} %get-tuple-element.99.d_attn_ref.refs_4_), channel_id=1, source_target_pairs={{0,4},{1,5},{2,6},{3,7},{16,20},{17,21},{18,22},{19,23}} | collective-permute-start | bytes 884744 | tf_op jit(solution)/shard_map/ppermute | solution.py:746
  516.1 8.7 %collective-permute-start.40 = (bf16[144,1024]{1,0:T(8,128)(2,1)S(1)}, bf16[144,1024]{1,0:T(8,128)(2,1)S(1)}, u32[]{:S(2)}, u32[]{:S(2)}) collective-permute-start(bf16[144,1024]{1,0:T(8,128)(2,1)S(1)} %get-tuple-element.99.d_attn_ref.refs_4_), channel_id=1, source_target_pairs={{8,4},{9,5},{10,6},{11,7},{24,20},{25,21},{26,22},{27,23}} | collective-permute-start | bytes 884744 | tf_op jit(solution)/shard_map/ppermute | solution.py:746
  516.8 25.2 %collective-permute-start.35 = (bf16[144,3072]{1,0:T(8,128)(2,1)S(1)}, bf16[144,3072]{1,0:T(8,128)(2,1)S(1)}, u32[]{:S(2)}, u32[]{:S(2)}) collective-permute-start(bf16[144,3072]{1,0:T(8,128)(2,1)S(1)} %get-tuple-element.105.refs_0_), channel_id=1, source_target_pairs={{8,0},{9,1},{10,2},{11,3},{24,16},{25,17},{26,18},{27,19}} | collective-permute-start | bytes 2654216 | tf_op jit(solution)/shard_map/ppermute | solution.py:746
  518.1 23.9 %collective-permute-start.36 = (bf16[144,3072]{1,0:T(8,128)(2,1)S(1)}, bf16[144,3072]{1,0:T(8,128)(2,1)S(1)}, u32[]{:S(2)}, u32[]{:S(2)}) collective-permute-start(bf16[144,3072]{1,0:T(8,128)(2,1)S(1)} %get-tuple-element.105.refs_0_), channel_id=1, source_target_pairs={{4,0},{5,1},{6,2},{7,3},{20,16},{21,17},{22,18},{23,19}} | collective-permute-start | bytes 2654216 | tf_op jit(solution)/shard_map/ppermute | solution.py:746
  519.5 23.2 %collective-permute-start.37 = (bf16[144,3072]{1,0:T(8,128)(2,1)S(1)}, bf16[144,3072]{1,0:T(8,128)(2,1)S(1)}, u32[]{:S(2)}, u32[]{:S(2)}) collective-permute-start(bf16[144,3072]{1,0:T(8,128)(2,1)S(1)} %get-tuple-element.105.refs_0_), channel_id=1, source_target_pairs={{12,0},{13,1},{14,2},{15,3},{28,16},{29,17},{30,18},{31,19}} | collective-permute-start | bytes 2654216 | tf_op jit(solution)/shard_map/ppermute | solution.py:746
  554.8 13.8 %collective-permute-start.48 = (bf16[256,1024]{1,0:T(8,128)(2,1)S(1)}, bf16[256,1024]{1,0:T(8,128)(2,1)S(1)}, u32[]{:S(2)}, u32[]{:S(2)}) collective-permute-start(bf16[256,1024]{1,0:T(8,128)(2,1)S(1)} %get-tuple-element.174), channel_id=1, source_target_pairs={{0,1},{4,5},{8,9},{12,13},{16,17},{20,21},{24,25},{28,29}} | collective-permute-start | bytes 1572872 | tf_op jit(solution)/shard_map/ppermute | solution.py:834
  556.2 13.0 %collective-permute-start.49 = (bf16[256,1024]{1,0:T(8,128)(2,1)S(1)}, bf16[256,1024]{1,0:T(8,128)(2,1)S(1)}, u32[]{:S(2)}, u32[]{:S(2)}) collective-permute-start(bf16[256,1024]{1,0:T(8,128)(2,1)S(1)} %get-tuple-element.174), channel_id=1, source_target_pairs={{3,2},{7,6},{11,10},{15,14},{19,18},{23,22},{27,26},{31,30}} | collective-permute-start | bytes 1572872 | tf_op jit(solution)/shard_map/ppermute | solution.py:835
  556.9 22.9 %collective-permute-start.54 = (bf16[256,1024]{1,0:T(8,128)(2,1)S(1)}, bf16[256,1024]{1,0:T(8,128)(2,1)S(1)}, u32[]{:S(2)}, u32[]{:S(2)}) collective-permute-start(bf16[256,1024]{1,0:T(8,128)(2,1)S(1)} %get-tuple-element.173), channel_id=1, source_target_pairs={{0,1},{4,5},{8,9},{12,13},{16,17},{20,21},{24,25},{28,29}} | collective-permute-start | bytes 1572872 | tf_op jit(solution)/shard_map/ppermute | solution.py:834
  558.3 22.5 %collective-permute-start.55 = (bf16[256,1024]{1,0:T(8,128)(2,1)S(1)}, bf16[256,1024]{1,0:T(8,128)(2,1)S(1)}, u32[]{:S(2)}, u32[]{:S(2)}) collective-permute-start(bf16[256,1024]{1,0:T(8,128)(2,1)S(1)} %get-tuple-element.173), channel_id=1, source_target_pairs={{3,2},{7,6},{11,10},{15,14},{19,18},{23,22},{27,26},{31,30}} | collective-permute-start | bytes 1572872 | tf_op jit(solution)/shard_map/ppermute | solution.py:835
  559.0 32.1 %collective-permute-start.42 = (bf16[256,1024]{1,0:T(8,128)(2,1)S(1)}, bf16[256,1024]{1,0:T(8,128)(2,1)S(1)}, u32[]{:S(2)}, u32[]{:S(2)}) collective-permute-start(bf16[256,1024]{1,0:T(8,128)(2,1)S(1)} %get-tuple-element.172), channel_id=1, source_target_pairs={{0,1},{4,5},{8,9},{12,13},{16,17},{20,21},{24,25},{28,29}} | collective-permute-start | bytes 1572872 | tf_op jit(solution)/shard_map/ppermute | solution.py:834
  568.6 23.2 %collective-permute-start.43 = (bf16[256,1024]{1,0:T(8,128)(2,1)S(1)}, bf16[256,1024]{1,0:T(8,128)(2,1)S(1)}, u32[]{:S(2)}, u32[]{:S(2)}) collective-permute-start(bf16[256,1024]{1,0:T(8,128)(2,1)S(1)} %get-tuple-element.172), channel_id=1, source_target_pairs={{3,2},{7,6},{11,10},{15,14},{19,18},{23,22},{27,26},{31,30}} | collective-permute-start | bytes 1572872 | tf_op jit(solution)/shard_map/ppermute | solution.py:835
  573.1 29.2 %collective-permute-start.50 = (bf16[256,1024]{1,0:T(8,128)(2,1)S(1)}, bf16[256,1024]{1,0:T(8,128)(2,1)S(1)}, u32[]{:S(2)}, u32[]{:S(2)}) collective-permute-start(bf16[256,1024]{1,0:T(8,128)(2,1)S(1)} %get-tuple-element.111), channel_id=1, source_target_pairs={{0,1},{1,2},{4,5},{5,6},{8,9},{9,10},{12,13},{13,14},{16,17},{17,1... | collective-permute-start | bytes 1572872 | tf_op jit(solution)/shard_map/ppermute | solution.py:834
  579.8 23.2 %collective-permute-start.51 = (bf16[256,1024]{1,0:T(8,128)(2,1)S(1)}, bf16[256,1024]{1,0:T(8,128)(2,1)S(1)}, u32[]{:S(2)}, u32[]{:S(2)}) collective-permute-start(bf16[256,1024]{1,0:T(8,128)(2,1)S(1)} %get-tuple-element.112), channel_id=1, source_target_pairs={{3,2},{2,1},{7,6},{6,5},{11,10},{10,9},{15,14},{14,13},{19,18},{18... | collective-permute-start | bytes 1572872 | tf_op jit(solution)/shard_map/ppermute | solution.py:835
  581.8 31.7 %collective-permute-start.56 = (bf16[256,1024]{1,0:T(8,128)(2,1)S(1)}, bf16[256,1024]{1,0:T(8,128)(2,1)S(1)}, u32[]{:S(2)}, u32[]{:S(2)}) collective-permute-start(bf16[256,1024]{1,0:T(8,128)(2,1)S(1)} %get-tuple-element.115), channel_id=1, source_target_pairs={{0,1},{1,2},{4,5},{5,6},{8,9},{9,10},{12,13},{13,14},{16,17},{17,1... | collective-permute-start | bytes 1572872 | tf_op jit(solution)/shard_map/ppermute | solution.py:834
  591.0 23.8 %collective-permute-start.57 = (bf16[256,1024]{1,0:T(8,128)(2,1)S(1)}, bf16[256,1024]{1,0:T(8,128)(2,1)S(1)}, u32[]{:S(2)}, u32[]{:S(2)}) collective-permute-start(bf16[256,1024]{1,0:T(8,128)(2,1)S(1)} %get-tuple-element.116), channel_id=1, source_target_pairs={{3,2},{2,1},{7,6},{6,5},{11,10},{10,9},{15,14},{14,13},{19,18},{18... | collective-permute-start | bytes 1572872 | tf_op jit(solution)/shard_map/ppermute | solution.py:835
  592.7 32.0 %collective-permute-start.44 = (bf16[256,1024]{1,0:T(8,128)(2,1)S(1)}, bf16[256,1024]{1,0:T(8,128)(2,1)S(1)}, u32[]{:S(2)}, u32[]{:S(2)}) collective-permute-start(bf16[256,1024]{1,0:T(8,128)(2,1)S(1)} %get-tuple-element.107), channel_id=1, source_target_pairs={{0,1},{1,2},{4,5},{5,6},{8,9},{9,10},{12,13},{13,14},{16,17},{17,1... | collective-permute-start | bytes 1572872 | tf_op jit(solution)/shard_map/ppermute | solution.py:834
  602.3 23.8 %collective-permute-start.45 = (bf16[256,1024]{1,0:T(8,128)(2,1)S(1)}, bf16[256,1024]{1,0:T(8,128)(2,1)S(1)}, u32[]{:S(2)}, u32[]{:S(2)}) collective-permute-start(bf16[256,1024]{1,0:T(8,128)(2,1)S(1)} %get-tuple-element.108), channel_id=1, source_target_pairs={{3,2},{2,1},{7,6},{6,5},{11,10},{10,9},{15,14},{14,13},{19,18},{18... | collective-permute-start | bytes 1572872 | tf_op jit(solution)/shard_map/ppermute | solution.py:835
  604.0 32.0 %collective-permute-start.52 = (bf16[256,1024]{1,0:T(8,128)(2,1)S(1)}, bf16[256,1024]{1,0:T(8,128)(2,1)S(1)}, u32[]{:S(2)}, u32[]{:S(2)}) collective-permute-start(bf16[256,1024]{1,0:T(8,128)(2,1)S(1)} %get-tuple-element.113), channel_id=1, source_target_pairs={{0,1},{1,2},{2,3},{4,5},{5,6},{6,7},{8,9},{9,10},{10,11},{12,13},{... | collective-permute-start | bytes 1572872 | tf_op jit(solution)/shard_map/ppermute | solution.py:834
  613.5 24.6 %collective-permute-start.53 = (bf16[256,1024]{1,0:T(8,128)(2,1)S(1)}, bf16[256,1024]{1,0:T(8,128)(2,1)}, u32[]{:S(2)}, u32[]{:S(2)}) collective-permute-start(bf16[256,1024]{1,0:T(8,128)(2,1)S(1)} %get-tuple-element.114), channel_id=1, source_target_pairs={{3,2},{2,1},{1,0},{7,6},{6,5},{5,4},{11,10},{10,9},{9,8},{15,14},{... | collective-permute-start | bytes 1572872 | tf_op jit(solution)/shard_map/ppermute | solution.py:835
  615.8 28.0 %collective-permute-start.58 = (bf16[256,1024]{1,0:T(8,128)(2,1)S(1)}, bf16[256,1024]{1,0:T(8,128)(2,1)}, u32[]{:S(2)}, u32[]{:S(2)}) collective-permute-start(bf16[256,1024]{1,0:T(8,128)(2,1)S(1)} %get-tuple-element.117), channel_id=1, source_target_pairs={{0,1},{1,2},{2,3},{4,5},{5,6},{6,7},{8,9},{9,10},{10,11},{12,13},{... | collective-permute-start | bytes 1572872 | tf_op jit(solution)/shard_map/ppermute | solution.py:834
  624.7 19.1 %collective-permute-start.59 = (bf16[256,1024]{1,0:T(8,128)(2,1)S(1)}, bf16[256,1024]{1,0:T(8,128)(2,1)}, u32[]{:S(2)}, u32[]{:S(2)}) collective-permute-start(bf16[256,1024]{1,0:T(8,128)(2,1)S(1)} %get-tuple-element.118), channel_id=1, source_target_pairs={{3,2},{2,1},{1,0},{7,6},{6,5},{5,4},{11,10},{10,9},{9,8},{15,14},{... | collective-permute-start | bytes 1572872 | tf_op jit(solution)/shard_map/ppermute | solution.py:835
  627.8 21.7 %collective-permute-start.46 = (bf16[256,1024]{1,0:T(8,128)(2,1)}, bf16[256,1024]{1,0:T(8,128)(2,1)}, u32[]{:S(2)}, u32[]{:S(2)}) collective-permute-start(bf16[256,1024]{1,0:T(8,128)(2,1)} %get-tuple-element.109), channel_id=1, source_target_pairs={{0,1},{1,2},{2,3},{4,5},{5,6},{6,7},{8,9},{9,10},{10,11},{12,13},{... | collective-permute-start | bytes 1572872 | tf_op jit(solution)/shard_map/ppermute | solution.py:834
  636.8 12.8 %collective-permute-start.47 = (bf16[256,1024]{1,0:T(8,128)(2,1)}, bf16[256,1024]{1,0:T(8,128)(2,1)}, u32[]{:S(2)}, u32[]{:S(2)}) collective-permute-start(bf16[256,1024]{1,0:T(8,128)(2,1)} %get-tuple-element.110), channel_id=1, source_target_pairs={{3,2},{2,1},{1,0},{7,6},{6,5},{5,4},{11,10},{10,9},{9,8},{15,14},{... | collective-permute-start | bytes 1572872 | tf_op jit(solution)/shard_map/ppermute | solution.py:835
  662.9 25.8 %collective-permute-start.60 = (bf16[768,512]{1,0:T(8,128)(2,1)}, bf16[768,512]{1,0:T(8,128)(2,1)}, u32[]{:S(2)}, u32[]{:S(2)}) collective-permute-start(bf16[768,512]{1,0:T(8,128)(2,1)} %dynamic-slice_convert_fusion), channel_id=1, source_target_pairs={{0,16},{16,0},{1,17},{17,1},{2,18},{18,2},{3,19},{19,3},{4,20},{20... | collective-permute-start | bytes 2359304 | tf_op jit(solution)/shard_map/ppermute | solution.py:930
  667.8 9.1 %collective-permute-start.63 = (f32[3,1024]{1,0:T(4,128)S(1)}, f32[3,1024]{1,0:T(4,128)S(1)}, u32[]{:S(2)}, u32[]{:S(2)}) collective-permute-start(f32[3,1024]{1,0:T(4,128)S(1)} %fusion.35), channel_id=1, source_target_pairs={{0,8},{4,12},{8,0},{12,4},{1,9},{5,13},{9,1},{13,5},{2,10},{6,14},... | collective-permute-start | bytes 36872 | tf_op jit(solution)/shard_map/ppermute | solution.py:653
  677.0 7.7 %collective-permute-start.64 = (f32[3,1024]{1,0:T(4,128)S(1)}, f32[3,1024]{1,0:T(4,128)S(1)}, u32[]{:S(2)}, u32[]{:S(2)}) collective-permute-start(f32[3,1024]{1,0:T(4,128)S(1)} %add.423), channel_id=1, source_target_pairs={{0,1},{1,0},{2,3},{3,2},{4,5},{5,4},{6,7},{7,6},{8,9},{9,8},{10,11... | collective-permute-start | bytes 36872 | tf_op jit(solution)/shard_map/ppermute | solution.py:653
  684.7 14.0 %collective-permute-start.65 = (f32[3,1024]{1,0:T(4,128)S(1)}, f32[3,1024]{1,0:T(4,128)S(1)}, u32[]{:S(2)}, u32[]{:S(2)}) collective-permute-start(f32[3,1024]{1,0:T(4,128)S(1)} %add.424), channel_id=1, source_target_pairs={{0,2},{1,3},{2,0},{3,1},{4,6},{5,7},{6,4},{7,5},{8,10},{9,11},{10,... | collective-permute-start | bytes 36872 | tf_op jit(solution)/shard_map/ppermute | solution.py:653
  693.5 20.3 %collective-permute-start.61 = (bf16[768,512]{1,0:T(8,128)(2,1)S(1)}, bf16[768,512]{1,0:T(8,128)(2,1)S(1)}, u32[]{:S(2)}, u32[]{:S(2)}) collective-permute-start(bf16[768,512]{1,0:T(8,128)(2,1)S(1)} %get-tuple-element.166), channel_id=1, source_target_pairs={{0,16},{16,0},{1,17},{17,1},{2,18},{18,2},{3,19},{19,3},{4,20},{20... | collective-permute-start | bytes 2359304 | tf_op jit(solution)/shard_map/ppermute | solution.py:944
  698.7 14.4 %collective-permute-start.66 = (f32[3,1024]{1,0:T(4,128)S(1)}, f32[3,1024]{1,0:T(4,128)S(1)}, u32[]{:S(2)}, u32[]{:S(2)}) collective-permute-start(f32[3,1024]{1,0:T(4,128)S(1)} %get-tuple-element.158), channel_id=1, source_target_pairs={{0,16},{16,0},{1,17},{17,1},{2,18},{18,2},{3,19},{19,3},{4,20},{20... | collective-permute-start | bytes 36872 | tf_op jit(solution)/shard_map/ppermute | solution.py:653
  (48 other events, 575.6 us)
Sparse Core Ops, SparseCore 0:
  10.7 142.8 all-gather.2
  337.7 141.6 all-gather.4

commit v3 on v2

--- a/solution.py
+++ b/solution.py
@@ -1,4 +1,5 @@
 import functools
+import math
 
 import jax
 import jax.numpy as jnp
@@ -26,6 +27,7 @@
 GELU_CUBE = 0.044715
 PIECES = 3
 LINE_FLOPS = 10**10
+SMALL_COST = pl.CostEstimate(flops=10**6, bytes_accessed=10**5, transcendentals=0)
 NOWHERE = 1 << 20
 
 
@@ -47,11 +49,38 @@
     )
 
 
-def weight_copies(weights, held, sems, sources, rows):
+def gathered_row(row, order):
+    planes, line, shard_rows = order
+    shard = row // shard_rows
+    return ((shard % line) * planes + shard // line) * shard_rows + row % shard_rows
+
+
+class WeightCopy:
+    def __init__(self, weights, held, sem, source, target, rows, order):
+        unit = math.gcd(order[2], rows)
+        self.parts = [
+            pltpu.make_async_copy(
+                weights.at[pl.ds(gathered_row(source * rows + at, order), unit)],
+                held.at[pl.ds(target * rows + at, unit)],
+                sem,
+            )
+            for at in range(0, rows, unit)
+        ]
+        self.whole = pltpu.make_async_copy(
+            weights.at[pl.ds(0, rows)], held.at[pl.ds(target * rows, rows)], sem
+        )
+
+    def start(self):
+        for part in self.parts:
+            part.start()
+
+    def wait(self):
+        self.whole.wait()
+
+
+def weight_copies(weights, held, sems, sources, rows, order):
     return [
-        pltpu.make_async_copy(
-            weights.at[pl.ds(source * rows, rows)], held.at[pl.ds(target * rows, rows)], sems.at[target]
-        )
+        WeightCopy(weights, held, sems.at[target], source, target, rows, order)
         for target, source in enumerate(sources)
     ]
 
@@ -113,22 +142,24 @@
             both_refs[step][at] = nn(chosen, held[step, at]).astype(jnp.bfloat16)
 
 
-def scatter_kernel(across_ref, base_ref, rows_ref, out_ref):
+def scatter_kernel(across_ref, base_ref, rows_ref, *refs):
+    out_ref = refs[-1]
     base = base_ref[0]
     across = across_ref[0]
     places = lax.broadcasted_iota(jnp.int32, (base.shape[0], across.shape[1]), 0)
     chosen = jnp.where(places == across, 1.0, 0.0)
     replaced = jnp.sum(chosen, axis=-1, keepdims=True) > 0.0
-    rows = nn(chosen.astype(jnp.bfloat16), rows_ref[0]).astype(jnp.bfloat16)
+    rows = nn(chosen.astype(jnp.bfloat16), rows_ref[...]).astype(jnp.bfloat16)
     out_ref[0] = jnp.where(replaced, rows, base)
 
 
 def attention_kernel(
-    weights, info, needs, moves, both_ref, vec_ref, mask_ref, proj_ref, lse_ref, pair_ref, first_ref, held, sems
+    weights, info, needs, moves, starts, rows, both_ref, vec_ref, mask_ref, *refs, order, extra
 ):
+    proj_ref, lse_ref, pair_ref, first_ref, held, sems = refs[extra:]
     rows_ref = both_ref.at[0]
     width = both_ref.shape[2]
-    copies = weight_copies(weights, held, sems, range(4), width)
+    copies = weight_copies(weights, held, sems, range(4), width, order)
     for copy in copies:
         copy.start()
     xs = rows_ref[...].astype(jnp.float32)
@@ -171,16 +202,17 @@
     grad_ref,
     *refs,
     keep,
+    order,
 ):
     held, sems = refs[-2:]
     rows_ref, cot_ref = both_ref.at[0], both_ref.at[1]
     width = both_ref.shape[2]
     hidden = (weights.shape[0] - 4 * width) // 2
     parts = hidden // width
-    order = []
+    matrices = []
     for part in range(parts):
-        order += [4 + part, 4 + parts + part]
-    copies = weight_copies(weights, held, sems, order, width)
+        matrices += [4 + part, 4 + parts + part]
+    copies = weight_copies(weights, held, sems, matrices, width, order)
     for copy in copies:
         copy.start()
 
@@ -221,37 +253,30 @@
 
 def attention_back_kernel(
     weights,
+    starts,
     d_attn_ref,
     proj_ref,
     lse_ref,
     mask_ref,
-    both_ref,
-    vec_ref,
-    base_hbm,
     pair_hbm,
     got_hbm,
-    late_ref,
-    d_rows_ref,
-    grad_ref,
+    cuts_hbm,
     pairs_hbm,
     held,
-    base_ref,
-    sems,
-    base_sem,
+    late_ref,
+    weight_sems,
     pair_sems,
+    cut_sems,
+    *,
+    order,
 ):
-    rows_ref = both_ref.at[0]
-    width = both_ref.shape[2]
-    copies = weight_copies(weights, held, sems, [3, 0, 1, 2], width)
-    for copy in copies:
-        copy.start()
-    base_copy = pltpu.make_async_copy(base_hbm, base_ref, base_sem)
-    base_copy.start()
+    width = held.shape[1]
+    copies = weight_copies(weights, held, weight_sems, [3], width, order)
     pair_copies = [
         pltpu.make_async_copy(pair_hbm, pairs_hbm.at[0], pair_sems.at[0]),
         pltpu.make_async_copy(got_hbm.at[0], pairs_hbm.at[1], pair_sems.at[1]),
     ]
-    for copy in pair_copies:
+    for copy in copies + pair_copies:
         copy.start()
     copies[0].wait()
     d_mixed = nn(d_attn_ref[...], held[pl.ds(0, width), :]).astype(jnp.bfloat16)
@@ -277,23 +302,55 @@
         late_ref[:, 2 * width + at : 2 * width + at + 128] = tn(probs_low, d_pair).astype(
             jnp.bfloat16
         )
-    xs = rows_ref[...].astype(jnp.float32)
+    cuts = starts.shape[0]
+    span = late_ref.shape[1] // cuts
+    cut_copies = []
+    for cut in range(cuts):
+        start = pl.multiple_of(starts[cut], 128)
+        cut_copies.append(
+            pltpu.make_async_copy(
+                late_ref.at[:, pl.ds(start, span)],
+                cuts_hbm.at[:, pl.ds(cut * span, span)],
+                cut_sems.at[cut],
+            )
+        )
+    for copy in cut_copies:
+        copy.start()
+    for copy in cut_copies + pair_copies:
+        copy.wait()
+
+
+def input_back_kernel(
+    weights, rows, cuts_ref, both_ref, vec_ref, base_ref, *refs, extra, order
+):
+    d_rows_ref, grad_ref, held, sems = refs[extra:]
+    cuts, span, width = held.shape
+    if order is None:
+        copies = [
+            pltpu.make_async_copy(
+                weights.at[pl.ds(pl.multiple_of(rows[cut], 128), span)], held.at[cut], sems.at[cut]
+            )
+            for cut in range(cuts)
+        ]
+    else:
+        copies = [
+            WeightCopy(weights, held.at[cut], sems.at[cut], cut, 0, span, order)
+            for cut in range(cuts)
+        ]
+    for copy in copies:
+        copy.start()
+    xs = both_ref[0].astype(jnp.float32)
     inverse = lax.rsqrt(row_mean(xs * xs) + EPS_NORM)
     normed = xs * inverse
     d_h1 = jnp.zeros(xs.shape, jnp.float32)
-    for index in range(3):
-        copies[1 + index].wait()
-        d_h1 = d_h1 + nn(
-            late_ref[:, index * width : (index + 1) * width], held[pl.ds((1 + index) * width, width), :]
-        )
+    for cut in range(cuts):
+        copies[cut].wait()
+        d_h1 = d_h1 + nn(cuts_ref[:, cut * span : (cut + 1) * span], held[cut])
     grad_ref[...] = jnp.sum(d_h1 * normed, axis=0, keepdims=True)
     d_normed = d_h1 * vec_ref[0:1, :]
-    base_copy.wait()
     d_rows_ref[...] = (
         base_ref[...] + inverse * (d_normed - normed * row_mean(d_normed * normed))
     ).astype(jnp.bfloat16)
-    for copy in pair_copies:
-        copy.wait()
 
 
 def plane_copies(refs, target, sems, tokens):
@@ -307,8 +364,8 @@
     return [ref.at[at, index] for ref in refs for at in range(ref.shape[0])]
 
 
-def feed_forward_products_kernel(info, needs, weights, d_down_ref, *refs):
-    pair_refs = refs[:-7]
+def feed_forward_products_kernel(info, needs, weights, d_down_ref, *refs, extra):
+    pair_refs = refs[: -7 - extra]
     out_ref, held, uppers, lowers, held_sems, upper_sems, lower_sems = refs[-7:]
     count, piece, _ = out_ref.shape
     sources, tokens, _ = d_down_ref.shape
@@ -353,91 +410,202 @@
 
         @pl.when(info[index, 0] == 2)
         def _():
-            slope = gelu_and_slope(nt(held[0], uppers[index]))[1]
-            d_pre = (nt(held[1], lowers[index]) * slope).astype(jnp.bfloat16)
-            out_ref[index] = tn(d_pre, held[0]).astype(jnp.bfloat16)
+            slope = gelu_and_slope(nt(uppers[index], held[0]))[1]
+            d_pre = (nt(lowers[index], held[1]) * slope).astype(jnp.bfloat16)
+            out_ref[index] = nn(d_pre, held[0]).astype(jnp.bfloat16)
 
         @pl.when(info[index, 0] == 3)
         def _():
-            act = gelu_and_slope(nt(held[0], uppers[index]))[0]
-            out_ref[index] = tn(act, held[1]).astype(jnp.bfloat16)
-
-
-def attention_products_kernel(info, needs, h1_ref, *refs, sources):
+            act = gelu_and_slope(nt(uppers[index], held[0]))[0]
+            out_ref[index] = nn(act, held[1]).astype(jnp.bfloat16)
+
+
+def attention_products_kernel(info, needs, h1_ref, *refs, sources, extra):
     proj_refs, attn_refs = refs[:sources], refs[sources : 2 * sources]
-    pair_refs = refs[2 * sources : -8]
-    _, out_ref, held, factors, made, held_sems, factor_sems, out_sems = refs[-8:]
+    pair_refs = refs[2 * sources : -9 - extra]
+    out_ref, held, projs, attns, made, held_sems, factor_sems, out_sems = refs[-8:]
     count, piece, _ = made.shape
     tokens = h1_ref.shape[1]
-
-    def factor_copies(index, parts):
-        start = pl.multiple_of(info[index, 1], 128)
-        return plane_copies(
-            [part.at[:, pl.ds(start, piece)] for part in parts],
-            factors.at[index],
-            factor_sems.at[index],
-            tokens,
-        )
-
-    def each_copy(index, act):
-        for kind, parts in enumerate((proj_refs, attn_refs)):
-
-            @pl.when(info[index, 0] == kind)
-            def _(parts=parts):
-                for copy in factor_copies(index, parts):
-                    act(copy)
-
-    def each_held(act):
-        for kind in range(2):
-            found = pair_refs_of(pair_refs, 0) if kind else [h1_ref.at[at] for at in range(sources)]
+    rights = ([h1_ref.at[at] for at in range(sources)], pair_refs_of(pair_refs, 0))
+
+    def each_operand(act):
+        for kind, (lefts, target) in enumerate(((proj_refs, projs), (attn_refs, attns))):
 
             @pl.when(needs[kind] > 0)
-            def _(kind=kind, found=found):
-                for copy in plane_copies(found, held.at[kind], held_sems.at[kind], tokens):
+            def _(kind=kind, lefts=lefts, target=target):
+                copies = plane_copies(rights[kind], held.at[kind], held_sems.at[kind], tokens)
+                copies += plane_copies(lefts, target, factor_sems.at[kind], tokens)
+                for copy in copies:
                     act(copy)
 
     def out_copy(index):
         return pltpu.make_async_copy(made.at[index], out_ref.at[index], out_sems.at[index])
 
-    each_held(lambda copy: copy.start())
-
-    @pl.loop(0, count)
-    def _(index):
-        each_copy(index, lambda copy: copy.start())
-
-    each_held(lambda copy: copy.wait())
-
-    @pl.loop(0, count)
-    def _(index):
-        each_copy(index, lambda copy: copy.wait())
+    each_operand(lambda copy: copy.start())
+    each_operand(lambda copy: copy.wait())
+    for index in range(count):
+
+        @pl.when(info[index, 0] == 0)
+        def _(index=index):
+            left = projs[:, index * piece : (index + 1) * piece]
+            made[index] = tn(left, held[0]).astype(jnp.bfloat16)
+            out_copy(index).start()
+
+        @pl.when(info[index, 0] == 1)
+        def _(index=index):
+            left = attns[:, pl.ds(pl.multiple_of(info[index, 1], 128), piece)]
+            made[index] = tn(left, held[1]).astype(jnp.bfloat16)
+            out_copy(index).start()
+
+    for index in range(count):
 
         @pl.when(info[index, 0] < 2)
-        def _():
-            made[index] = tn(factors[index], held[info[index, 0]]).astype(jnp.bfloat16)
-            out_copy(index).start()
-
-    @pl.loop(0, count)
-    def _(index):
-        @pl.when(info[index, 0] < 2)
-        def _():
+        def _(index=index):
             out_copy(index).wait()
 
 
-def line_kernel(moves, below_ref, above_ref, terms_ref, up_ref, down_ref, held, sems, *, step, piece):
-    pieces = terms_ref.shape[0] // (moves.shape[0] + 1)
+def line_kernel(moves, below_ref, above_ref, terms_ref, *refs, step, piece, passed):
+    up_ref, down_ref = refs[-4 - passed : -2 - passed]
+    held, sems = refs[-2:]
+    for source, target in zip(refs[:passed], refs[-2 - passed : -2]):
+        target[...] = source[...]
+
+    def each_copy(way, act):
+        source = terms_ref.at[moves[step, way] * PIECES + piece]
+        act(pltpu.make_async_copy(source, held.at[way], sems.at[way]))
+
+    for way in range(2):
+        each_copy(way, lambda copy: copy.start())
+    for way, (came, leaves) in enumerate(((below_ref, up_ref), (above_ref, down_ref))):
+        each_copy(way, lambda copy: copy.wait())
+        leaves[...] = (held[way].astype(jnp.float32) + came[...].astype(jnp.float32)).astype(
+            jnp.bfloat16
+        )
+
+
+def update_kernel(place, below_ref, above_ref, *refs, piece, own, step_count, last, chained, extra):
+    arrays = refs[: 5 if last else 4]
+    results = refs[len(arrays) + chained + extra : len(arrays) + chained + extra + 4]
+    held, term, made, low, in_sems, out_sems = refs[-6:]
+    rows = below_ref.shape[0]
+    blocks = in_sems.shape[0]
+    block = rows // blocks
+    loads, stores = [], []
+    for index in range(blocks):
+        here = pl.ds(index * block, block)
+        there = pl.ds(piece * rows + index * block, block)
+        sources = [arrays[0].at[own, here]] + [array.at[there] for array in arrays[1:]]
+        targets = [term.at[here]] + [held.at[at, here] for at in range(len(arrays) - 1)]
+        loads.append(
+            [
+                pltpu.make_async_copy(source, target, in_sems.at[index, at])
+                for at, (source, target) in enumerate(zip(sources, targets))
+            ]
+        )
+        outs = [(made.at[1, here], results[0]), (made.at[2, here], results[1])]
+        if not last:
+            outs += [(made.at[0, here], results[2]), (low.at[here], results[3])]
+        stores.append(
+            [
+                pltpu.make_async_copy(source, target.at[there], out_sems.at[index, at])
+                for at, (source, target) in enumerate(outs)
+            ]
+        )
+    for copies in loads:
+        for copy in copies:
+            copy.start()
+    fixed_one = 1.0 / (1.0 - BETA_ONE**step_count)
+    fixed_two = 1.0 / (1.0 - BETA_TWO**step_count)
+    for index in range(blocks):
+        for copy in loads[index]:
+            copy.wait()
+        some = pl.ds(index * block, block)
+        grad = (term[some, :].astype(jnp.float32) + below_ref[some, :].astype(jnp.float32)) + above_ref[
+            some, :
+        ].astype(jnp.float32)
+        param = held[0, some, :]
+        first = BETA_ONE * held[1, some, :] + (1.0 - BETA_ONE) * grad
+        second = BETA_TWO * held[2, some, :] + (1.0 - BETA_TWO) * grad * grad
+        direction = first * fixed_one / (jnp.sqrt(second * fixed_two) + EPS_ADAM)
+        param = param - INNER_RATE * (direction + DECAY_RATE * param)
+        made[1, some, :] = first
+        made[2, some, :] = second
+        if last:
+            made[0, some, :] = held[3, some, :] - param
+        else:
+            made[0, some, :] = param
+            low[some, :] = param.astype(jnp.bfloat16)
+        for copy in stores[index]:
+            copy.start()
+    if last:
+        own_ref, other_ref = results[2:]
+        columns = own_ref.shape[1]
+        groups = other_ref.shape[0] + 1
+        for step in range(groups):
+            start = pl.multiple_of(lax.rem(place[0] + step, groups) * columns, 128)
+            if step == 0:
+                own_ref[...] = made[0, :, pl.ds(start, columns)]
+            else:
+                other_ref[step - 1] = made[0, :, pl.ds(start, columns)].astype(jnp.bfloat16)
+    for copies in stores:
+        for copy in copies:
+            copy.wait()
+
+
+def outer_kernel(place, own_ref, *refs, piece, groups, chained, extra):
+    got_refs = refs[: groups - 1]
+    arrays = refs[groups - 1 : groups + 2]
+    results = refs[groups + 2 + chained + extra : groups + 6 + chained + extra]
+    held, made, in_sems, out_sems = refs[-4:]
+    rows, columns = own_ref.shape
+    at = pl.ds(piece * rows, rows)
+    start = pl.multiple_of(place[0] * columns, 128)
+    sources = [arrays[0].at[at, pl.ds(start, columns)], arrays[1].at[at], arrays[2].at[at]]
     copies = [
-        pltpu.make_async_copy(
-            terms_ref.at[moves[step, way] * pieces + piece], held.at[way], sems.at[way]
-        )
-        for way in range(2)
+        pltpu.make_async_copy(source, held.at[index], in_sems.at[index])
+        for index, source in enumerate(sources)
     ]
     for copy in copies:
         copy.start()
-    for way, (came, leaves) in enumerate(((below_ref, up_ref), (above_ref, down_ref))):
-        copies[way].wait()
-        leaves[...] = (held[way].astype(jnp.float32) + came[...].astype(jnp.float32)).astype(
-            jnp.bfloat16
-        )
+    for copy in copies:
+        copy.wait()
+    share = own_ref[...]
+    for index in range(groups - 1):
+        share = share + got_refs[index][...].astype(jnp.float32)
+    share = share / groups
+    moment = OUTER_MOMENTUM * held[1] + share
+    new_share = held[0] - OUTER_RATE * (share + OUTER_MOMENTUM * moment)
+    made[0] = moment
+    made[1] = share
+    made[2] = AVERAGE_KEEP * held[2] + (1.0 - AVERAGE_KEEP) * new_share
+    results[3][...] = new_share.astype(jnp.bfloat16)
+    copies = [
+        pltpu.make_async_copy(made.at[index], results[index].at[at], out_sems.at[index])
+        for index in range(3)
+    ]
+    for copy in copies:
+        copy.start()
+    for copy in copies:
+        copy.wait()
+
+
+def join_kernel(place, *refs, piece, groups, chained):
+    parts = refs[:groups]
+    wide_hbm, low_hbm = refs[groups + chained : groups + chained + 2]
+    wide, sems = refs[-2:]
+    rows, columns = parts[0].shape
+    at = pl.ds(piece * rows, rows)
+    copies = []
+    for step in range(groups):
+        start = pl.multiple_of(lax.rem(place[0] + groups - step, groups) * columns, 128)
+        wide[step] = parts[step][...].astype(jnp.float32)
+        target = (at, pl.ds(start, columns))
+        copies.append(pltpu.make_async_copy(wide.at[step], wide_hbm.at[target], sems.at[0, step]))
+        copies.append(pltpu.make_async_copy(parts[step], low_hbm.at[target], sems.at[1, step]))
+    for copy in copies:
+        copy.start()
+    for copy in copies:
+        copy.wait()
 
 
 def vmem(count):
@@ -466,30 +634,34 @@
     return (made[:steps], made[steps:], padded[:, None, :])
 
 
-def run_scatter(across, base, rows):
-    steps, places, width = base.shape
-    tokens = rows.shape[1]
+def run_scatter(across, base, rows, step, chain, known):
+    _, places, width = base.shape
+    tokens = rows.shape[0]
+    here = pl.BlockSpec((1, places, width), lambda index: (step, 0, 0))
     return pl.pallas_call(
         scatter_kernel,
-        grid=(steps,),
+        grid=(1,),
         in_specs=[
-            pl.BlockSpec((1, 1, tokens), lambda step: (step, 0, 0)),
-            pl.BlockSpec((1, places, width), lambda step: (step, 0, 0)),
-            pl.BlockSpec((1, tokens, width), lambda step: (step, 0, 0)),
-        ],
-        out_specs=pl.BlockSpec((1, places, width), lambda step: (step, 0, 0)),
+            pl.BlockSpec((1, 1, tokens), lambda index: (step, 0, 0)),
+            here,
+            pl.BlockSpec((tokens, width), lambda index: (0, 0)),
+        ]
+        + anywhere(len(chain) + len(known)),
+        out_specs=here,
         out_shape=jax.ShapeDtypeStruct(base.shape, base.dtype),
-        compiler_params=pltpu.CompilerParams(vmem_limit_bytes=44 << 20),
+        input_output_aliases=chain_aliases(3, chain),
+        compiler_params=pltpu.CompilerParams(vmem_limit_bytes=56 << 20),
+        cost_estimate=SMALL_COST,
         name="scatter_rows",
-    )(across, base, rows)
-
-
-def run_attention(gathered, info, needs, moves, both, vec_now, mask):
+    )(across, base, rows, *chain, *known)
+
+
+def run_attention(order, gathered, plan, both, vec_now, mask, known):
     _, tokens, width = both.shape
     shape = jax.ShapeDtypeStruct
     return pl.pallas_call(
-        attention_kernel,
-        in_specs=anywhere(1) + smem(3) + vmem(3),
+        functools.partial(attention_kernel, order=order, extra=len(known)),
+        in_specs=anywhere(1) + smem(len(plan)) + vmem(3) + anywhere(len(known)),
         out_specs=vmem(4),
         out_shape=[
             shape((tokens, 3 * width), jnp.bfloat16),
@@ -506,16 +678,16 @@
             flops=8 * tokens * width * width, bytes_accessed=8 * width * width, transcendentals=0
         ),
         name="attention",
-    )(gathered, info, needs, moves, both, vec_now, mask)
-
-
-def run_feed_forward(gathered, both, vec_now, first_sum, keep):
+    )(gathered, *plan, both, vec_now, mask, *known)
+
+
+def run_feed_forward(order, gathered, both, vec_now, first_sum, keep):
     _, tokens, width = both.shape
     wide = gathered.shape[0]
     shape = jax.ShapeDtypeStruct
     kept = [shape((tokens, wide - 4 * width), jnp.bfloat16)] if keep else []
     return pl.pallas_call(
-        functools.partial(feed_forward_kernel, keep=keep),
+        functools.partial(feed_forward_kernel, keep=keep, order=order),
         in_specs=anywhere(1) + vmem(3),
         out_specs=vmem(4 + len(kept)),
         out_shape=[
@@ -547,41 +719,65 @@
     return [pl.BlockSpec(memory_space=pl.ANY)] * count
 
 
-def run_attention_back(gathered, d_attn_low, proj, lse, mask, both, vec_now, base, pair, got):
-    _, tokens, width = both.shape
+def run_attention_back(order, gathered, starts, d_attn_low, proj, lse, mask, pair, got):
+    tokens, width = d_attn_low.shape
+    cuts = starts.shape[0]
     shape = jax.ShapeDtypeStruct
     return pl.pallas_call(
-        attention_back_kernel,
-        in_specs=anywhere(1) + vmem(6) + anywhere(3),
-        out_specs=vmem(3) + anywhere(1),
+        functools.partial(attention_back_kernel, order=order),
+        in_specs=anywhere(1) + smem(1) + vmem(4) + anywhere(2),
+        out_specs=anywhere(2),
         out_shape=[
             shape((tokens, 3 * width), jnp.bfloat16),
-            shape((tokens, width), jnp.bfloat16),
-            shape((1, width), jnp.float32),
             shape((2,) + pair.shape, jnp.bfloat16),
         ],
         scratch_shapes=[
-            pltpu.VMEM((4 * width, width), jnp.bfloat16),
-            pltpu.VMEM((tokens, width), jnp.float32),
-            pltpu.SemaphoreType.DMA((4,)),
-            pltpu.SemaphoreType.DMA,
+            pltpu.VMEM((width, width), jnp.bfloat16),
+            pltpu.VMEM((tokens, 3 * width), jnp.bfloat16),
+            pltpu.SemaphoreType.DMA((1,)),
             pltpu.SemaphoreType.DMA((2,)),
+            pltpu.SemaphoreType.DMA((cuts,)),
         ],
         compiler_params=pltpu.CompilerParams(vmem_limit_bytes=44 << 20),
         cost_estimate=pl.CostEstimate(
-            flops=16 * tokens * width * width, bytes_accessed=8 * width * width, transcendentals=0
+            flops=10 * tokens * width * width, bytes_accessed=4 * width * width, transcendentals=0
         ),
         name="attention_back",
-    )(gathered, d_attn_low, proj, lse, mask, both, vec_now, base, pair, got)
-
-
-def run_line(moves, below, above, terms, step, piece):
+    )(gathered, starts, d_attn_low, proj, lse, mask, pair, got)
+
+
+def run_input_back(order, gathered, rows, d_proj, both, vec_now, base, known):
+    _, tokens, width = both.shape
+    cuts = rows.shape[0]
+    shape = jax.ShapeDtypeStruct
+    return pl.pallas_call(
+        functools.partial(
+            input_back_kernel, extra=len(known), order=order
+        ),
+        in_specs=anywhere(1) + smem(1) + vmem(4) + anywhere(len(known)),
+        out_specs=vmem(2),
+        out_shape=[
+            shape((tokens, width), jnp.bfloat16),
+            shape((1, width), jnp.float32),
+        ],
+        scratch_shapes=[
+            pltpu.VMEM((cuts, 3 * width // cuts, width), jnp.bfloat16),
+            pltpu.SemaphoreType.DMA((cuts,)),
+        ],
+        compiler_params=pltpu.CompilerParams(vmem_limit_bytes=44 << 20),
+        cost_estimate=SMALL_COST,
+        name="input_back",
+    )(gathered, rows, d_proj, both, vec_now, base, *known)
+
+
+def run_line(moves, below, above, terms, step, piece, passed, known):
     shape = jax.ShapeDtypeStruct(below.shape, jnp.bfloat16)
     return pl.pallas_call(
-        functools.partial(line_kernel, step=step, piece=piece),
-        in_specs=smem(1) + vmem(2) + anywhere(1),
-        out_specs=vmem(2),
-        out_shape=[shape, shape],
+        functools.partial(line_kernel, step=step, piece=piece, passed=len(passed)),
+        in_specs=smem(1) + vmem(2) + anywhere(1) + vmem(len(passed)) + anywhere(len(known)),
+        out_specs=vmem(2 + len(passed)),
+        out_shape=[shape, shape]
+        + [jax.ShapeDtypeStruct(values.shape, values.dtype) for values in passed],
         scratch_shapes=[
             pltpu.VMEM((2,) + below.shape, jnp.bfloat16),
             pltpu.SemaphoreType.DMA((2,)),
@@ -591,16 +787,122 @@
             flops=LINE_FLOPS, bytes_accessed=6 * below.size * 2, transcendentals=0
         ),
         name="line",
-    )(moves, below, above, terms)
-
-
-def run_products(info, needs, gathered, proj_parts, attn_parts, plane_h1, plane_d_down, pairs, piece):
+    )(moves, below, above, terms, *passed, *known)
+
+
+def chain_aliases(first, chain):
+    return {first + index: index for index in range(len(chain))}
+
+
+def run_update(place, below, above, terms, states, piece, step_count, last, groups, chain, known):
+    rows, width = below.shape
+    own = terms.shape[0] - PIECES + piece
+    shape = jax.ShapeDtypeStruct
+    wide = shape(states[0].shape, jnp.float32)
+    columns = width // groups
+    if last:
+        out_shape = [wide, wide, shape((rows, columns), jnp.float32)]
+        out_shape.append(shape((groups - 1, rows, columns), jnp.bfloat16))
+        out_specs = anywhere(2) + vmem(2)
+    else:
+        out_shape = [wide, wide, wide, shape(states[0].shape, jnp.bfloat16)]
+        out_specs = anywhere(4)
+    operands = (place, below, above, terms, *states, *chain, *known)
+    return pl.pallas_call(
+        functools.partial(
+            update_kernel,
+            piece=piece,
+            own=own,
+            step_count=step_count,
+            last=last,
+            chained=len(chain),
+            extra=len(known),
+        ),
+        in_specs=smem(1) + vmem(2) + anywhere(len(operands) - 3),
+        out_specs=out_specs,
+        out_shape=out_shape,
+        scratch_shapes=[
+            pltpu.VMEM((len(states), rows, width), jnp.float32),
+            pltpu.VMEM((rows, width), jnp.bfloat16),
+            pltpu.VMEM((3, rows, width), jnp.float32),
+            pltpu.VMEM((rows, width), jnp.bfloat16),
+            pltpu.SemaphoreType.DMA((4, len(states) + 1)),
+            pltpu.SemaphoreType.DMA((4, 4)),
+        ],
+        input_output_aliases=chain_aliases(4 + len(states), chain),
+        compiler_params=pltpu.CompilerParams(vmem_limit_bytes=52 << 20),
+        cost_estimate=pl.CostEstimate(
+            flops=LINE_FLOPS, bytes_accessed=24 * rows * width, transcendentals=0
+        ),
+        name="update",
+    )(*operands)
+
+
+def run_outer(place, own, got, arrays, piece, chain, known):
+    rows, columns = own.shape
+    shape = jax.ShapeDtypeStruct
+    narrow = shape(arrays[1].shape, jnp.float32)
+    operands = (place, own, *got, *arrays, *chain, *known)
+    return pl.pallas_call(
+        functools.partial(
+            outer_kernel,
+            piece=piece,
+            groups=len(got) + 1,
+            chained=len(chain),
+            extra=len(known),
+        ),
+        in_specs=smem(1) + vmem(1 + len(got)) + anywhere(len(operands) - 2 - len(got)),
+        out_specs=anywhere(3) + vmem(1),
+        out_shape=[narrow] * 3 + [shape(own.shape, jnp.bfloat16)],
+        scratch_shapes=[
+            pltpu.VMEM((3, rows, columns), jnp.float32),
+            pltpu.VMEM((3, rows, columns), jnp.float32),
+            pltpu.SemaphoreType.DMA((3,)),
+            pltpu.SemaphoreType.DMA((3,)),
+        ],
+        input_output_aliases=chain_aliases(5 + len(got), chain),
+        compiler_params=pltpu.CompilerParams(vmem_limit_bytes=52 << 20),
+        cost_estimate=pl.CostEstimate(
+            flops=LINE_FLOPS, bytes_accessed=24 * rows * columns, transcendentals=0
+        ),
+        name="outer",
+    )(*operands)
+
+
+def run_join(place, parts, like, piece, chain):
+    rows, columns = parts[0].shape
+    groups = len(parts)
+    operands = (place, *parts, *chain)
+    return pl.pallas_call(
+        functools.partial(join_kernel, piece=piece, groups=groups, chained=len(chain)),
+        in_specs=smem(1) + vmem(groups) + anywhere(len(chain)),
+        out_specs=anywhere(2),
+        out_shape=[
+            jax.ShapeDtypeStruct(like.shape, jnp.float32),
+            jax.ShapeDtypeStruct(like.shape, jnp.bfloat16),
+        ],
+        scratch_shapes=[
+            pltpu.VMEM((groups, rows, columns), jnp.float32),
+            pltpu.SemaphoreType.DMA((2, groups)),
+        ],
+        input_output_aliases=chain_aliases(1 + groups, chain),
+        compiler_params=pltpu.CompilerParams(vmem_limit_bytes=52 << 20),
+        cost_estimate=pl.CostEstimate(
+            flops=LINE_FLOPS, bytes_accessed=12 * rows * columns * groups, transcendentals=0
+        ),
+        name="join",
+    )(*operands)
+
+
+def run_products(
+    info, needs, gathered, proj_parts, attn_parts, plane_h1, plane_d_down, pairs, piece, known
+):
     count = info.shape[0]
     sources, tokens, width = plane_h1.shape
     shape = jax.ShapeDtypeStruct((count, piece, width), jnp.bfloat16)
     made = pl.pallas_call(
-        feed_forward_products_kernel,
-        in_specs=smem(2) + anywhere(2 + len(pairs)),
+        functools.partial(feed_forward_products_kernel, extra=len(attn_parts)),
+        in_specs=smem(2) + anywhere(2 + len(pairs) + len(attn_parts)),
         out_specs=vmem(1)[0],
         out_shape=shape,
         scratch_shapes=[
@@ -618,19 +920,22 @@
             transcendentals=0,
         ),
         name="feed_forward_products",
-    )(info, needs, gathered, plane_d_down, *pairs)
-    operands = (info, needs, plane_h1, *proj_parts, *attn_parts, *pairs, made)
+    )(info, needs, gathered, plane_d_down, *pairs, *attn_parts)
+    operands = (info, needs, plane_h1, *proj_parts, *attn_parts, *pairs, *known, made)
     return pl.pallas_call(
-        functools.partial(attention_products_kernel, sources=sources),
+        functools.partial(
+            attention_products_kernel, sources=sources, extra=len(known)
+        ),
         in_specs=smem(2) + anywhere(len(operands) - 2),
         out_specs=anywhere(1)[0],
         out_shape=shape,
         scratch_shapes=[
             pltpu.VMEM((2, sources * tokens, width), jnp.bfloat16),
-            pltpu.VMEM((count, sources * tokens, piece), jnp.bfloat16),
+            pltpu.VMEM((sources * tokens, 3 * width), jnp.bfloat16),
+            pltpu.VMEM((sources * tokens, width), jnp.bfloat16),
             pltpu.VMEM((count, piece, width), jnp.bfloat16),
             pltpu.SemaphoreType.DMA((2, sources)),
-            pltpu.SemaphoreType.DMA((count, sources)),
+            pltpu.SemaphoreType.DMA((2, sources)),
             pltpu.SemaphoreType.DMA((count,)),
         ],
         input_output_aliases={len(operands) - 1: 0},
@@ -655,11 +960,16 @@
 
 def sum_over(values, axes):
     for axis in axes:
-        delta = 1
-        while delta < lax.axis_size(axis):
-            values = values + swap(values, axis, delta)
-            delta *= 2
+        parts = [values]
+        parts += [swap(values, axis, delta) for delta in range(1, lax.axis_size(axis))]
+        while len(parts) > 1:
+            parts = [parts[at] + parts[at + 1] for at in range(0, len(parts), 2)]
+        values = parts[0]
     return values
+
+
+def gathered_rows(values):
+    return lax.all_gather(pad_rows(values), ("dp", "fsdp"), axis=0, tiled=False)
 
 
 def line_order(line):
@@ -723,34 +1033,11 @@
     return (h1, (gate * cot_rows).astype(jnp.bfloat16))
 
 
-def send_window(values, start, block):
+def send_to(target, values):
     planes = lax.axis_size("fsdp")
-    plane = lax.axis_index("fsdp")
-    span = min(block, values.shape[1])
-    stop = start + values.shape[1]
-
-    def first(target):
-        return jnp.clip(target * block - start, 0, values.shape[1] - span)
-
-    def window(target):
-        if span == values.shape[1]:
-            return values
-        return lax.dynamic_slice_in_dim(values, first(target), span, axis=1)
-
-    def goes(target):
-        return target * block < stop and (target + 1) * block > start
-
-    parts = [window(plane)]
-    for delta in plane_order(planes)[1:]:
-        pairs = [(i, i ^ delta) for i in range(planes) if goes(i ^ delta)]
-        parts.append(lax.ppermute(window(plane ^ delta), "fsdp", pairs))
-    return parts
-
-
-def window_start(width, start, block):
-    return start + jnp.clip(
-        lax.axis_index("fsdp") * block - start, 0, width - min(block, width)
-    )
+    return [values] + [
+        lax.ppermute(values, "fsdp", [(target ^ delta, target)]) for delta in plane_order(planes)[1:]
+    ]
 
 
 def gradient_plan(shard_rows, model_width, columns):
@@ -762,20 +1049,16 @@
     def kind_of(row):
         return sum((row >= edge).astype(jnp.int32) for edge in edges)
 
-    block = line * shard_rows
-    proj_start = window_start(3 * model_width, 0, block)
-    attn_start = window_start(model_width, 3 * model_width, block)
     piece = shard_rows // PIECES
     theres = jnp.asarray(line_order(line))[here]
     rows = (plane * line + theres)[:, None] * shard_rows + jnp.arange(PIECES) * piece
     rows = rows.reshape(-1)
     kinds = kind_of(rows)
-    at = jnp.select(
-        [kinds == 0, kinds == 1, kinds == 2],
-        [rows - proj_start, rows - attn_start, rows],
-        rows - hidden_units,
-    )
-    info = jnp.stack([kinds, at, jnp.minimum(rows + hidden_units, columns - piece)], axis=1)
+    at = rows - 3 * model_width
+    order = (planes, line, shard_rows)
+    uppers = gathered_row(jnp.where(kinds == 2, rows, rows - hidden_units), order)
+    lowers = gathered_row(jnp.minimum(rows + hidden_units, columns - piece), order)
+    info = jnp.stack([kinds, jnp.where(kinds >= 2, uppers, at), lowers], axis=1)
     low, high = kind_of(plane * line * shard_rows), kind_of((plane + 1) * line * shard_rows - 1)
     ff = (high >= 2).astype(jnp.int32)
     has_proj = (low == 0).astype(jnp.int32)
@@ -784,8 +1067,16 @@
     return (info.astype(jnp.int32), jnp.stack([has_proj, has_attn, ff, ff]), moves)
 
 
-def in_planes(shard_rows):
-    return (shard_rows // PIECES) % 128 == 0
+def gradient_starts(shard_rows, model_width, split):
+    line, here = lax.axis_size("dp"), lax.axis_index("dp")
+    if split:
+        return jnp.asarray(line_order(line) * shard_rows)[here]
+    return jnp.arange(4, dtype=jnp.int32) * (3 * model_width // 4)
+
+
+def in_planes(shard_rows, model_width):
+    line = lax.axis_size("dp")
+    return (shard_rows // PIECES) % 128 == 0 and line * shard_rows == 3 * model_width
 
 
 def gradient_whole(columns, operands):
@@ -798,31 +1089,29 @@
 
 
 def plane_terms(
-    gathered, late, d_attn_low, pairs, plane_h1, plane_d_down, info, needs, shard_rows
+    gathered, d_proj, d_attn_low, pairs, plane_h1, plane_d_down, info, needs, shard_rows, known
 ):
-    planes, line = lax.axis_size("fsdp"), lax.axis_size("dp")
-    block = line * shard_rows
-    attn_parts = send_window(d_attn_low, late.shape[1], block)
+    attn_parts = send_to(1, d_attn_low)
     pairs = [pairs]
-    bit = planes // 4
+    bit = lax.axis_size("fsdp") // 4
     while bit >= 1:
         pairs.append(swap(jnp.concatenate(pairs, axis=0), "fsdp", bit))
         bit //= 2
-    proj_parts = send_window(late, 0, block)
     return run_products(
         info,
         needs,
         gathered,
-        proj_parts,
+        send_to(0, d_proj),
         attn_parts,
         plane_h1,
         plane_d_down,
         pairs,
         shard_rows // PIECES,
+        known,
     )
 
 
-def gradient_share(terms, moves):
+def gradient_share(terms, moves, passed, meanwhile):
     line = lax.axis_size("dp")
     below, above = [None] * PIECES, [None] * PIECES
     for step in range(line - 1):
@@ -830,14 +1119,18 @@
             if step == 0:
                 up = down = terms[index]
             else:
-                up, down = run_line(moves, below[index], above[index], terms, step, index)
+                due = known[index] if step == line - 2 else ()
+                given = passed if step == 1 and index == 0 else ()
+                up, down, *given = run_line(
+                    moves, below[index], above[index], terms, step, index, given, due
+                )
+                if step == 1 and index == 0:
+                    known = meanwhile(up, given)
             below[index] = lax.ppermute(up, "dp", [(p, p + 1) for p in range(step + 1)])
             above[index] = lax.ppermute(
                 down, "dp", [(line - 1 - p, line - 2 - p) for p in range(step + 1)]
             )
-    own = (line - 1) * PIECES
-    sums = [added(terms[own + index], below[index], above[index]) for index in range(PIECES)]
-    return jnp.concatenate(sums, axis=0)
+    return (below, above)
 
 
 def adamw(param, grad, first, second, step_count, rate, decay):
@@ -851,6 +1144,36 @@
 
 def vector_rates():
     return jnp.array([[0.1], [0.1], [0.02]], dtype=jnp.float32)
+
+
+def outer_whole(weights, master, outer_moment, smoothed_matrix_mean):
+    groups = lax.axis_size("grp")
+    here = lax.axis_index("grp")
+    delta = weights - master
+    col_width = weights.shape[1] // groups
+    col_start = here * col_width
+    diff_share = lax.dynamic_slice_in_dim(delta, col_start, col_width, 1)
+    for step in range(1, groups):
+        there = lax.rem(here + step, groups)
+        part = lax.dynamic_slice_in_dim(delta, there * col_width, col_width, 1)
+        diff_share = diff_share + shift_group(part.astype(jnp.bfloat16), step).astype(jnp.float32)
+    diff_share = diff_share / groups
+    moment_share = OUTER_MOMENTUM * outer_moment + diff_share
+    base_share = lax.dynamic_slice_in_dim(weights, col_start, col_width, 1)
+    new_share = base_share - OUTER_RATE * (diff_share + OUTER_MOMENTUM * moment_share)
+    low_share = new_share.astype(jnp.bfloat16)
+    weights_low = jnp.zeros(weights.shape, jnp.bfloat16)
+    for step in range(groups):
+        there = lax.rem(here + groups - step, groups)
+        part = shift_group(low_share, step) if step else low_share
+        weights_low = lax.dynamic_update_slice_in_dim(weights_low, part, there * col_width, 1)
+    average_new = AVERAGE_KEEP * smoothed_matrix_mean + (1.0 - AVERAGE_KEEP) * new_share
+    return (weights_low.astype(jnp.float32), weights_low, moment_share, diff_share, average_new)
+
+
+def shift_group(values, step):
+    groups = lax.axis_size("grp")
+    return lax.ppermute(values, "grp", [(i, (i + step) % groups) for i in range(groups)])
 
 
 def on_device(
@@ -876,87 +1199,178 @@
     vfirst_now = vec_first[0]
     vsecond_now = vec_second[0]
     model_width = tokens.shape[2]
-    forward_steps = []
-    backward_steps = []
     planes, line = lax.axis_size("fsdp"), lax.axis_size("dp")
     shard_rows = weights.shape[0]
     info, needs, moves = gradient_plan(shard_rows, model_width, weights.shape[0] * planes * line)
     boths, masks, across = run_gather(lengths[:, 0], selected[:, 0], tokens, cotangent)
+    plane_rows = plane_gather(boths[0])
+    split = in_planes(shard_rows, model_width)
+    starts = gradient_starts(shard_rows, model_width, split)
+    order = (planes, line, shard_rows)
+    weight_starts = gathered_row(starts, order)
+    plan = (info, needs, moves, starts, weight_starts)
+    groups = lax.axis_size("grp")
+    place = lax.axis_index("grp").astype(jnp.int32)[None]
+    shard_low = master.astype(jnp.bfloat16)
+    activations, input_grad, outers = [], [], []
     for inner_step in range(INNER):
         both, mask = boths[inner_step], masks[inner_step]
-        plane_rows = plane_gather(both)
-        shard_low = master.astype(jnp.bfloat16)
-        gathered = lax.all_gather(shard_low, ("fsdp", "dp"), axis=0, tiled=True)
+        gathered = lax.all_gather(shard_low, ("dp", "fsdp"), axis=0, tiled=True)
         plane_h1, plane_d_down = plane_operands(plane_rows, vec_now)
-        proj, lse, pair, first_sum = run_attention(gathered, info, needs, moves, both, vec_now, mask)
-        split = in_planes(shard_rows)
+        proj, lse, pair, first_sum = run_attention(
+            order,
+            gathered,
+            plan,
+            both,
+            vec_now,
+            mask,
+            [plane_h1, plane_d_down, *activations, *input_grad],
+        )
         d_attn_low, out_rows, base, grad_two, *kept = run_feed_forward(
-            gathered, both, vec_now, first_sum, not split
+            order, gathered, both, vec_now, first_sum, not split
         )
         got = swap(pair[None], "fsdp", planes // 2)
-        late, d_rows, grad_one, pairs = run_attention_back(
-            gathered, d_attn_low, proj, lse, mask, both, vec_now, base, pair, got
+        d_proj, pairs = run_attention_back(
+            order, gathered, starts, d_attn_low, proj, lse, mask, pair, got
         )
-        grad_vec = jnp.concatenate([grad_one, grad_two], axis=0)
-        forward_steps.append(out_rows)
-        backward_steps.append(d_rows)
+        following = list(boths[inner_step + 1 : inner_step + 2])
+        last = not following
+        step_count = STEP + inner_step
+        results = []
+
+        def input_step(marks):
+            d_rows, grad_one = run_input_back(
+                None if split else order, gathered, weight_starts, d_proj, both, vec_now, base, marks
+            )
+            results.append(jnp.concatenate([grad_one, grad_two], axis=0))
+            return d_rows
+
+        def scatter_step(d_rows, marks):
+            activations[:] = [
+                run_scatter(across, tokens, out_rows, inner_step, activations, marks)
+            ]
+            input_grad[:] = [
+                run_scatter(across, cotangent, d_rows, inner_step, input_grad, marks)
+            ]
+
+        if split and last:
+            d_rows = input_step([])
+            results[0] = gathered_rows(results[0])
+
+        def meanwhile(mark, passed):
+            if not last:
+                results.append(plane_gather(passed[0]))
+                return (results[-1:], (), ())
+            return ((), (), ())
+
         if split:
             terms = plane_terms(
-                gathered, late, d_attn_low, pairs, plane_h1, plane_d_down, info, needs, shard_rows
+                gathered,
+                d_proj,
+                d_attn_low,
+                pairs,
+                plane_h1,
+                plane_d_down,
+                info,
+                needs,
+                shard_rows,
+                [d_rows] if last else (),
             )
-            grad_shard = gradient_share(terms, moves)
+            below, above = gradient_share(terms, moves, following, meanwhile)
+            grad_mark = below[-1]
         else:
-            grad_shard = gradient_whole(
-                (late, d_attn_low, *kept), (plane_h1[0], pair[0], pair[1], plane_d_down[0])
+            grad_mark = gradient_whole(
+                (d_proj, d_attn_low, *kept), (plane_h1[0], pair[0], pair[1], plane_d_down[0])
             )
-        grad_vec = sum_over(due_after(grad_vec, grad_shard), ("fsdp", "dp"))
-        step_count = STEP + inner_step
-        master, first_now, second_now = adamw(
-            master, grad_shard, first_now, second_now, step_count, INNER_RATE, DECAY_RATE
+            results.extend(plane_gather(values) for values in following)
+        if split and last:
+            made = []
+            for index in range(PIECES):
+                made.append(
+                    run_update(
+                        place,
+                        below[index],
+                        above[index],
+                        terms,
+                        (master, first_now, second_now, weights),
+                        index,
+                        step_count,
+                        last,
+                        groups,
+                        made[-1][:2] if index else (),
+                        [outers[0][3]] + input_grad if index == PIECES - 1 else activations,
+                    )
+                )
+                own, other = made[-1][2:]
+                if index == 0:
+                    scatter_step(d_rows, [own])
+                outers.append(
+                    run_outer(
+                        place,
+                        own,
+                        [shift_group(other[step - 1], step) for step in range(1, groups)],
+                        (weights, outer_moment, smoothed_matrix_mean),
+                        index,
+                        outers[-1][:3] if index else (),
+                        [],
+                    )
+                )
+            first_now, second_now = made[-1][:2]
+        else:
+            grad_shard = grad_mark
+            if split:
+                own = (line - 1) * PIECES
+                grad_shard = jnp.concatenate(
+                    [
+                        added(terms[own + index], below[index], above[index])
+                        for index in range(PIECES)
+                    ],
+                    axis=0,
+                )
+            master, first_now, second_now = adamw(
+                master, grad_shard, first_now, second_now, step_count, INNER_RATE, DECAY_RATE
+            )
+            shard_low = master.astype(jnp.bfloat16)
+        if not last:
+            plane_rows = results.pop()
+        if split and last:
+            grad_vec = jnp.sum(due_after(results[0][:, : vec_now.shape[0]], made[0][2]), axis=0)
+            vec_now, vfirst_now, vsecond_now = adamw(
+                vec_now, grad_vec, vfirst_now, vsecond_now, step_count, vector_rates(), 0.0
+            )
+            vec_diff = sum_over(vectors - vec_now, ("grp",)) / groups
+        else:
+            scatter_step(input_step([grad_mark]), [grad_mark])
+            grad_vec = sum_over(due_after(results[0], grad_mark), ("fsdp", "dp"))
+            vec_now, vfirst_now, vsecond_now = adamw(
+                vec_now, grad_vec, vfirst_now, vsecond_now, step_count, vector_rates(), 0.0
+            )
+    if split:
+        joined = []
+        for index in range(PIECES):
+            low = outers[index][3]
+            parts = [low] + [shift_group(low, step) for step in range(1, groups)]
+            joined = run_join(place, parts, weights, index, joined)
+        weights_new, weights_low = joined
+        outer_new, diff_new, average_new = outers[-1][:3]
+    else:
+        weights_new, weights_low, outer_new, diff_new, average_new = outer_whole(
+            weights, master, outer_moment, smoothed_matrix_mean
         )
-        vec_now, vfirst_now, vsecond_now = adamw(
-            vec_now, grad_vec, vfirst_now, vsecond_now, step_count, vector_rates(), 0.0
-        )
-    groups = lax.axis_size("grp")
-    delta = weights - master
-    vector_change = vectors - vec_now
-    col_width = weights.shape[1] // groups
-    col_start = lax.axis_index("grp") * col_width
-    here = lax.axis_index("grp")
-    diff_share = lax.dynamic_slice_in_dim(delta, col_start, col_width, 1)
-    for step in range(1, groups):
-        there = lax.rem(here + step, groups)
-        part = lax.dynamic_slice_in_dim(delta, there * col_width, col_width, 1)
-        part = lax.ppermute(
-            part.astype(jnp.bfloat16), "grp", [(i, (i + step) % groups) for i in range(groups)]
-        )
-        diff_share = diff_share + part.astype(jnp.float32)
-    diff_share = diff_share / groups
-    vec_diff = sum_over(vector_change, ("grp",)) / groups
-    moment_share = OUTER_MOMENTUM * outer_moment + diff_share
-    base_share = lax.dynamic_slice_in_dim(weights, col_start, col_width, 1)
-    new_share = base_share - OUTER_RATE * (diff_share + OUTER_MOMENTUM * moment_share)
-    low_share = new_share.astype(jnp.bfloat16)
-    weights_low = jnp.zeros(weights.shape, jnp.bfloat16)
-    weights_low = lax.dynamic_update_slice_in_dim(weights_low, low_share, col_start, 1)
-    for step in range(1, groups):
-        there = lax.rem(here + groups - step, groups)
-        part = lax.ppermute(low_share, "grp", [(i, (i + step) % groups) for i in range(groups)])
-        weights_low = lax.dynamic_update_slice_in_dim(weights_low, part, there * col_width, 1)
-    weights_new = weights_low.astype(jnp.float32)
-    average_new = AVERAGE_KEEP * smoothed_matrix_mean + (1.0 - AVERAGE_KEEP) * new_share
+    if not split:
+        vec_diff = sum_over(vectors - vec_now, ("grp",)) / groups
     vec_moment = OUTER_MOMENTUM * vec_outer + vec_diff
     vectors_new = vectors - OUTER_RATE * (vec_diff + OUTER_MOMENTUM * vec_moment)
     vec_average_new = AVERAGE_KEEP * vec_average + (1.0 - AVERAGE_KEEP) * vectors_new
     return (
-        run_scatter(across, tokens, jnp.stack(forward_steps)),
-        run_scatter(across, cotangent, jnp.stack(backward_steps)),
+        activations[0],
+        input_grad[0],
         weights_new,
         weights_low,
         first_now[None],
         second_now[None],
-        moment_share,
-        diff_share,
+        outer_new,
+        diff_new,
         average_new,
         vectors_new,
         vfirst_now[None],

time: 727 us -> 697 us (0.959); the launches traced: 723 us -> 686 us
  Pallas kernels: 101 us -> 146 us
  waiting for transfers between devices: 392 us -> 359 us
  starting transfers between devices: 142 us -> 119 us
  other arithmetic: 39 us -> 17.9 us
    pallas_call x22 -> x35, Pallas kernels: 75.5 us -> 121 us  [the longest x2 24.8 us: run_feed_forward(): pl.pallas_call(functools.partial(feed_forward_kernel, keep=keep, order=or...]
    ppermute x17 -> x15, starting transfers between devices: 37.7 us -> 13.4 us  [swap(): return lax.ppermute(values, axis, [(i, i ^ delta) for i in range(size)])]
    ppermute x17 -> x15, waiting for transfers between devices: 52.8 us -> 31.8 us  [swap(): return lax.ppermute(values, axis, [(i, i ^ delta) for i in range(size)])]
    all_gather x2 -> x3, waiting for transfers between devices: 219 us -> 205 us  [the longest x2 205 us: on_device(): gathered = lax.all_gather(shard_low, ('dp', 'fsdp'), axis=0, tiled=True)]
    add x8 -> x3, other arithmetic: 7.95 us -> 0.65 us  [the longest x1 0.56 us: gathered_row(): (shard % line * planes + shard // line) * shard_rows + row % shard_rows]
    sub x2 -> x1, other arithmetic: 7.35 us -> 0.07 us  [on_device(): vec_diff = sum_over(vectors - vec_now, ('grp',)) / groups]
    unnamed x88 -> x110, local copies, waits for them, and re-layouts: 23 us -> 17.7 us
    ppermute x14 -> x18, starting transfers between devices: 18.8 us -> 22.8 us  [the longest x12 16.5 us: send_to(): lax.ppermute(values, 'fsdp', [(target ^ delta, target)])]
  transfers between devices with their start and end apart: 69 -> 72, of which waited for: 34 -> 29; matrix products, arithmetic and copies ran while one was open for 3% -> 2% of each run, Pallas kernels for 9% -> 14%
where the time goes in v3:
time: 697 us; the launch traced here: 686 us
  waiting for transfers between devices  359 us (52%)
  Pallas kernels  146 us (21%)
  starting transfers between devices  119 us (17%)
  local copies, waits for them, and re-layouts  26.1 us (4%)
  between operations  18.4 us (3%)
  other arithmetic  17.9 us (3%)
    all_gather x2, waiting for transfers between devices, on_device(): gathered = lax.all_gather(shard_low, ('dp', 'fsdp'), axis=0, tiled=True)  205 us
    ppermute x18, waiting for transfers between devices, gradient_share(): below[index] = lax.ppermute(up, 'dp', [(p, p + 1) for p in range(step + 1)])  81.4 us
    ppermute x18, starting transfers between devices, gradient_share(): below[index] = lax.ppermute(up, 'dp', [(p, p + 1) for p in range(step + 1)])  66.3 us
    ppermute x15, waiting for transfers between devices, swap(): return lax.ppermute(values, axis, [(i, i ^ delta) for i in range(size)])  31.8 us
    ppermute x12, waiting for transfers between devices, send_to(): lax.ppermute(values, 'fsdp', [(target ^ delta, target)])  31.3 us
    pallas_call x2, Pallas kernels, run_feed_forward(): pl.pallas_call(functools.partial(feed_forward_kernel, keep=keep, order=or...  24.8 us
    pallas_call x2, Pallas kernels, run_products(): pl.pallas_call(functools.partial(attention_products_kernel, sources=sourc...  20.2 us
    unnamed x110, local copies, waits for them, and re-layouts  17.7 us
  transfers between devices with their start and end apart: 72, of which 29 were waited for; matrix products, arithmetic and copies ran while one was open for 2% of the time, Pallas kernels for 14%

profile of v3, /device:TPU:0, one launch (start us, length us, event | category | flops | bytes accessed | tf_op | source)
XLA Modules:
  0.0 686.0 jit_solution(16842105374601492180)
XLA Ops:
  7.2 3.3 convert_element_type.171
  13.1 4.2 gather_rows.1
  18.1 3.0 collective-permute-start
  21.7 25.3 %collective-permute-done = bf16[1,2,144,1024]{3,2,0,1:T(8,128)(2,1)S(1)} collective-permute-done((bf16[1,2,144,1024]{3,2,0,1:T(8,128)(2,1)S(1)}, bf16[1,2,144,1024]{3,2,0,1:T(8,128)(2,1)S(1)}, u32[]{:S(2)}, u32[]{:S(2)}) %collective-permute-start) | collective-permute-done | bytes 589856 | tf_op jit(solution)/shard_map/ppermute | solution.py:958
  53.7 100.4 %all-gather.5.cloned.1.call-done.weights = bf16[12288,1024]{1,0:T(8,128)(2,1)} async-done(((bf16[768,1024]{1,0:T(8,128)(2,1)}), bf16[12288,1024]{1,0:T(8,128)(2,1)}) %all-gather.5.cloned.1.call-update) | async-done | bytes 25165840 | tf_op jit(solution)/shard_map/all_gather | solution.py:1218
  158.3 7.3 %attention.2 = (bf16[144,3072]{1,0:T(8,128)(2,1)S(1)}, f32[288,128]{1,0:T(8,128)S(1)}, bf16[2,144,1024]{2,1,0:T(8,128)(2,1)S(1)}, f32[144,1024]{1,0:T(8,128)S(1)}) custom-call(bf16[12288,1024]{1,0:T(8,128)(2,1)} %all-gather.5.cloned.1.call-done.weights, s32[12,3]{1,0:T(8,128)S(1)} %copy-done.21, s32[4]{0:T(128)S(1)} %copy-done.30, s32[3,2]{1,0:T(4,128)S(1)} %copy-done.27, ...), custom_call_target="tpu_custom_call" | custom-call | flops 1207959552 | bytes 8388608 | tf_op jit(solution)/shard_map/attention/pallas_call | solution.py:662
  166.5 12.5 %feed_forward.2 = (bf16[144,1024]{1,0:T(8,128)(2,1)S(1)}, bf16[144,1024]{1,0:T(8,128)(2,1)S(1)}, f32[144,1024]{1,0:T(8,128)S(1)}, f32[2,1024]{1,0:T(2,128)S(1)}) custom-call(bf16[12288,1024]{1,0:T(8,128)(2,1)} %all-gather.5.cloned.1.call-done.weights, bf16[2,144,1024]{2,1,0:T(8,128)(2,1)S(1)} %get-tuple-element.98.both_ref, f32[3,1024]{1,0:T(4,128)S(1)} %copy-done.17, ...), custom_call_target="tpu_custom_call" | custom-call | flops 9663676416 | bytes 25165824 | tf_op jit(solution)/shard_map/feed_forward/pallas_call | solution.py:689
  181.2 6.2 attention_back.2
  188.2 3.0 collective-permute-start.7
  195.9 4.1 feed_forward_products.2.refs_10_
  200.0 17.1 %collective-permute-done.3.refs_1_ = bf16[144,3072]{1,0:T(8,128)(2,1)S(1)} collective-permute-done((bf16[144,3072]{1,0:T(8,128)(2,1)S(1)}, bf16[144,3072]{1,0:T(8,128)(2,1)S(1)}, u32[]{:S(2)}, u32[]{:S(2)}) %collective-permute-start.3) | collective-permute-done | bytes 884768 | tf_op jit(solution)/shard_map/ppermute | solution.py:1039
  217.8 10.2 %attention_products.2.terms_ref = bf16[12,256,1024]{2,1,0:T(8,128)(2,1)} custom-call(s32[12,3]{1,0:T(8,128)S(1)} %copy-done.22, s32[4]{0:T(128)S(1)} %copy-done.31, bf16[4,144,1024]{2,1,0:T(8,128)(2,1)S(1)} %get-tuple-element.238.refs_0_.h1_ref, bf16[144,3072]{1,0:T(8,128)(2,1)S(1)} %get-tuple-element.105.refs_0_.cuts_ref, ...), custom_call_target="tpu_custom_call", output_to_operand_aliasing={{}: (13, {})} | custom-call | flops 3623878656 | bytes 6291456 | tf_op jit(solution)/shard_map/attention_products/pallas_call | solution.py:925
  234.8 8.3 %collective-permute-done.24.below_ref = bf16[256,1024]{1,0:T(8,128)(2,1)S(1)} collective-permute-done((bf16[256,1024]{1,0:T(8,128)(2,1)S(1)}, bf16[256,1024]{1,0:T(8,128)(2,1)S(1)}, u32[]{:S(2)}, u32[]{:S(2)}) %collective-permute-start.24) | collective-permute-done | bytes 524320 | tf_op jit(solution)/shard_map/ppermute | solution.py:1129
  243.8 2.8 copy-done.2
  247.5 4.4 collective-permute-start.26
  256.1 9.4 %collective-permute-done.18.below_ref = bf16[256,1024]{1,0:T(8,128)(2,1)S(1)} collective-permute-done((bf16[256,1024]{1,0:T(8,128)(2,1)S(1)}, bf16[256,1024]{1,0:T(8,128)(2,1)S(1)}, u32[]{:S(2)}, u32[]{:S(2)}) %collective-permute-start.18) | collective-permute-done | bytes 524320 | tf_op jit(solution)/shard_map/ppermute | solution.py:1129
  266.5 4.4 collective-permute-start.20
  271.6 6.1 collective-permute-start.12
  279.6 6.4 collective-permute-done.20.below_ref
  286.0 4.4 collective-permute-start.28
  299.5 5.0 collective-permute-start.16
  304.6 3.9 collective-permute-done.28.refs_0_
  310.0 9.4 %collective-permute-done.22 = bf16[256,1024]{1,0:T(8,128)(2,1)S(1)} collective-permute-done((bf16[256,1024]{1,0:T(8,128)(2,1)S(1)}, bf16[256,1024]{1,0:T(8,128)(2,1)S(1)}, u32[]{:S(2)}, u32[]{:S(2)}) %collective-permute-start.22) | collective-permute-done | bytes 524320 | tf_op jit(solution)/shard_map/ppermute | solution.py:1129
  321.3 3.7 collective-permute-done.16
  325.0 3.4 collective-permute-done.17
  329.5 5.0 fusion.34
  336.6 4.0 input_back.2
  343.3 2.4 collective-permute-done.31
  350.2 3.8 scatter_rows.5.refs_3_.refs_0_
  354.0 4.0 scatter_rows.4.refs_2_.refs_5_.refs_0_
  359.2 104.4 %all-gather.7.cloned.1.call-done.weights = bf16[12288,1024]{1,0:T(8,128)(2,1)} async-done(((bf16[768,1024]{1,0:T(8,128)(2,1)}), bf16[12288,1024]{1,0:T(8,128)(2,1)}) %all-gather.7.cloned.1.call-update) | async-done | bytes 25165840 | tf_op jit(solution)/shard_map/all_gather | solution.py:1218
  465.9 7.3 %attention.3 = (bf16[144,3072]{1,0:T(8,128)(2,1)S(1)}, f32[288,128]{1,0:T(8,128)S(1)}, bf16[2,144,1024]{2,1,0:T(8,128)(2,1)S(1)}, f32[144,1024]{1,0:T(8,128)S(1)}) custom-call(bf16[12288,1024]{1,0:T(8,128)(2,1)} %all-gather.7.cloned.1.call-done.weights, s32[12,3]{1,0:T(8,128)S(1)} %copy-done.23, s32[4]{0:T(128)S(1)} %copy-done.32, s32[3,2]{1,0:T(4,128)S(1)} %copy-done.29, ...), custom_call_target="tpu_custom_call" | custom-call | flops 1207959552 | bytes 8388608 | tf_op jit(solution)/shard_map/attention/pallas_call | solution.py:662
  474.5 12.3 %feed_forward.3 = (bf16[144,1024]{1,0:T(8,128)(2,1)S(1)}, bf16[144,1024]{1,0:T(8,128)(2,1)S(1)}, f32[144,1024]{1,0:T(8,128)S(1)}, f32[2,1024]{1,0:T(2,128)S(1)}) custom-call(bf16[12288,1024]{1,0:T(8,128)(2,1)} %all-gather.7.cloned.1.call-done.weights, bf16[2,144,1024]{2,1,0:T(8,128)(2,1)S(1)} %get-tuple-element.107.refs_0_.both_ref, ...), custom_call_target="tpu_custom_call" | custom-call | flops 9663676416 | bytes 25165824 | tf_op jit(solution)/shard_map/feed_forward/pallas_call | solution.py:689
  488.8 6.2 attention_back.3
  495.7 3.0 collective-permute-start.41
  500.7 4.0 input_back.3
  507.4 4.4 feed_forward_products.3.refs_11_
  511.8 8.8 %collective-permute-done.37.refs_1_ = bf16[144,3072]{1,0:T(8,128)(2,1)S(1)} collective-permute-done((bf16[144,3072]{1,0:T(8,128)(2,1)S(1)}, bf16[144,3072]{1,0:T(8,128)(2,1)S(1)}, u32[]{:S(2)}, u32[]{:S(2)}) %collective-permute-start.37) | collective-permute-done | bytes 884768 | tf_op jit(solution)/shard_map/ppermute | solution.py:1039
  520.6 4.7 collective-permute-done.39.refs_3_
  525.3 10.0 %attention_products.3.terms_ref.refs_0_ = bf16[12,256,1024]{2,1,0:T(8,128)(2,1)} custom-call(s32[12,3]{1,0:T(8,128)S(1)} %copy-done.23, s32[4]{0:T(128)S(1)} %copy-done.32, bf16[4,144,1024]{2,1,0:T(8,128)(2,1)S(1)} %get-tuple-element.236.refs_0_.h1_ref, bf16[144,3072]{1,0:T(8,128)(2,1)S(1)} %get-tuple-element.133.cuts_ref.refs_0_, ...), custom_call_target="tpu_custom_call", output_to_operand_aliasing={{}: (14, {})} | custom-call | flops 3623878656 | bytes 6291456 | tf_op jit(solution)/shard_map/attention_products/pallas_call | solution.py:925
  536.8 3.8 collective-permute-start.44
  545.3 8.7 %collective-permute-done.44.below_ref = bf16[256,1024]{1,0:T(8,128)(2,1)S(1)} collective-permute-done((bf16[256,1024]{1,0:T(8,128)(2,1)S(1)}, bf16[256,1024]{1,0:T(8,128)(2,1)S(1)}, u32[]{:S(2)}, u32[]{:S(2)}) %collective-permute-start.44) | collective-permute-done | bytes 524320 | tf_op jit(solution)/shard_map/ppermute | solution.py:1129
  554.7 2.8 copy-done.3
  558.4 4.4 collective-permute-start.46
  562.9 4.3 collective-permute-done.56.below_ref
  568.8 5.0 collective-permute-start.58
  573.8 7.9 %collective-permute-done.50.below_ref = bf16[256,1024]{1,0:T(8,128)(2,1)S(1)} collective-permute-done((bf16[256,1024]{1,0:T(8,128)(2,1)S(1)}, bf16[256,1024]{1,0:T(8,128)(2,1)S(1)}, u32[]{:S(2)}, u32[]{:S(2)}) %collective-permute-start.50) | collective-permute-done | bytes 524320 | tf_op jit(solution)/shard_map/ppermute | solution.py:1129
  583.3 5.0 collective-permute-start.52
  588.3 4.6 collective-permute-done.46.below_ref
  594.5 5.0 collective-permute-start.48
  599.6 4.6 collective-permute-done.58.below_ref
  607.1 5.0 collective-permute-start.60
  612.1 3.3 collective-permute-done.52.below_ref
  617.6 5.0 collective-permute-start.54
  622.7 4.0 collective-permute-done.48.below_ref
  627.9 3.9 update.3
  636.6 3.8 scatter_rows.6.refs_7_
  641.0 4.9 update.4
  649.2 3.8 scatter_rows.7.refs_8_
  653.7 2.8 outer.3
  657.1 4.9 update.5
  663.6 2.8 outer.4
  668.5 2.8 outer.5
  675.3 2.4 collective-permute-done.65.refs_1_
  (277 shorter events, 109.4 us)
Async XLA Ops:
  7.2 146.9 %all-gather.5.cloned.1.call-start = ((), (), s32[]{:S(2)}) async-start(), calls=%async_computation | async-start | bytes 26738688 | tf_op jit(solution)/shard_map/all_gather | solution.py:1218
  10.6 453.1 %all-gather.7.cloned.1.call-start = ((), (), s32[]{:S(2)}) async-start(), calls=%async_computation.1 | async-start | bytes 26738688 | tf_op jit(solution)/shard_map/all_gather | solution.py:1218
  18.1 28.9 %collective-permute-start = (bf16[1,2,144,1024]{3,2,0,1:T(8,128)(2,1)S(1)}, bf16[1,2,144,1024]{3,2,0,1:T(8,128)(2,1)S(1)}, u32[]{:S(2)}, u32[]{:S(2)}) collective-permute-start(bf16[1,2,144,1024]{3,2,0,1:T(8,128)(2,1)S(1)} %bitcast.118), channel_id=1, source_target_pairs={{0,8},{4,12},{8,0},{12,4},{1,9},{5,13},{9,1},{13,5},{2,10},{6,14},... | collective-permute-start | bytes 1769480 | tf_op jit(solution)/shard_map/ppermute | solution.py:958
  165.6 15.6 %collective-permute-start.2 = (bf16[1,2,144,1024]{3,2,1,0:T(8,128)(2,1)S(1)}, bf16[1,2,144,1024]{3,2,1,0:T(8,128)(2,1)S(1)}, u32[]{:S(2)}, u32[]{:S(2)}) collective-permute-start(bf16[1,2,144,1024]{3,2,1,0:T(8,128)(2,1)S(1)} %bitcast.125), channel_id=1, source_target_pairs={{0,8},{4,12},{8,0},{12,4},{1,9},{5,13},{9,1},{13,5},{2,10},{6,14},... | collective-permute-start | bytes 1769480 | tf_op jit(solution)/shard_map/ppermute | solution.py:958
  187.4 8.4 %collective-permute-start.9 = (bf16[2,2,144,1024]{3,2,1,0:T(8,128)(2,1)S(1)}, bf16[2,2,144,1024]{3,2,1,0:T(8,128)(2,1)S(1)}, u32[]{:S(2)}, u32[]{:S(2)}) collective-permute-start(bf16[2,2,144,1024]{3,2,1,0:T(8,128)(2,1)S(1)} %get-tuple-element.106.refs_0_.refs_8_), channel_id=1, source_target_pairs={{0,4},{4,0},{8,12},{12,8},{1,5},{5,1},{9,13},{13,9},{2,6},{6,2},{1... | collective-permute-start | bytes 3538952 | tf_op jit(solution)/shard_map/ppermute | solution.py:958
  191.9 25.2 %collective-permute-start.3 = (bf16[144,3072]{1,0:T(8,128)(2,1)S(1)}, bf16[144,3072]{1,0:T(8,128)(2,1)S(1)}, u32[]{:S(2)}, u32[]{:S(2)}) collective-permute-start(bf16[144,3072]{1,0:T(8,128)(2,1)S(1)} %get-tuple-element.105.refs_0_.cuts_ref), channel_id=1, source_target_pairs={{8,0},{9,1},{10,2},{11,3},{24,16},{25,17},{26,18},{27,19}} | collective-permute-start | bytes 2654216 | tf_op jit(solution)/shard_map/ppermute | solution.py:1039
  193.2 23.9 %collective-permute-start.4 = (bf16[144,3072]{1,0:T(8,128)(2,1)S(1)}, bf16[144,3072]{1,0:T(8,128)(2,1)S(1)}, u32[]{:S(2)}, u32[]{:S(2)}) collective-permute-start(bf16[144,3072]{1,0:T(8,128)(2,1)S(1)} %get-tuple-element.105.refs_0_.cuts_ref), channel_id=1, source_target_pairs={{4,0},{5,1},{6,2},{7,3},{20,16},{21,17},{22,18},{23,19}} | collective-permute-start | bytes 2654216 | tf_op jit(solution)/shard_map/ppermute | solution.py:1039
  194.5 23.2 %collective-permute-start.5 = (bf16[144,3072]{1,0:T(8,128)(2,1)S(1)}, bf16[144,3072]{1,0:T(8,128)(2,1)S(1)}, u32[]{:S(2)}, u32[]{:S(2)}) collective-permute-start(bf16[144,3072]{1,0:T(8,128)(2,1)S(1)} %get-tuple-element.105.refs_0_.cuts_ref), channel_id=1, source_target_pairs={{12,0},{13,1},{14,2},{15,3},{28,16},{29,17},{30,18},{31,19}} | collective-permute-start | bytes 2654216 | tf_op jit(solution)/shard_map/ppermute | solution.py:1039
  229.4 13.7 %collective-permute-start.24 = (bf16[256,1024]{1,0:T(8,128)(2,1)S(1)}, bf16[256,1024]{1,0:T(8,128)(2,1)S(1)}, u32[]{:S(2)}, u32[]{:S(2)}) collective-permute-start(bf16[256,1024]{1,0:T(8,128)(2,1)S(1)} %get-tuple-element.233), channel_id=1, source_target_pairs={{0,1},{4,5},{8,9},{12,13},{16,17},{20,21},{24,25},{28,29}} | collective-permute-start | bytes 1572872 | tf_op jit(solution)/shard_map/ppermute | solution.py:1129
  230.8 13.0 %collective-permute-start.25 = (bf16[256,1024]{1,0:T(8,128)(2,1)S(1)}, bf16[256,1024]{1,0:T(8,128)(2,1)S(1)}, u32[]{:S(2)}, u32[]{:S(2)}) collective-permute-start(bf16[256,1024]{1,0:T(8,128)(2,1)S(1)} %get-tuple-element.233), channel_id=1, source_target_pairs={{3,2},{7,6},{11,10},{15,14},{19,18},{23,22},{27,26},{31,30}} | collective-permute-start | bytes 1572872 | tf_op jit(solution)/shard_map/ppermute | solution.py:1130
  231.5 22.9 %collective-permute-start.10 = (bf16[256,1024]{1,0:T(8,128)(2,1)S(1)}, bf16[256,1024]{1,0:T(8,128)(2,1)S(1)}, u32[]{:S(2)}, u32[]{:S(2)}) collective-permute-start(bf16[256,1024]{1,0:T(8,128)(2,1)S(1)} %get-tuple-element.232), channel_id=1, source_target_pairs={{0,1},{4,5},{8,9},{12,13},{16,17},{20,21},{24,25},{28,29}} | collective-permute-start | bytes 1572872 | tf_op jit(solution)/shard_map/ppermute | solution.py:1129
  232.8 22.2 %collective-permute-start.11 = (bf16[256,1024]{1,0:T(8,128)(2,1)S(1)}, bf16[256,1024]{1,0:T(8,128)(2,1)S(1)}, u32[]{:S(2)}, u32[]{:S(2)}) collective-permute-start(bf16[256,1024]{1,0:T(8,128)(2,1)S(1)} %get-tuple-element.232), channel_id=1, source_target_pairs={{3,2},{7,6},{11,10},{15,14},{19,18},{23,22},{27,26},{31,30}} | collective-permute-start | bytes 1572872 | tf_op jit(solution)/shard_map/ppermute | solution.py:1130
  233.5 32.1 %collective-permute-start.18 = (bf16[256,1024]{1,0:T(8,128)(2,1)S(1)}, bf16[256,1024]{1,0:T(8,128)(2,1)S(1)}, u32[]{:S(2)}, u32[]{:S(2)}) collective-permute-start(bf16[256,1024]{1,0:T(8,128)(2,1)S(1)} %get-tuple-element.234), channel_id=1, source_target_pairs={{0,1},{4,5},{8,9},{12,13},{16,17},{20,21},{24,25},{28,29}} | collective-permute-start | bytes 1572872 | tf_op jit(solution)/shard_map/ppermute | solution.py:1129
  243.1 22.5 %collective-permute-start.19 = (bf16[256,1024]{1,0:T(8,128)(2,1)S(1)}, bf16[256,1024]{1,0:T(8,128)(2,1)S(1)}, u32[]{:S(2)}, u32[]{:S(2)}) collective-permute-start(bf16[256,1024]{1,0:T(8,128)(2,1)S(1)} %get-tuple-element.234), channel_id=1, source_target_pairs={{3,2},{7,6},{11,10},{15,14},{19,18},{23,22},{27,26},{31,30}} | collective-permute-start | bytes 1572872 | tf_op jit(solution)/shard_map/ppermute | solution.py:1130
  247.5 30.4 %collective-permute-start.26 = (bf16[256,1024]{1,0:T(8,128)(2,1)S(1)}, bf16[256,1024]{1,0:T(8,128)(2,1)S(1)}, u32[]{:S(2)}, u32[]{:S(2)}) collective-permute-start(bf16[256,1024]{1,0:T(8,128)(2,1)S(1)} %get-tuple-element.117), channel_id=1, source_target_pairs={{0,1},{1,2},{4,5},{5,6},{8,9},{9,10},{12,13},{13,14},{16,17},{17,1... | collective-permute-start | bytes 1572872 | tf_op jit(solution)/shard_map/ppermute | solution.py:1129
  254.3 24.3 %collective-permute-start.27 = (bf16[256,1024]{1,0:T(8,128)(2,1)S(1)}, bf16[256,1024]{1,0:T(8,128)(2,1)S(1)}, u32[]{:S(2)}, u32[]{:S(2)}) collective-permute-start(bf16[256,1024]{1,0:T(8,128)(2,1)S(1)} %get-tuple-element.118), channel_id=1, source_target_pairs={{3,2},{2,1},{7,6},{6,5},{11,10},{10,9},{15,14},{14,13},{19,18},{18... | collective-permute-start | bytes 1572872 | tf_op jit(solution)/shard_map/ppermute | solution.py:1130
  256.0 15.6 %collective-permute-start.14 = (bf16[1,2,144,1024]{3,2,0,1:T(8,128)(2,1)S(1)}, bf16[1,2,144,1024]{3,2,0,1:T(8,128)(2,1)S(1)}, u32[]{:S(2)}, u32[]{:S(2)}) collective-permute-start(bf16[1,2,144,1024]{3,2,0,1:T(8,128)(2,1)S(1)} %bitcast.121), channel_id=1, source_target_pairs={{0,8},{4,12},{8,0},{12,4},{1,9},{5,13},{9,1},{13,5},{2,10},{6,14},... | collective-permute-start | bytes 1769480 | tf_op jit(solution)/shard_map/ppermute | solution.py:958
  266.5 19.5 %collective-permute-start.20 = (bf16[256,1024]{1,0:T(8,128)(2,1)S(1)}, bf16[256,1024]{1,0:T(8,128)(2,1)S(1)}, u32[]{:S(2)}, u32[]{:S(2)}) collective-permute-start(bf16[256,1024]{1,0:T(8,128)(2,1)S(1)} %get-tuple-element.113), channel_id=1, source_target_pairs={{0,1},{1,2},{4,5},{5,6},{8,9},{9,10},{12,13},{13,14},{16,17},{17,1... | collective-permute-start | bytes 1572872 | tf_op jit(solution)/shard_map/ppermute | solution.py:1129
  270.9 19.5 %collective-permute-start.21 = (bf16[256,1024]{1,0:T(8,128)(2,1)S(1)}, bf16[256,1024]{1,0:T(8,128)(2,1)S(1)}, u32[]{:S(2)}, u32[]{:S(2)}) collective-permute-start(bf16[256,1024]{1,0:T(8,128)(2,1)S(1)} %get-tuple-element.114), channel_id=1, source_target_pairs={{3,2},{2,1},{7,6},{6,5},{11,10},{10,9},{15,14},{14,13},{19,18},{18... | collective-permute-start | bytes 1572872 | tf_op jit(solution)/shard_map/ppermute | solution.py:1130
  271.6 25.6 %collective-permute-start.12 = (bf16[256,1024]{1,0:T(8,128)(2,1)S(1)}, bf16[256,1024]{1,0:T(8,128)(2,1)S(1)}, u32[]{:S(2)}, u32[]{:S(2)}) collective-permute-start(bf16[256,1024]{1,0:T(8,128)(2,1)S(1)} %get-tuple-element.108), channel_id=1, source_target_pairs={{0,1},{1,2},{4,5},{5,6},{8,9},{9,10},{12,13},{13,14},{16,17},{17,1... | collective-permute-start | bytes 1572872 | tf_op jit(solution)/shard_map/ppermute | solution.py:1129
  277.9 20.6 %collective-permute-start.13 = (bf16[256,1024]{1,0:T(8,128)(2,1)S(1)}, bf16[256,1024]{1,0:T(8,128)(2,1)S(1)}, u32[]{:S(2)}, u32[]{:S(2)}) collective-permute-start(bf16[256,1024]{1,0:T(8,128)(2,1)S(1)} %get-tuple-element.109), channel_id=1, source_target_pairs={{3,2},{2,1},{7,6},{6,5},{11,10},{10,9},{15,14},{14,13},{19,18},{18... | collective-permute-start | bytes 1572872 | tf_op jit(solution)/shard_map/ppermute | solution.py:1130
  278.6 14.7 %collective-permute-start.15 = (bf16[2,2,144,1024]{3,2,0,1:T(8,128)(2,1)S(1)}, bf16[2,2,144,1024]{3,2,0,1:T(8,128)(2,1)S(1)}, u32[]{:S(2)}, u32[]{:S(2)}) collective-permute-start(bf16[2,2,144,1024]{3,2,0,1:T(8,128)(2,1)S(1)} %pad_maximum_fusion.4), channel_id=1, source_target_pairs={{0,4},{4,0},{8,12},{12,8},{1,5},{5,1},{9,13},{13,9},{2,6},{6,2},{1... | collective-permute-start | bytes 3538952 | tf_op jit(solution)/shard_map/ppermute | solution.py:958
  286.0 22.5 %collective-permute-start.28 = (bf16[256,1024]{1,0:T(8,128)(2,1)S(1)}, bf16[256,1024]{1,0:T(8,128)(2,1)S(1)}, u32[]{:S(2)}, u32[]{:S(2)}) collective-permute-start(bf16[256,1024]{1,0:T(8,128)(2,1)S(1)} %get-tuple-element.119), channel_id=1, source_target_pairs={{0,1},{1,2},{2,3},{4,5},{5,6},{6,7},{8,9},{9,10},{10,11},{12,13},{... | collective-permute-start | bytes 1572872 | tf_op jit(solution)/shard_map/ppermute | solution.py:1129
  291.4 28.0 %collective-permute-start.22 = (bf16[256,1024]{1,0:T(8,128)(2,1)S(1)}, bf16[256,1024]{1,0:T(8,128)(2,1)S(1)}, u32[]{:S(2)}, u32[]{:S(2)}) collective-permute-start(bf16[256,1024]{1,0:T(8,128)(2,1)S(1)} %get-tuple-element.115), channel_id=1, source_target_pairs={{0,1},{1,2},{2,3},{4,5},{5,6},{6,7},{8,9},{9,10},{10,11},{12,13},{... | collective-permute-start | bytes 1572872 | tf_op jit(solution)/shard_map/ppermute | solution.py:1129
  293.3 26.1 %collective-permute-start.23 = (bf16[256,1024]{1,0:T(8,128)(2,1)S(1)}, bf16[256,1024]{1,0:T(8,128)(2,1)S(1)}, u32[]{:S(2)}, u32[]{:S(2)}) collective-permute-start(bf16[256,1024]{1,0:T(8,128)(2,1)S(1)} %get-tuple-element.116), channel_id=1, source_target_pairs={{3,2},{2,1},{1,0},{7,6},{6,5},{5,4},{11,10},{10,9},{9,8},{15,14},{... | collective-permute-start | bytes 1572872 | tf_op jit(solution)/shard_map/ppermute | solution.py:1130
  297.3 24.1 %collective-permute-start.29 = (bf16[256,1024]{1,0:T(8,128)(2,1)S(1)}, bf16[256,1024]{1,0:T(8,128)(2,1)S(1)}, u32[]{:S(2)}, u32[]{:S(2)}) collective-permute-start(bf16[256,1024]{1,0:T(8,128)(2,1)S(1)} %get-tuple-element.120), channel_id=1, source_target_pairs={{3,2},{2,1},{1,0},{7,6},{6,5},{5,4},{11,10},{10,9},{9,8},{15,14},{... | collective-permute-start | bytes 1572872 | tf_op jit(solution)/shard_map/ppermute | solution.py:1130
  299.5 25.5 %collective-permute-start.16 = (bf16[256,1024]{1,0:T(8,128)(2,1)S(1)}, bf16[256,1024]{1,0:T(8,128)(2,1)S(1)}, u32[]{:S(2)}, u32[]{:S(2)}) collective-permute-start(bf16[256,1024]{1,0:T(8,128)(2,1)S(1)} %get-tuple-element.111), channel_id=1, source_target_pairs={{0,1},{1,2},{2,3},{4,5},{5,6},{6,7},{8,9},{9,10},{10,11},{12,13},{... | collective-permute-start | bytes 1572872 | tf_op jit(solution)/shard_map/ppermute | solution.py:1129
  308.5 19.9 %collective-permute-start.17 = (bf16[256,1024]{1,0:T(8,128)(2,1)S(1)}, bf16[256,1024]{1,0:T(8,128)(2,1)S(1)}, u32[]{:S(2)}, u32[]{:S(2)}) collective-permute-start(bf16[256,1024]{1,0:T(8,128)(2,1)S(1)} %get-tuple-element.112), channel_id=1, source_target_pairs={{3,2},{2,1},{1,0},{7,6},{6,5},{5,4},{11,10},{10,9},{9,8},{15,14},{... | collective-permute-start | bytes 1572872 | tf_op jit(solution)/shard_map/ppermute | solution.py:1130
  334.6 299.3 %all-gather.9.cloned.1.call-start = ((), (), s32[]{:S(2)}) async-start(), calls=%async_computation.2 | async-start | bytes 1114112 | tf_op jit(solution)/shard_map/all_gather | solution.py:972
  345.7 12.3 %collective-permute-start.33 = (f32[3,1024]{1,0:T(4,128)S(1)}, f32[3,1024]{1,0:T(4,128)S(1)}, u32[]{:S(2)}, u32[]{:S(2)}) collective-permute-start(f32[3,1024]{1,0:T(4,128)S(1)} %add_add_fusion.1), channel_id=1, source_target_pairs={{0,1},{1,0},{2,3},{3,2},{4,5},{5,4},{6,7},{7,6},{8,9},{9,8},{10,11... | collective-permute-start | bytes 36872 | tf_op jit(solution)/shard_map/ppermute | solution.py:958
  345.8 12.2 %collective-permute-start.34 = (f32[3,1024]{1,0:T(4,128)S(1)}, f32[3,1024]{1,0:T(4,128)S(1)}, u32[]{:S(2)}, u32[]{:S(2)}) collective-permute-start(f32[3,1024]{1,0:T(4,128)S(1)} %add_add_fusion.1), channel_id=1, source_target_pairs={{0,2},{1,3},{2,0},{3,1},{4,6},{5,7},{6,4},{7,5},{8,10},{9,11},{10,... | collective-permute-start | bytes 36872 | tf_op jit(solution)/shard_map/ppermute | solution.py:958
  348.0 10.0 %collective-permute-start.35 = (f32[3,1024]{1,0:T(4,128)S(1)}, f32[3,1024]{1,0:T(4,128)S(1)}, u32[]{:S(2)}, u32[]{:S(2)}) collective-permute-start(f32[3,1024]{1,0:T(4,128)S(1)} %add_add_fusion.1), channel_id=1, source_target_pairs={{0,3},{1,2},{2,1},{3,0},{4,7},{5,6},{6,5},{7,4},{8,11},{9,10},{10,... | collective-permute-start | bytes 36872 | tf_op jit(solution)/shard_map/ppermute | solution.py:958
  473.2 15.6 %collective-permute-start.36 = (bf16[1,2,144,1024]{3,2,1,0:T(8,128)(2,1)S(1)}, bf16[1,2,144,1024]{3,2,1,0:T(8,128)(2,1)S(1)}, u32[]{:S(2)}, u32[]{:S(2)}) collective-permute-start(bf16[1,2,144,1024]{3,2,1,0:T(8,128)(2,1)S(1)} %bitcast.124), channel_id=1, source_target_pairs={{0,8},{4,12},{8,0},{12,4},{1,9},{5,13},{9,1},{13,5},{2,10},{6,14},... | collective-permute-start | bytes 1769480 | tf_op jit(solution)/shard_map/ppermute | solution.py:958
  494.9 12.5 %collective-permute-start.43 = (bf16[2,2,144,1024]{3,2,1,0:T(8,128)(2,1)S(1)}, bf16[2,2,144,1024]{3,2,1,0:T(8,128)(2,1)S(1)}, u32[]{:S(2)}, u32[]{:S(2)}) collective-permute-start(bf16[2,2,144,1024]{3,2,1,0:T(8,128)(2,1)S(1)} %get-tuple-element.134.refs_0_.refs_8_), channel_id=1, source_target_pairs={{0,4},{4,0},{8,12},{12,8},{1,5},{5,1},{9,13},{13,9},{2,6},{6,2},{1... | collective-permute-start | bytes 3538952 | tf_op jit(solution)/shard_map/ppermute | solution.py:958
  495.0 9.7 %collective-permute-start.40 = (bf16[144,1024]{1,0:T(8,128)(2,1)S(1)}, bf16[144,1024]{1,0:T(8,128)(2,1)S(1)}, u32[]{:S(2)}, u32[]{:S(2)}) collective-permute-start(bf16[144,1024]{1,0:T(8,128)(2,1)S(1)} %get-tuple-element.129.d_attn_ref.refs_2_.refs_4_), channel_id=1, source_target_pairs={{12,4},{13,5},{14,6},{15,7},{28,20},{29,21},{30,22},{31,23}} | collective-permute-start | bytes 884744 | tf_op jit(solution)/shard_map/ppermute | solution.py:1039
  495.7 10.4 %collective-permute-start.41 = (bf16[144,1024]{1,0:T(8,128)(2,1)S(1)}, bf16[144,1024]{1,0:T(8,128)(2,1)S(1)}, u32[]{:S(2)}, u32[]{:S(2)}) collective-permute-start(bf16[144,1024]{1,0:T(8,128)(2,1)S(1)} %get-tuple-element.129.d_attn_ref.refs_2_.refs_4_), channel_id=1, source_target_pairs={{0,4},{1,5},{2,6},{3,7},{16,20},{17,21},{18,22},{19,23}} | collective-permute-start | bytes 884744 | tf_op jit(solution)/shard_map/ppermute | solution.py:1039
  498.7 8.7 %collective-permute-start.42 = (bf16[144,1024]{1,0:T(8,128)(2,1)S(1)}, bf16[144,1024]{1,0:T(8,128)(2,1)S(1)}, u32[]{:S(2)}, u32[]{:S(2)}) collective-permute-start(bf16[144,1024]{1,0:T(8,128)(2,1)S(1)} %get-tuple-element.129.d_attn_ref.refs_2_.refs_4_), channel_id=1, source_target_pairs={{8,4},{9,5},{10,6},{11,7},{24,20},{25,21},{26,22},{27,23}} | collective-permute-start | bytes 884744 | tf_op jit(solution)/shard_map/ppermute | solution.py:1039
  499.4 21.2 %collective-permute-start.37 = (bf16[144,3072]{1,0:T(8,128)(2,1)S(1)}, bf16[144,3072]{1,0:T(8,128)(2,1)S(1)}, u32[]{:S(2)}, u32[]{:S(2)}) collective-permute-start(bf16[144,3072]{1,0:T(8,128)(2,1)S(1)} %get-tuple-element.133.cuts_ref.refs_0_), channel_id=1, source_target_pairs={{8,0},{9,1},{10,2},{11,3},{24,16},{25,17},{26,18},{27,19}} | collective-permute-start | bytes 2654216 | tf_op jit(solution)/shard_map/ppermute | solution.py:1039
  504.8 15.8 %collective-permute-start.38 = (bf16[144,3072]{1,0:T(8,128)(2,1)S(1)}, bf16[144,3072]{1,0:T(8,128)(2,1)S(1)}, u32[]{:S(2)}, u32[]{:S(2)}) collective-permute-start(bf16[144,3072]{1,0:T(8,128)(2,1)S(1)} %get-tuple-element.133.cuts_ref.refs_0_), channel_id=1, source_target_pairs={{4,0},{5,1},{6,2},{7,3},{20,16},{21,17},{22,18},{23,19}} | collective-permute-start | bytes 2654216 | tf_op jit(solution)/shard_map/ppermute | solution.py:1039
  506.1 19.2 %collective-permute-start.39 = (bf16[144,3072]{1,0:T(8,128)(2,1)S(1)}, bf16[144,3072]{1,0:T(8,128)(2,1)S(1)}, u32[]{:S(2)}, u32[]{:S(2)}) collective-permute-start(bf16[144,3072]{1,0:T(8,128)(2,1)S(1)} %get-tuple-element.133.cuts_ref.refs_0_), channel_id=1, source_target_pairs={{12,0},{13,1},{14,2},{15,3},{28,16},{29,17},{30,18},{31,19}} | collective-permute-start | bytes 2654216 | tf_op jit(solution)/shard_map/ppermute | solution.py:1039
  536.8 17.2 %collective-permute-start.44 = (bf16[256,1024]{1,0:T(8,128)(2,1)S(1)}, bf16[256,1024]{1,0:T(8,128)(2,1)S(1)}, u32[]{:S(2)}, u32[]{:S(2)}) collective-permute-start(bf16[256,1024]{1,0:T(8,128)(2,1)S(1)} %get-tuple-element.228), channel_id=1, source_target_pairs={{0,1},{4,5},{8,9},{12,13},{16,17},{20,21},{24,25},{28,29}} | collective-permute-start | bytes 1572872 | tf_op jit(solution)/shard_map/ppermute | solution.py:1129
  540.6 14.1 %collective-permute-start.45 = (bf16[256,1024]{1,0:T(8,128)(2,1)S(1)}, bf16[256,1024]{1,0:T(8,128)(2,1)S(1)}, u32[]{:S(2)}, u32[]{:S(2)}) collective-permute-start(bf16[256,1024]{1,0:T(8,128)(2,1)S(1)} %get-tuple-element.228), channel_id=1, source_target_pairs={{3,2},{7,6},{11,10},{15,14},{19,18},{23,22},{27,26},{31,30}} | collective-permute-start | bytes 1572872 | tf_op jit(solution)/shard_map/ppermute | solution.py:1130
  542.0 25.2 %collective-permute-start.56 = (bf16[256,1024]{1,0:T(8,128)(2,1)S(1)}, bf16[256,1024]{1,0:T(8,128)(2,1)S(1)}, u32[]{:S(2)}, u32[]{:S(2)}) collective-permute-start(bf16[256,1024]{1,0:T(8,128)(2,1)S(1)} %get-tuple-element.226), channel_id=1, source_target_pairs={{0,1},{4,5},{8,9},{12,13},{16,17},{20,21},{24,25},{28,29}} | collective-permute-start | bytes 1572872 | tf_op jit(solution)/shard_map/ppermute | solution.py:1129
  543.3 24.6 %collective-permute-start.57 = (bf16[256,1024]{1,0:T(8,128)(2,1)S(1)}, bf16[256,1024]{1,0:T(8,128)(2,1)S(1)}, u32[]{:S(2)}, u32[]{:S(2)}) collective-permute-start(bf16[256,1024]{1,0:T(8,128)(2,1)S(1)} %get-tuple-element.226), channel_id=1, source_target_pairs={{3,2},{7,6},{11,10},{15,14},{19,18},{23,22},{27,26},{31,30}} | collective-permute-start | bytes 1572872 | tf_op jit(solution)/shard_map/ppermute | solution.py:1130
  544.0 37.7 %collective-permute-start.50 = (bf16[256,1024]{1,0:T(8,128)(2,1)S(1)}, bf16[256,1024]{1,0:T(8,128)(2,1)S(1)}, u32[]{:S(2)}, u32[]{:S(2)}) collective-permute-start(bf16[256,1024]{1,0:T(8,128)(2,1)S(1)} %get-tuple-element.227), channel_id=1, source_target_pairs={{0,1},{4,5},{8,9},{12,13},{16,17},{20,21},{24,25},{28,29}} | collective-permute-start | bytes 1572872 | tf_op jit(solution)/shard_map/ppermute | solution.py:1129
  554.0 28.4 %collective-permute-start.51 = (bf16[256,1024]{1,0:T(8,128)(2,1)S(1)}, bf16[256,1024]{1,0:T(8,128)(2,1)S(1)}, u32[]{:S(2)}, u32[]{:S(2)}) collective-permute-start(bf16[256,1024]{1,0:T(8,128)(2,1)S(1)} %get-tuple-element.227), channel_id=1, source_target_pairs={{3,2},{7,6},{11,10},{15,14},{19,18},{23,22},{27,26},{31,30}} | collective-permute-start | bytes 1572872 | tf_op jit(solution)/shard_map/ppermute | solution.py:1130
  558.4 34.5 %collective-permute-start.46 = (bf16[256,1024]{1,0:T(8,128)(2,1)S(1)}, bf16[256,1024]{1,0:T(8,128)(2,1)S(1)}, u32[]{:S(2)}, u32[]{:S(2)}) collective-permute-start(bf16[256,1024]{1,0:T(8,128)(2,1)S(1)} %get-tuple-element.137), channel_id=1, source_target_pairs={{0,1},{1,2},{4,5},{5,6},{8,9},{9,10},{12,13},{13,14},{16,17},{17,1... | collective-permute-start | bytes 1572872 | tf_op jit(solution)/shard_map/ppermute | solution.py:1129
  567.1 26.5 %collective-permute-start.47 = (bf16[256,1024]{1,0:T(8,128)(2,1)S(1)}, bf16[256,1024]{1,0:T(8,128)(2,1)S(1)}, u32[]{:S(2)}, u32[]{:S(2)}) collective-permute-start(bf16[256,1024]{1,0:T(8,128)(2,1)S(1)} %get-tuple-element.138), channel_id=1, source_target_pairs={{3,2},{2,1},{7,6},{6,5},{11,10},{10,9},{15,14},{14,13},{19,18},{18... | collective-permute-start | bytes 1572872 | tf_op jit(solution)/shard_map/ppermute | solution.py:1130
  568.8 35.4 %collective-permute-start.58 = (bf16[256,1024]{1,0:T(8,128)(2,1)S(1)}, bf16[256,1024]{1,0:T(8,128)(2,1)S(1)}, u32[]{:S(2)}, u32[]{:S(2)}) collective-permute-start(bf16[256,1024]{1,0:T(8,128)(2,1)S(1)} %get-tuple-element.146), channel_id=1, source_target_pairs={{0,1},{1,2},{4,5},{5,6},{8,9},{9,10},{12,13},{13,14},{16,17},{17,1... | collective-permute-start | bytes 1572872 | tf_op jit(solution)/shard_map/ppermute | solution.py:1129
  581.7 23.8 %collective-permute-start.59 = (bf16[256,1024]{1,0:T(8,128)(2,1)S(1)}, bf16[256,1024]{1,0:T(8,128)(2,1)S(1)}, u32[]{:S(2)}, u32[]{:S(2)}) collective-permute-start(bf16[256,1024]{1,0:T(8,128)(2,1)S(1)} %get-tuple-element.147), channel_id=1, source_target_pairs={{3,2},{2,1},{7,6},{6,5},{11,10},{10,9},{15,14},{14,13},{19,18},{18... | collective-permute-start | bytes 1572872 | tf_op jit(solution)/shard_map/ppermute | solution.py:1130
  583.3 32.1 %collective-permute-start.52 = (bf16[256,1024]{1,0:T(8,128)(2,1)S(1)}, bf16[256,1024]{1,0:T(8,128)(2,1)S(1)}, u32[]{:S(2)}, u32[]{:S(2)}) collective-permute-start(bf16[256,1024]{1,0:T(8,128)(2,1)S(1)} %get-tuple-element.142), channel_id=1, source_target_pairs={{0,1},{1,2},{4,5},{5,6},{8,9},{9,10},{12,13},{13,14},{16,17},{17,1... | collective-permute-start | bytes 1572872 | tf_op jit(solution)/shard_map/ppermute | solution.py:1129
  592.9 23.8 %collective-permute-start.53 = (bf16[256,1024]{1,0:T(8,128)(2,1)S(1)}, bf16[256,1024]{1,0:T(8,128)(2,1)S(1)}, u32[]{:S(2)}, u32[]{:S(2)}) collective-permute-start(bf16[256,1024]{1,0:T(8,128)(2,1)S(1)} %get-tuple-element.143), channel_id=1, source_target_pairs={{3,2},{2,1},{7,6},{6,5},{11,10},{10,9},{15,14},{14,13},{19,18},{18... | collective-permute-start | bytes 1572872 | tf_op jit(solution)/shard_map/ppermute | solution.py:1130
  594.5 32.1 %collective-permute-start.48 = (bf16[256,1024]{1,0:T(8,128)(2,1)S(1)}, bf16[256,1024]{1,0:T(8,128)(2,1)S(1)}, u32[]{:S(2)}, u32[]{:S(2)}) collective-permute-start(bf16[256,1024]{1,0:T(8,128)(2,1)S(1)} %get-tuple-element.139), channel_id=1, source_target_pairs={{0,1},{1,2},{2,3},{4,5},{5,6},{6,7},{8,9},{9,10},{10,11},{12,13},{... | collective-permute-start | bytes 1572872 | tf_op jit(solution)/shard_map/ppermute | solution.py:1129
  604.2 23.8 %collective-permute-start.49 = (bf16[256,1024]{1,0:T(8,128)(2,1)S(1)}, bf16[256,1024]{1,0:T(8,128)(2,1)S(1)}, u32[]{:S(2)}, u32[]{:S(2)}) collective-permute-start(bf16[256,1024]{1,0:T(8,128)(2,1)S(1)} %get-tuple-element.140), channel_id=1, source_target_pairs={{3,2},{2,1},{1,0},{7,6},{6,5},{5,4},{11,10},{10,9},{9,8},{15,14},{... | collective-permute-start | bytes 1572872 | tf_op jit(solution)/shard_map/ppermute | solution.py:1130
  607.1 33.3 %collective-permute-start.60 = (bf16[256,1024]{1,0:T(8,128)(2,1)}, bf16[256,1024]{1,0:T(8,128)(2,1)S(1)}, u32[]{:S(2)}, u32[]{:S(2)}) collective-permute-start(bf16[256,1024]{1,0:T(8,128)(2,1)} %get-tuple-element.148), channel_id=1, source_target_pairs={{0,1},{1,2},{2,3},{4,5},{5,6},{6,7},{8,9},{9,10},{10,11},{12,13},{... | collective-permute-start | bytes 1572872 | tf_op jit(solution)/shard_map/ppermute | solution.py:1129
  615.4 25.6 %collective-permute-start.61 = (bf16[256,1024]{1,0:T(8,128)(2,1)S(1)}, bf16[256,1024]{1,0:T(8,128)(2,1)}, u32[]{:S(2)}, u32[]{:S(2)}) collective-permute-start(bf16[256,1024]{1,0:T(8,128)(2,1)S(1)} %get-tuple-element.149), channel_id=1, source_target_pairs={{3,2},{2,1},{1,0},{7,6},{6,5},{5,4},{11,10},{10,9},{9,8},{15,14},{... | collective-permute-start | bytes 1572872 | tf_op jit(solution)/shard_map/ppermute | solution.py:1130
  617.6 39.5 %collective-permute-start.54 = (bf16[256,1024]{1,0:T(8,128)(2,1)S(1)}, bf16[256,1024]{1,0:T(8,128)(2,1)S(1)}, u32[]{:S(2)}, u32[]{:S(2)}) collective-permute-start(bf16[256,1024]{1,0:T(8,128)(2,1)S(1)} %get-tuple-element.144), channel_id=1, source_target_pairs={{0,1},{1,2},{2,3},{4,5},{5,6},{6,7},{8,9},{9,10},{10,11},{12,13},{... | collective-permute-start | bytes 1572872 | tf_op jit(solution)/shard_map/ppermute | solution.py:1129
  626.6 30.5 %collective-permute-start.55 = (bf16[256,1024]{1,0:T(8,128)(2,1)S(1)}, bf16[256,1024]{1,0:T(8,128)(2,1)}, u32[]{:S(2)}, u32[]{:S(2)}) collective-permute-start(bf16[256,1024]{1,0:T(8,128)(2,1)S(1)} %get-tuple-element.145), channel_id=1, source_target_pairs={{3,2},{2,1},{1,0},{7,6},{6,5},{5,4},{11,10},{10,9},{9,8},{15,14},{... | collective-permute-start | bytes 1572872 | tf_op jit(solution)/shard_map/ppermute | solution.py:1130
  635.1 18.0 %collective-permute-start.68 = (f32[3,1024]{1,0:T(4,128)S(1)}, f32[3,1024]{1,0:T(4,128)S(1)}, u32[]{:S(2)}, u32[]{:S(2)}) collective-permute-start(f32[3,1024]{1,0:T(4,128)S(1)} %get-tuple-element.218), channel_id=1, source_target_pairs={{0,16},{16,0},{1,17},{17,1},{2,18},{18,2},{3,19},{19,3},{4,20},{20... | collective-permute-start | bytes 36872 | tf_op jit(solution)/shard_map/ppermute | solution.py:958
  640.4 13.3 %collective-permute-start.62 = (bf16[256,512]{1,0:T(8,128)(2,1)S(1)}, bf16[256,512]{1,0:T(8,128)(2,1)S(1)}, u32[]{:S(2)}, u32[]{:S(2)}) collective-permute-start(bf16[256,512]{1,0:T(8,128)(2,1)S(1)} %bitcast.127), channel_id=1, source_target_pairs={{0,16},{16,0},{1,17},{17,1},{2,18},{18,2},{3,19},{19,3},{4,20},{20... | collective-permute-start | bytes 786440 | tf_op jit(solution)/shard_map/ppermute | solution.py:1176
  647.7 15.9 %collective-permute-start.64 = (bf16[256,512]{1,0:T(8,128)(2,1)S(1)}, bf16[256,512]{1,0:T(8,128)(2,1)S(1)}, u32[]{:S(2)}, u32[]{:S(2)}) collective-permute-start(bf16[256,512]{1,0:T(8,128)(2,1)S(1)} %bitcast.128), channel_id=1, source_target_pairs={{0,16},{16,0},{1,17},{17,1},{2,18},{18,2},{3,19},{19,3},{4,20},{20... | collective-permute-start | bytes 786440 | tf_op jit(solution)/shard_map/ppermute | solution.py:1176
  656.5 16.4 %collective-permute-start.67 = (bf16[256,512]{1,0:T(8,128)(2,1)S(1)}, bf16[256,512]{1,0:T(8,128)(2,1)S(1)}, u32[]{:S(2)}, u32[]{:S(2)}) collective-permute-start(bf16[256,512]{1,0:T(8,128)(2,1)S(1)} %get-tuple-element.155.refs_7_.refs_0_), channel_id=1, source_target_pairs={{0,16},{16,0},{1,17},{17,1},{2,18},{18,2},{3,19},{19,3},{4,20},{20... | collective-permute-start | bytes 786440 | tf_op jit(solution)/shard_map/ppermute | solution.py:1176
  662.1 6.5 collective-permute-start.63
  666.4 7.7 %collective-permute-start.66 = (bf16[256,512]{1,0:T(8,128)(2,1)S(1)}, bf16[256,512]{1,0:T(8,128)(2,1)S(1)}, u32[]{:S(2)}, u32[]{:S(2)}) collective-permute-start(bf16[256,512]{1,0:T(8,128)(2,1)S(1)} %get-tuple-element.167.refs_0_), channel_id=1, source_target_pairs={{0,16},{16,0},{1,17},{17,1},{2,18},{18,2},{3,19},{19,3},{4,20},{20... | collective-permute-start | bytes 786440 | tf_op jit(solution)/shard_map/ppermute | solution.py:1176
  (62 other events, 1165.6 us)
Sparse Core Ops, SparseCore 0:
  10.7 143.4 all-gather.4
  334.7 128.9 all-gather.6
  542.1 37.9 all-gather.8

commit v4 on v3

--- a/solution.py
+++ b/solution.py
@@ -111,7 +111,8 @@
     return ((pre * half).astype(jnp.bfloat16), slope)
 
 
-def gather_kernel(lengths, picked_ref, across_ref, tokens_hbm, cot_hbm, *refs, steps):
+def gather_kernel(lengths, picked_ref, across_ref, tokens_hbm, cot_hbm, *refs, steps, extra):
+    refs = refs[extra:]
     both_refs, mask_refs = refs[:steps], refs[steps : 2 * steps]
     held, sems = refs[2 * steps :]
     copies = [
@@ -143,7 +144,8 @@
 
 
 def scatter_kernel(across_ref, base_ref, rows_ref, *refs):
-    out_ref = refs[-1]
+    out_ref, mark_ref = refs[-2:]
+    mark_ref[...] = jnp.zeros_like(mark_ref)
     base = base_ref[0]
     across = across_ref[0]
     places = lax.broadcasted_iota(jnp.int32, (base.shape[0], across.shape[1]), 0)
@@ -154,12 +156,14 @@
 
 
 def attention_kernel(
-    weights, info, needs, moves, starts, rows, both_ref, vec_ref, mask_ref, *refs, order, extra
+    weights, mask_hbm, both_ref, vec_ref, *refs, order, extra
 ):
-    proj_ref, lse_ref, pair_ref, first_ref, held, sems = refs[extra:]
+    proj_ref, lse_ref, pair_ref, first_ref, held, mask_ref, sems, mask_sem = refs[extra:]
     rows_ref = both_ref.at[0]
     width = both_ref.shape[2]
     copies = weight_copies(weights, held, sems, range(4), width, order)
+    mask_copy = pltpu.make_async_copy(mask_hbm, mask_ref, mask_sem)
+    mask_copy.start()
     for copy in copies:
         copy.start()
     xs = rows_ref[...].astype(jnp.float32)
@@ -169,6 +173,7 @@
         proj_ref[:, index * width : (index + 1) * width] = nt(
             h1, held[pl.ds(index * width, width), :]
         ).astype(jnp.bfloat16)
+    mask_copy.wait()
     allowed = mask_ref[...] > 0
     lane = lax.broadcasted_iota(jnp.int32, lse_ref.shape, 1)
     lse = jnp.zeros(lse_ref.shape, jnp.float32)
@@ -420,48 +425,65 @@
             out_ref[index] = nn(act, held[1]).astype(jnp.bfloat16)
 
 
-def attention_products_kernel(info, needs, h1_ref, *refs, sources, extra):
+def attention_products_kernel(info, needs, h1_ref, *refs, sources, extra, first, last):
     proj_refs, attn_refs = refs[:sources], refs[sources : 2 * sources]
-    pair_refs = refs[2 * sources : -9 - extra]
-    out_ref, held, projs, attns, made, held_sems, factor_sems, out_sems = refs[-8:]
-    count, piece, _ = made.shape
+    pair_refs = refs[2 * sources : -10 - extra]
+    near_ref, given_ref, out_ref, held, projs, attns, made, held_sems, factor_sems, out_sems = refs[-10:]
+    _, piece, _ = made.shape
     tokens = h1_ref.shape[1]
     rights = ([h1_ref.at[at] for at in range(sources)], pair_refs_of(pair_refs, 0))
+    columns = pl.ds(first * piece, (last - first) * piece)
+    lefts = ([ref.at[:, columns] for ref in proj_refs], attn_refs)
 
     def each_operand(act):
-        for kind, (lefts, target) in enumerate(((proj_refs, projs), (attn_refs, attns))):
+        for kind, target in enumerate((projs, attns)):
 
             @pl.when(needs[kind] > 0)
-            def _(kind=kind, lefts=lefts, target=target):
+            def _(kind=kind, target=target):
                 copies = plane_copies(rights[kind], held.at[kind], held_sems.at[kind], tokens)
-                copies += plane_copies(lefts, target, factor_sems.at[kind], tokens)
+                copies += plane_copies(lefts[kind], target, factor_sems.at[kind], tokens)
                 for copy in copies:
                     act(copy)
 
     def out_copy(index):
-        return pltpu.make_async_copy(made.at[index], out_ref.at[index], out_sems.at[index])
+        return pltpu.make_async_copy(made.at[index - first], out_ref.at[index], out_sems.at[index])
+
+    def passed_copy(index):
+        source = near_ref if first else given_ref
+        return pltpu.make_async_copy(source.at[index], out_ref.at[index], out_sems.at[index])
+
+    def each_passed(act):
+        for index in range(first if first else last):
+            kind = info[index, 0]
+
+            @pl.when((kind < 2) if first else (kind >= 2))
+            def _(index=index):
+                act(passed_copy(index))
 
     each_operand(lambda copy: copy.start())
+    each_passed(lambda copy: copy.start())
     each_operand(lambda copy: copy.wait())
-    for index in range(count):
+    for index in range(first, last):
 
         @pl.when(info[index, 0] == 0)
         def _(index=index):
-            left = projs[:, index * piece : (index + 1) * piece]
-            made[index] = tn(left, held[0]).astype(jnp.bfloat16)
+            left = projs[:, (index - first) * piece : (index - first + 1) * piece]
+            made[index - first] = tn(left, held[0]).astype(jnp.bfloat16)
             out_copy(index).start()
 
         @pl.when(info[index, 0] == 1)
         def _(index=index):
             left = attns[:, pl.ds(pl.multiple_of(info[index, 1], 128), piece)]
-            made[index] = tn(left, held[1]).astype(jnp.bfloat16)
+            made[index - first] = tn(left, held[1]).astype(jnp.bfloat16)
             out_copy(index).start()
 
-    for index in range(count):
+    for index in range(first, last):
 
         @pl.when(info[index, 0] < 2)
         def _(index=index):
             out_copy(index).wait()
+
+    each_passed(lambda copy: copy.wait())
 
 
 def line_kernel(moves, below_ref, above_ref, terms_ref, *refs, step, piece, passed):
@@ -612,15 +634,15 @@
     return [pl.BlockSpec(memory_space=pltpu.VMEM)] * count
 
 
-def run_gather(lengths, picked, tokens_in, cot_in):
+def run_gather(lengths, picked, tokens_in, cot_in, plan):
     steps, count = picked.shape
     _, places, width = tokens_in.shape
     tokens = count + -count % 16
     padded = jnp.pad(picked, ((0, 0), (0, tokens - count)), constant_values=NOWHERE)
     shape = jax.ShapeDtypeStruct
     made = pl.pallas_call(
-        functools.partial(gather_kernel, steps=steps),
-        in_specs=[pl.BlockSpec(memory_space=pltpu.SMEM)] + vmem(2) + anywhere(2),
+        functools.partial(gather_kernel, steps=steps, extra=len(plan)),
+        in_specs=smem(1) + vmem(2) + anywhere(2) + smem(len(plan)),
         out_specs=vmem(2 * steps),
         out_shape=[shape((2, tokens, width), jnp.bfloat16)] * steps
         + [shape((2 * tokens, tokens), jnp.int32)] * steps,
@@ -628,9 +650,9 @@
             pltpu.VMEM((steps, 2, places, width), jnp.bfloat16),
             pltpu.SemaphoreType.DMA((steps, 2)),
         ],
-        compiler_params=pltpu.CompilerParams(vmem_limit_bytes=44 << 20),
+        compiler_params=pltpu.CompilerParams(vmem_limit_bytes=37 << 20),
         name="gather_rows",
-    )(lengths, padded[:, :, None], padded[:, None, :], tokens_in, cot_in)
+    )(lengths, padded[:, :, None], padded[:, None, :], tokens_in, cot_in, *plan)
     return (made[:steps], made[steps:], padded[:, None, :])
 
 
@@ -647,8 +669,11 @@
             pl.BlockSpec((tokens, width), lambda index: (0, 0)),
         ]
         + anywhere(len(chain) + len(known)),
-        out_specs=here,
-        out_shape=jax.ShapeDtypeStruct(base.shape, base.dtype),
+        out_specs=[here, pl.BlockSpec((8, 128), lambda index: (0, 0))],
+        out_shape=[
+            jax.ShapeDtypeStruct(base.shape, base.dtype),
+            jax.ShapeDtypeStruct((8, 128), jnp.float32),
+        ],
         input_output_aliases=chain_aliases(3, chain),
         compiler_params=pltpu.CompilerParams(vmem_limit_bytes=56 << 20),
         cost_estimate=SMALL_COST,
@@ -656,12 +681,12 @@
     )(across, base, rows, *chain, *known)
 
 
-def run_attention(order, gathered, plan, both, vec_now, mask, known):
+def run_attention(order, gathered, both, vec_now, mask, known):
     _, tokens, width = both.shape
     shape = jax.ShapeDtypeStruct
     return pl.pallas_call(
         functools.partial(attention_kernel, order=order, extra=len(known)),
-        in_specs=anywhere(1) + smem(len(plan)) + vmem(3) + anywhere(len(known)),
+        in_specs=anywhere(2) + vmem(2) + anywhere(len(known)),
         out_specs=vmem(4),
         out_shape=[
             shape((tokens, 3 * width), jnp.bfloat16),
@@ -671,14 +696,16 @@
         ],
         scratch_shapes=[
             pltpu.VMEM((4 * width, width), jnp.bfloat16),
+            pltpu.VMEM(mask.shape, jnp.int32),
             pltpu.SemaphoreType.DMA((4,)),
+            pltpu.SemaphoreType.DMA,
         ],
-        compiler_params=pltpu.CompilerParams(vmem_limit_bytes=44 << 20),
+        compiler_params=pltpu.CompilerParams(vmem_limit_bytes=37 << 20),
         cost_estimate=pl.CostEstimate(
             flops=8 * tokens * width * width, bytes_accessed=8 * width * width, transcendentals=0
         ),
         name="attention",
-    )(gathered, *plan, both, vec_now, mask, *known)
+    )(gathered, mask, both, vec_now, *known)
 
 
 def run_feed_forward(order, gathered, both, vec_now, first_sum, keep):
@@ -701,7 +728,7 @@
             pltpu.VMEM((wide - 4 * width, width), jnp.bfloat16),
             pltpu.SemaphoreType.DMA(((wide - 4 * width) // width,)),
         ],
-        compiler_params=pltpu.CompilerParams(vmem_limit_bytes=44 << 20),
+        compiler_params=pltpu.CompilerParams(vmem_limit_bytes=37 << 20),
         cost_estimate=pl.CostEstimate(
             flops=8 * tokens * (wide - 4 * width) * width,
             bytes_accessed=2 * wide * width,
@@ -738,7 +765,7 @@
             pltpu.SemaphoreType.DMA((2,)),
             pltpu.SemaphoreType.DMA((cuts,)),
         ],
-        compiler_params=pltpu.CompilerParams(vmem_limit_bytes=44 << 20),
+        compiler_params=pltpu.CompilerParams(vmem_limit_bytes=37 << 20),
         cost_estimate=pl.CostEstimate(
             flops=10 * tokens * width * width, bytes_accessed=4 * width * width, transcendentals=0
         ),
@@ -764,7 +791,7 @@
             pltpu.VMEM((cuts, 3 * width // cuts, width), jnp.bfloat16),
             pltpu.SemaphoreType.DMA((cuts,)),
         ],
-        compiler_params=pltpu.CompilerParams(vmem_limit_bytes=44 << 20),
+        compiler_params=pltpu.CompilerParams(vmem_limit_bytes=37 << 20),
         cost_estimate=SMALL_COST,
         name="input_back",
     )(gathered, rows, d_proj, both, vec_now, base, *known)
@@ -913,7 +940,7 @@
             pltpu.SemaphoreType.DMA((count,)),
             pltpu.SemaphoreType.DMA((count,)),
         ],
-        compiler_params=pltpu.CompilerParams(vmem_limit_bytes=44 << 20),
+        compiler_params=pltpu.CompilerParams(vmem_limit_bytes=37 << 20),
         cost_estimate=pl.CostEstimate(
             flops=6 * count * sources * tokens * piece * width,
             bytes_accessed=6 * count * piece * width,
@@ -921,32 +948,39 @@
         ),
         name="feed_forward_products",
     )(info, needs, gathered, plane_d_down, *pairs, *attn_parts)
-    operands = (info, needs, plane_h1, *proj_parts, *attn_parts, *pairs, *known, made)
-    return pl.pallas_call(
-        functools.partial(
-            attention_products_kernel, sources=sources, extra=len(known)
-        ),
-        in_specs=smem(2) + anywhere(len(operands) - 2),
-        out_specs=anywhere(1)[0],
-        out_shape=shape,
-        scratch_shapes=[
-            pltpu.VMEM((2, sources * tokens, width), jnp.bfloat16),
-            pltpu.VMEM((sources * tokens, 3 * width), jnp.bfloat16),
-            pltpu.VMEM((sources * tokens, width), jnp.bfloat16),
-            pltpu.VMEM((count, piece, width), jnp.bfloat16),
-            pltpu.SemaphoreType.DMA((2, sources)),
-            pltpu.SemaphoreType.DMA((2, sources)),
-            pltpu.SemaphoreType.DMA((count,)),
-        ],
-        input_output_aliases={len(operands) - 1: 0},
-        compiler_params=pltpu.CompilerParams(vmem_limit_bytes=44 << 20),
-        cost_estimate=pl.CostEstimate(
-            flops=2 * count * sources * tokens * piece * width,
-            bytes_accessed=2 * count * piece * width,
-            transcendentals=0,
-        ),
-        name="attention_products",
-    )(*operands)
+    near = made
+    for first, last in ((0, PIECES), (PIECES, count)):
+        known = () if first else known
+        operands = (info, needs, plane_h1, *proj_parts, *attn_parts, *pairs, *known, near, made)
+        blocks = last - first
+        found = pl.pallas_call(
+            functools.partial(
+                attention_products_kernel,
+                sources=sources,
+                extra=len(known),
+                first=first,
+                last=last,
+            ),
+            in_specs=smem(2) + anywhere(len(operands) - 2),
+            out_specs=anywhere(1)[0],
+            out_shape=jax.ShapeDtypeStruct((count if first else last, piece, width), jnp.bfloat16),
+            scratch_shapes=[
+                pltpu.VMEM((2, sources * tokens, width), jnp.bfloat16),
+                pltpu.VMEM((sources * tokens, blocks * piece), jnp.bfloat16),
+                pltpu.VMEM((sources * tokens, width), jnp.bfloat16),
+                pltpu.VMEM((blocks, piece, width), jnp.bfloat16),
+                pltpu.SemaphoreType.DMA((2, sources)),
+                pltpu.SemaphoreType.DMA((2, sources)),
+                pltpu.SemaphoreType.DMA((count,)),
+            ],
+            input_output_aliases={len(operands) - 1: 0} if first else {},
+            compiler_params=pltpu.CompilerParams(vmem_limit_bytes=16 << 20),
+            cost_estimate=SMALL_COST,
+            name="attention_products",
+        )(*operands)
+        if first:
+            return (near, found)
+        near = found
 
 
 def pad_rows(rows):
@@ -1111,13 +1145,13 @@
     )
 
 
-def gradient_share(terms, moves, passed, meanwhile):
+def gradient_share(near, terms, moves, passed, meanwhile):
     line = lax.axis_size("dp")
     below, above = [None] * PIECES, [None] * PIECES
     for step in range(line - 1):
         for index in range(PIECES):
             if step == 0:
-                up = down = terms[index]
+                up = down = near[index]
             else:
                 due = known[index] if step == line - 2 else ()
                 given = passed if step == 1 and index == 0 else ()
@@ -1202,13 +1236,13 @@
     planes, line = lax.axis_size("fsdp"), lax.axis_size("dp")
     shard_rows = weights.shape[0]
     info, needs, moves = gradient_plan(shard_rows, model_width, weights.shape[0] * planes * line)
-    boths, masks, across = run_gather(lengths[:, 0], selected[:, 0], tokens, cotangent)
-    plane_rows = plane_gather(boths[0])
     split = in_planes(shard_rows, model_width)
     starts = gradient_starts(shard_rows, model_width, split)
     order = (planes, line, shard_rows)
     weight_starts = gathered_row(starts, order)
     plan = (info, needs, moves, starts, weight_starts)
+    boths, masks, across = run_gather(lengths[:, 0], selected[:, 0], tokens, cotangent, plan)
+    plane_rows = plane_gather(boths[0])
     groups = lax.axis_size("grp")
     place = lax.axis_index("grp").astype(jnp.int32)[None]
     shard_low = master.astype(jnp.bfloat16)
@@ -1220,11 +1254,10 @@
         proj, lse, pair, first_sum = run_attention(
             order,
             gathered,
-            plan,
             both,
             vec_now,
             mask,
-            [plane_h1, plane_d_down, *activations, *input_grad],
+            [plane_h1, plane_d_down, *activations[1:], *input_grad[1:]],
         )
         d_attn_low, out_rows, base, grad_two, *kept = run_feed_forward(
             order, gathered, both, vec_now, first_sum, not split
@@ -1246,12 +1279,12 @@
             return d_rows
 
         def scatter_step(d_rows, marks):
-            activations[:] = [
-                run_scatter(across, tokens, out_rows, inner_step, activations, marks)
-            ]
-            input_grad[:] = [
-                run_scatter(across, cotangent, d_rows, inner_step, input_grad, marks)
-            ]
+            activations[:] = run_scatter(
+                across, tokens, out_rows, inner_step, activations[:1], marks
+            )
+            input_grad[:] = run_scatter(
+                across, cotangent, d_rows, inner_step, input_grad[:1], marks
+            )
 
         if split and last:
             d_rows = input_step([])
@@ -1264,7 +1297,7 @@
             return ((), (), ())
 
         if split:
-            terms = plane_terms(
+            near, terms = plane_terms(
                 gathered,
                 d_proj,
                 d_attn_low,
@@ -1276,7 +1309,7 @@
                 shard_rows,
                 [d_rows] if last else (),
             )
-            below, above = gradient_share(terms, moves, following, meanwhile)
+            below, above = gradient_share(near, terms, moves, following, meanwhile)
             grad_mark = below[-1]
         else:
             grad_mark = gradient_whole(
@@ -1298,7 +1331,9 @@
                         last,
                         groups,
                         made[-1][:2] if index else (),
-                        [outers[0][3]] + input_grad if index == PIECES - 1 else activations,
+                        [outers[0][3], input_grad[1]]
+                        if index == PIECES - 1
+                        else activations[1:],
                     )
                 )
                 own, other = made[-1][2:]

time: 697 us -> 681 us (0.977)
  waiting for transfers between devices: 359 us -> 346 us
  local copies, waits for them, and re-layouts: 26.1 us -> 33.4 us
    ppermute x18, waiting for transfers between devices: 81.4 us -> 58.5 us  [gradient_share(): below[index] = lax.ppermute(up, 'dp', [(p, p + 1) for p in range(step + 1)])]
    unnamed x110 -> x176, local copies, waits for them, and re-layouts: 17.7 us -> 28.3 us
    pallas_call x2 -> x4, Pallas kernels: 20.2 us -> 21.5 us  [run_products(): pl.pallas_call(functools.partial(attention_products_kernel, sources=sourc...]
  transfers between devices with their start and end apart: 72 -> 72, of which waited for: 29 -> 29; matrix products, arithmetic and copies ran while one was open for 2% -> 2% of each run, Pallas kernels for 14% -> 16%
where the time goes in v4:
time: 681 us; the launch traced here: 673 us
  waiting for transfers between devices  346 us (51%)
  Pallas kernels  142 us (21%)
  starting transfers between devices  117 us (17%)
  local copies, waits for them, and re-layouts  33.4 us (5%)
  between operations  18.7 us (3%)
  other arithmetic  16.1 us (2%)
    all_gather x2, waiting for transfers between devices, on_device(): gathered = lax.all_gather(shard_low, ('dp', 'fsdp'), axis=0, tiled=True)  203 us
    ppermute x18, starting transfers between devices, gradient_share(): below[index] = lax.ppermute(up, 'dp', [(p, p + 1) for p in range(step + 1)])  61.5 us
    ppermute x18, waiting for transfers between devices, gradient_share(): below[index] = lax.ppermute(up, 'dp', [(p, p + 1) for p in range(step + 1)])  58.5 us
    ppermute x12, waiting for transfers between devices, send_to(): lax.ppermute(values, 'fsdp', [(target ^ delta, target)])  36.7 us
    ppermute x15, waiting for transfers between devices, swap(): return lax.ppermute(values, axis, [(i, i ^ delta) for i in range(size)])  35.4 us
    unnamed x176, local copies, waits for them, and re-layouts  28.3 us
    pallas_call x2, Pallas kernels, run_feed_forward(): pl.pallas_call(functools.partial(feed_forward_kernel, keep=keep, order=or...  24.3 us
    pallas_call x4, Pallas kernels, run_products(): pl.pallas_call(functools.partial(attention_products_kernel, sources=sourc...  21.5 us
  transfers between devices with their start and end apart: 72, of which 29 were waited for; matrix products, arithmetic and copies ran while one was open for 2% of the time, Pallas kernels for 16%

profile of v4, /device:TPU:0, one launch (start us, length us, event | category | flops | bytes accessed | tf_op | source)
XLA Modules:
  0.0 673.2 jit_solution(5386224037852186105)
XLA Ops:
  7.3 3.3 convert_element_type.171
  17.3 4.5 gather_rows.1
  22.0 3.0 collective-permute-start
  25.0 26.5 %collective-permute-done = bf16[1,2,144,1024]{3,2,0,1:T(8,128)(2,1)S(1)} collective-permute-done((bf16[1,2,144,1024]{3,2,0,1:T(8,128)(2,1)S(1)}, bf16[1,2,144,1024]{3,2,0,1:T(8,128)(2,1)S(1)}, u32[]{:S(2)}, u32[]{:S(2)}) %collective-permute-start) | collective-permute-done | bytes 589856 | tf_op jit(solution)/shard_map/ppermute | solution.py:992
  51.7 2.8 collective-permute-done.1
  55.8 98.5 %all-gather.5.cloned.1.call-done.weights = bf16[12288,1024]{1,0:T(8,128)(2,1)} async-done(((bf16[768,1024]{1,0:T(8,128)(2,1)}), bf16[12288,1024]{1,0:T(8,128)(2,1)}) %all-gather.5.cloned.1.call-update) | async-done | bytes 25165840 | tf_op jit(solution)/shard_map/all_gather | solution.py:1252
  155.3 7.0 %attention.2 = (bf16[144,3072]{1,0:T(8,128)(2,1)S(1)}, f32[288,128]{1,0:T(8,128)S(1)}, bf16[2,144,1024]{2,1,0:T(8,128)(2,1)S(1)}, f32[144,1024]{1,0:T(8,128)S(1)}) custom-call(bf16[12288,1024]{1,0:T(8,128)(2,1)} %all-gather.5.cloned.1.call-done.weights, s32[288,144]{1,0:T(8,128)S(1)} %copy-done.36, bf16[2,144,1024]{2,1,0:T(8,128)(2,1)S(1)} %get-tuple-element.106.both_ref, ...), custom_call_target="tpu_custom_call" | custom-call | flops 1207959552 | bytes 8388608 | tf_op jit(solution)/shard_map/attention/pallas_call | solution.py:687
  163.0 12.2 %feed_forward.2 = (bf16[144,1024]{1,0:T(8,128)(2,1)S(1)}, bf16[144,1024]{1,0:T(8,128)(2,1)S(1)}, f32[144,1024]{1,0:T(8,128)S(1)}, f32[2,1024]{1,0:T(2,128)S(1)}) custom-call(bf16[12288,1024]{1,0:T(8,128)(2,1)} %all-gather.5.cloned.1.call-done.weights, bf16[2,144,1024]{2,1,0:T(8,128)(2,1)S(1)} %get-tuple-element.106.both_ref, f32[3,1024]{1,0:T(4,128)S(1)} %copy-done.40, ...), custom_call_target="tpu_custom_call" | custom-call | flops 9663676416 | bytes 25165824 | tf_op jit(solution)/shard_map/feed_forward/pallas_call | solution.py:716
  177.9 6.2 attention_back.2
  184.9 3.0 collective-permute-start.7
  194.1 19.7 %collective-permute-done.3.refs_1_ = bf16[144,3072]{1,0:T(8,128)(2,1)S(1)} collective-permute-done((bf16[144,3072]{1,0:T(8,128)(2,1)S(1)}, bf16[144,3072]{1,0:T(8,128)(2,1)S(1)}, u32[]{:S(2)}, u32[]{:S(2)}) %collective-permute-start.3) | collective-permute-done | bytes 884768 | tf_op jit(solution)/shard_map/ppermute | solution.py:1073
  214.5 3.3 attention_products.4.refs_10_
  223.3 7.5 %attention_products.5.terms_ref = bf16[12,256,1024]{2,1,0:T(8,128)(2,1)S(1)} custom-call(s32[12,3]{1,0:T(8,128)S(1)} %copy-done.47, s32[4]{0:T(128)S(1)} %copy-done.53, bf16[4,144,1024]{2,1,0:T(8,128)(2,1)S(1)} %get-tuple-element.248.refs_0_.h1_ref, bf16[144,3072]{1,0:T(8,128)(2,1)S(1)} %get-tuple-element.113.refs_0_.cuts_ref, ...), custom_call_target="tpu_custom_call", output_to_operand_aliasing={{}: (14, {})} | custom-call | flops 1000000 | bytes 100000 | tf_op jit(solution)/shard_map/attention_products/pallas_call | solution.py:956
  233.2 4.4 collective-permute-start.26
  237.6 5.2 collective-permute-done.10.below_ref
  244.5 9.5 %collective-permute-done.18.below_ref = bf16[256,1024]{1,0:T(8,128)(2,1)S(1)} collective-permute-done((bf16[256,1024]{1,0:T(8,128)(2,1)S(1)}, bf16[256,1024]{1,0:T(8,128)(2,1)S(1)}, u32[]{:S(2)}, u32[]{:S(2)}) %collective-permute-start.18) | collective-permute-done | bytes 524320 | tf_op jit(solution)/shard_map/ppermute | solution.py:1163
  254.9 4.4 collective-permute-start.20
  260.1 5.9 collective-permute-start.12
  267.8 8.7 %collective-permute-done.20.below_ref = bf16[256,1024]{1,0:T(8,128)(2,1)S(1)} collective-permute-done((bf16[256,1024]{1,0:T(8,128)(2,1)S(1)}, bf16[256,1024]{1,0:T(8,128)(2,1)S(1)}, u32[]{:S(2)}, u32[]{:S(2)}) %collective-permute-start.20) | collective-permute-done | bytes 524320 | tf_op jit(solution)/shard_map/ppermute | solution.py:1163
  276.5 4.4 collective-permute-start.28
  290.0 5.2 collective-permute-start.16
  295.1 3.8 collective-permute-done.28.refs_0_
  300.7 8.0 %collective-permute-done.22 = bf16[256,1024]{1,0:T(8,128)(2,1)S(1)} collective-permute-done((bf16[256,1024]{1,0:T(8,128)(2,1)S(1)}, bf16[256,1024]{1,0:T(8,128)(2,1)S(1)}, u32[]{:S(2)}, u32[]{:S(2)}) %collective-permute-start.22) | collective-permute-done | bytes 524320 | tf_op jit(solution)/shard_map/ppermute | solution.py:1163
  311.0 3.3 collective-permute-done.16
  314.4 2.3 collective-permute-done.17
  317.7 5.0 fusion.34
  324.8 4.0 input_back.2
  334.8 2.5 collective-permute-start.33
  337.3 2.9 collective-permute-start.34
  341.6 3.9 scatter_rows.5
  345.5 4.0 scatter_rows.4
  351.3 104.6 %all-gather.7.cloned.1.call-done.weights = bf16[12288,1024]{1,0:T(8,128)(2,1)} async-done(((bf16[768,1024]{1,0:T(8,128)(2,1)}), bf16[12288,1024]{1,0:T(8,128)(2,1)}) %all-gather.7.cloned.1.call-update) | async-done | bytes 25165840 | tf_op jit(solution)/shard_map/all_gather | solution.py:1252
  455.9 7.2 %attention.3 = (bf16[144,3072]{1,0:T(8,128)(2,1)S(1)}, f32[288,128]{1,0:T(8,128)S(1)}, bf16[2,144,1024]{2,1,0:T(8,128)(2,1)S(1)}, f32[144,1024]{1,0:T(8,128)S(1)}) custom-call(bf16[12288,1024]{1,0:T(8,128)(2,1)} %all-gather.7.cloned.1.call-done.weights, s32[288,144]{1,0:T(8,128)S(1)} %copy-done.34, ...), custom_call_target="tpu_custom_call" | custom-call | flops 1207959552 | bytes 8388608 | tf_op jit(solution)/shard_map/attention/pallas_call | solution.py:687
  465.5 12.1 %feed_forward.3 = (bf16[144,1024]{1,0:T(8,128)(2,1)S(1)}, bf16[144,1024]{1,0:T(8,128)(2,1)S(1)}, f32[144,1024]{1,0:T(8,128)S(1)}, f32[2,1024]{1,0:T(2,128)S(1)}) custom-call(bf16[12288,1024]{1,0:T(8,128)(2,1)} %all-gather.7.cloned.1.call-done.weights, bf16[2,144,1024]{2,1,0:T(8,128)(2,1)S(1)} %copy-done.22, f32[3,1024]{1,0:T(4,128)S(1)} %get-tuple-element.236.vec_ref, ...), custom_call_target="tpu_custom_call" | custom-call | flops 9663676416 | bytes 25165824 | tf_op jit(solution)/shard_map/feed_forward/pallas_call | solution.py:716
  478.7 6.2 attention_back.3
  485.7 3.0 collective-permute-start.41
  490.7 4.0 input_back.3
  499.0 11.5 %collective-permute-done.37.refs_1_ = bf16[144,3072]{1,0:T(8,128)(2,1)S(1)} collective-permute-done((bf16[144,3072]{1,0:T(8,128)(2,1)S(1)}, bf16[144,3072]{1,0:T(8,128)(2,1)S(1)}, u32[]{:S(2)}, u32[]{:S(2)}) %collective-permute-start.37) | collective-permute-done | bytes 884768 | tf_op jit(solution)/shard_map/ppermute | solution.py:1073
  510.5 4.8 collective-permute-done.39.refs_3_
  515.3 3.3 attention_products.6.refs_10_
  519.8 4.5 collective-permute-start.44
  530.1 2.8 copy-done.1
  542.0 7.4 %attention_products.7.terms_ref.refs_0_ = bf16[12,256,1024]{2,1,0:T(8,128)(2,1)S(1)} custom-call(s32[12,3]{1,0:T(8,128)S(1)} %copy-done.48, s32[4]{0:T(128)S(1)} %copy-done.54, bf16[4,144,1024]{2,1,0:T(8,128)(2,1)S(1)} %get-tuple-element.246.refs_0_.h1_ref, bf16[144,3072]{1,0:T(8,128)(2,1)S(1)} %copy-done.8, ...), custom_call_target="tpu_custom_call", output_to_operand_aliasing={{}: (14, {})} | custom-call | flops 1000000 | bytes 100000 | tf_op jit(solution)/shard_map/attention_products/pallas_call | solution.py:956
  549.4 2.7 copy-done.2
  552.8 2.8 copy-done.3
  560.1 2.8 collective-permute-start.58
  566.7 4.9 collective-permute-start.52
  571.6 4.6 collective-permute-done.46.below_ref
  577.8 5.0 collective-permute-start.48
  582.8 4.6 collective-permute-done.58.below_ref
  590.3 5.0 collective-permute-start.60
  595.4 3.3 collective-permute-done.52.below_ref
  601.0 5.0 collective-permute-start.54
  606.1 3.8 collective-permute-done.48.below_ref
  611.5 3.9 update.3
  620.2 3.8 scatter_rows.6
  625.3 4.9 update.4
  633.5 3.9 scatter_rows.7
  638.0 2.8 outer.3
  641.5 5.0 update.5
  648.0 2.8 outer.4
  651.4 4.3 collective-permute-done.63.refs_0_
  655.7 2.8 outer.5
  661.7 3.2 collective-permute-done.65.refs_1_
  (344 shorter events, 116.1 us)
Async XLA Ops:
  7.2 147.2 %all-gather.5.cloned.1.call-start = ((), (), s32[]{:S(2)}) async-start(), calls=%async_computation | async-start | bytes 26738688 | tf_op jit(solution)/shard_map/all_gather | solution.py:1252
  10.6 445.3 %all-gather.7.cloned.1.call-start = ((), (), s32[]{:S(2)}) async-start(), calls=%async_computation.1 | async-start | bytes 26738688 | tf_op jit(solution)/shard_map/all_gather | solution.py:1252
  22.0 29.5 %collective-permute-start = (bf16[1,2,144,1024]{3,2,0,1:T(8,128)(2,1)S(1)}, bf16[1,2,144,1024]{3,2,0,1:T(8,128)(2,1)S(1)}, u32[]{:S(2)}, u32[]{:S(2)}) collective-permute-start(bf16[1,2,144,1024]{3,2,0,1:T(8,128)(2,1)S(1)} %bitcast.116), channel_id=1, source_target_pairs={{0,8},{4,12},{8,0},{12,4},{1,9},{5,13},{9,1},{13,5},{2,10},{6,14},... | collective-permute-start | bytes 1769480 | tf_op jit(solution)/shard_map/ppermute | solution.py:992
  162.3 15.5 %collective-permute-start.2 = (bf16[1,2,144,1024]{3,2,1,0:T(8,128)(2,1)S(1)}, bf16[1,2,144,1024]{3,2,1,0:T(8,128)(2,1)S(1)}, u32[]{:S(2)}, u32[]{:S(2)}) collective-permute-start(bf16[1,2,144,1024]{3,2,1,0:T(8,128)(2,1)S(1)} %bitcast.123), channel_id=1, source_target_pairs={{0,8},{4,12},{8,0},{12,4},{1,9},{5,13},{9,1},{13,5},{2,10},{6,14},... | collective-permute-start | bytes 1769480 | tf_op jit(solution)/shard_map/ppermute | solution.py:992
  184.1 8.4 %collective-permute-start.9 = (bf16[2,2,144,1024]{3,2,1,0:T(8,128)(2,1)S(1)}, bf16[2,2,144,1024]{3,2,1,0:T(8,128)(2,1)S(1)}, u32[]{:S(2)}, u32[]{:S(2)}) collective-permute-start(bf16[2,2,144,1024]{3,2,1,0:T(8,128)(2,1)S(1)} %get-tuple-element.114.refs_0_.refs_8_), channel_id=1, source_target_pairs={{0,4},{4,0},{8,12},{12,8},{1,5},{5,1},{9,13},{13,9},{2,6},{6,2},{1... | collective-permute-start | bytes 3538952 | tf_op jit(solution)/shard_map/ppermute | solution.py:992
  188.6 25.2 %collective-permute-start.3 = (bf16[144,3072]{1,0:T(8,128)(2,1)S(1)}, bf16[144,3072]{1,0:T(8,128)(2,1)S(1)}, u32[]{:S(2)}, u32[]{:S(2)}) collective-permute-start(bf16[144,3072]{1,0:T(8,128)(2,1)S(1)} %get-tuple-element.113.refs_0_.cuts_ref), channel_id=1, source_target_pairs={{8,0},{9,1},{10,2},{11,3},{24,16},{25,17},{26,18},{27,19}} | collective-permute-start | bytes 2654216 | tf_op jit(solution)/shard_map/ppermute | solution.py:1073
  189.9 23.9 %collective-permute-start.4 = (bf16[144,3072]{1,0:T(8,128)(2,1)S(1)}, bf16[144,3072]{1,0:T(8,128)(2,1)S(1)}, u32[]{:S(2)}, u32[]{:S(2)}) collective-permute-start(bf16[144,3072]{1,0:T(8,128)(2,1)S(1)} %get-tuple-element.113.refs_0_.cuts_ref), channel_id=1, source_target_pairs={{4,0},{5,1},{6,2},{7,3},{20,16},{21,17},{22,18},{23,19}} | collective-permute-start | bytes 2654216 | tf_op jit(solution)/shard_map/ppermute | solution.py:1073
  191.2 23.2 %collective-permute-start.5 = (bf16[144,3072]{1,0:T(8,128)(2,1)S(1)}, bf16[144,3072]{1,0:T(8,128)(2,1)S(1)}, u32[]{:S(2)}, u32[]{:S(2)}) collective-permute-start(bf16[144,3072]{1,0:T(8,128)(2,1)S(1)} %get-tuple-element.113.refs_0_.cuts_ref), channel_id=1, source_target_pairs={{12,0},{13,1},{14,2},{15,3},{28,16},{29,17},{30,18},{31,19}} | collective-permute-start | bytes 2654216 | tf_op jit(solution)/shard_map/ppermute | solution.py:1073
  217.9 13.7 %collective-permute-start.24 = (bf16[256,1024]{1,0:T(8,128)(2,1)S(1)}, bf16[256,1024]{1,0:T(8,128)(2,1)S(1)}, u32[]{:S(2)}, u32[]{:S(2)}) collective-permute-start(bf16[256,1024]{1,0:T(8,128)(2,1)S(1)} %get-tuple-element.253), channel_id=1, source_target_pairs={{0,1},{4,5},{8,9},{12,13},{16,17},{20,21},{24,25},{28,29}} | collective-permute-start | bytes 1572872 | tf_op jit(solution)/shard_map/ppermute | solution.py:1163
  219.2 13.0 %collective-permute-start.25 = (bf16[256,1024]{1,0:T(8,128)(2,1)S(1)}, bf16[256,1024]{1,0:T(8,128)(2,1)S(1)}, u32[]{:S(2)}, u32[]{:S(2)}) collective-permute-start(bf16[256,1024]{1,0:T(8,128)(2,1)S(1)} %get-tuple-element.253), channel_id=1, source_target_pairs={{3,2},{7,6},{11,10},{15,14},{19,18},{23,22},{27,26},{31,30}} | collective-permute-start | bytes 1572872 | tf_op jit(solution)/shard_map/ppermute | solution.py:1164
  219.9 22.9 %collective-permute-start.10 = (bf16[256,1024]{1,0:T(8,128)(2,1)S(1)}, bf16[256,1024]{1,0:T(8,128)(2,1)S(1)}, u32[]{:S(2)}, u32[]{:S(2)}) collective-permute-start(bf16[256,1024]{1,0:T(8,128)(2,1)S(1)} %get-tuple-element.252), channel_id=1, source_target_pairs={{0,1},{4,5},{8,9},{12,13},{16,17},{20,21},{24,25},{28,29}} | collective-permute-start | bytes 1572872 | tf_op jit(solution)/shard_map/ppermute | solution.py:1163
  221.3 22.2 %collective-permute-start.11 = (bf16[256,1024]{1,0:T(8,128)(2,1)S(1)}, bf16[256,1024]{1,0:T(8,128)(2,1)S(1)}, u32[]{:S(2)}, u32[]{:S(2)}) collective-permute-start(bf16[256,1024]{1,0:T(8,128)(2,1)S(1)} %get-tuple-element.252), channel_id=1, source_target_pairs={{3,2},{7,6},{11,10},{15,14},{19,18},{23,22},{27,26},{31,30}} | collective-permute-start | bytes 1572872 | tf_op jit(solution)/shard_map/ppermute | solution.py:1164
  222.0 32.1 %collective-permute-start.18 = (bf16[256,1024]{1,0:T(8,128)(2,1)S(1)}, bf16[256,1024]{1,0:T(8,128)(2,1)S(1)}, u32[]{:S(2)}, u32[]{:S(2)}) collective-permute-start(bf16[256,1024]{1,0:T(8,128)(2,1)S(1)} %get-tuple-element.254), channel_id=1, source_target_pairs={{0,1},{4,5},{8,9},{12,13},{16,17},{20,21},{24,25},{28,29}} | collective-permute-start | bytes 1572872 | tf_op jit(solution)/shard_map/ppermute | solution.py:1163
  231.5 22.5 %collective-permute-start.19 = (bf16[256,1024]{1,0:T(8,128)(2,1)S(1)}, bf16[256,1024]{1,0:T(8,128)(2,1)S(1)}, u32[]{:S(2)}, u32[]{:S(2)}) collective-permute-start(bf16[256,1024]{1,0:T(8,128)(2,1)S(1)} %get-tuple-element.254), channel_id=1, source_target_pairs={{3,2},{7,6},{11,10},{15,14},{19,18},{23,22},{27,26},{31,30}} | collective-permute-start | bytes 1572872 | tf_op jit(solution)/shard_map/ppermute | solution.py:1164
  233.2 32.9 %collective-permute-start.26 = (bf16[256,1024]{1,0:T(8,128)(2,1)S(1)}, bf16[256,1024]{1,0:T(8,128)(2,1)S(1)}, u32[]{:S(2)}, u32[]{:S(2)}) collective-permute-start(bf16[256,1024]{1,0:T(8,128)(2,1)S(1)} %get-tuple-element.125), channel_id=1, source_target_pairs={{0,1},{1,2},{4,5},{5,6},{8,9},{9,10},{12,13},{13,14},{16,17},{17,1... | collective-permute-start | bytes 1572872 | tf_op jit(solution)/shard_map/ppermute | solution.py:1163
  242.8 24.0 %collective-permute-start.27 = (bf16[256,1024]{1,0:T(8,128)(2,1)S(1)}, bf16[256,1024]{1,0:T(8,128)(2,1)S(1)}, u32[]{:S(2)}, u32[]{:S(2)}) collective-permute-start(bf16[256,1024]{1,0:T(8,128)(2,1)S(1)} %get-tuple-element.126), channel_id=1, source_target_pairs={{3,2},{2,1},{7,6},{6,5},{11,10},{10,9},{15,14},{14,13},{19,18},{18... | collective-permute-start | bytes 1572872 | tf_op jit(solution)/shard_map/ppermute | solution.py:1164
  244.4 15.6 %collective-permute-start.14 = (bf16[1,2,144,1024]{3,2,0,1:T(8,128)(2,1)S(1)}, bf16[1,2,144,1024]{3,2,0,1:T(8,128)(2,1)S(1)}, u32[]{:S(2)}, u32[]{:S(2)}) collective-permute-start(bf16[1,2,144,1024]{3,2,0,1:T(8,128)(2,1)S(1)} %bitcast.119), channel_id=1, source_target_pairs={{0,8},{4,12},{8,0},{12,4},{1,9},{5,13},{9,1},{13,5},{2,10},{6,14},... | collective-permute-start | bytes 1769480 | tf_op jit(solution)/shard_map/ppermute | solution.py:992
  254.9 21.6 %collective-permute-start.20 = (bf16[256,1024]{1,0:T(8,128)(2,1)S(1)}, bf16[256,1024]{1,0:T(8,128)(2,1)S(1)}, u32[]{:S(2)}, u32[]{:S(2)}) collective-permute-start(bf16[256,1024]{1,0:T(8,128)(2,1)S(1)} %get-tuple-element.121), channel_id=1, source_target_pairs={{0,1},{1,2},{4,5},{5,6},{8,9},{9,10},{12,13},{13,14},{16,17},{17,1... | collective-permute-start | bytes 1572872 | tf_op jit(solution)/shard_map/ppermute | solution.py:1163
  259.4 21.5 %collective-permute-start.21 = (bf16[256,1024]{1,0:T(8,128)(2,1)S(1)}, bf16[256,1024]{1,0:T(8,128)(2,1)S(1)}, u32[]{:S(2)}, u32[]{:S(2)}) collective-permute-start(bf16[256,1024]{1,0:T(8,128)(2,1)S(1)} %get-tuple-element.122), channel_id=1, source_target_pairs={{3,2},{2,1},{7,6},{6,5},{11,10},{10,9},{15,14},{14,13},{19,18},{18... | collective-permute-start | bytes 1572872 | tf_op jit(solution)/shard_map/ppermute | solution.py:1164
  260.1 27.6 %collective-permute-start.12 = (bf16[256,1024]{1,0:T(8,128)(2,1)S(1)}, bf16[256,1024]{1,0:T(8,128)(2,1)S(1)}, u32[]{:S(2)}, u32[]{:S(2)}) collective-permute-start(bf16[256,1024]{1,0:T(8,128)(2,1)S(1)} %get-tuple-element.116), channel_id=1, source_target_pairs={{0,1},{1,2},{4,5},{5,6},{8,9},{9,10},{12,13},{13,14},{16,17},{17,1... | collective-permute-start | bytes 1572872 | tf_op jit(solution)/shard_map/ppermute | solution.py:1163
  266.1 22.9 %collective-permute-start.13 = (bf16[256,1024]{1,0:T(8,128)(2,1)S(1)}, bf16[256,1024]{1,0:T(8,128)(2,1)S(1)}, u32[]{:S(2)}, u32[]{:S(2)}) collective-permute-start(bf16[256,1024]{1,0:T(8,128)(2,1)S(1)} %get-tuple-element.117), channel_id=1, source_target_pairs={{3,2},{2,1},{7,6},{6,5},{11,10},{10,9},{15,14},{14,13},{19,18},{18... | collective-permute-start | bytes 1572872 | tf_op jit(solution)/shard_map/ppermute | solution.py:1164
  266.8 17.0 %collective-permute-start.15 = (bf16[2,2,144,1024]{3,2,0,1:T(8,128)(2,1)S(1)}, bf16[2,2,144,1024]{3,2,0,1:T(8,128)(2,1)S(1)}, u32[]{:S(2)}, u32[]{:S(2)}) collective-permute-start(bf16[2,2,144,1024]{3,2,0,1:T(8,128)(2,1)S(1)} %pad_maximum_fusion.4), channel_id=1, source_target_pairs={{0,4},{4,0},{8,12},{12,8},{1,5},{5,1},{9,13},{13,9},{2,6},{6,2},{1... | collective-permute-start | bytes 3538952 | tf_op jit(solution)/shard_map/ppermute | solution.py:992
  276.5 22.5 %collective-permute-start.28 = (bf16[256,1024]{1,0:T(8,128)(2,1)S(1)}, bf16[256,1024]{1,0:T(8,128)(2,1)S(1)}, u32[]{:S(2)}, u32[]{:S(2)}) collective-permute-start(bf16[256,1024]{1,0:T(8,128)(2,1)S(1)} %get-tuple-element.127), channel_id=1, source_target_pairs={{0,1},{1,2},{2,3},{4,5},{5,6},{6,7},{8,9},{9,10},{10,11},{12,13},{... | collective-permute-start | bytes 1572872 | tf_op jit(solution)/shard_map/ppermute | solution.py:1163
  281.9 26.9 %collective-permute-start.22 = (bf16[256,1024]{1,0:T(8,128)(2,1)S(1)}, bf16[256,1024]{1,0:T(8,128)(2,1)S(1)}, u32[]{:S(2)}, u32[]{:S(2)}) collective-permute-start(bf16[256,1024]{1,0:T(8,128)(2,1)S(1)} %get-tuple-element.123), channel_id=1, source_target_pairs={{0,1},{1,2},{2,3},{4,5},{5,6},{6,7},{8,9},{9,10},{10,11},{12,13},{... | collective-permute-start | bytes 1572872 | tf_op jit(solution)/shard_map/ppermute | solution.py:1163
  283.8 24.9 %collective-permute-start.23 = (bf16[256,1024]{1,0:T(8,128)(2,1)S(1)}, bf16[256,1024]{1,0:T(8,128)(2,1)S(1)}, u32[]{:S(2)}, u32[]{:S(2)}) collective-permute-start(bf16[256,1024]{1,0:T(8,128)(2,1)S(1)} %get-tuple-element.124), channel_id=1, source_target_pairs={{3,2},{2,1},{1,0},{7,6},{6,5},{5,4},{11,10},{10,9},{9,8},{15,14},{... | collective-permute-start | bytes 1572872 | tf_op jit(solution)/shard_map/ppermute | solution.py:1164
  287.7 23.3 %collective-permute-start.29 = (bf16[256,1024]{1,0:T(8,128)(2,1)S(1)}, bf16[256,1024]{1,0:T(8,128)(2,1)S(1)}, u32[]{:S(2)}, u32[]{:S(2)}) collective-permute-start(bf16[256,1024]{1,0:T(8,128)(2,1)S(1)} %get-tuple-element.128), channel_id=1, source_target_pairs={{3,2},{2,1},{1,0},{7,6},{6,5},{5,4},{11,10},{10,9},{9,8},{15,14},{... | collective-permute-start | bytes 1572872 | tf_op jit(solution)/shard_map/ppermute | solution.py:1164
  290.0 24.4 %collective-permute-start.16 = (bf16[256,1024]{1,0:T(8,128)(2,1)S(1)}, bf16[256,1024]{1,0:T(8,128)(2,1)S(1)}, u32[]{:S(2)}, u32[]{:S(2)}) collective-permute-start(bf16[256,1024]{1,0:T(8,128)(2,1)S(1)} %get-tuple-element.119), channel_id=1, source_target_pairs={{0,1},{1,2},{2,3},{4,5},{5,6},{6,7},{8,9},{9,10},{10,11},{12,13},{... | collective-permute-start | bytes 1572872 | tf_op jit(solution)/shard_map/ppermute | solution.py:1163
  299.0 17.7 %collective-permute-start.17 = (bf16[256,1024]{1,0:T(8,128)(2,1)S(1)}, bf16[256,1024]{1,0:T(8,128)(2,1)S(1)}, u32[]{:S(2)}, u32[]{:S(2)}) collective-permute-start(bf16[256,1024]{1,0:T(8,128)(2,1)S(1)} %get-tuple-element.120), channel_id=1, source_target_pairs={{3,2},{2,1},{1,0},{7,6},{6,5},{5,4},{11,10},{10,9},{9,8},{15,14},{... | collective-permute-start | bytes 1572872 | tf_op jit(solution)/shard_map/ppermute | solution.py:1164
  322.8 294.7 %all-gather.9.cloned.1.call-start = ((), (), s32[]{:S(2)}) async-start(), calls=%async_computation.2 | async-start | bytes 1114112 | tf_op jit(solution)/shard_map/all_gather | solution.py:1006
  334.8 14.7 %collective-permute-start.33 = (f32[3,1024]{1,0:T(4,128)S(1)}, f32[3,1024]{1,0:T(4,128)S(1)}, u32[]{:S(2)}, u32[]{:S(2)}) collective-permute-start(f32[3,1024]{1,0:T(4,128)S(1)} %add_add_fusion.1), channel_id=1, source_target_pairs={{0,1},{1,0},{2,3},{3,2},{4,5},{5,4},{6,7},{7,6},{8,9},{9,8},{10,11... | collective-permute-start | bytes 36872 | tf_op jit(solution)/shard_map/ppermute | solution.py:992
  337.3 12.2 %collective-permute-start.34 = (f32[3,1024]{1,0:T(4,128)S(1)}, f32[3,1024]{1,0:T(4,128)S(1)}, u32[]{:S(2)}, u32[]{:S(2)}) collective-permute-start(f32[3,1024]{1,0:T(4,128)S(1)} %add_add_fusion.1), channel_id=1, source_target_pairs={{0,2},{1,3},{2,0},{3,1},{4,6},{5,7},{6,4},{7,5},{8,10},{9,11},{10,... | collective-permute-start | bytes 36872 | tf_op jit(solution)/shard_map/ppermute | solution.py:992
  340.2 9.3 %collective-permute-start.35 = (f32[3,1024]{1,0:T(4,128)S(1)}, f32[3,1024]{1,0:T(4,128)S(1)}, u32[]{:S(2)}, u32[]{:S(2)}) collective-permute-start(f32[3,1024]{1,0:T(4,128)S(1)} %add_add_fusion.1), channel_id=1, source_target_pairs={{0,3},{1,2},{2,1},{3,0},{4,7},{5,6},{6,5},{7,4},{8,11},{9,10},{10,... | collective-permute-start | bytes 36872 | tf_op jit(solution)/shard_map/ppermute | solution.py:992
  463.1 15.6 %collective-permute-start.36 = (bf16[1,2,144,1024]{3,2,1,0:T(8,128)(2,1)S(1)}, bf16[1,2,144,1024]{3,2,1,0:T(8,128)(2,1)S(1)}, u32[]{:S(2)}, u32[]{:S(2)}) collective-permute-start(bf16[1,2,144,1024]{3,2,1,0:T(8,128)(2,1)S(1)} %bitcast.122), channel_id=1, source_target_pairs={{0,8},{4,12},{8,0},{12,4},{1,9},{5,13},{9,1},{13,5},{2,10},{6,14},... | collective-permute-start | bytes 1769480 | tf_op jit(solution)/shard_map/ppermute | solution.py:992
  484.9 12.5 %collective-permute-start.43 = (bf16[2,2,144,1024]{3,2,1,0:T(8,128)(2,1)S(1)}, bf16[2,2,144,1024]{3,2,1,0:T(8,128)(2,1)S(1)}, u32[]{:S(2)}, u32[]{:S(2)}) collective-permute-start(bf16[2,2,144,1024]{3,2,1,0:T(8,128)(2,1)S(1)} %get-tuple-element.145.refs_0_.refs_8_), channel_id=1, source_target_pairs={{0,4},{4,0},{8,12},{12,8},{1,5},{5,1},{9,13},{13,9},{2,6},{6,2},{1... | collective-permute-start | bytes 3538952 | tf_op jit(solution)/shard_map/ppermute | solution.py:992
  485.0 9.8 %collective-permute-start.40 = (bf16[144,1024]{1,0:T(8,128)(2,1)S(1)}, bf16[144,1024]{1,0:T(8,128)(2,1)S(1)}, u32[]{:S(2)}, u32[]{:S(2)}) collective-permute-start(bf16[144,1024]{1,0:T(8,128)(2,1)S(1)} %get-tuple-element.140.d_attn_ref.refs_2_.refs_4_), channel_id=1, source_target_pairs={{12,4},{13,5},{14,6},{15,7},{28,20},{29,21},{30,22},{31,23}} | collective-permute-start | bytes 884744 | tf_op jit(solution)/shard_map/ppermute | solution.py:1073
  485.7 10.4 %collective-permute-start.41 = (bf16[144,1024]{1,0:T(8,128)(2,1)S(1)}, bf16[144,1024]{1,0:T(8,128)(2,1)S(1)}, u32[]{:S(2)}, u32[]{:S(2)}) collective-permute-start(bf16[144,1024]{1,0:T(8,128)(2,1)S(1)} %get-tuple-element.140.d_attn_ref.refs_2_.refs_4_), channel_id=1, source_target_pairs={{0,4},{1,5},{2,6},{3,7},{16,20},{17,21},{18,22},{19,23}} | collective-permute-start | bytes 884744 | tf_op jit(solution)/shard_map/ppermute | solution.py:1073
  488.7 8.7 %collective-permute-start.42 = (bf16[144,1024]{1,0:T(8,128)(2,1)S(1)}, bf16[144,1024]{1,0:T(8,128)(2,1)S(1)}, u32[]{:S(2)}, u32[]{:S(2)}) collective-permute-start(bf16[144,1024]{1,0:T(8,128)(2,1)S(1)} %get-tuple-element.140.d_attn_ref.refs_2_.refs_4_), channel_id=1, source_target_pairs={{8,4},{9,5},{10,6},{11,7},{24,20},{25,21},{26,22},{27,23}} | collective-permute-start | bytes 884744 | tf_op jit(solution)/shard_map/ppermute | solution.py:1073
  489.4 21.1 %collective-permute-start.37 = (bf16[144,3072]{1,0:T(8,128)(2,1)S(1)}, bf16[144,3072]{1,0:T(8,128)(2,1)S(1)}, u32[]{:S(2)}, u32[]{:S(2)}) collective-permute-start(bf16[144,3072]{1,0:T(8,128)(2,1)S(1)} %get-tuple-element.144.cuts_ref.refs_0_), channel_id=1, source_target_pairs={{8,0},{9,1},{10,2},{11,3},{24,16},{25,17},{26,18},{27,19}} | collective-permute-start | bytes 2654216 | tf_op jit(solution)/shard_map/ppermute | solution.py:1073
  494.8 15.7 %collective-permute-start.38 = (bf16[144,3072]{1,0:T(8,128)(2,1)S(1)}, bf16[144,3072]{1,0:T(8,128)(2,1)S(1)}, u32[]{:S(2)}, u32[]{:S(2)}) collective-permute-start(bf16[144,3072]{1,0:T(8,128)(2,1)S(1)} %get-tuple-element.144.cuts_ref.refs_0_), channel_id=1, source_target_pairs={{4,0},{5,1},{6,2},{7,3},{20,16},{21,17},{22,18},{23,19}} | collective-permute-start | bytes 2654216 | tf_op jit(solution)/shard_map/ppermute | solution.py:1073
  496.1 19.1 %collective-permute-start.39 = (bf16[144,3072]{1,0:T(8,128)(2,1)S(1)}, bf16[144,3072]{1,0:T(8,128)(2,1)S(1)}, u32[]{:S(2)}, u32[]{:S(2)}) collective-permute-start(bf16[144,3072]{1,0:T(8,128)(2,1)S(1)} %get-tuple-element.144.cuts_ref.refs_0_), channel_id=1, source_target_pairs={{12,0},{13,1},{14,2},{15,3},{28,16},{29,17},{30,18},{31,19}} | collective-permute-start | bytes 2654216 | tf_op jit(solution)/shard_map/ppermute | solution.py:1073
  519.8 32.3 %collective-permute-start.44 = (bf16[256,1024]{1,0:T(8,128)(2,1)}, bf16[256,1024]{1,0:T(8,128)(2,1)}, u32[]{:S(2)}, u32[]{:S(2)}) collective-permute-start(bf16[256,1024]{1,0:T(8,128)(2,1)} %get-tuple-element.251), channel_id=1, source_target_pairs={{0,1},{4,5},{8,9},{12,13},{16,17},{20,21},{24,25},{28,29}} | collective-permute-start | bytes 1572872 | tf_op jit(solution)/shard_map/ppermute | solution.py:1163
  524.4 28.4 %collective-permute-start.45 = (bf16[256,1024]{1,0:T(8,128)(2,1)}, bf16[256,1024]{1,0:T(8,128)(2,1)}, u32[]{:S(2)}, u32[]{:S(2)}) collective-permute-start(bf16[256,1024]{1,0:T(8,128)(2,1)} %get-tuple-element.251), channel_id=1, source_target_pairs={{3,2},{7,6},{11,10},{15,14},{19,18},{23,22},{27,26},{31,30}} | collective-permute-start | bytes 1572872 | tf_op jit(solution)/shard_map/ppermute | solution.py:1164
  526.5 32.0 %collective-permute-start.56 = (bf16[256,1024]{1,0:T(8,128)(2,1)}, bf16[256,1024]{1,0:T(8,128)(2,1)S(1)}, u32[]{:S(2)}, u32[]{:S(2)}) collective-permute-start(bf16[256,1024]{1,0:T(8,128)(2,1)} %get-tuple-element.249), channel_id=1, source_target_pairs={{0,1},{4,5},{8,9},{12,13},{16,17},{20,21},{24,25},{28,29}} | collective-permute-start | bytes 1572872 | tf_op jit(solution)/shard_map/ppermute | solution.py:1163
  527.8 31.4 %collective-permute-start.57 = (bf16[256,1024]{1,0:T(8,128)(2,1)}, bf16[256,1024]{1,0:T(8,128)(2,1)S(1)}, u32[]{:S(2)}, u32[]{:S(2)}) collective-permute-start(bf16[256,1024]{1,0:T(8,128)(2,1)} %get-tuple-element.249), channel_id=1, source_target_pairs={{3,2},{7,6},{11,10},{15,14},{19,18},{23,22},{27,26},{31,30}} | collective-permute-start | bytes 1572872 | tf_op jit(solution)/shard_map/ppermute | solution.py:1164
  528.8 36.3 %collective-permute-start.50 = (bf16[256,1024]{1,0:T(8,128)(2,1)}, bf16[256,1024]{1,0:T(8,128)(2,1)S(1)}, u32[]{:S(2)}, u32[]{:S(2)}) collective-permute-start(bf16[256,1024]{1,0:T(8,128)(2,1)} %get-tuple-element.250), channel_id=1, source_target_pairs={{0,1},{4,5},{8,9},{12,13},{16,17},{20,21},{24,25},{28,29}} | collective-permute-start | bytes 1572872 | tf_op jit(solution)/shard_map/ppermute | solution.py:1163
  552.1 13.6 %collective-permute-start.51 = (bf16[256,1024]{1,0:T(8,128)(2,1)S(1)}, bf16[256,1024]{1,0:T(8,128)(2,1)S(1)}, u32[]{:S(2)}, u32[]{:S(2)}) collective-permute-start(bf16[256,1024]{1,0:T(8,128)(2,1)S(1)} %copy-done.75), channel_id=1, source_target_pairs={{3,2},{7,6},{11,10},{15,14},{19,18},{23,22},{27,26},{31,30}} | collective-permute-start | bytes 1572872 | tf_op jit(solution)/shard_map/ppermute | solution.py:1164
  557.2 19.0 %collective-permute-start.46 = (bf16[256,1024]{1,0:T(8,128)(2,1)S(1)}, bf16[256,1024]{1,0:T(8,128)(2,1)S(1)}, u32[]{:S(2)}, u32[]{:S(2)}) collective-permute-start(bf16[256,1024]{1,0:T(8,128)(2,1)S(1)} %get-tuple-element.148), channel_id=1, source_target_pairs={{0,1},{1,2},{4,5},{5,6},{8,9},{9,10},{12,13},{13,14},{16,17},{17,1... | collective-permute-start | bytes 1572872 | tf_op jit(solution)/shard_map/ppermute | solution.py:1163
  558.5 18.4 %collective-permute-start.47 = (bf16[256,1024]{1,0:T(8,128)(2,1)S(1)}, bf16[256,1024]{1,0:T(8,128)(2,1)S(1)}, u32[]{:S(2)}, u32[]{:S(2)}) collective-permute-start(bf16[256,1024]{1,0:T(8,128)(2,1)S(1)} %get-tuple-element.149), channel_id=1, source_target_pairs={{3,2},{2,1},{7,6},{6,5},{11,10},{10,9},{15,14},{14,13},{19,18},{18... | collective-permute-start | bytes 1572872 | tf_op jit(solution)/shard_map/ppermute | solution.py:1164
  560.1 27.3 %collective-permute-start.58 = (bf16[256,1024]{1,0:T(8,128)(2,1)S(1)}, bf16[256,1024]{1,0:T(8,128)(2,1)S(1)}, u32[]{:S(2)}, u32[]{:S(2)}) collective-permute-start(bf16[256,1024]{1,0:T(8,128)(2,1)S(1)} %get-tuple-element.160), channel_id=1, source_target_pairs={{0,1},{1,2},{4,5},{5,6},{8,9},{9,10},{12,13},{13,14},{16,17},{17,1... | collective-permute-start | bytes 1572872 | tf_op jit(solution)/shard_map/ppermute | solution.py:1163
  565.0 23.7 %collective-permute-start.59 = (bf16[256,1024]{1,0:T(8,128)(2,1)S(1)}, bf16[256,1024]{1,0:T(8,128)(2,1)S(1)}, u32[]{:S(2)}, u32[]{:S(2)}) collective-permute-start(bf16[256,1024]{1,0:T(8,128)(2,1)S(1)} %get-tuple-element.161), channel_id=1, source_target_pairs={{3,2},{2,1},{7,6},{6,5},{11,10},{10,9},{15,14},{14,13},{19,18},{18... | collective-permute-start | bytes 1572872 | tf_op jit(solution)/shard_map/ppermute | solution.py:1164
  566.7 32.0 %collective-permute-start.52 = (bf16[256,1024]{1,0:T(8,128)(2,1)S(1)}, bf16[256,1024]{1,0:T(8,128)(2,1)S(1)}, u32[]{:S(2)}, u32[]{:S(2)}) collective-permute-start(bf16[256,1024]{1,0:T(8,128)(2,1)S(1)} %get-tuple-element.156), channel_id=1, source_target_pairs={{0,1},{1,2},{4,5},{5,6},{8,9},{9,10},{12,13},{13,14},{16,17},{17,1... | collective-permute-start | bytes 1572872 | tf_op jit(solution)/shard_map/ppermute | solution.py:1163
  576.2 23.9 %collective-permute-start.53 = (bf16[256,1024]{1,0:T(8,128)(2,1)S(1)}, bf16[256,1024]{1,0:T(8,128)(2,1)S(1)}, u32[]{:S(2)}, u32[]{:S(2)}) collective-permute-start(bf16[256,1024]{1,0:T(8,128)(2,1)S(1)} %get-tuple-element.157), channel_id=1, source_target_pairs={{3,2},{2,1},{7,6},{6,5},{11,10},{10,9},{15,14},{14,13},{19,18},{18... | collective-permute-start | bytes 1572872 | tf_op jit(solution)/shard_map/ppermute | solution.py:1164
  577.8 32.1 %collective-permute-start.48 = (bf16[256,1024]{1,0:T(8,128)(2,1)S(1)}, bf16[256,1024]{1,0:T(8,128)(2,1)S(1)}, u32[]{:S(2)}, u32[]{:S(2)}) collective-permute-start(bf16[256,1024]{1,0:T(8,128)(2,1)S(1)} %get-tuple-element.150), channel_id=1, source_target_pairs={{0,1},{1,2},{2,3},{4,5},{5,6},{6,7},{8,9},{9,10},{10,11},{12,13},{... | collective-permute-start | bytes 1572872 | tf_op jit(solution)/shard_map/ppermute | solution.py:1163
  587.4 24.0 %collective-permute-start.49 = (bf16[256,1024]{1,0:T(8,128)(2,1)S(1)}, bf16[256,1024]{1,0:T(8,128)(2,1)S(1)}, u32[]{:S(2)}, u32[]{:S(2)}) collective-permute-start(bf16[256,1024]{1,0:T(8,128)(2,1)S(1)} %get-tuple-element.151), channel_id=1, source_target_pairs={{3,2},{2,1},{1,0},{7,6},{6,5},{5,4},{11,10},{10,9},{9,8},{15,14},{... | collective-permute-start | bytes 1572872 | tf_op jit(solution)/shard_map/ppermute | solution.py:1164
  590.3 33.7 %collective-permute-start.60 = (bf16[256,1024]{1,0:T(8,128)(2,1)}, bf16[256,1024]{1,0:T(8,128)(2,1)S(1)}, u32[]{:S(2)}, u32[]{:S(2)}) collective-permute-start(bf16[256,1024]{1,0:T(8,128)(2,1)} %get-tuple-element.162), channel_id=1, source_target_pairs={{0,1},{1,2},{2,3},{4,5},{5,6},{6,7},{8,9},{9,10},{10,11},{12,13},{... | collective-permute-start | bytes 1572872 | tf_op jit(solution)/shard_map/ppermute | solution.py:1163
  598.6 25.9 %collective-permute-start.61 = (bf16[256,1024]{1,0:T(8,128)(2,1)S(1)}, bf16[256,1024]{1,0:T(8,128)(2,1)}, u32[]{:S(2)}, u32[]{:S(2)}) collective-permute-start(bf16[256,1024]{1,0:T(8,128)(2,1)S(1)} %get-tuple-element.163), channel_id=1, source_target_pairs={{3,2},{2,1},{1,0},{7,6},{6,5},{5,4},{11,10},{10,9},{9,8},{15,14},{... | collective-permute-start | bytes 1572872 | tf_op jit(solution)/shard_map/ppermute | solution.py:1164
  601.0 40.5 %collective-permute-start.54 = (bf16[256,1024]{1,0:T(8,128)(2,1)S(1)}, bf16[256,1024]{1,0:T(8,128)(2,1)S(1)}, u32[]{:S(2)}, u32[]{:S(2)}) collective-permute-start(bf16[256,1024]{1,0:T(8,128)(2,1)S(1)} %get-tuple-element.158), channel_id=1, source_target_pairs={{0,1},{1,2},{2,3},{4,5},{5,6},{6,7},{8,9},{9,10},{10,11},{12,13},{... | collective-permute-start | bytes 1572872 | tf_op jit(solution)/shard_map/ppermute | solution.py:1163
  609.9 31.6 %collective-permute-start.55 = (bf16[256,1024]{1,0:T(8,128)(2,1)S(1)}, bf16[256,1024]{1,0:T(8,128)(2,1)}, u32[]{:S(2)}, u32[]{:S(2)}) collective-permute-start(bf16[256,1024]{1,0:T(8,128)(2,1)S(1)} %get-tuple-element.159), channel_id=1, source_target_pairs={{3,2},{2,1},{1,0},{7,6},{6,5},{5,4},{11,10},{10,9},{9,8},{15,14},{... | collective-permute-start | bytes 1572872 | tf_op jit(solution)/shard_map/ppermute | solution.py:1164
  618.7 18.7 %collective-permute-start.68 = (f32[3,1024]{1,0:T(4,128)S(1)}, f32[3,1024]{1,0:T(4,128)S(1)}, u32[]{:S(2)}, u32[]{:S(2)}) collective-permute-start(f32[3,1024]{1,0:T(4,128)S(1)} %get-tuple-element.234), channel_id=1, source_target_pairs={{0,16},{16,0},{1,17},{17,1},{2,18},{18,2},{3,19},{19,3},{4,20},{20... | collective-permute-start | bytes 36872 | tf_op jit(solution)/shard_map/ppermute | solution.py:992
  624.0 14.0 %collective-permute-start.62 = (bf16[256,512]{1,0:T(8,128)(2,1)S(1)}, bf16[256,512]{1,0:T(8,128)(2,1)S(1)}, u32[]{:S(2)}, u32[]{:S(2)}) collective-permute-start(bf16[256,512]{1,0:T(8,128)(2,1)S(1)} %bitcast.125), channel_id=1, source_target_pairs={{0,16},{16,0},{1,17},{17,1},{2,18},{18,2},{3,19},{19,3},{4,20},{20... | collective-permute-start | bytes 786440 | tf_op jit(solution)/shard_map/ppermute | solution.py:1210
  632.0 15.9 %collective-permute-start.64 = (bf16[256,512]{1,0:T(8,128)(2,1)S(1)}, bf16[256,512]{1,0:T(8,128)(2,1)S(1)}, u32[]{:S(2)}, u32[]{:S(2)}) collective-permute-start(bf16[256,512]{1,0:T(8,128)(2,1)S(1)} %bitcast.126), channel_id=1, source_target_pairs={{0,16},{16,0},{1,17},{17,1},{2,18},{18,2},{3,19},{19,3},{4,20},{20... | collective-permute-start | bytes 786440 | tf_op jit(solution)/shard_map/ppermute | solution.py:1210
  640.8 18.4 %collective-permute-start.67 = (bf16[256,512]{1,0:T(8,128)(2,1)S(1)}, bf16[256,512]{1,0:T(8,128)(2,1)S(1)}, u32[]{:S(2)}, u32[]{:S(2)}) collective-permute-start(bf16[256,512]{1,0:T(8,128)(2,1)S(1)} %get-tuple-element.170.refs_7_.refs_0_), channel_id=1, source_target_pairs={{0,16},{16,0},{1,17},{17,1},{2,18},{18,2},{3,19},{19,3},{4,20},{20... | collective-permute-start | bytes 786440 | tf_op jit(solution)/shard_map/ppermute | solution.py:1210
  646.4 9.3 %collective-permute-start.63 = (bf16[256,512]{1,0:T(8,128)(2,1)S(1)}, bf16[256,512]{1,0:T(8,128)(2,1)S(1)}, u32[]{:S(2)}, u32[]{:S(2)}) collective-permute-start(bf16[256,512]{1,0:T(8,128)(2,1)S(1)} %bitcast.127), channel_id=1, source_target_pairs={{0,16},{16,0},{1,17},{17,1},{2,18},{18,2},{3,19},{19,3},{4,20},{20... | collective-permute-start | bytes 786440 | tf_op jit(solution)/shard_map/ppermute | solution.py:1210
  650.8 9.7 %collective-permute-start.66 = (bf16[256,512]{1,0:T(8,128)(2,1)S(1)}, bf16[256,512]{1,0:T(8,128)(2,1)S(1)}, u32[]{:S(2)}, u32[]{:S(2)}) collective-permute-start(bf16[256,512]{1,0:T(8,128)(2,1)S(1)} %get-tuple-element.183.refs_0_), channel_id=1, source_target_pairs={{0,16},{16,0},{1,17},{17,1},{2,18},{18,2},{3,19},{19,3},{4,20},{20... | collective-permute-start | bytes 786440 | tf_op jit(solution)/shard_map/ppermute | solution.py:1210
  (95 other events, 1810.6 us)
Sparse Core Ops, SparseCore 0:
  10.7 143.6 all-gather.4
  322.9 132.9 all-gather.6
  526.6 41.0 all-gather.8

commit v5 on v4

--- a/solution.py
+++ b/solution.py
@@ -1278,10 +1278,12 @@
             results.append(jnp.concatenate([grad_one, grad_two], axis=0))
             return d_rows
 
-        def scatter_step(d_rows, marks):
+        def scatter_out(marks):
             activations[:] = run_scatter(
                 across, tokens, out_rows, inner_step, activations[:1], marks
             )
+
+        def scatter_grad(d_rows, marks):
             input_grad[:] = run_scatter(
                 across, cotangent, d_rows, inner_step, input_grad[:1], marks
             )
@@ -1331,14 +1333,14 @@
                         last,
                         groups,
                         made[-1][:2] if index else (),
-                        [outers[0][3], input_grad[1]]
-                        if index == PIECES - 1
-                        else activations[1:],
+                        [outers[0][3]] if index == PIECES - 1 else activations[1:],
                     )
                 )
                 own, other = made[-1][2:]
                 if index == 0:
-                    scatter_step(d_rows, [own])
+                    scatter_out([own])
+                if index == PIECES - 1:
+                    scatter_grad(d_rows, [own])
                 outers.append(
                     run_outer(
                         place,
@@ -1347,7 +1349,7 @@
                         (weights, outer_moment, smoothed_matrix_mean),
                         index,
                         outers[-1][:3] if index else (),
-                        [],
+                        input_grad[1:] if index == PIECES - 1 else [],
                     )
                 )
             first_now, second_now = made[-1][:2]
@@ -1375,7 +1377,8 @@
             )
             vec_diff = sum_over(vectors - vec_now, ("grp",)) / groups
         else:
-            scatter_step(input_step([grad_mark]), [grad_mark])
+            scatter_out([grad_mark])
+            scatter_grad(input_step([grad_mark]), [grad_mark])
             grad_vec = sum_over(due_after(results[0], grad_mark), ("fsdp", "dp"))
             vec_now, vfirst_now, vsecond_now = adamw(
                 vec_now, grad_vec, vfirst_now, vsecond_now, step_count, vector_rates(), 0.0

time: 681 us -> 679 us (level)
    unnamed x176 -> x180, local copies, waits for them, and re-layouts: 28.3 us -> 29.7 us
  transfers between devices with their start and end apart: 72 -> 72, of which waited for: 29 -> 28; matrix products, arithmetic and copies ran while one was open for 2% -> 2% of each run, Pallas kernels for 16% -> 16%
where the time goes in v5:
time: 679 us; the launch traced here: 670 us
  waiting for transfers between devices  341 us (50%)
  Pallas kernels  142 us (21%)
  starting transfers between devices  118 us (17%)
  local copies, waits for them, and re-layouts  34.8 us (5%)
  between operations  18.7 us (3%)
  other arithmetic  16.1 us (2%)
    all_gather x2, waiting for transfers between devices, on_device(): gathered = lax.all_gather(shard_low, ('dp', 'fsdp'), axis=0, tiled=True)  203 us
    ppermute x18, starting transfers between devices, gradient_share(): below[index] = lax.ppermute(up, 'dp', [(p, p + 1) for p in range(step + 1)])  61.5 us
    ppermute x18, waiting for transfers between devices, gradient_share(): below[index] = lax.ppermute(up, 'dp', [(p, p + 1) for p in range(step + 1)])  58.5 us
    ppermute x12, waiting for transfers between devices, send_to(): lax.ppermute(values, 'fsdp', [(target ^ delta, target)])  36.7 us
    ppermute x15, waiting for transfers between devices, swap(): return lax.ppermute(values, axis, [(i, i ^ delta) for i in range(size)])  35.4 us
    unnamed x180, local copies, waits for them, and re-layouts  29.7 us
    pallas_call x2, Pallas kernels, run_feed_forward(): pl.pallas_call(functools.partial(feed_forward_kernel, keep=keep, order=or...  24.3 us
    pallas_call x4, Pallas kernels, run_products(): pl.pallas_call(functools.partial(attention_products_kernel, sources=sourc...  21.5 us
  transfers between devices with their start and end apart: 72, of which 28 were waited for; matrix products, arithmetic and copies ran while one was open for 2% of the time, Pallas kernels for 16%

profile of v5, /device:TPU:0, one launch (start us, length us, event | category | flops | bytes accessed | tf_op | source)
XLA Modules:
  0.0 670.3 jit_solution(17918363639441768567)
XLA Ops:
  7.3 3.3 convert_element_type.171
  17.3 4.5 gather_rows.1
  22.0 3.0 collective-permute-start
  25.0 26.5 %collective-permute-done = bf16[1,2,144,1024]{3,2,0,1:T(8,128)(2,1)S(1)} collective-permute-done((bf16[1,2,144,1024]{3,2,0,1:T(8,128)(2,1)S(1)}, bf16[1,2,144,1024]{3,2,0,1:T(8,128)(2,1)S(1)}, u32[]{:S(2)}, u32[]{:S(2)}) %collective-permute-start) | collective-permute-done | bytes 589856 | tf_op jit(solution)/shard_map/ppermute | solution.py:992
  51.7 2.8 collective-permute-done.1
  55.8 98.5 %all-gather.5.cloned.1.call-done.weights = bf16[12288,1024]{1,0:T(8,128)(2,1)} async-done(((bf16[768,1024]{1,0:T(8,128)(2,1)}), bf16[12288,1024]{1,0:T(8,128)(2,1)}) %all-gather.5.cloned.1.call-update) | async-done | bytes 25165840 | tf_op jit(solution)/shard_map/all_gather | solution.py:1252
  155.3 7.0 %attention.2 = (bf16[144,3072]{1,0:T(8,128)(2,1)S(1)}, f32[288,128]{1,0:T(8,128)S(1)}, bf16[2,144,1024]{2,1,0:T(8,128)(2,1)S(1)}, f32[144,1024]{1,0:T(8,128)S(1)}) custom-call(bf16[12288,1024]{1,0:T(8,128)(2,1)} %all-gather.5.cloned.1.call-done.weights, s32[288,144]{1,0:T(8,128)S(1)} %copy-done.34, bf16[2,144,1024]{2,1,0:T(8,128)(2,1)S(1)} %get-tuple-element.106.both_ref, ...), custom_call_target="tpu_custom_call" | custom-call | flops 1207959552 | bytes 8388608 | tf_op jit(solution)/shard_map/attention/pallas_call | solution.py:687
  163.0 12.2 %feed_forward.2 = (bf16[144,1024]{1,0:T(8,128)(2,1)S(1)}, bf16[144,1024]{1,0:T(8,128)(2,1)S(1)}, f32[144,1024]{1,0:T(8,128)S(1)}, f32[2,1024]{1,0:T(2,128)S(1)}) custom-call(bf16[12288,1024]{1,0:T(8,128)(2,1)} %all-gather.5.cloned.1.call-done.weights, bf16[2,144,1024]{2,1,0:T(8,128)(2,1)S(1)} %get-tuple-element.106.both_ref, f32[3,1024]{1,0:T(4,128)S(1)} %copy-done.42, ...), custom_call_target="tpu_custom_call" | custom-call | flops 9663676416 | bytes 25165824 | tf_op jit(solution)/shard_map/feed_forward/pallas_call | solution.py:716
  177.9 6.2 attention_back.2
  184.9 3.0 collective-permute-start.7
  194.1 19.7 %collective-permute-done.3.refs_1_ = bf16[144,3072]{1,0:T(8,128)(2,1)S(1)} collective-permute-done((bf16[144,3072]{1,0:T(8,128)(2,1)S(1)}, bf16[144,3072]{1,0:T(8,128)(2,1)S(1)}, u32[]{:S(2)}, u32[]{:S(2)}) %collective-permute-start.3) | collective-permute-done | bytes 884768 | tf_op jit(solution)/shard_map/ppermute | solution.py:1073
  214.5 3.3 attention_products.4.refs_10_
  223.3 7.5 %attention_products.5.terms_ref = bf16[12,256,1024]{2,1,0:T(8,128)(2,1)S(1)} custom-call(s32[12,3]{1,0:T(8,128)S(1)} %copy-done.49, s32[4]{0:T(128)S(1)} %copy-done.55, bf16[4,144,1024]{2,1,0:T(8,128)(2,1)S(1)} %get-tuple-element.248.refs_0_.h1_ref, bf16[144,3072]{1,0:T(8,128)(2,1)S(1)} %get-tuple-element.113.refs_0_.cuts_ref, ...), custom_call_target="tpu_custom_call", output_to_operand_aliasing={{}: (14, {})} | custom-call | flops 1000000 | bytes 100000 | tf_op jit(solution)/shard_map/attention_products/pallas_call | solution.py:956
  233.2 4.4 collective-permute-start.26
  237.6 5.2 collective-permute-done.10.below_ref
  244.5 9.5 %collective-permute-done.18.below_ref = bf16[256,1024]{1,0:T(8,128)(2,1)S(1)} collective-permute-done((bf16[256,1024]{1,0:T(8,128)(2,1)S(1)}, bf16[256,1024]{1,0:T(8,128)(2,1)S(1)}, u32[]{:S(2)}, u32[]{:S(2)}) %collective-permute-start.18) | collective-permute-done | bytes 524320 | tf_op jit(solution)/shard_map/ppermute | solution.py:1163
  254.9 4.4 collective-permute-start.20
  260.1 5.9 collective-permute-start.12
  267.8 8.7 %collective-permute-done.20.below_ref = bf16[256,1024]{1,0:T(8,128)(2,1)S(1)} collective-permute-done((bf16[256,1024]{1,0:T(8,128)(2,1)S(1)}, bf16[256,1024]{1,0:T(8,128)(2,1)S(1)}, u32[]{:S(2)}, u32[]{:S(2)}) %collective-permute-start.20) | collective-permute-done | bytes 524320 | tf_op jit(solution)/shard_map/ppermute | solution.py:1163
  276.5 4.4 collective-permute-start.28
  290.0 5.2 collective-permute-start.16
  295.1 3.8 collective-permute-done.28.refs_0_
  300.7 8.0 %collective-permute-done.22 = bf16[256,1024]{1,0:T(8,128)(2,1)S(1)} collective-permute-done((bf16[256,1024]{1,0:T(8,128)(2,1)S(1)}, bf16[256,1024]{1,0:T(8,128)(2,1)S(1)}, u32[]{:S(2)}, u32[]{:S(2)}) %collective-permute-start.22) | collective-permute-done | bytes 524320 | tf_op jit(solution)/shard_map/ppermute | solution.py:1163
  308.8 2.3 collective-permute-done.29
  311.0 3.3 collective-permute-done.16
  314.4 2.3 collective-permute-done.17
  317.7 5.0 fusion.34
  324.8 4.0 input_back.2
  334.8 2.5 collective-permute-start.33
  337.3 2.9 collective-permute-start.34
  341.6 3.8 scatter_rows.5
  345.4 4.0 scatter_rows.4
  351.2 104.7 %all-gather.7.cloned.1.call-done.weights = bf16[12288,1024]{1,0:T(8,128)(2,1)} async-done(((bf16[768,1024]{1,0:T(8,128)(2,1)}), bf16[12288,1024]{1,0:T(8,128)(2,1)}) %all-gather.7.cloned.1.call-update) | async-done | bytes 25165840 | tf_op jit(solution)/shard_map/all_gather | solution.py:1252
  455.9 7.2 %attention.3 = (bf16[144,3072]{1,0:T(8,128)(2,1)S(1)}, f32[288,128]{1,0:T(8,128)S(1)}, bf16[2,144,1024]{2,1,0:T(8,128)(2,1)S(1)}, f32[144,1024]{1,0:T(8,128)S(1)}) custom-call(bf16[12288,1024]{1,0:T(8,128)(2,1)} %all-gather.7.cloned.1.call-done.weights, s32[288,144]{1,0:T(8,128)S(1)} %copy-done.32, ...), custom_call_target="tpu_custom_call" | custom-call | flops 1207959552 | bytes 8388608 | tf_op jit(solution)/shard_map/attention/pallas_call | solution.py:687
  465.4 12.1 %feed_forward.3 = (bf16[144,1024]{1,0:T(8,128)(2,1)S(1)}, bf16[144,1024]{1,0:T(8,128)(2,1)S(1)}, f32[144,1024]{1,0:T(8,128)S(1)}, f32[2,1024]{1,0:T(2,128)S(1)}) custom-call(bf16[12288,1024]{1,0:T(8,128)(2,1)} %all-gather.7.cloned.1.call-done.weights, bf16[2,144,1024]{2,1,0:T(8,128)(2,1)S(1)} %copy-done.22, f32[3,1024]{1,0:T(4,128)S(1)} %get-tuple-element.236.vec_ref, ...), custom_call_target="tpu_custom_call" | custom-call | flops 9663676416 | bytes 25165824 | tf_op jit(solution)/shard_map/feed_forward/pallas_call | solution.py:716
  478.7 6.2 attention_back.3
  485.7 3.0 collective-permute-start.41
  490.7 4.0 input_back.3
  499.0 11.5 %collective-permute-done.37.refs_1_ = bf16[144,3072]{1,0:T(8,128)(2,1)S(1)} collective-permute-done((bf16[144,3072]{1,0:T(8,128)(2,1)S(1)}, bf16[144,3072]{1,0:T(8,128)(2,1)S(1)}, u32[]{:S(2)}, u32[]{:S(2)}) %collective-permute-start.37) | collective-permute-done | bytes 884768 | tf_op jit(solution)/shard_map/ppermute | solution.py:1073
  510.4 4.8 collective-permute-done.39.refs_3_
  515.3 3.3 attention_products.6.refs_10_
  519.8 4.5 collective-permute-start.44
  530.1 2.8 copy-done.1
  542.0 7.4 %attention_products.7.terms_ref.refs_0_ = bf16[12,256,1024]{2,1,0:T(8,128)(2,1)S(1)} custom-call(s32[12,3]{1,0:T(8,128)S(1)} %copy-done.50, s32[4]{0:T(128)S(1)} %copy-done.56, bf16[4,144,1024]{2,1,0:T(8,128)(2,1)S(1)} %get-tuple-element.246.refs_0_.h1_ref, bf16[144,3072]{1,0:T(8,128)(2,1)S(1)} %copy-done.8, ...), custom_call_target="tpu_custom_call", output_to_operand_aliasing={{}: (14, {})} | custom-call | flops 1000000 | bytes 100000 | tf_op jit(solution)/shard_map/attention_products/pallas_call | solution.py:956
  549.4 2.7 copy-done.2
  552.8 2.8 copy-done.3
  560.1 2.8 collective-permute-start.58
  566.7 4.9 collective-permute-start.52
  571.6 4.6 collective-permute-done.46.below_ref
  577.8 5.0 collective-permute-start.48
  582.8 4.6 collective-permute-done.58.below_ref
  590.3 5.0 collective-permute-start.60
  595.4 3.3 collective-permute-done.52.below_ref
  601.0 5.0 collective-permute-start.54
  606.0 3.8 collective-permute-done.48.below_ref
  611.5 3.9 update.3
  620.2 3.8 scatter_rows.6
  625.2 5.0 update.4
  634.2 2.8 outer.3
  637.6 4.9 update.5
  644.9 2.8 outer.4
  648.3 3.9 scatter_rows.7
  652.8 2.8 outer.5
  659.7 2.4 collective-permute-done.65.refs_1_
  (348 shorter events, 116.0 us)
Async XLA Ops:
  7.2 147.2 %all-gather.5.cloned.1.call-start = ((), (), s32[]{:S(2)}) async-start(), calls=%async_computation | async-start | bytes 26738688 | tf_op jit(solution)/shard_map/all_gather | solution.py:1252
  10.6 445.3 %all-gather.7.cloned.1.call-start = ((), (), s32[]{:S(2)}) async-start(), calls=%async_computation.1 | async-start | bytes 26738688 | tf_op jit(solution)/shard_map/all_gather | solution.py:1252
  22.0 29.5 %collective-permute-start = (bf16[1,2,144,1024]{3,2,0,1:T(8,128)(2,1)S(1)}, bf16[1,2,144,1024]{3,2,0,1:T(8,128)(2,1)S(1)}, u32[]{:S(2)}, u32[]{:S(2)}) collective-permute-start(bf16[1,2,144,1024]{3,2,0,1:T(8,128)(2,1)S(1)} %bitcast.116), channel_id=1, source_target_pairs={{0,8},{4,12},{8,0},{12,4},{1,9},{5,13},{9,1},{13,5},{2,10},{6,14},... | collective-permute-start | bytes 1769480 | tf_op jit(solution)/shard_map/ppermute | solution.py:992
  162.3 15.6 %collective-permute-start.2 = (bf16[1,2,144,1024]{3,2,1,0:T(8,128)(2,1)S(1)}, bf16[1,2,144,1024]{3,2,1,0:T(8,128)(2,1)S(1)}, u32[]{:S(2)}, u32[]{:S(2)}) collective-permute-start(bf16[1,2,144,1024]{3,2,1,0:T(8,128)(2,1)S(1)} %bitcast.123), channel_id=1, source_target_pairs={{0,8},{4,12},{8,0},{12,4},{1,9},{5,13},{9,1},{13,5},{2,10},{6,14},... | collective-permute-start | bytes 1769480 | tf_op jit(solution)/shard_map/ppermute | solution.py:992
  184.1 8.4 %collective-permute-start.9 = (bf16[2,2,144,1024]{3,2,1,0:T(8,128)(2,1)S(1)}, bf16[2,2,144,1024]{3,2,1,0:T(8,128)(2,1)S(1)}, u32[]{:S(2)}, u32[]{:S(2)}) collective-permute-start(bf16[2,2,144,1024]{3,2,1,0:T(8,128)(2,1)S(1)} %get-tuple-element.114.refs_0_.refs_8_), channel_id=1, source_target_pairs={{0,4},{4,0},{8,12},{12,8},{1,5},{5,1},{9,13},{13,9},{2,6},{6,2},{1... | collective-permute-start | bytes 3538952 | tf_op jit(solution)/shard_map/ppermute | solution.py:992
  188.6 25.2 %collective-permute-start.3 = (bf16[144,3072]{1,0:T(8,128)(2,1)S(1)}, bf16[144,3072]{1,0:T(8,128)(2,1)S(1)}, u32[]{:S(2)}, u32[]{:S(2)}) collective-permute-start(bf16[144,3072]{1,0:T(8,128)(2,1)S(1)} %get-tuple-element.113.refs_0_.cuts_ref), channel_id=1, source_target_pairs={{8,0},{9,1},{10,2},{11,3},{24,16},{25,17},{26,18},{27,19}} | collective-permute-start | bytes 2654216 | tf_op jit(solution)/shard_map/ppermute | solution.py:1073
  189.9 23.9 %collective-permute-start.4 = (bf16[144,3072]{1,0:T(8,128)(2,1)S(1)}, bf16[144,3072]{1,0:T(8,128)(2,1)S(1)}, u32[]{:S(2)}, u32[]{:S(2)}) collective-permute-start(bf16[144,3072]{1,0:T(8,128)(2,1)S(1)} %get-tuple-element.113.refs_0_.cuts_ref), channel_id=1, source_target_pairs={{4,0},{5,1},{6,2},{7,3},{20,16},{21,17},{22,18},{23,19}} | collective-permute-start | bytes 2654216 | tf_op jit(solution)/shard_map/ppermute | solution.py:1073
  191.2 23.2 %collective-permute-start.5 = (bf16[144,3072]{1,0:T(8,128)(2,1)S(1)}, bf16[144,3072]{1,0:T(8,128)(2,1)S(1)}, u32[]{:S(2)}, u32[]{:S(2)}) collective-permute-start(bf16[144,3072]{1,0:T(8,128)(2,1)S(1)} %get-tuple-element.113.refs_0_.cuts_ref), channel_id=1, source_target_pairs={{12,0},{13,1},{14,2},{15,3},{28,16},{29,17},{30,18},{31,19}} | collective-permute-start | bytes 2654216 | tf_op jit(solution)/shard_map/ppermute | solution.py:1073
  217.9 13.7 %collective-permute-start.24 = (bf16[256,1024]{1,0:T(8,128)(2,1)S(1)}, bf16[256,1024]{1,0:T(8,128)(2,1)S(1)}, u32[]{:S(2)}, u32[]{:S(2)}) collective-permute-start(bf16[256,1024]{1,0:T(8,128)(2,1)S(1)} %get-tuple-element.253), channel_id=1, source_target_pairs={{0,1},{4,5},{8,9},{12,13},{16,17},{20,21},{24,25},{28,29}} | collective-permute-start | bytes 1572872 | tf_op jit(solution)/shard_map/ppermute | solution.py:1163
  219.2 13.0 %collective-permute-start.25 = (bf16[256,1024]{1,0:T(8,128)(2,1)S(1)}, bf16[256,1024]{1,0:T(8,128)(2,1)S(1)}, u32[]{:S(2)}, u32[]{:S(2)}) collective-permute-start(bf16[256,1024]{1,0:T(8,128)(2,1)S(1)} %get-tuple-element.253), channel_id=1, source_target_pairs={{3,2},{7,6},{11,10},{15,14},{19,18},{23,22},{27,26},{31,30}} | collective-permute-start | bytes 1572872 | tf_op jit(solution)/shard_map/ppermute | solution.py:1164
  219.9 22.9 %collective-permute-start.10 = (bf16[256,1024]{1,0:T(8,128)(2,1)S(1)}, bf16[256,1024]{1,0:T(8,128)(2,1)S(1)}, u32[]{:S(2)}, u32[]{:S(2)}) collective-permute-start(bf16[256,1024]{1,0:T(8,128)(2,1)S(1)} %get-tuple-element.252), channel_id=1, source_target_pairs={{0,1},{4,5},{8,9},{12,13},{16,17},{20,21},{24,25},{28,29}} | collective-permute-start | bytes 1572872 | tf_op jit(solution)/shard_map/ppermute | solution.py:1163
  221.3 22.2 %collective-permute-start.11 = (bf16[256,1024]{1,0:T(8,128)(2,1)S(1)}, bf16[256,1024]{1,0:T(8,128)(2,1)S(1)}, u32[]{:S(2)}, u32[]{:S(2)}) collective-permute-start(bf16[256,1024]{1,0:T(8,128)(2,1)S(1)} %get-tuple-element.252), channel_id=1, source_target_pairs={{3,2},{7,6},{11,10},{15,14},{19,18},{23,22},{27,26},{31,30}} | collective-permute-start | bytes 1572872 | tf_op jit(solution)/shard_map/ppermute | solution.py:1164
  222.0 32.1 %collective-permute-start.18 = (bf16[256,1024]{1,0:T(8,128)(2,1)S(1)}, bf16[256,1024]{1,0:T(8,128)(2,1)S(1)}, u32[]{:S(2)}, u32[]{:S(2)}) collective-permute-start(bf16[256,1024]{1,0:T(8,128)(2,1)S(1)} %get-tuple-element.254), channel_id=1, source_target_pairs={{0,1},{4,5},{8,9},{12,13},{16,17},{20,21},{24,25},{28,29}} | collective-permute-start | bytes 1572872 | tf_op jit(solution)/shard_map/ppermute | solution.py:1163
  231.6 22.5 %collective-permute-start.19 = (bf16[256,1024]{1,0:T(8,128)(2,1)S(1)}, bf16[256,1024]{1,0:T(8,128)(2,1)S(1)}, u32[]{:S(2)}, u32[]{:S(2)}) collective-permute-start(bf16[256,1024]{1,0:T(8,128)(2,1)S(1)} %get-tuple-element.254), channel_id=1, source_target_pairs={{3,2},{7,6},{11,10},{15,14},{19,18},{23,22},{27,26},{31,30}} | collective-permute-start | bytes 1572872 | tf_op jit(solution)/shard_map/ppermute | solution.py:1164
  233.2 32.9 %collective-permute-start.26 = (bf16[256,1024]{1,0:T(8,128)(2,1)S(1)}, bf16[256,1024]{1,0:T(8,128)(2,1)S(1)}, u32[]{:S(2)}, u32[]{:S(2)}) collective-permute-start(bf16[256,1024]{1,0:T(8,128)(2,1)S(1)} %get-tuple-element.125), channel_id=1, source_target_pairs={{0,1},{1,2},{4,5},{5,6},{8,9},{9,10},{12,13},{13,14},{16,17},{17,1... | collective-permute-start | bytes 1572872 | tf_op jit(solution)/shard_map/ppermute | solution.py:1163
  242.8 24.0 %collective-permute-start.27 = (bf16[256,1024]{1,0:T(8,128)(2,1)S(1)}, bf16[256,1024]{1,0:T(8,128)(2,1)S(1)}, u32[]{:S(2)}, u32[]{:S(2)}) collective-permute-start(bf16[256,1024]{1,0:T(8,128)(2,1)S(1)} %get-tuple-element.126), channel_id=1, source_target_pairs={{3,2},{2,1},{7,6},{6,5},{11,10},{10,9},{15,14},{14,13},{19,18},{18... | collective-permute-start | bytes 1572872 | tf_op jit(solution)/shard_map/ppermute | solution.py:1164
  244.4 15.6 %collective-permute-start.14 = (bf16[1,2,144,1024]{3,2,0,1:T(8,128)(2,1)S(1)}, bf16[1,2,144,1024]{3,2,0,1:T(8,128)(2,1)S(1)}, u32[]{:S(2)}, u32[]{:S(2)}) collective-permute-start(bf16[1,2,144,1024]{3,2,0,1:T(8,128)(2,1)S(1)} %bitcast.119), channel_id=1, source_target_pairs={{0,8},{4,12},{8,0},{12,4},{1,9},{5,13},{9,1},{13,5},{2,10},{6,14},... | collective-permute-start | bytes 1769480 | tf_op jit(solution)/shard_map/ppermute | solution.py:992
  254.9 21.6 %collective-permute-start.20 = (bf16[256,1024]{1,0:T(8,128)(2,1)S(1)}, bf16[256,1024]{1,0:T(8,128)(2,1)S(1)}, u32[]{:S(2)}, u32[]{:S(2)}) collective-permute-start(bf16[256,1024]{1,0:T(8,128)(2,1)S(1)} %get-tuple-element.121), channel_id=1, source_target_pairs={{0,1},{1,2},{4,5},{5,6},{8,9},{9,10},{12,13},{13,14},{16,17},{17,1... | collective-permute-start | bytes 1572872 | tf_op jit(solution)/shard_map/ppermute | solution.py:1163
  259.4 21.5 %collective-permute-start.21 = (bf16[256,1024]{1,0:T(8,128)(2,1)S(1)}, bf16[256,1024]{1,0:T(8,128)(2,1)S(1)}, u32[]{:S(2)}, u32[]{:S(2)}) collective-permute-start(bf16[256,1024]{1,0:T(8,128)(2,1)S(1)} %get-tuple-element.122), channel_id=1, source_target_pairs={{3,2},{2,1},{7,6},{6,5},{11,10},{10,9},{15,14},{14,13},{19,18},{18... | collective-permute-start | bytes 1572872 | tf_op jit(solution)/shard_map/ppermute | solution.py:1164
  260.1 27.6 %collective-permute-start.12 = (bf16[256,1024]{1,0:T(8,128)(2,1)S(1)}, bf16[256,1024]{1,0:T(8,128)(2,1)S(1)}, u32[]{:S(2)}, u32[]{:S(2)}) collective-permute-start(bf16[256,1024]{1,0:T(8,128)(2,1)S(1)} %get-tuple-element.116), channel_id=1, source_target_pairs={{0,1},{1,2},{4,5},{5,6},{8,9},{9,10},{12,13},{13,14},{16,17},{17,1... | collective-permute-start | bytes 1572872 | tf_op jit(solution)/shard_map/ppermute | solution.py:1163
  266.1 22.9 %collective-permute-start.13 = (bf16[256,1024]{1,0:T(8,128)(2,1)S(1)}, bf16[256,1024]{1,0:T(8,128)(2,1)S(1)}, u32[]{:S(2)}, u32[]{:S(2)}) collective-permute-start(bf16[256,1024]{1,0:T(8,128)(2,1)S(1)} %get-tuple-element.117), channel_id=1, source_target_pairs={{3,2},{2,1},{7,6},{6,5},{11,10},{10,9},{15,14},{14,13},{19,18},{18... | collective-permute-start | bytes 1572872 | tf_op jit(solution)/shard_map/ppermute | solution.py:1164
  266.8 17.0 %collective-permute-start.15 = (bf16[2,2,144,1024]{3,2,0,1:T(8,128)(2,1)S(1)}, bf16[2,2,144,1024]{3,2,0,1:T(8,128)(2,1)S(1)}, u32[]{:S(2)}, u32[]{:S(2)}) collective-permute-start(bf16[2,2,144,1024]{3,2,0,1:T(8,128)(2,1)S(1)} %pad_maximum_fusion.4), channel_id=1, source_target_pairs={{0,4},{4,0},{8,12},{12,8},{1,5},{5,1},{9,13},{13,9},{2,6},{6,2},{1... | collective-permute-start | bytes 3538952 | tf_op jit(solution)/shard_map/ppermute | solution.py:992
  276.5 22.5 %collective-permute-start.28 = (bf16[256,1024]{1,0:T(8,128)(2,1)S(1)}, bf16[256,1024]{1,0:T(8,128)(2,1)S(1)}, u32[]{:S(2)}, u32[]{:S(2)}) collective-permute-start(bf16[256,1024]{1,0:T(8,128)(2,1)S(1)} %get-tuple-element.127), channel_id=1, source_target_pairs={{0,1},{1,2},{2,3},{4,5},{5,6},{6,7},{8,9},{9,10},{10,11},{12,13},{... | collective-permute-start | bytes 1572872 | tf_op jit(solution)/shard_map/ppermute | solution.py:1163
  281.9 26.9 %collective-permute-start.22 = (bf16[256,1024]{1,0:T(8,128)(2,1)S(1)}, bf16[256,1024]{1,0:T(8,128)(2,1)S(1)}, u32[]{:S(2)}, u32[]{:S(2)}) collective-permute-start(bf16[256,1024]{1,0:T(8,128)(2,1)S(1)} %get-tuple-element.123), channel_id=1, source_target_pairs={{0,1},{1,2},{2,3},{4,5},{5,6},{6,7},{8,9},{9,10},{10,11},{12,13},{... | collective-permute-start | bytes 1572872 | tf_op jit(solution)/shard_map/ppermute | solution.py:1163
  283.8 24.9 %collective-permute-start.23 = (bf16[256,1024]{1,0:T(8,128)(2,1)S(1)}, bf16[256,1024]{1,0:T(8,128)(2,1)S(1)}, u32[]{:S(2)}, u32[]{:S(2)}) collective-permute-start(bf16[256,1024]{1,0:T(8,128)(2,1)S(1)} %get-tuple-element.124), channel_id=1, source_target_pairs={{3,2},{2,1},{1,0},{7,6},{6,5},{5,4},{11,10},{10,9},{9,8},{15,14},{... | collective-permute-start | bytes 1572872 | tf_op jit(solution)/shard_map/ppermute | solution.py:1164
  287.7 23.3 %collective-permute-start.29 = (bf16[256,1024]{1,0:T(8,128)(2,1)S(1)}, bf16[256,1024]{1,0:T(8,128)(2,1)S(1)}, u32[]{:S(2)}, u32[]{:S(2)}) collective-permute-start(bf16[256,1024]{1,0:T(8,128)(2,1)S(1)} %get-tuple-element.128), channel_id=1, source_target_pairs={{3,2},{2,1},{1,0},{7,6},{6,5},{5,4},{11,10},{10,9},{9,8},{15,14},{... | collective-permute-start | bytes 1572872 | tf_op jit(solution)/shard_map/ppermute | solution.py:1164
  290.0 24.4 %collective-permute-start.16 = (bf16[256,1024]{1,0:T(8,128)(2,1)S(1)}, bf16[256,1024]{1,0:T(8,128)(2,1)S(1)}, u32[]{:S(2)}, u32[]{:S(2)}) collective-permute-start(bf16[256,1024]{1,0:T(8,128)(2,1)S(1)} %get-tuple-element.119), channel_id=1, source_target_pairs={{0,1},{1,2},{2,3},{4,5},{5,6},{6,7},{8,9},{9,10},{10,11},{12,13},{... | collective-permute-start | bytes 1572872 | tf_op jit(solution)/shard_map/ppermute | solution.py:1163
  299.0 17.7 %collective-permute-start.17 = (bf16[256,1024]{1,0:T(8,128)(2,1)S(1)}, bf16[256,1024]{1,0:T(8,128)(2,1)S(1)}, u32[]{:S(2)}, u32[]{:S(2)}) collective-permute-start(bf16[256,1024]{1,0:T(8,128)(2,1)S(1)} %get-tuple-element.120), channel_id=1, source_target_pairs={{3,2},{2,1},{1,0},{7,6},{6,5},{5,4},{11,10},{10,9},{9,8},{15,14},{... | collective-permute-start | bytes 1572872 | tf_op jit(solution)/shard_map/ppermute | solution.py:1164
  322.8 294.6 %all-gather.9.cloned.1.call-start = ((), (), s32[]{:S(2)}) async-start(), calls=%async_computation.2 | async-start | bytes 1114112 | tf_op jit(solution)/shard_map/all_gather | solution.py:1006
  334.8 14.7 %collective-permute-start.33 = (f32[3,1024]{1,0:T(4,128)S(1)}, f32[3,1024]{1,0:T(4,128)S(1)}, u32[]{:S(2)}, u32[]{:S(2)}) collective-permute-start(f32[3,1024]{1,0:T(4,128)S(1)} %add_add_fusion.1), channel_id=1, source_target_pairs={{0,1},{1,0},{2,3},{3,2},{4,5},{5,4},{6,7},{7,6},{8,9},{9,8},{10,11... | collective-permute-start | bytes 36872 | tf_op jit(solution)/shard_map/ppermute | solution.py:992
  337.3 12.2 %collective-permute-start.34 = (f32[3,1024]{1,0:T(4,128)S(1)}, f32[3,1024]{1,0:T(4,128)S(1)}, u32[]{:S(2)}, u32[]{:S(2)}) collective-permute-start(f32[3,1024]{1,0:T(4,128)S(1)} %add_add_fusion.1), channel_id=1, source_target_pairs={{0,2},{1,3},{2,0},{3,1},{4,6},{5,7},{6,4},{7,5},{8,10},{9,11},{10,... | collective-permute-start | bytes 36872 | tf_op jit(solution)/shard_map/ppermute | solution.py:992
  340.2 9.3 %collective-permute-start.35 = (f32[3,1024]{1,0:T(4,128)S(1)}, f32[3,1024]{1,0:T(4,128)S(1)}, u32[]{:S(2)}, u32[]{:S(2)}) collective-permute-start(f32[3,1024]{1,0:T(4,128)S(1)} %add_add_fusion.1), channel_id=1, source_target_pairs={{0,3},{1,2},{2,1},{3,0},{4,7},{5,6},{6,5},{7,4},{8,11},{9,10},{10,... | collective-permute-start | bytes 36872 | tf_op jit(solution)/shard_map/ppermute | solution.py:992
  463.1 15.6 %collective-permute-start.36 = (bf16[1,2,144,1024]{3,2,1,0:T(8,128)(2,1)S(1)}, bf16[1,2,144,1024]{3,2,1,0:T(8,128)(2,1)S(1)}, u32[]{:S(2)}, u32[]{:S(2)}) collective-permute-start(bf16[1,2,144,1024]{3,2,1,0:T(8,128)(2,1)S(1)} %bitcast.122), channel_id=1, source_target_pairs={{0,8},{4,12},{8,0},{12,4},{1,9},{5,13},{9,1},{13,5},{2,10},{6,14},... | collective-permute-start | bytes 1769480 | tf_op jit(solution)/shard_map/ppermute | solution.py:992
  484.9 12.5 %collective-permute-start.43 = (bf16[2,2,144,1024]{3,2,1,0:T(8,128)(2,1)S(1)}, bf16[2,2,144,1024]{3,2,1,0:T(8,128)(2,1)S(1)}, u32[]{:S(2)}, u32[]{:S(2)}) collective-permute-start(bf16[2,2,144,1024]{3,2,1,0:T(8,128)(2,1)S(1)} %get-tuple-element.145.refs_0_.refs_8_), channel_id=1, source_target_pairs={{0,4},{4,0},{8,12},{12,8},{1,5},{5,1},{9,13},{13,9},{2,6},{6,2},{1... | collective-permute-start | bytes 3538952 | tf_op jit(solution)/shard_map/ppermute | solution.py:992
  485.0 9.8 %collective-permute-start.40 = (bf16[144,1024]{1,0:T(8,128)(2,1)S(1)}, bf16[144,1024]{1,0:T(8,128)(2,1)S(1)}, u32[]{:S(2)}, u32[]{:S(2)}) collective-permute-start(bf16[144,1024]{1,0:T(8,128)(2,1)S(1)} %get-tuple-element.140.d_attn_ref.refs_2_.refs_4_), channel_id=1, source_target_pairs={{12,4},{13,5},{14,6},{15,7},{28,20},{29,21},{30,22},{31,23}} | collective-permute-start | bytes 884744 | tf_op jit(solution)/shard_map/ppermute | solution.py:1073
  485.7 10.4 %collective-permute-start.41 = (bf16[144,1024]{1,0:T(8,128)(2,1)S(1)}, bf16[144,1024]{1,0:T(8,128)(2,1)S(1)}, u32[]{:S(2)}, u32[]{:S(2)}) collective-permute-start(bf16[144,1024]{1,0:T(8,128)(2,1)S(1)} %get-tuple-element.140.d_attn_ref.refs_2_.refs_4_), channel_id=1, source_target_pairs={{0,4},{1,5},{2,6},{3,7},{16,20},{17,21},{18,22},{19,23}} | collective-permute-start | bytes 884744 | tf_op jit(solution)/shard_map/ppermute | solution.py:1073
  488.7 8.7 %collective-permute-start.42 = (bf16[144,1024]{1,0:T(8,128)(2,1)S(1)}, bf16[144,1024]{1,0:T(8,128)(2,1)S(1)}, u32[]{:S(2)}, u32[]{:S(2)}) collective-permute-start(bf16[144,1024]{1,0:T(8,128)(2,1)S(1)} %get-tuple-element.140.d_attn_ref.refs_2_.refs_4_), channel_id=1, source_target_pairs={{8,4},{9,5},{10,6},{11,7},{24,20},{25,21},{26,22},{27,23}} | collective-permute-start | bytes 884744 | tf_op jit(solution)/shard_map/ppermute | solution.py:1073
  489.4 21.1 %collective-permute-start.37 = (bf16[144,3072]{1,0:T(8,128)(2,1)S(1)}, bf16[144,3072]{1,0:T(8,128)(2,1)S(1)}, u32[]{:S(2)}, u32[]{:S(2)}) collective-permute-start(bf16[144,3072]{1,0:T(8,128)(2,1)S(1)} %get-tuple-element.144.cuts_ref.refs_0_), channel_id=1, source_target_pairs={{8,0},{9,1},{10,2},{11,3},{24,16},{25,17},{26,18},{27,19}} | collective-permute-start | bytes 2654216 | tf_op jit(solution)/shard_map/ppermute | solution.py:1073
  494.8 15.7 %collective-permute-start.38 = (bf16[144,3072]{1,0:T(8,128)(2,1)S(1)}, bf16[144,3072]{1,0:T(8,128)(2,1)S(1)}, u32[]{:S(2)}, u32[]{:S(2)}) collective-permute-start(bf16[144,3072]{1,0:T(8,128)(2,1)S(1)} %get-tuple-element.144.cuts_ref.refs_0_), channel_id=1, source_target_pairs={{4,0},{5,1},{6,2},{7,3},{20,16},{21,17},{22,18},{23,19}} | collective-permute-start | bytes 2654216 | tf_op jit(solution)/shard_map/ppermute | solution.py:1073
  496.1 19.1 %collective-permute-start.39 = (bf16[144,3072]{1,0:T(8,128)(2,1)S(1)}, bf16[144,3072]{1,0:T(8,128)(2,1)S(1)}, u32[]{:S(2)}, u32[]{:S(2)}) collective-permute-start(bf16[144,3072]{1,0:T(8,128)(2,1)S(1)} %get-tuple-element.144.cuts_ref.refs_0_), channel_id=1, source_target_pairs={{12,0},{13,1},{14,2},{15,3},{28,16},{29,17},{30,18},{31,19}} | collective-permute-start | bytes 2654216 | tf_op jit(solution)/shard_map/ppermute | solution.py:1073
  519.8 32.3 %collective-permute-start.44 = (bf16[256,1024]{1,0:T(8,128)(2,1)}, bf16[256,1024]{1,0:T(8,128)(2,1)}, u32[]{:S(2)}, u32[]{:S(2)}) collective-permute-start(bf16[256,1024]{1,0:T(8,128)(2,1)} %get-tuple-element.251), channel_id=1, source_target_pairs={{0,1},{4,5},{8,9},{12,13},{16,17},{20,21},{24,25},{28,29}} | collective-permute-start | bytes 1572872 | tf_op jit(solution)/shard_map/ppermute | solution.py:1163
  524.4 28.4 %collective-permute-start.45 = (bf16[256,1024]{1,0:T(8,128)(2,1)}, bf16[256,1024]{1,0:T(8,128)(2,1)}, u32[]{:S(2)}, u32[]{:S(2)}) collective-permute-start(bf16[256,1024]{1,0:T(8,128)(2,1)} %get-tuple-element.251), channel_id=1, source_target_pairs={{3,2},{7,6},{11,10},{15,14},{19,18},{23,22},{27,26},{31,30}} | collective-permute-start | bytes 1572872 | tf_op jit(solution)/shard_map/ppermute | solution.py:1164
  526.5 32.0 %collective-permute-start.56 = (bf16[256,1024]{1,0:T(8,128)(2,1)}, bf16[256,1024]{1,0:T(8,128)(2,1)S(1)}, u32[]{:S(2)}, u32[]{:S(2)}) collective-permute-start(bf16[256,1024]{1,0:T(8,128)(2,1)} %get-tuple-element.249), channel_id=1, source_target_pairs={{0,1},{4,5},{8,9},{12,13},{16,17},{20,21},{24,25},{28,29}} | collective-permute-start | bytes 1572872 | tf_op jit(solution)/shard_map/ppermute | solution.py:1163
  527.8 31.4 %collective-permute-start.57 = (bf16[256,1024]{1,0:T(8,128)(2,1)}, bf16[256,1024]{1,0:T(8,128)(2,1)S(1)}, u32[]{:S(2)}, u32[]{:S(2)}) collective-permute-start(bf16[256,1024]{1,0:T(8,128)(2,1)} %get-tuple-element.249), channel_id=1, source_target_pairs={{3,2},{7,6},{11,10},{15,14},{19,18},{23,22},{27,26},{31,30}} | collective-permute-start | bytes 1572872 | tf_op jit(solution)/shard_map/ppermute | solution.py:1164
  528.7 36.3 %collective-permute-start.50 = (bf16[256,1024]{1,0:T(8,128)(2,1)}, bf16[256,1024]{1,0:T(8,128)(2,1)S(1)}, u32[]{:S(2)}, u32[]{:S(2)}) collective-permute-start(bf16[256,1024]{1,0:T(8,128)(2,1)} %get-tuple-element.250), channel_id=1, source_target_pairs={{0,1},{4,5},{8,9},{12,13},{16,17},{20,21},{24,25},{28,29}} | collective-permute-start | bytes 1572872 | tf_op jit(solution)/shard_map/ppermute | solution.py:1163
  552.1 13.6 %collective-permute-start.51 = (bf16[256,1024]{1,0:T(8,128)(2,1)S(1)}, bf16[256,1024]{1,0:T(8,128)(2,1)S(1)}, u32[]{:S(2)}, u32[]{:S(2)}) collective-permute-start(bf16[256,1024]{1,0:T(8,128)(2,1)S(1)} %copy-done.77), channel_id=1, source_target_pairs={{3,2},{7,6},{11,10},{15,14},{19,18},{23,22},{27,26},{31,30}} | collective-permute-start | bytes 1572872 | tf_op jit(solution)/shard_map/ppermute | solution.py:1164
  557.1 19.0 %collective-permute-start.46 = (bf16[256,1024]{1,0:T(8,128)(2,1)S(1)}, bf16[256,1024]{1,0:T(8,128)(2,1)S(1)}, u32[]{:S(2)}, u32[]{:S(2)}) collective-permute-start(bf16[256,1024]{1,0:T(8,128)(2,1)S(1)} %get-tuple-element.148), channel_id=1, source_target_pairs={{0,1},{1,2},{4,5},{5,6},{8,9},{9,10},{12,13},{13,14},{16,17},{17,1... | collective-permute-start | bytes 1572872 | tf_op jit(solution)/shard_map/ppermute | solution.py:1163
  558.5 18.4 %collective-permute-start.47 = (bf16[256,1024]{1,0:T(8,128)(2,1)S(1)}, bf16[256,1024]{1,0:T(8,128)(2,1)S(1)}, u32[]{:S(2)}, u32[]{:S(2)}) collective-permute-start(bf16[256,1024]{1,0:T(8,128)(2,1)S(1)} %get-tuple-element.149), channel_id=1, source_target_pairs={{3,2},{2,1},{7,6},{6,5},{11,10},{10,9},{15,14},{14,13},{19,18},{18... | collective-permute-start | bytes 1572872 | tf_op jit(solution)/shard_map/ppermute | solution.py:1164
  560.1 27.3 %collective-permute-start.58 = (bf16[256,1024]{1,0:T(8,128)(2,1)S(1)}, bf16[256,1024]{1,0:T(8,128)(2,1)S(1)}, u32[]{:S(2)}, u32[]{:S(2)}) collective-permute-start(bf16[256,1024]{1,0:T(8,128)(2,1)S(1)} %get-tuple-element.159), channel_id=1, source_target_pairs={{0,1},{1,2},{4,5},{5,6},{8,9},{9,10},{12,13},{13,14},{16,17},{17,1... | collective-permute-start | bytes 1572872 | tf_op jit(solution)/shard_map/ppermute | solution.py:1163
  565.0 23.7 %collective-permute-start.59 = (bf16[256,1024]{1,0:T(8,128)(2,1)S(1)}, bf16[256,1024]{1,0:T(8,128)(2,1)S(1)}, u32[]{:S(2)}, u32[]{:S(2)}) collective-permute-start(bf16[256,1024]{1,0:T(8,128)(2,1)S(1)} %get-tuple-element.160), channel_id=1, source_target_pairs={{3,2},{2,1},{7,6},{6,5},{11,10},{10,9},{15,14},{14,13},{19,18},{18... | collective-permute-start | bytes 1572872 | tf_op jit(solution)/shard_map/ppermute | solution.py:1164
  566.7 32.0 %collective-permute-start.52 = (bf16[256,1024]{1,0:T(8,128)(2,1)S(1)}, bf16[256,1024]{1,0:T(8,128)(2,1)S(1)}, u32[]{:S(2)}, u32[]{:S(2)}) collective-permute-start(bf16[256,1024]{1,0:T(8,128)(2,1)S(1)} %get-tuple-element.155), channel_id=1, source_target_pairs={{0,1},{1,2},{4,5},{5,6},{8,9},{9,10},{12,13},{13,14},{16,17},{17,1... | collective-permute-start | bytes 1572872 | tf_op jit(solution)/shard_map/ppermute | solution.py:1163
  576.1 23.9 %collective-permute-start.53 = (bf16[256,1024]{1,0:T(8,128)(2,1)S(1)}, bf16[256,1024]{1,0:T(8,128)(2,1)S(1)}, u32[]{:S(2)}, u32[]{:S(2)}) collective-permute-start(bf16[256,1024]{1,0:T(8,128)(2,1)S(1)} %get-tuple-element.156), channel_id=1, source_target_pairs={{3,2},{2,1},{7,6},{6,5},{11,10},{10,9},{15,14},{14,13},{19,18},{18... | collective-permute-start | bytes 1572872 | tf_op jit(solution)/shard_map/ppermute | solution.py:1164
  577.8 32.1 %collective-permute-start.48 = (bf16[256,1024]{1,0:T(8,128)(2,1)S(1)}, bf16[256,1024]{1,0:T(8,128)(2,1)S(1)}, u32[]{:S(2)}, u32[]{:S(2)}) collective-permute-start(bf16[256,1024]{1,0:T(8,128)(2,1)S(1)} %get-tuple-element.150), channel_id=1, source_target_pairs={{0,1},{1,2},{2,3},{4,5},{5,6},{6,7},{8,9},{9,10},{10,11},{12,13},{... | collective-permute-start | bytes 1572872 | tf_op jit(solution)/shard_map/ppermute | solution.py:1163
  587.4 24.0 %collective-permute-start.49 = (bf16[256,1024]{1,0:T(8,128)(2,1)S(1)}, bf16[256,1024]{1,0:T(8,128)(2,1)S(1)}, u32[]{:S(2)}, u32[]{:S(2)}) collective-permute-start(bf16[256,1024]{1,0:T(8,128)(2,1)S(1)} %get-tuple-element.151), channel_id=1, source_target_pairs={{3,2},{2,1},{1,0},{7,6},{6,5},{5,4},{11,10},{10,9},{9,8},{15,14},{... | collective-permute-start | bytes 1572872 | tf_op jit(solution)/shard_map/ppermute | solution.py:1164
  590.3 33.7 %collective-permute-start.60 = (bf16[256,1024]{1,0:T(8,128)(2,1)}, bf16[256,1024]{1,0:T(8,128)(2,1)S(1)}, u32[]{:S(2)}, u32[]{:S(2)}) collective-permute-start(bf16[256,1024]{1,0:T(8,128)(2,1)} %get-tuple-element.161), channel_id=1, source_target_pairs={{0,1},{1,2},{2,3},{4,5},{5,6},{6,7},{8,9},{9,10},{10,11},{12,13},{... | collective-permute-start | bytes 1572872 | tf_op jit(solution)/shard_map/ppermute | solution.py:1163
  598.6 25.9 %collective-permute-start.61 = (bf16[256,1024]{1,0:T(8,128)(2,1)S(1)}, bf16[256,1024]{1,0:T(8,128)(2,1)}, u32[]{:S(2)}, u32[]{:S(2)}) collective-permute-start(bf16[256,1024]{1,0:T(8,128)(2,1)S(1)} %get-tuple-element.162), channel_id=1, source_target_pairs={{3,2},{2,1},{1,0},{7,6},{6,5},{5,4},{11,10},{10,9},{9,8},{15,14},{... | collective-permute-start | bytes 1572872 | tf_op jit(solution)/shard_map/ppermute | solution.py:1164
  601.0 36.6 %collective-permute-start.54 = (bf16[256,1024]{1,0:T(8,128)(2,1)S(1)}, bf16[256,1024]{1,0:T(8,128)(2,1)S(1)}, u32[]{:S(2)}, u32[]{:S(2)}) collective-permute-start(bf16[256,1024]{1,0:T(8,128)(2,1)S(1)} %get-tuple-element.157), channel_id=1, source_target_pairs={{0,1},{1,2},{2,3},{4,5},{5,6},{6,7},{8,9},{9,10},{10,11},{12,13},{... | collective-permute-start | bytes 1572872 | tf_op jit(solution)/shard_map/ppermute | solution.py:1163
  609.9 27.8 %collective-permute-start.55 = (bf16[256,1024]{1,0:T(8,128)(2,1)S(1)}, bf16[256,1024]{1,0:T(8,128)(2,1)}, u32[]{:S(2)}, u32[]{:S(2)}) collective-permute-start(bf16[256,1024]{1,0:T(8,128)(2,1)S(1)} %get-tuple-element.158), channel_id=1, source_target_pairs={{3,2},{2,1},{1,0},{7,6},{6,5},{5,4},{11,10},{10,9},{9,8},{15,14},{... | collective-permute-start | bytes 1572872 | tf_op jit(solution)/shard_map/ppermute | solution.py:1164
  618.7 14.9 %collective-permute-start.68 = (f32[3,1024]{1,0:T(4,128)S(1)}, f32[3,1024]{1,0:T(4,128)S(1)}, u32[]{:S(2)}, u32[]{:S(2)}) collective-permute-start(f32[3,1024]{1,0:T(4,128)S(1)} %get-tuple-element.234), channel_id=1, source_target_pairs={{0,16},{16,0},{1,17},{17,1},{2,18},{18,2},{3,19},{19,3},{4,20},{20... | collective-permute-start | bytes 36872 | tf_op jit(solution)/shard_map/ppermute | solution.py:992
  624.0 10.2 %collective-permute-start.62 = (bf16[256,512]{1,0:T(8,128)(2,1)S(1)}, bf16[256,512]{1,0:T(8,128)(2,1)S(1)}, u32[]{:S(2)}, u32[]{:S(2)}) collective-permute-start(bf16[256,512]{1,0:T(8,128)(2,1)S(1)} %bitcast.125), channel_id=1, source_target_pairs={{0,16},{16,0},{1,17},{17,1},{2,18},{18,2},{3,19},{19,3},{4,20},{20... | collective-permute-start | bytes 786440 | tf_op jit(solution)/shard_map/ppermute | solution.py:1210
  632.1 12.8 %collective-permute-start.64 = (bf16[256,512]{1,0:T(8,128)(2,1)S(1)}, bf16[256,512]{1,0:T(8,128)(2,1)S(1)}, u32[]{:S(2)}, u32[]{:S(2)}) collective-permute-start(bf16[256,512]{1,0:T(8,128)(2,1)S(1)} %bitcast.126), channel_id=1, source_target_pairs={{0,16},{16,0},{1,17},{17,1},{2,18},{18,2},{3,19},{19,3},{4,20},{20... | collective-permute-start | bytes 786440 | tf_op jit(solution)/shard_map/ppermute | solution.py:1210
  637.0 20.2 %collective-permute-start.67 = (bf16[256,512]{1,0:T(8,128)(2,1)S(1)}, bf16[256,512]{1,0:T(8,128)(2,1)S(1)}, u32[]{:S(2)}, u32[]{:S(2)}) collective-permute-start(bf16[256,512]{1,0:T(8,128)(2,1)S(1)} %get-tuple-element.169.refs_7_.refs_0_), channel_id=1, source_target_pairs={{0,16},{16,0},{1,17},{17,1},{2,18},{18,2},{3,19},{19,3},{4,20},{20... | collective-permute-start | bytes 786440 | tf_op jit(solution)/shard_map/ppermute | solution.py:1210
  643.4 8.8 %collective-permute-start.63 = (bf16[256,512]{1,0:T(8,128)(2,1)S(1)}, bf16[256,512]{1,0:T(8,128)(2,1)S(1)}, u32[]{:S(2)}, u32[]{:S(2)}) collective-permute-start(bf16[256,512]{1,0:T(8,128)(2,1)S(1)} %bitcast.127), channel_id=1, source_target_pairs={{0,16},{16,0},{1,17},{17,1},{2,18},{18,2},{3,19},{19,3},{4,20},{20... | collective-permute-start | bytes 786440 | tf_op jit(solution)/shard_map/ppermute | solution.py:1210
  647.6 10.8 %collective-permute-start.66 = (bf16[256,512]{1,0:T(8,128)(2,1)S(1)}, bf16[256,512]{1,0:T(8,128)(2,1)S(1)}, u32[]{:S(2)}, u32[]{:S(2)}) collective-permute-start(bf16[256,512]{1,0:T(8,128)(2,1)S(1)} %get-tuple-element.183.refs_0_), channel_id=1, source_target_pairs={{0,16},{16,0},{1,17},{17,1},{2,18},{18,2},{3,19},{19,3},{4,20},{20... | collective-permute-start | bytes 786440 | tf_op jit(solution)/shard_map/ppermute | solution.py:1210
  (97 other events, 1825.9 us)
Sparse Core Ops, SparseCore 0:
  10.7 143.6 all-gather.4
  322.9 132.9 all-gather.6
  526.6 41.0 all-gather.8

commit v6 on v5

--- a/solution.py
+++ b/solution.py
@@ -156,16 +156,20 @@
 
 
 def attention_kernel(
-    weights, mask_hbm, both_ref, vec_ref, *refs, order, extra
+    weights, mask_hbm, both_hbm, vec_ref, *refs, order, extra
 ):
-    proj_ref, lse_ref, pair_ref, first_ref, held, mask_ref, sems, mask_sem = refs[extra:]
-    rows_ref = both_ref.at[0]
-    width = both_ref.shape[2]
+    proj_ref, lse_ref, pair_ref, first_ref, held, mask_ref, rows_ref, sems, mask_sem, rows_sem = refs[
+        extra:
+    ]
+    width = rows_ref.shape[1]
+    rows_copy = pltpu.make_async_copy(both_hbm.at[0], rows_ref, rows_sem)
+    rows_copy.start()
     copies = weight_copies(weights, held, sems, range(4), width, order)
     mask_copy = pltpu.make_async_copy(mask_hbm, mask_ref, mask_sem)
     mask_copy.start()
     for copy in copies:
         copy.start()
+    rows_copy.wait()
     xs = rows_ref[...].astype(jnp.float32)
     h1 = (xs * lax.rsqrt(row_mean(xs * xs) + EPS_NORM) * vec_ref[0:1, :]).astype(jnp.bfloat16)
     for index in range(3):
@@ -262,7 +266,7 @@
     d_attn_ref,
     proj_ref,
     lse_ref,
-    mask_ref,
+    mask_hbm,
     pair_hbm,
     got_hbm,
     cuts_hbm,
@@ -272,6 +276,8 @@
     weight_sems,
     pair_sems,
     cut_sems,
+    mask_ref,
+    mask_sem,
     *,
     order,
 ):
@@ -281,10 +287,12 @@
         pltpu.make_async_copy(pair_hbm, pairs_hbm.at[0], pair_sems.at[0]),
         pltpu.make_async_copy(got_hbm.at[0], pairs_hbm.at[1], pair_sems.at[1]),
     ]
-    for copy in copies + pair_copies:
+    mask_copy = pltpu.make_async_copy(mask_hbm, mask_ref, mask_sem)
+    for copy in copies + [mask_copy] + pair_copies:
         copy.start()
     copies[0].wait()
     d_mixed = nn(d_attn_ref[...], held[pl.ds(0, width), :]).astype(jnp.bfloat16)
+    mask_copy.wait()
     allowed = mask_ref[...] > 0
     for pair in range(width // 128):
         at = pair * 128
@@ -686,7 +694,7 @@
     shape = jax.ShapeDtypeStruct
     return pl.pallas_call(
         functools.partial(attention_kernel, order=order, extra=len(known)),
-        in_specs=anywhere(2) + vmem(2) + anywhere(len(known)),
+        in_specs=anywhere(3) + vmem(1) + anywhere(len(known)),
         out_specs=vmem(4),
         out_shape=[
             shape((tokens, 3 * width), jnp.bfloat16),
@@ -697,7 +705,9 @@
         scratch_shapes=[
             pltpu.VMEM((4 * width, width), jnp.bfloat16),
             pltpu.VMEM(mask.shape, jnp.int32),
+            pltpu.VMEM((tokens, width), jnp.bfloat16),
             pltpu.SemaphoreType.DMA((4,)),
+            pltpu.SemaphoreType.DMA,
             pltpu.SemaphoreType.DMA,
         ],
         compiler_params=pltpu.CompilerParams(vmem_limit_bytes=37 << 20),
@@ -752,7 +762,7 @@
     shape = jax.ShapeDtypeStruct
     return pl.pallas_call(
         functools.partial(attention_back_kernel, order=order),
-        in_specs=anywhere(1) + smem(1) + vmem(4) + anywhere(2),
+        in_specs=anywhere(1) + smem(1) + vmem(3) + anywhere(3),
         out_specs=anywhere(2),
         out_shape=[
             shape((tokens, 3 * width), jnp.bfloat16),
@@ -764,6 +774,8 @@
             pltpu.SemaphoreType.DMA((1,)),
             pltpu.SemaphoreType.DMA((2,)),
             pltpu.SemaphoreType.DMA((cuts,)),
+            pltpu.VMEM(mask.shape, jnp.int32),
+            pltpu.SemaphoreType.DMA,
         ],
         compiler_params=pltpu.CompilerParams(vmem_limit_bytes=37 << 20),
         cost_estimate=pl.CostEstimate(

time: 679 us -> 679 us (level)
  no operation moved by 1% of the time
where the time goes in v6:
time: 679 us; the launch traced here: 671 us
  waiting for transfers between devices  341 us (50%)
  Pallas kernels  142 us (21%)
  starting transfers between devices  118 us (17%)
  local copies, waits for them, and re-layouts  34.8 us (5%)
  between operations  18.7 us (3%)
  other arithmetic  16.1 us (2%)
    all_gather x2, waiting for transfers between devices, on_device(): gathered = lax.all_gather(shard_low, ('dp', 'fsdp'), axis=0, tiled=True)  203 us
    ppermute x18, starting transfers between devices, gradient_share(): below[index] = lax.ppermute(up, 'dp', [(p, p + 1) for p in range(step + 1)])  61.8 us
    ppermute x18, waiting for transfers between devices, gradient_share(): below[index] = lax.ppermute(up, 'dp', [(p, p + 1) for p in range(step + 1)])  58.5 us
    ppermute x12, waiting for transfers between devices, send_to(): lax.ppermute(values, 'fsdp', [(target ^ delta, target)])  36.7 us
    ppermute x15, waiting for transfers between devices, swap(): return lax.ppermute(values, axis, [(i, i ^ delta) for i in range(size)])  35.4 us
    unnamed x180, local copies, waits for them, and re-layouts  29.7 us
    pallas_call x2, Pallas kernels, run_feed_forward(): pl.pallas_call(functools.partial(feed_forward_kernel, keep=keep, order=or...  24.3 us
    pallas_call x4, Pallas kernels, run_products(): pl.pallas_call(functools.partial(attention_products_kernel, sources=sourc...  21.5 us
  transfers between devices with their start and end apart: 72, of which 28 were waited for; matrix products, arithmetic and copies ran while one was open for 2% of the time, Pallas kernels for 16%

profile of v6, /device:TPU:0, one launch (start us, length us, event | category | flops | bytes accessed | tf_op | source)
XLA Modules:
  0.0 670.7 jit_solution(3980373304714611237)
XLA Ops:
  7.3 3.3 convert_element_type.171
  17.3 4.5 gather_rows.1
  22.0 3.0 collective-permute-start
  25.0 26.5 %collective-permute-done = bf16[1,2,144,1024]{3,2,0,1:T(8,128)(2,1)S(1)} collective-permute-done((bf16[1,2,144,1024]{3,2,0,1:T(8,128)(2,1)S(1)}, bf16[1,2,144,1024]{3,2,0,1:T(8,128)(2,1)S(1)}, u32[]{:S(2)}, u32[]{:S(2)}) %collective-permute-start) | collective-permute-done | bytes 589856 | tf_op jit(solution)/shard_map/ppermute | solution.py:1004
  51.7 2.8 collective-permute-done.1
  55.8 98.5 %all-gather.5.cloned.1.call-done.weights = bf16[12288,1024]{1,0:T(8,128)(2,1)} async-done(((bf16[768,1024]{1,0:T(8,128)(2,1)}), bf16[12288,1024]{1,0:T(8,128)(2,1)}) %all-gather.5.cloned.1.call-update) | async-done | bytes 25165840 | tf_op jit(solution)/shard_map/all_gather | solution.py:1264
  155.3 7.0 %attention.2 = (bf16[144,3072]{1,0:T(8,128)(2,1)S(1)}, f32[288,128]{1,0:T(8,128)S(1)}, bf16[2,144,1024]{2,1,0:T(8,128)(2,1)S(1)}, f32[144,1024]{1,0:T(8,128)S(1)}) custom-call(bf16[12288,1024]{1,0:T(8,128)(2,1)} %all-gather.5.cloned.1.call-done.weights, s32[288,144]{1,0:T(8,128)S(1)} %copy-done.34, ...), custom_call_target="tpu_custom_call" | custom-call | flops 1207959552 | bytes 8388608 | tf_op jit(solution)/shard_map/attention/pallas_call | solution.py:695
  163.0 12.2 %feed_forward.2 = (bf16[144,1024]{1,0:T(8,128)(2,1)S(1)}, bf16[144,1024]{1,0:T(8,128)(2,1)S(1)}, f32[144,1024]{1,0:T(8,128)S(1)}, f32[2,1024]{1,0:T(2,128)S(1)}) custom-call(bf16[12288,1024]{1,0:T(8,128)(2,1)} %all-gather.5.cloned.1.call-done.weights, bf16[2,144,1024]{2,1,0:T(8,128)(2,1)S(1)} %get-tuple-element.106.both_hbm.both_ref, ...), custom_call_target="tpu_custom_call" | custom-call | flops 9663676416 | bytes 25165824 | tf_op jit(solution)/shard_map/feed_forward/pallas_call | solution.py:726
  177.9 6.4 attention_back.2
  185.1 3.0 collective-permute-start.7
  194.3 19.7 %collective-permute-done.3.refs_1_ = bf16[144,3072]{1,0:T(8,128)(2,1)S(1)} collective-permute-done((bf16[144,3072]{1,0:T(8,128)(2,1)S(1)}, bf16[144,3072]{1,0:T(8,128)(2,1)S(1)}, u32[]{:S(2)}, u32[]{:S(2)}) %collective-permute-start.3) | collective-permute-done | bytes 884768 | tf_op jit(solution)/shard_map/ppermute | solution.py:1085
  214.7 3.3 attention_products.4.refs_10_
  223.5 7.5 %attention_products.5.terms_ref = bf16[12,256,1024]{2,1,0:T(8,128)(2,1)S(1)} custom-call(s32[12,3]{1,0:T(8,128)S(1)} %copy-done.49, s32[4]{0:T(128)S(1)} %copy-done.55, bf16[4,144,1024]{2,1,0:T(8,128)(2,1)S(1)} %get-tuple-element.248.refs_0_.h1_ref, bf16[144,3072]{1,0:T(8,128)(2,1)S(1)} %get-tuple-element.113.refs_0_.cuts_ref, ...), custom_call_target="tpu_custom_call", output_to_operand_aliasing={{}: (14, {})} | custom-call | flops 1000000 | bytes 100000 | tf_op jit(solution)/shard_map/attention_products/pallas_call | solution.py:968
  233.4 4.4 collective-permute-start.26
  237.8 5.2 collective-permute-done.10.below_ref
  244.7 9.5 %collective-permute-done.18.below_ref = bf16[256,1024]{1,0:T(8,128)(2,1)S(1)} collective-permute-done((bf16[256,1024]{1,0:T(8,128)(2,1)S(1)}, bf16[256,1024]{1,0:T(8,128)(2,1)S(1)}, u32[]{:S(2)}, u32[]{:S(2)}) %collective-permute-start.18) | collective-permute-done | bytes 524320 | tf_op jit(solution)/shard_map/ppermute | solution.py:1175
  255.1 4.4 collective-permute-start.20
  260.3 5.9 collective-permute-start.12
  268.0 8.7 %collective-permute-done.20.below_ref = bf16[256,1024]{1,0:T(8,128)(2,1)S(1)} collective-permute-done((bf16[256,1024]{1,0:T(8,128)(2,1)S(1)}, bf16[256,1024]{1,0:T(8,128)(2,1)S(1)}, u32[]{:S(2)}, u32[]{:S(2)}) %collective-permute-start.20) | collective-permute-done | bytes 524320 | tf_op jit(solution)/shard_map/ppermute | solution.py:1175
  276.7 4.4 collective-permute-start.28
  290.2 5.2 collective-permute-start.16
  295.3 3.8 collective-permute-done.28.refs_0_
  300.9 8.0 %collective-permute-done.22 = bf16[256,1024]{1,0:T(8,128)(2,1)S(1)} collective-permute-done((bf16[256,1024]{1,0:T(8,128)(2,1)S(1)}, bf16[256,1024]{1,0:T(8,128)(2,1)S(1)}, u32[]{:S(2)}, u32[]{:S(2)}) %collective-permute-start.22) | collective-permute-done | bytes 524320 | tf_op jit(solution)/shard_map/ppermute | solution.py:1175
  309.0 2.3 collective-permute-done.29
  311.2 3.3 collective-permute-done.16
  314.6 2.3 collective-permute-done.17
  317.9 5.0 fusion.34
  325.0 4.0 input_back.2
  335.0 2.5 collective-permute-start.33
  337.5 2.9 collective-permute-start.34
  341.8 3.8 scatter_rows.5
  345.6 4.0 scatter_rows.4
  351.4 104.7 %all-gather.7.cloned.1.call-done.weights = bf16[12288,1024]{1,0:T(8,128)(2,1)} async-done(((bf16[768,1024]{1,0:T(8,128)(2,1)}), bf16[12288,1024]{1,0:T(8,128)(2,1)}) %all-gather.7.cloned.1.call-update) | async-done | bytes 25165840 | tf_op jit(solution)/shard_map/all_gather | solution.py:1264
  456.1 7.2 %attention.3 = (bf16[144,3072]{1,0:T(8,128)(2,1)S(1)}, f32[288,128]{1,0:T(8,128)S(1)}, bf16[2,144,1024]{2,1,0:T(8,128)(2,1)S(1)}, f32[144,1024]{1,0:T(8,128)S(1)}) custom-call(bf16[12288,1024]{1,0:T(8,128)(2,1)} %all-gather.7.cloned.1.call-done.weights, s32[288,144]{1,0:T(8,128)S(1)} %copy-done.32, ...), custom_call_target="tpu_custom_call" | custom-call | flops 1207959552 | bytes 8388608 | tf_op jit(solution)/shard_map/attention/pallas_call | solution.py:695
  465.7 12.1 %feed_forward.3 = (bf16[144,1024]{1,0:T(8,128)(2,1)S(1)}, bf16[144,1024]{1,0:T(8,128)(2,1)S(1)}, f32[144,1024]{1,0:T(8,128)S(1)}, f32[2,1024]{1,0:T(2,128)S(1)}) custom-call(bf16[12288,1024]{1,0:T(8,128)(2,1)} %all-gather.7.cloned.1.call-done.weights, bf16[2,144,1024]{2,1,0:T(8,128)(2,1)S(1)} %copy-done.22, f32[3,1024]{1,0:T(4,128)S(1)} %get-tuple-element.236.vec_ref, ...), custom_call_target="tpu_custom_call" | custom-call | flops 9663676416 | bytes 25165824 | tf_op jit(solution)/shard_map/feed_forward/pallas_call | solution.py:726
  478.9 6.4 attention_back.3
  486.0 3.0 collective-permute-start.41
  491.1 4.0 input_back.3
  499.4 11.5 %collective-permute-done.37.refs_1_ = bf16[144,3072]{1,0:T(8,128)(2,1)S(1)} collective-permute-done((bf16[144,3072]{1,0:T(8,128)(2,1)S(1)}, bf16[144,3072]{1,0:T(8,128)(2,1)S(1)}, u32[]{:S(2)}, u32[]{:S(2)}) %collective-permute-start.37) | collective-permute-done | bytes 884768 | tf_op jit(solution)/shard_map/ppermute | solution.py:1085
  510.8 4.8 collective-permute-done.39.refs_3_
  515.7 3.3 attention_products.6.refs_10_
  520.2 4.6 collective-permute-start.44
  530.5 2.8 copy-done.1
  542.4 7.4 %attention_products.7.terms_ref.refs_0_ = bf16[12,256,1024]{2,1,0:T(8,128)(2,1)S(1)} custom-call(s32[12,3]{1,0:T(8,128)S(1)} %copy-done.50, s32[4]{0:T(128)S(1)} %copy-done.56, bf16[4,144,1024]{2,1,0:T(8,128)(2,1)S(1)} %get-tuple-element.246.refs_0_.h1_ref, bf16[144,3072]{1,0:T(8,128)(2,1)S(1)} %copy-done.8, ...), custom_call_target="tpu_custom_call", output_to_operand_aliasing={{}: (14, {})} | custom-call | flops 1000000 | bytes 100000 | tf_op jit(solution)/shard_map/attention_products/pallas_call | solution.py:968
  549.8 2.7 copy-done.2
  553.2 2.8 copy-done.3
  560.5 2.8 collective-permute-start.58
  567.1 4.9 collective-permute-start.52
  572.0 4.6 collective-permute-done.46.below_ref
  578.2 5.0 collective-permute-start.48
  583.2 4.6 collective-permute-done.58.below_ref
  590.7 5.0 collective-permute-start.60
  595.7 3.3 collective-permute-done.52.below_ref
  601.4 5.0 collective-permute-start.54
  606.4 3.8 collective-permute-done.48.below_ref
  611.9 3.9 update.3
  620.6 3.8 scatter_rows.6
  625.6 5.0 update.4
  634.6 2.8 outer.3
  638.0 4.9 update.5
  645.2 2.8 outer.4
  648.7 3.9 scatter_rows.7
  653.2 2.8 outer.5
  660.1 2.4 collective-permute-done.65.refs_1_
  (348 shorter events, 116.0 us)
Async XLA Ops:
  7.2 147.2 %all-gather.5.cloned.1.call-start = ((), (), s32[]{:S(2)}) async-start(), calls=%async_computation | async-start | bytes 26738688 | tf_op jit(solution)/shard_map/all_gather | solution.py:1264
  10.6 445.5 %all-gather.7.cloned.1.call-start = ((), (), s32[]{:S(2)}) async-start(), calls=%async_computation.1 | async-start | bytes 26738688 | tf_op jit(solution)/shard_map/all_gather | solution.py:1264
  22.0 29.5 %collective-permute-start = (bf16[1,2,144,1024]{3,2,0,1:T(8,128)(2,1)S(1)}, bf16[1,2,144,1024]{3,2,0,1:T(8,128)(2,1)S(1)}, u32[]{:S(2)}, u32[]{:S(2)}) collective-permute-start(bf16[1,2,144,1024]{3,2,0,1:T(8,128)(2,1)S(1)} %bitcast.116), channel_id=1, source_target_pairs={{0,8},{4,12},{8,0},{12,4},{1,9},{5,13},{9,1},{13,5},{2,10},{6,14},... | collective-permute-start | bytes 1769480 | tf_op jit(solution)/shard_map/ppermute | solution.py:1004
  162.3 15.6 %collective-permute-start.2 = (bf16[1,2,144,1024]{3,2,1,0:T(8,128)(2,1)S(1)}, bf16[1,2,144,1024]{3,2,1,0:T(8,128)(2,1)S(1)}, u32[]{:S(2)}, u32[]{:S(2)}) collective-permute-start(bf16[1,2,144,1024]{3,2,1,0:T(8,128)(2,1)S(1)} %bitcast.123), channel_id=1, source_target_pairs={{0,8},{4,12},{8,0},{12,4},{1,9},{5,13},{9,1},{13,5},{2,10},{6,14},... | collective-permute-start | bytes 1769480 | tf_op jit(solution)/shard_map/ppermute | solution.py:1004
  184.3 8.4 %collective-permute-start.9 = (bf16[2,2,144,1024]{3,2,1,0:T(8,128)(2,1)S(1)}, bf16[2,2,144,1024]{3,2,1,0:T(8,128)(2,1)S(1)}, u32[]{:S(2)}, u32[]{:S(2)}) collective-permute-start(bf16[2,2,144,1024]{3,2,1,0:T(8,128)(2,1)S(1)} %get-tuple-element.114.refs_0_.refs_8_), channel_id=1, source_target_pairs={{0,4},{4,0},{8,12},{12,8},{1,5},{5,1},{9,13},{13,9},{2,6},{6,2},{1... | collective-permute-start | bytes 3538952 | tf_op jit(solution)/shard_map/ppermute | solution.py:1004
  188.8 25.2 %collective-permute-start.3 = (bf16[144,3072]{1,0:T(8,128)(2,1)S(1)}, bf16[144,3072]{1,0:T(8,128)(2,1)S(1)}, u32[]{:S(2)}, u32[]{:S(2)}) collective-permute-start(bf16[144,3072]{1,0:T(8,128)(2,1)S(1)} %get-tuple-element.113.refs_0_.cuts_ref), channel_id=1, source_target_pairs={{8,0},{9,1},{10,2},{11,3},{24,16},{25,17},{26,18},{27,19}} | collective-permute-start | bytes 2654216 | tf_op jit(solution)/shard_map/ppermute | solution.py:1085
  190.1 23.9 %collective-permute-start.4 = (bf16[144,3072]{1,0:T(8,128)(2,1)S(1)}, bf16[144,3072]{1,0:T(8,128)(2,1)S(1)}, u32[]{:S(2)}, u32[]{:S(2)}) collective-permute-start(bf16[144,3072]{1,0:T(8,128)(2,1)S(1)} %get-tuple-element.113.refs_0_.cuts_ref), channel_id=1, source_target_pairs={{4,0},{5,1},{6,2},{7,3},{20,16},{21,17},{22,18},{23,19}} | collective-permute-start | bytes 2654216 | tf_op jit(solution)/shard_map/ppermute | solution.py:1085
  191.4 23.2 %collective-permute-start.5 = (bf16[144,3072]{1,0:T(8,128)(2,1)S(1)}, bf16[144,3072]{1,0:T(8,128)(2,1)S(1)}, u32[]{:S(2)}, u32[]{:S(2)}) collective-permute-start(bf16[144,3072]{1,0:T(8,128)(2,1)S(1)} %get-tuple-element.113.refs_0_.cuts_ref), channel_id=1, source_target_pairs={{12,0},{13,1},{14,2},{15,3},{28,16},{29,17},{30,18},{31,19}} | collective-permute-start | bytes 2654216 | tf_op jit(solution)/shard_map/ppermute | solution.py:1085
  218.1 13.7 %collective-permute-start.24 = (bf16[256,1024]{1,0:T(8,128)(2,1)S(1)}, bf16[256,1024]{1,0:T(8,128)(2,1)S(1)}, u32[]{:S(2)}, u32[]{:S(2)}) collective-permute-start(bf16[256,1024]{1,0:T(8,128)(2,1)S(1)} %get-tuple-element.253), channel_id=1, source_target_pairs={{0,1},{4,5},{8,9},{12,13},{16,17},{20,21},{24,25},{28,29}} | collective-permute-start | bytes 1572872 | tf_op jit(solution)/shard_map/ppermute | solution.py:1175
  219.4 13.0 %collective-permute-start.25 = (bf16[256,1024]{1,0:T(8,128)(2,1)S(1)}, bf16[256,1024]{1,0:T(8,128)(2,1)S(1)}, u32[]{:S(2)}, u32[]{:S(2)}) collective-permute-start(bf16[256,1024]{1,0:T(8,128)(2,1)S(1)} %get-tuple-element.253), channel_id=1, source_target_pairs={{3,2},{7,6},{11,10},{15,14},{19,18},{23,22},{27,26},{31,30}} | collective-permute-start | bytes 1572872 | tf_op jit(solution)/shard_map/ppermute | solution.py:1176
  220.1 22.9 %collective-permute-start.10 = (bf16[256,1024]{1,0:T(8,128)(2,1)S(1)}, bf16[256,1024]{1,0:T(8,128)(2,1)S(1)}, u32[]{:S(2)}, u32[]{:S(2)}) collective-permute-start(bf16[256,1024]{1,0:T(8,128)(2,1)S(1)} %get-tuple-element.252), channel_id=1, source_target_pairs={{0,1},{4,5},{8,9},{12,13},{16,17},{20,21},{24,25},{28,29}} | collective-permute-start | bytes 1572872 | tf_op jit(solution)/shard_map/ppermute | solution.py:1175
  221.5 22.2 %collective-permute-start.11 = (bf16[256,1024]{1,0:T(8,128)(2,1)S(1)}, bf16[256,1024]{1,0:T(8,128)(2,1)S(1)}, u32[]{:S(2)}, u32[]{:S(2)}) collective-permute-start(bf16[256,1024]{1,0:T(8,128)(2,1)S(1)} %get-tuple-element.252), channel_id=1, source_target_pairs={{3,2},{7,6},{11,10},{15,14},{19,18},{23,22},{27,26},{31,30}} | collective-permute-start | bytes 1572872 | tf_op jit(solution)/shard_map/ppermute | solution.py:1176
  222.2 32.1 %collective-permute-start.18 = (bf16[256,1024]{1,0:T(8,128)(2,1)S(1)}, bf16[256,1024]{1,0:T(8,128)(2,1)S(1)}, u32[]{:S(2)}, u32[]{:S(2)}) collective-permute-start(bf16[256,1024]{1,0:T(8,128)(2,1)S(1)} %get-tuple-element.254), channel_id=1, source_target_pairs={{0,1},{4,5},{8,9},{12,13},{16,17},{20,21},{24,25},{28,29}} | collective-permute-start | bytes 1572872 | tf_op jit(solution)/shard_map/ppermute | solution.py:1175
  231.8 22.5 %collective-permute-start.19 = (bf16[256,1024]{1,0:T(8,128)(2,1)S(1)}, bf16[256,1024]{1,0:T(8,128)(2,1)S(1)}, u32[]{:S(2)}, u32[]{:S(2)}) collective-permute-start(bf16[256,1024]{1,0:T(8,128)(2,1)S(1)} %get-tuple-element.254), channel_id=1, source_target_pairs={{3,2},{7,6},{11,10},{15,14},{19,18},{23,22},{27,26},{31,30}} | collective-permute-start | bytes 1572872 | tf_op jit(solution)/shard_map/ppermute | solution.py:1176
  233.4 32.9 %collective-permute-start.26 = (bf16[256,1024]{1,0:T(8,128)(2,1)S(1)}, bf16[256,1024]{1,0:T(8,128)(2,1)S(1)}, u32[]{:S(2)}, u32[]{:S(2)}) collective-permute-start(bf16[256,1024]{1,0:T(8,128)(2,1)S(1)} %get-tuple-element.125), channel_id=1, source_target_pairs={{0,1},{1,2},{4,5},{5,6},{8,9},{9,10},{12,13},{13,14},{16,17},{17,1... | collective-permute-start | bytes 1572872 | tf_op jit(solution)/shard_map/ppermute | solution.py:1175
  243.0 24.0 %collective-permute-start.27 = (bf16[256,1024]{1,0:T(8,128)(2,1)S(1)}, bf16[256,1024]{1,0:T(8,128)(2,1)S(1)}, u32[]{:S(2)}, u32[]{:S(2)}) collective-permute-start(bf16[256,1024]{1,0:T(8,128)(2,1)S(1)} %get-tuple-element.126), channel_id=1, source_target_pairs={{3,2},{2,1},{7,6},{6,5},{11,10},{10,9},{15,14},{14,13},{19,18},{18... | collective-permute-start | bytes 1572872 | tf_op jit(solution)/shard_map/ppermute | solution.py:1176
  244.6 15.6 %collective-permute-start.14 = (bf16[1,2,144,1024]{3,2,0,1:T(8,128)(2,1)S(1)}, bf16[1,2,144,1024]{3,2,0,1:T(8,128)(2,1)S(1)}, u32[]{:S(2)}, u32[]{:S(2)}) collective-permute-start(bf16[1,2,144,1024]{3,2,0,1:T(8,128)(2,1)S(1)} %bitcast.119), channel_id=1, source_target_pairs={{0,8},{4,12},{8,0},{12,4},{1,9},{5,13},{9,1},{13,5},{2,10},{6,14},... | collective-permute-start | bytes 1769480 | tf_op jit(solution)/shard_map/ppermute | solution.py:1004
  255.1 21.6 %collective-permute-start.20 = (bf16[256,1024]{1,0:T(8,128)(2,1)S(1)}, bf16[256,1024]{1,0:T(8,128)(2,1)S(1)}, u32[]{:S(2)}, u32[]{:S(2)}) collective-permute-start(bf16[256,1024]{1,0:T(8,128)(2,1)S(1)} %get-tuple-element.121), channel_id=1, source_target_pairs={{0,1},{1,2},{4,5},{5,6},{8,9},{9,10},{12,13},{13,14},{16,17},{17,1... | collective-permute-start | bytes 1572872 | tf_op jit(solution)/shard_map/ppermute | solution.py:1175
  259.6 21.5 %collective-permute-start.21 = (bf16[256,1024]{1,0:T(8,128)(2,1)S(1)}, bf16[256,1024]{1,0:T(8,128)(2,1)S(1)}, u32[]{:S(2)}, u32[]{:S(2)}) collective-permute-start(bf16[256,1024]{1,0:T(8,128)(2,1)S(1)} %get-tuple-element.122), channel_id=1, source_target_pairs={{3,2},{2,1},{7,6},{6,5},{11,10},{10,9},{15,14},{14,13},{19,18},{18... | collective-permute-start | bytes 1572872 | tf_op jit(solution)/shard_map/ppermute | solution.py:1176
  260.3 27.6 %collective-permute-start.12 = (bf16[256,1024]{1,0:T(8,128)(2,1)S(1)}, bf16[256,1024]{1,0:T(8,128)(2,1)S(1)}, u32[]{:S(2)}, u32[]{:S(2)}) collective-permute-start(bf16[256,1024]{1,0:T(8,128)(2,1)S(1)} %get-tuple-element.116), channel_id=1, source_target_pairs={{0,1},{1,2},{4,5},{5,6},{8,9},{9,10},{12,13},{13,14},{16,17},{17,1... | collective-permute-start | bytes 1572872 | tf_op jit(solution)/shard_map/ppermute | solution.py:1175
  266.3 22.9 %collective-permute-start.13 = (bf16[256,1024]{1,0:T(8,128)(2,1)S(1)}, bf16[256,1024]{1,0:T(8,128)(2,1)S(1)}, u32[]{:S(2)}, u32[]{:S(2)}) collective-permute-start(bf16[256,1024]{1,0:T(8,128)(2,1)S(1)} %get-tuple-element.117), channel_id=1, source_target_pairs={{3,2},{2,1},{7,6},{6,5},{11,10},{10,9},{15,14},{14,13},{19,18},{18... | collective-permute-start | bytes 1572872 | tf_op jit(solution)/shard_map/ppermute | solution.py:1176
  267.0 17.0 %collective-permute-start.15 = (bf16[2,2,144,1024]{3,2,0,1:T(8,128)(2,1)S(1)}, bf16[2,2,144,1024]{3,2,0,1:T(8,128)(2,1)S(1)}, u32[]{:S(2)}, u32[]{:S(2)}) collective-permute-start(bf16[2,2,144,1024]{3,2,0,1:T(8,128)(2,1)S(1)} %pad_maximum_fusion.4), channel_id=1, source_target_pairs={{0,4},{4,0},{8,12},{12,8},{1,5},{5,1},{9,13},{13,9},{2,6},{6,2},{1... | collective-permute-start | bytes 3538952 | tf_op jit(solution)/shard_map/ppermute | solution.py:1004
  276.7 22.5 %collective-permute-start.28 = (bf16[256,1024]{1,0:T(8,128)(2,1)S(1)}, bf16[256,1024]{1,0:T(8,128)(2,1)S(1)}, u32[]{:S(2)}, u32[]{:S(2)}) collective-permute-start(bf16[256,1024]{1,0:T(8,128)(2,1)S(1)} %get-tuple-element.127), channel_id=1, source_target_pairs={{0,1},{1,2},{2,3},{4,5},{5,6},{6,7},{8,9},{9,10},{10,11},{12,13},{... | collective-permute-start | bytes 1572872 | tf_op jit(solution)/shard_map/ppermute | solution.py:1175
  282.1 26.9 %collective-permute-start.22 = (bf16[256,1024]{1,0:T(8,128)(2,1)S(1)}, bf16[256,1024]{1,0:T(8,128)(2,1)S(1)}, u32[]{:S(2)}, u32[]{:S(2)}) collective-permute-start(bf16[256,1024]{1,0:T(8,128)(2,1)S(1)} %get-tuple-element.123), channel_id=1, source_target_pairs={{0,1},{1,2},{2,3},{4,5},{5,6},{6,7},{8,9},{9,10},{10,11},{12,13},{... | collective-permute-start | bytes 1572872 | tf_op jit(solution)/shard_map/ppermute | solution.py:1175
  284.0 24.9 %collective-permute-start.23 = (bf16[256,1024]{1,0:T(8,128)(2,1)S(1)}, bf16[256,1024]{1,0:T(8,128)(2,1)S(1)}, u32[]{:S(2)}, u32[]{:S(2)}) collective-permute-start(bf16[256,1024]{1,0:T(8,128)(2,1)S(1)} %get-tuple-element.124), channel_id=1, source_target_pairs={{3,2},{2,1},{1,0},{7,6},{6,5},{5,4},{11,10},{10,9},{9,8},{15,14},{... | collective-permute-start | bytes 1572872 | tf_op jit(solution)/shard_map/ppermute | solution.py:1176
  287.9 23.3 %collective-permute-start.29 = (bf16[256,1024]{1,0:T(8,128)(2,1)S(1)}, bf16[256,1024]{1,0:T(8,128)(2,1)S(1)}, u32[]{:S(2)}, u32[]{:S(2)}) collective-permute-start(bf16[256,1024]{1,0:T(8,128)(2,1)S(1)} %get-tuple-element.128), channel_id=1, source_target_pairs={{3,2},{2,1},{1,0},{7,6},{6,5},{5,4},{11,10},{10,9},{9,8},{15,14},{... | collective-permute-start | bytes 1572872 | tf_op jit(solution)/shard_map/ppermute | solution.py:1176
  290.2 24.4 %collective-permute-start.16 = (bf16[256,1024]{1,0:T(8,128)(2,1)S(1)}, bf16[256,1024]{1,0:T(8,128)(2,1)S(1)}, u32[]{:S(2)}, u32[]{:S(2)}) collective-permute-start(bf16[256,1024]{1,0:T(8,128)(2,1)S(1)} %get-tuple-element.119), channel_id=1, source_target_pairs={{0,1},{1,2},{2,3},{4,5},{5,6},{6,7},{8,9},{9,10},{10,11},{12,13},{... | collective-permute-start | bytes 1572872 | tf_op jit(solution)/shard_map/ppermute | solution.py:1175
  299.2 17.7 %collective-permute-start.17 = (bf16[256,1024]{1,0:T(8,128)(2,1)S(1)}, bf16[256,1024]{1,0:T(8,128)(2,1)S(1)}, u32[]{:S(2)}, u32[]{:S(2)}) collective-permute-start(bf16[256,1024]{1,0:T(8,128)(2,1)S(1)} %get-tuple-element.120), channel_id=1, source_target_pairs={{3,2},{2,1},{1,0},{7,6},{6,5},{5,4},{11,10},{10,9},{9,8},{15,14},{... | collective-permute-start | bytes 1572872 | tf_op jit(solution)/shard_map/ppermute | solution.py:1176
  323.0 294.8 %all-gather.9.cloned.1.call-start = ((), (), s32[]{:S(2)}) async-start(), calls=%async_computation.2 | async-start | bytes 1114112 | tf_op jit(solution)/shard_map/all_gather | solution.py:1018
  335.0 14.7 %collective-permute-start.33 = (f32[3,1024]{1,0:T(4,128)S(1)}, f32[3,1024]{1,0:T(4,128)S(1)}, u32[]{:S(2)}, u32[]{:S(2)}) collective-permute-start(f32[3,1024]{1,0:T(4,128)S(1)} %add_add_fusion.1), channel_id=1, source_target_pairs={{0,1},{1,0},{2,3},{3,2},{4,5},{5,4},{6,7},{7,6},{8,9},{9,8},{10,11... | collective-permute-start | bytes 36872 | tf_op jit(solution)/shard_map/ppermute | solution.py:1004
  337.5 12.2 %collective-permute-start.34 = (f32[3,1024]{1,0:T(4,128)S(1)}, f32[3,1024]{1,0:T(4,128)S(1)}, u32[]{:S(2)}, u32[]{:S(2)}) collective-permute-start(f32[3,1024]{1,0:T(4,128)S(1)} %add_add_fusion.1), channel_id=1, source_target_pairs={{0,2},{1,3},{2,0},{3,1},{4,6},{5,7},{6,4},{7,5},{8,10},{9,11},{10,... | collective-permute-start | bytes 36872 | tf_op jit(solution)/shard_map/ppermute | solution.py:1004
  340.4 9.3 %collective-permute-start.35 = (f32[3,1024]{1,0:T(4,128)S(1)}, f32[3,1024]{1,0:T(4,128)S(1)}, u32[]{:S(2)}, u32[]{:S(2)}) collective-permute-start(f32[3,1024]{1,0:T(4,128)S(1)} %add_add_fusion.1), channel_id=1, source_target_pairs={{0,3},{1,2},{2,1},{3,0},{4,7},{5,6},{6,5},{7,4},{8,11},{9,10},{10,... | collective-permute-start | bytes 36872 | tf_op jit(solution)/shard_map/ppermute | solution.py:1004
  463.3 15.6 %collective-permute-start.36 = (bf16[1,2,144,1024]{3,2,1,0:T(8,128)(2,1)S(1)}, bf16[1,2,144,1024]{3,2,1,0:T(8,128)(2,1)S(1)}, u32[]{:S(2)}, u32[]{:S(2)}) collective-permute-start(bf16[1,2,144,1024]{3,2,1,0:T(8,128)(2,1)S(1)} %bitcast.122), channel_id=1, source_target_pairs={{0,8},{4,12},{8,0},{12,4},{1,9},{5,13},{9,1},{13,5},{2,10},{6,14},... | collective-permute-start | bytes 1769480 | tf_op jit(solution)/shard_map/ppermute | solution.py:1004
  485.3 12.5 %collective-permute-start.43 = (bf16[2,2,144,1024]{3,2,1,0:T(8,128)(2,1)S(1)}, bf16[2,2,144,1024]{3,2,1,0:T(8,128)(2,1)S(1)}, u32[]{:S(2)}, u32[]{:S(2)}) collective-permute-start(bf16[2,2,144,1024]{3,2,1,0:T(8,128)(2,1)S(1)} %get-tuple-element.145.refs_0_.refs_8_), channel_id=1, source_target_pairs={{0,4},{4,0},{8,12},{12,8},{1,5},{5,1},{9,13},{13,9},{2,6},{6,2},{1... | collective-permute-start | bytes 3538952 | tf_op jit(solution)/shard_map/ppermute | solution.py:1004
  485.4 9.8 %collective-permute-start.40 = (bf16[144,1024]{1,0:T(8,128)(2,1)S(1)}, bf16[144,1024]{1,0:T(8,128)(2,1)S(1)}, u32[]{:S(2)}, u32[]{:S(2)}) collective-permute-start(bf16[144,1024]{1,0:T(8,128)(2,1)S(1)} %get-tuple-element.140.d_attn_ref.refs_2_.refs_4_), channel_id=1, source_target_pairs={{12,4},{13,5},{14,6},{15,7},{28,20},{29,21},{30,22},{31,23}} | collective-permute-start | bytes 884744 | tf_op jit(solution)/shard_map/ppermute | solution.py:1085
  486.0 10.4 %collective-permute-start.41 = (bf16[144,1024]{1,0:T(8,128)(2,1)S(1)}, bf16[144,1024]{1,0:T(8,128)(2,1)S(1)}, u32[]{:S(2)}, u32[]{:S(2)}) collective-permute-start(bf16[144,1024]{1,0:T(8,128)(2,1)S(1)} %get-tuple-element.140.d_attn_ref.refs_2_.refs_4_), channel_id=1, source_target_pairs={{0,4},{1,5},{2,6},{3,7},{16,20},{17,21},{18,22},{19,23}} | collective-permute-start | bytes 884744 | tf_op jit(solution)/shard_map/ppermute | solution.py:1085
  489.1 8.7 %collective-permute-start.42 = (bf16[144,1024]{1,0:T(8,128)(2,1)S(1)}, bf16[144,1024]{1,0:T(8,128)(2,1)S(1)}, u32[]{:S(2)}, u32[]{:S(2)}) collective-permute-start(bf16[144,1024]{1,0:T(8,128)(2,1)S(1)} %get-tuple-element.140.d_attn_ref.refs_2_.refs_4_), channel_id=1, source_target_pairs={{8,4},{9,5},{10,6},{11,7},{24,20},{25,21},{26,22},{27,23}} | collective-permute-start | bytes 884744 | tf_op jit(solution)/shard_map/ppermute | solution.py:1085
  489.8 21.1 %collective-permute-start.37 = (bf16[144,3072]{1,0:T(8,128)(2,1)S(1)}, bf16[144,3072]{1,0:T(8,128)(2,1)S(1)}, u32[]{:S(2)}, u32[]{:S(2)}) collective-permute-start(bf16[144,3072]{1,0:T(8,128)(2,1)S(1)} %get-tuple-element.144.cuts_ref.refs_0_), channel_id=1, source_target_pairs={{8,0},{9,1},{10,2},{11,3},{24,16},{25,17},{26,18},{27,19}} | collective-permute-start | bytes 2654216 | tf_op jit(solution)/shard_map/ppermute | solution.py:1085
  495.2 15.7 %collective-permute-start.38 = (bf16[144,3072]{1,0:T(8,128)(2,1)S(1)}, bf16[144,3072]{1,0:T(8,128)(2,1)S(1)}, u32[]{:S(2)}, u32[]{:S(2)}) collective-permute-start(bf16[144,3072]{1,0:T(8,128)(2,1)S(1)} %get-tuple-element.144.cuts_ref.refs_0_), channel_id=1, source_target_pairs={{4,0},{5,1},{6,2},{7,3},{20,16},{21,17},{22,18},{23,19}} | collective-permute-start | bytes 2654216 | tf_op jit(solution)/shard_map/ppermute | solution.py:1085
  496.5 19.1 %collective-permute-start.39 = (bf16[144,3072]{1,0:T(8,128)(2,1)S(1)}, bf16[144,3072]{1,0:T(8,128)(2,1)S(1)}, u32[]{:S(2)}, u32[]{:S(2)}) collective-permute-start(bf16[144,3072]{1,0:T(8,128)(2,1)S(1)} %get-tuple-element.144.cuts_ref.refs_0_), channel_id=1, source_target_pairs={{12,0},{13,1},{14,2},{15,3},{28,16},{29,17},{30,18},{31,19}} | collective-permute-start | bytes 2654216 | tf_op jit(solution)/shard_map/ppermute | solution.py:1085
  520.2 32.3 %collective-permute-start.44 = (bf16[256,1024]{1,0:T(8,128)(2,1)}, bf16[256,1024]{1,0:T(8,128)(2,1)}, u32[]{:S(2)}, u32[]{:S(2)}) collective-permute-start(bf16[256,1024]{1,0:T(8,128)(2,1)} %get-tuple-element.251), channel_id=1, source_target_pairs={{0,1},{4,5},{8,9},{12,13},{16,17},{20,21},{24,25},{28,29}} | collective-permute-start | bytes 1572872 | tf_op jit(solution)/shard_map/ppermute | solution.py:1175
  524.8 28.4 %collective-permute-start.45 = (bf16[256,1024]{1,0:T(8,128)(2,1)}, bf16[256,1024]{1,0:T(8,128)(2,1)}, u32[]{:S(2)}, u32[]{:S(2)}) collective-permute-start(bf16[256,1024]{1,0:T(8,128)(2,1)} %get-tuple-element.251), channel_id=1, source_target_pairs={{3,2},{7,6},{11,10},{15,14},{19,18},{23,22},{27,26},{31,30}} | collective-permute-start | bytes 1572872 | tf_op jit(solution)/shard_map/ppermute | solution.py:1176
  526.9 32.0 %collective-permute-start.56 = (bf16[256,1024]{1,0:T(8,128)(2,1)}, bf16[256,1024]{1,0:T(8,128)(2,1)S(1)}, u32[]{:S(2)}, u32[]{:S(2)}) collective-permute-start(bf16[256,1024]{1,0:T(8,128)(2,1)} %get-tuple-element.249), channel_id=1, source_target_pairs={{0,1},{4,5},{8,9},{12,13},{16,17},{20,21},{24,25},{28,29}} | collective-permute-start | bytes 1572872 | tf_op jit(solution)/shard_map/ppermute | solution.py:1175
  528.2 31.4 %collective-permute-start.57 = (bf16[256,1024]{1,0:T(8,128)(2,1)}, bf16[256,1024]{1,0:T(8,128)(2,1)S(1)}, u32[]{:S(2)}, u32[]{:S(2)}) collective-permute-start(bf16[256,1024]{1,0:T(8,128)(2,1)} %get-tuple-element.249), channel_id=1, source_target_pairs={{3,2},{7,6},{11,10},{15,14},{19,18},{23,22},{27,26},{31,30}} | collective-permute-start | bytes 1572872 | tf_op jit(solution)/shard_map/ppermute | solution.py:1176
  528.9 36.5 %collective-permute-start.50 = (bf16[256,1024]{1,0:T(8,128)(2,1)}, bf16[256,1024]{1,0:T(8,128)(2,1)S(1)}, u32[]{:S(2)}, u32[]{:S(2)}) collective-permute-start(bf16[256,1024]{1,0:T(8,128)(2,1)} %get-tuple-element.250), channel_id=1, source_target_pairs={{0,1},{4,5},{8,9},{12,13},{16,17},{20,21},{24,25},{28,29}} | collective-permute-start | bytes 1572872 | tf_op jit(solution)/shard_map/ppermute | solution.py:1175
  552.5 13.6 %collective-permute-start.51 = (bf16[256,1024]{1,0:T(8,128)(2,1)S(1)}, bf16[256,1024]{1,0:T(8,128)(2,1)S(1)}, u32[]{:S(2)}, u32[]{:S(2)}) collective-permute-start(bf16[256,1024]{1,0:T(8,128)(2,1)S(1)} %copy-done.77), channel_id=1, source_target_pairs={{3,2},{7,6},{11,10},{15,14},{19,18},{23,22},{27,26},{31,30}} | collective-permute-start | bytes 1572872 | tf_op jit(solution)/shard_map/ppermute | solution.py:1176
  557.5 19.0 %collective-permute-start.46 = (bf16[256,1024]{1,0:T(8,128)(2,1)S(1)}, bf16[256,1024]{1,0:T(8,128)(2,1)S(1)}, u32[]{:S(2)}, u32[]{:S(2)}) collective-permute-start(bf16[256,1024]{1,0:T(8,128)(2,1)S(1)} %get-tuple-element.148), channel_id=1, source_target_pairs={{0,1},{1,2},{4,5},{5,6},{8,9},{9,10},{12,13},{13,14},{16,17},{17,1... | collective-permute-start | bytes 1572872 | tf_op jit(solution)/shard_map/ppermute | solution.py:1175
  558.9 18.4 %collective-permute-start.47 = (bf16[256,1024]{1,0:T(8,128)(2,1)S(1)}, bf16[256,1024]{1,0:T(8,128)(2,1)S(1)}, u32[]{:S(2)}, u32[]{:S(2)}) collective-permute-start(bf16[256,1024]{1,0:T(8,128)(2,1)S(1)} %get-tuple-element.149), channel_id=1, source_target_pairs={{3,2},{2,1},{7,6},{6,5},{11,10},{10,9},{15,14},{14,13},{19,18},{18... | collective-permute-start | bytes 1572872 | tf_op jit(solution)/shard_map/ppermute | solution.py:1176
  560.5 27.3 %collective-permute-start.58 = (bf16[256,1024]{1,0:T(8,128)(2,1)S(1)}, bf16[256,1024]{1,0:T(8,128)(2,1)S(1)}, u32[]{:S(2)}, u32[]{:S(2)}) collective-permute-start(bf16[256,1024]{1,0:T(8,128)(2,1)S(1)} %get-tuple-element.159), channel_id=1, source_target_pairs={{0,1},{1,2},{4,5},{5,6},{8,9},{9,10},{12,13},{13,14},{16,17},{17,1... | collective-permute-start | bytes 1572872 | tf_op jit(solution)/shard_map/ppermute | solution.py:1175
  565.4 23.7 %collective-permute-start.59 = (bf16[256,1024]{1,0:T(8,128)(2,1)S(1)}, bf16[256,1024]{1,0:T(8,128)(2,1)S(1)}, u32[]{:S(2)}, u32[]{:S(2)}) collective-permute-start(bf16[256,1024]{1,0:T(8,128)(2,1)S(1)} %get-tuple-element.160), channel_id=1, source_target_pairs={{3,2},{2,1},{7,6},{6,5},{11,10},{10,9},{15,14},{14,13},{19,18},{18... | collective-permute-start | bytes 1572872 | tf_op jit(solution)/shard_map/ppermute | solution.py:1176
  567.1 32.0 %collective-permute-start.52 = (bf16[256,1024]{1,0:T(8,128)(2,1)S(1)}, bf16[256,1024]{1,0:T(8,128)(2,1)S(1)}, u32[]{:S(2)}, u32[]{:S(2)}) collective-permute-start(bf16[256,1024]{1,0:T(8,128)(2,1)S(1)} %get-tuple-element.155), channel_id=1, source_target_pairs={{0,1},{1,2},{4,5},{5,6},{8,9},{9,10},{12,13},{13,14},{16,17},{17,1... | collective-permute-start | bytes 1572872 | tf_op jit(solution)/shard_map/ppermute | solution.py:1175
  576.5 23.9 %collective-permute-start.53 = (bf16[256,1024]{1,0:T(8,128)(2,1)S(1)}, bf16[256,1024]{1,0:T(8,128)(2,1)S(1)}, u32[]{:S(2)}, u32[]{:S(2)}) collective-permute-start(bf16[256,1024]{1,0:T(8,128)(2,1)S(1)} %get-tuple-element.156), channel_id=1, source_target_pairs={{3,2},{2,1},{7,6},{6,5},{11,10},{10,9},{15,14},{14,13},{19,18},{18... | collective-permute-start | bytes 1572872 | tf_op jit(solution)/shard_map/ppermute | solution.py:1176
  578.2 32.1 %collective-permute-start.48 = (bf16[256,1024]{1,0:T(8,128)(2,1)S(1)}, bf16[256,1024]{1,0:T(8,128)(2,1)S(1)}, u32[]{:S(2)}, u32[]{:S(2)}) collective-permute-start(bf16[256,1024]{1,0:T(8,128)(2,1)S(1)} %get-tuple-element.150), channel_id=1, source_target_pairs={{0,1},{1,2},{2,3},{4,5},{5,6},{6,7},{8,9},{9,10},{10,11},{12,13},{... | collective-permute-start | bytes 1572872 | tf_op jit(solution)/shard_map/ppermute | solution.py:1175
  587.8 24.0 %collective-permute-start.49 = (bf16[256,1024]{1,0:T(8,128)(2,1)S(1)}, bf16[256,1024]{1,0:T(8,128)(2,1)S(1)}, u32[]{:S(2)}, u32[]{:S(2)}) collective-permute-start(bf16[256,1024]{1,0:T(8,128)(2,1)S(1)} %get-tuple-element.151), channel_id=1, source_target_pairs={{3,2},{2,1},{1,0},{7,6},{6,5},{5,4},{11,10},{10,9},{9,8},{15,14},{... | collective-permute-start | bytes 1572872 | tf_op jit(solution)/shard_map/ppermute | solution.py:1176
  590.7 33.7 %collective-permute-start.60 = (bf16[256,1024]{1,0:T(8,128)(2,1)}, bf16[256,1024]{1,0:T(8,128)(2,1)S(1)}, u32[]{:S(2)}, u32[]{:S(2)}) collective-permute-start(bf16[256,1024]{1,0:T(8,128)(2,1)} %get-tuple-element.161), channel_id=1, source_target_pairs={{0,1},{1,2},{2,3},{4,5},{5,6},{6,7},{8,9},{9,10},{10,11},{12,13},{... | collective-permute-start | bytes 1572872 | tf_op jit(solution)/shard_map/ppermute | solution.py:1175
  599.0 25.9 %collective-permute-start.61 = (bf16[256,1024]{1,0:T(8,128)(2,1)S(1)}, bf16[256,1024]{1,0:T(8,128)(2,1)}, u32[]{:S(2)}, u32[]{:S(2)}) collective-permute-start(bf16[256,1024]{1,0:T(8,128)(2,1)S(1)} %get-tuple-element.162), channel_id=1, source_target_pairs={{3,2},{2,1},{1,0},{7,6},{6,5},{5,4},{11,10},{10,9},{9,8},{15,14},{... | collective-permute-start | bytes 1572872 | tf_op jit(solution)/shard_map/ppermute | solution.py:1176
  601.4 36.6 %collective-permute-start.54 = (bf16[256,1024]{1,0:T(8,128)(2,1)S(1)}, bf16[256,1024]{1,0:T(8,128)(2,1)S(1)}, u32[]{:S(2)}, u32[]{:S(2)}) collective-permute-start(bf16[256,1024]{1,0:T(8,128)(2,1)S(1)} %get-tuple-element.157), channel_id=1, source_target_pairs={{0,1},{1,2},{2,3},{4,5},{5,6},{6,7},{8,9},{9,10},{10,11},{12,13},{... | collective-permute-start | bytes 1572872 | tf_op jit(solution)/shard_map/ppermute | solution.py:1175
  610.2 27.8 %collective-permute-start.55 = (bf16[256,1024]{1,0:T(8,128)(2,1)S(1)}, bf16[256,1024]{1,0:T(8,128)(2,1)}, u32[]{:S(2)}, u32[]{:S(2)}) collective-permute-start(bf16[256,1024]{1,0:T(8,128)(2,1)S(1)} %get-tuple-element.158), channel_id=1, source_target_pairs={{3,2},{2,1},{1,0},{7,6},{6,5},{5,4},{11,10},{10,9},{9,8},{15,14},{... | collective-permute-start | bytes 1572872 | tf_op jit(solution)/shard_map/ppermute | solution.py:1176
  619.1 14.9 %collective-permute-start.68 = (f32[3,1024]{1,0:T(4,128)S(1)}, f32[3,1024]{1,0:T(4,128)S(1)}, u32[]{:S(2)}, u32[]{:S(2)}) collective-permute-start(f32[3,1024]{1,0:T(4,128)S(1)} %get-tuple-element.234), channel_id=1, source_target_pairs={{0,16},{16,0},{1,17},{17,1},{2,18},{18,2},{3,19},{19,3},{4,20},{20... | collective-permute-start | bytes 36872 | tf_op jit(solution)/shard_map/ppermute | solution.py:1004
  624.4 10.2 %collective-permute-start.62 = (bf16[256,512]{1,0:T(8,128)(2,1)S(1)}, bf16[256,512]{1,0:T(8,128)(2,1)S(1)}, u32[]{:S(2)}, u32[]{:S(2)}) collective-permute-start(bf16[256,512]{1,0:T(8,128)(2,1)S(1)} %bitcast.125), channel_id=1, source_target_pairs={{0,16},{16,0},{1,17},{17,1},{2,18},{18,2},{3,19},{19,3},{4,20},{20... | collective-permute-start | bytes 786440 | tf_op jit(solution)/shard_map/ppermute | solution.py:1222
  632.5 12.8 %collective-permute-start.64 = (bf16[256,512]{1,0:T(8,128)(2,1)S(1)}, bf16[256,512]{1,0:T(8,128)(2,1)S(1)}, u32[]{:S(2)}, u32[]{:S(2)}) collective-permute-start(bf16[256,512]{1,0:T(8,128)(2,1)S(1)} %bitcast.126), channel_id=1, source_target_pairs={{0,16},{16,0},{1,17},{17,1},{2,18},{18,2},{3,19},{19,3},{4,20},{20... | collective-permute-start | bytes 786440 | tf_op jit(solution)/shard_map/ppermute | solution.py:1222
  637.4 20.2 %collective-permute-start.67 = (bf16[256,512]{1,0:T(8,128)(2,1)S(1)}, bf16[256,512]{1,0:T(8,128)(2,1)S(1)}, u32[]{:S(2)}, u32[]{:S(2)}) collective-permute-start(bf16[256,512]{1,0:T(8,128)(2,1)S(1)} %get-tuple-element.169.refs_7_.refs_0_), channel_id=1, source_target_pairs={{0,16},{16,0},{1,17},{17,1},{2,18},{18,2},{3,19},{19,3},{4,20},{20... | collective-permute-start | bytes 786440 | tf_op jit(solution)/shard_map/ppermute | solution.py:1222
  643.8 8.8 %collective-permute-start.63 = (bf16[256,512]{1,0:T(8,128)(2,1)S(1)}, bf16[256,512]{1,0:T(8,128)(2,1)S(1)}, u32[]{:S(2)}, u32[]{:S(2)}) collective-permute-start(bf16[256,512]{1,0:T(8,128)(2,1)S(1)} %bitcast.127), channel_id=1, source_target_pairs={{0,16},{16,0},{1,17},{17,1},{2,18},{18,2},{3,19},{19,3},{4,20},{20... | collective-permute-start | bytes 786440 | tf_op jit(solution)/shard_map/ppermute | solution.py:1222
  648.0 10.8 %collective-permute-start.66 = (bf16[256,512]{1,0:T(8,128)(2,1)S(1)}, bf16[256,512]{1,0:T(8,128)(2,1)S(1)}, u32[]{:S(2)}, u32[]{:S(2)}) collective-permute-start(bf16[256,512]{1,0:T(8,128)(2,1)S(1)} %get-tuple-element.183.refs_0_), channel_id=1, source_target_pairs={{0,16},{16,0},{1,17},{17,1},{2,18},{18,2},{3,19},{19,3},{4,20},{20... | collective-permute-start | bytes 786440 | tf_op jit(solution)/shard_map/ppermute | solution.py:1222
  (97 other events, 1827.8 us)
Sparse Core Ops, SparseCore 0:
  10.7 143.6 all-gather.4
  323.1 132.9 all-gather.6
  527.0 41.0 all-gather.8
